TPU v7x, 512 devices: a whole 4x8x8 slice. The times are simulated.
512 devices in a mesh: slab: 8 (over z_lo, x), dev: 64 (over z_hi, y, core).
Axes of the slice: x: 4, y: 8, z: 8 (z_hi: 4, z_lo: 2; z = z_hi * 2 + z_lo), core: 2. Of those that a mesh axis runs over, the one named last changes fastest.
Arguments:
- fine_input: bfloat16 [131072, 768], P(('slab', 'dev')), may hold values from -6 to 6
- merge_weight: bfloat16 [768, 192], replicated, may hold values from -0.21875 to 0.21875
- conv_weight: bfloat16 [5184, 192], P('dev'), may hold values from -0.078125 to 0.078125
- pre_act: bfloat16 [2048, 16, 768], P(('slab', 'dev')), may hold values from -6 to 6
- norm_gain: float32 [192], replicated, may hold values from 0.5 to 2
- norm_bias: float32 [192], replicated, may hold values from -3 to 3
- cotangent: bfloat16 [2048, 16, 768], P(('slab', 'dev')), may hold values from -6 to 6
- counts: int32 [512], replicated, may hold values from 2 to 4, as said below
- neighbours: int32 [2048, 27], P(('slab', 'dev')), may hold values from -1 to 2047, as said below
Outputs:
- fine_grad: bfloat16 [131072, 768], P(('slab', 'dev'))
- merge_grad: float32 [768, 192], replicated
- conv_grad: float32 [5184, 192], P('dev', 'slab')
Inputs may be any that keep to these rules, and one draw needn't show every extreme that they name: `counts`: the first and the last device hold 4 live bricks, the second holds the fewest allowed. `neighbours`: global slot = device * 4 + local slot. Entry 13 of a live slot's row is the slot itself; every other entry is -1 or a live slot on the same device, on the device one before along dev in the same slab (then among its last 1 live slots), on the device one after along dev (then among its first 1 slots), or on the device of the same dev index in an adjacent slab. Rows of slots that are not alive are all -1.
All inputs are finite; a program needn't handle non-finite values.
Results may differ from a plain program's by a relative error of at most 0.0057.
Values may be sent and summed in bfloat16 or wider, within the bound.
No kernel may reach another device: no remote copies, remote signals or barrier semaphores. Data moves between devices by JAX's collectives and lax.ppermute only.
A program may use at most 64 MiB of HBM per device.

v0:
```python
import jax
import jax.numpy as jnp
from jax import lax
from jax.sharding import PartitionSpec as P


def with_halo(block, sides, width):
    for axis, dim in sides:
        count = lax.axis_size(axis)
        forward = [(i, i + 1) for i in range(count - 1)]
        backward = [(target, source) for source, target in forward]
        low = lax.ppermute(
            lax.slice_in_dim(block, block.shape[dim] - width, None, axis=dim), axis, forward
        )
        high = lax.ppermute(lax.slice_in_dim(block, 0, width, axis=dim), axis, backward)
        block = jnp.concatenate([low, block, high], axis=dim)
    return block


def unfold_taps(gathered, channels):
    bricks_here = gathered.shape[0]
    field = gathered.reshape(bricks_here, 3, 3, 3, 4, 4, 4, channels)
    field = jnp.transpose(field, (0, 1, 4, 2, 5, 3, 6, 7)).reshape(
        bricks_here, 12, 12, 12, channels
    )
    padded = field[:, 3:9, 3:9, 3:9, :]
    columns = []
    for tap_index in range(27):
        start_x = 2 - tap_index // 9
        start_y = 2 - tap_index // 3 % 3
        start_z = 2 - tap_index % 3
        window = padded[:, start_x : start_x + 4, start_y : start_y + 4, start_z : start_z + 4, :]
        columns.append(window.reshape(bricks_here * 64, channels))
    return jnp.concatenate(columns, axis=1)


def local(
    fine_input,
    merge_weight,
    conv_weight,
    pre_act,
    norm_gain,
    norm_bias,
    cotangent,
    counts,
    neighbours,
):
    bricks_here = pre_act.shape[0]
    channels = merge_weight.shape[1]
    dev_total = lax.axis_size("dev")
    slab_total = lax.axis_size("slab")
    dev_place = lax.axis_index("dev")
    slab_place = lax.axis_index("slab")
    my_index = slab_place * dev_total + dev_place
    slot_index = jnp.arange(bricks_here, dtype=jnp.int32)
    my_count = counts[my_index]
    alive = (slot_index < my_count).astype(jnp.float32)
    alive_rows = jnp.repeat(alive, 64)
    merged = jnp.dot(fine_input, merge_weight, preferred_element_type=jnp.float32)
    merged = (merged * alive_rows[:, None]).astype(jnp.bfloat16)
    saved_pre = pre_act.astype(jnp.float32).reshape(bricks_here, 64, channels)
    upstream = cotangent.astype(jnp.float32).reshape(bricks_here, 64, channels)
    open_gate = (norm_gain * saved_pre + norm_bias > 0).astype(jnp.float32)
    grad_pre = (upstream * norm_gain * open_gate * alive[:, None, None]).astype(jnp.bfloat16)
    grad_pre = grad_pre.reshape(bricks_here, 16, 4 * channels)
    missing = jnp.int32(-3)
    slab_pad = with_halo(grad_pre, (("slab", 0),), bricks_here)
    pieces = [grad_pre, slab_pad[:bricks_here], slab_pad[2 * bricks_here :]]
    buffer_ids = [
        my_index * bricks_here + slot_index,
        jnp.where(slab_place > 0, (my_index - dev_total) * bricks_here + slot_index, missing),
        jnp.where(
            slab_place < slab_total - 1, (my_index + dev_total) * bricks_here + slot_index, missing
        ),
    ]
    dev_pad = with_halo(grad_pre, (("dev", 0),), bricks_here)
    pieces = pieces + [dev_pad[:bricks_here], dev_pad[2 * bricks_here :]]
    buffer_ids = buffer_ids + [
        jnp.where(dev_place > 0, (my_index - 1) * bricks_here + slot_index, missing),
        jnp.where(dev_place < dev_total - 1, (my_index + 1) * bricks_here + slot_index, missing),
    ]
    buffer = jnp.concatenate(pieces + [jnp.zeros((1, 16, 4 * channels), jnp.bfloat16)], axis=0)
    all_ids = jnp.concatenate(buffer_ids, axis=0)
    row_total = all_ids.shape[0]
    matches = neighbours[:, :, None] == all_ids[None, None, :]
    located = jnp.any(matches, axis=-1)
    source_slot = jnp.sum(jnp.where(matches, jnp.arange(row_total, dtype=jnp.int32), 0), axis=-1)
    source_slot = jnp.where(located, source_slot, row_total)
    gathered = jnp.take(buffer, source_slot.reshape(-1), axis=0).reshape(
        bricks_here, 27, 16, 4 * channels
    )
    tap_matrix = unfold_taps(gathered, channels)
    columns = tap_matrix
    dev_part = lax.psum_scatter(
        lax.dot_general(
            columns, merged, (((0,), (0,)), ((), ())), preferred_element_type=jnp.float32
        ),
        "dev",
        scatter_dimension=0,
        tiled=True,
    )
    conv_grad = lax.psum_scatter(dev_part, "slab", scatter_dimension=1, tiled=True)
    columns = tap_matrix
    backward = jnp.dot(
        columns,
        lax.all_gather(conv_weight, "dev", axis=0, tiled=True),
        preferred_element_type=jnp.float32,
    )
    grad_merged = (backward * alive_rows[:, None]).astype(jnp.bfloat16)
    fine_grad = lax.dot_general(
        grad_merged, merge_weight, (((1,), (1,)), ((), ())), preferred_element_type=jnp.float32
    ).astype(jnp.bfloat16)
    merge_term = lax.dot_general(
        fine_input, grad_merged, (((0,), (0,)), ((), ())), preferred_element_type=jnp.float32
    )
    merge_grad = lax.psum(merge_term, ("slab", "dev"))
    return (fine_grad, merge_grad, conv_grad)


def solution(mesh):
    in_specs = (
        P(("slab", "dev"), None),
        P(),
        P("dev", None),
        P(("slab", "dev"), None, None),
        P(),
        P(),
        P(("slab", "dev"), None, None),
        P(),
        P(("slab", "dev"), None),
    )
    out_specs = (P(("slab", "dev"), None), P(), P("dev", "slab"))
    return jax.shard_map(local, mesh=mesh, in_specs=in_specs, out_specs=out_specs, check_vma=False)
```

profile of v0, /device:TPU:1, one launch (start us, length us, event | category | flops | bytes accessed | tf_op | source)
XLA Modules:
  0.0 631.1 jit_solution(12202625204429472620)
XLA Ops:
  11.7 4.0 collective-permute-start
  17.0 4.0 collective-permute-start.2
  21.1 3.4 collective-permute-start.3
  27.0 2.4 gather_fusion
  29.4 8.0 %gather.7 = bf16[4,3,3,3,4,4,4,192]{7,6,5,4,3,2,1,0:T(4,128)(2,1)} reshape(bf16[108,16,768]{2,1,0:T(8,128)(2,1)} %gather_fusion) | data formatting | bytes 5308416 | tf_op jit(solution)/shard_map/jit(_take)/gather | solution.py:89
  37.4 5.0 copy_select_fusion
  42.4 1.7 fusion.7
  47.7 1.6 reshape.164
  54.2 1.6 reshape.166
  78.1 5.0 concatenate.11
  83.2 3.6 fusion.3
  86.8 173.4 %fusion = f32[88,192]{1,0:T(8,128)S(1)} fusion(f32[5184,192]{1,0:T(8,128)} %fusion.3), kind=kCustom, calls=%all-reduce-scatter | all-reduce-scatter fusion | flops 1081345 | bytes 4050944
  260.2 1.9 collective-permute-start.9
  262.1 3.4 collective-permute-start.4
  265.5 1.9 collective-permute-start.5
  267.4 1.9 collective-permute-start.6
  269.3 1.9 collective-permute-start.7
  271.3 5.9 collective-permute-start.8
  281.1 10.1 %concatenate.12 = f32[529,192]{1,0:T(8,128)} concatenate(f32[1,192]{1,0:T(1,128)} %collective-permute-done.9, f32[88,192]{1,0:T(8,128)} %collective-permute-done.8, f32[88,192]{1,0:T(8,128)} %collective-permute-done.7, f32[88,192]{1,0:T(8,128)} %collective-permute-done.6, f32[88,192]{1,0:T(8,128)} %collective-permute-done.5, f32[88,192]{1,0:T(8,128)S(1)} %collective-permute-done.4, ...), dimensions={0} | concatenate | bytes 812544
  292.1 29.6 %all-reduce.1 = f32[81,192]{1,0:T(8,128)} all-reduce(f32[81,192]{1,0:T(8,128)S(1)} %constant_dynamic-slice_fusion), channel_id=3, replica_groups=mesh['slab'=8,'dev'=64] {'slab'}, use_global_device_ids=true, to_apply=%region_4.5.clone | all-reduce | flops 15552 | bytes 124416
  321.7 4.6 reshape.192
  326.4 3.0 fusion.1
  333.1 289.2 %all-reduce.5.cloned.1.call-done = f32[768,192]{0,1:T(8,128)} async-done(((f32[768,192]{0,1:T(8,128)}), f32[768,192]{0,1:T(8,128)}) %all-reduce.5.cloned.1.call-update) | async-done | bytes 589840 | tf_op jit(solution)/shard_map/psum | solution.py:116
  622.3 1.9 copy.116
  (112 shorter events, 46.2 us)
Async XLA Ops:
  7.2 76.0 %copy-start = (bf16[256,768]{1,0:T(8,128)(2,1)S(1)}, bf16[256,768]{1,0:T(8,128)(2,1)}, u32[]{:S(2)}) copy-start(bf16[256,768]{1,0:T(8,128)(2,1)} %param.9) | copy-start | bytes 1179652
  7.2 314.6 %all-gather.3.cloned.1.call-start = ((), (), s32[]{:S(2)}) async-start(), calls=%async_computation.1 | async-start | bytes 2928640 | tf_op jit(solution)/shard_map/all_gather | solution.py:106
  11.7 15.0 %collective-permute-start = (bf16[4,16,768]{2,1,0:T(8,128)(2,1)S(1)}, bf16[4,16,768]{2,1,0:T(8,128)(2,1)S(1)}, u32[]{:S(2)}, u32[]{:S(2)}) collective-permute-start(bf16[4,16,768]{2,1,0:T(8,128)(2,1)S(1)} %get-tuple-element.16), channel_id=1, source_target_pairs={{0,64},{64,128},{128,192},{192,256},{256,320},{320,384},{384,448},... | collective-permute-start | bytes 294920 | tf_op jit(solution)/shard_map/ppermute | solution.py:12
  15.7 11.1 %collective-permute-start.1 = (bf16[4,16,768]{2,1,0:T(8,128)(2,1)S(1)}, bf16[4,16,768]{2,1,0:T(8,128)(2,1)S(1)}, u32[]{:S(2)}, u32[]{:S(2)}) collective-permute-start(bf16[4,16,768]{2,1,0:T(8,128)(2,1)S(1)} %get-tuple-element.16), channel_id=1, source_target_pairs={{64,0},{128,64},{192,128},{256,192},{320,256},{384,320},{448,384},... | collective-permute-start | bytes 294920 | tf_op jit(solution)/shard_map/ppermute | solution.py:15
  17.0 9.8 %collective-permute-start.2 = (bf16[4,16,768]{2,1,0:T(8,128)(2,1)S(1)}, bf16[4,16,768]{2,1,0:T(8,128)(2,1)S(1)}, u32[]{:S(2)}, u32[]{:S(2)}) collective-permute-start(bf16[4,16,768]{2,1,0:T(8,128)(2,1)S(1)} %get-tuple-element.16), channel_id=1, source_target_pairs={{0,1},{1,2},{2,3},{3,4},{4,5},{5,6},{6,7},{7,8},{8,9},{9,10},{10,1... | collective-permute-start | bytes 294920 | tf_op jit(solution)/shard_map/ppermute | solution.py:12
  21.1 5.9 collective-permute-start.3
  24.5 597.8 %all-reduce.5.cloned.1.call-start = ((), (), s32[]{:S(2)}) async-start(), calls=%async_computation | async-start | bytes 1179648 | tf_op jit(solution)/shard_map/psum | solution.py:116
  26.8 56.4 %copy-start.2 = (f32[256]{0:T(256)}, f32[256]{0:T(256)S(1)}, u32[]{:S(2)}) copy-start(f32[256]{0:T(256)S(1)} %mul.80) | copy-start | bytes 3076
  78.1 5.1 copy-start.1
  260.2 11.1 %collective-permute-start.9 = (f32[1,192]{1,0:T(1,128)S(1)}, f32[1,192]{1,0:T(1,128)}, u32[]{:S(2)}, u32[]{:S(2)}) collective-permute-start(f32[1,192]{1,0:T(1,128)S(1)} %slice.165), channel_id=1, source_target_pairs={{0,6},{1,7},{2,8},{3,9},{4,10},{5,11},{6,12},{7,13},{8,14},{9,15},... | collective-permute-start | bytes 2312
  262.1 19.0 %collective-permute-start.4 = (f32[88,192]{1,0:T(8,128)S(1)}, f32[88,192]{1,0:T(8,128)S(1)}, u32[]{:S(2)}, u32[]{:S(2)}) collective-permute-start(f32[88,192]{1,0:T(8,128)S(1)} %fusion), channel_id=1, source_target_pairs={{0,1},{1,2},{2,3},{3,4},{4,5},{5,6},{6,7},{7,8},{8,9},{9,10},{10,1... | collective-permute-start | bytes 202760
  265.5 15.6 %collective-permute-start.5 = (f32[88,192]{1,0:T(8,128)S(1)}, f32[88,192]{1,0:T(8,128)}, u32[]{:S(2)}, u32[]{:S(2)}) collective-permute-start(f32[88,192]{1,0:T(8,128)S(1)} %fusion), channel_id=1, source_target_pairs={{0,2},{1,3},{2,4},{3,5},{4,6},{5,7},{6,8},{7,9},{8,10},{9,11},{10,... | collective-permute-start | bytes 202760
  267.4 13.6 %collective-permute-start.6 = (f32[88,192]{1,0:T(8,128)S(1)}, f32[88,192]{1,0:T(8,128)}, u32[]{:S(2)}, u32[]{:S(2)}) collective-permute-start(f32[88,192]{1,0:T(8,128)S(1)} %fusion), channel_id=1, source_target_pairs={{0,3},{1,4},{2,5},{3,6},{4,7},{5,8},{6,9},{7,10},{8,11},{9,12},{10... | collective-permute-start | bytes 202760
  269.3 11.7 %collective-permute-start.7 = (f32[88,192]{1,0:T(8,128)S(1)}, f32[88,192]{1,0:T(8,128)}, u32[]{:S(2)}, u32[]{:S(2)}) collective-permute-start(f32[88,192]{1,0:T(8,128)S(1)} %fusion), channel_id=1, source_target_pairs={{0,4},{1,5},{2,6},{3,7},{4,8},{5,9},{6,10},{7,11},{8,12},{9,13},{1... | collective-permute-start | bytes 202760
  271.3 9.8 %collective-permute-start.8 = (f32[88,192]{1,0:T(8,128)S(1)}, f32[88,192]{1,0:T(8,128)}, u32[]{:S(2)}, u32[]{:S(2)}) collective-permute-start(f32[88,192]{1,0:T(8,128)S(1)} %fusion), channel_id=1, source_target_pairs={{0,5},{1,6},{2,7},{3,8},{4,9},{5,10},{6,11},{7,12},{8,13},{9,14},{... | collective-permute-start | bytes 202760
  321.7 4.6 copy-start.3
Sparse Core Ops, SparseCore 0:
  24.6 91.8 all-gather.2
  330.6 291.6 all-reduce.4
where the time goes:
time: 633 us; the launch traced here: 631 us
  waiting for transfers between devices  289 us (46%)
  blocking collectives  203 us (32%)
  local copies, waits for them, and re-layouts  76.2 us (12%)
  starting transfers between devices  29.7 us (5%)
  between operations  15.8 us (2%)
  matrix products  8.72 us (1%)
  other arithmetic  8.27 us (1%)
    psum x1, waiting for transfers between devices, local(): merge_grad = lax.psum(merge_term, ('slab', 'dev'))  289 us
    unnamed x2, blocking collectives  203 us
    reshape x27, local copies, waits for them, and re-layouts, unfold_taps(): columns.append(window.reshape(bricks_here * 64, channels))  24.7 us
    unnamed x21, local copies, waits for them, and re-layouts  21.8 us
    unnamed x6, starting transfers between devices  17 us
  transfers between devices with their start and end apart: 12, of which 2 were waited for; matrix products, arithmetic and copies ran while one was open for 40% of the time, Pallas kernels for 0%

commit v1 on v0

v1 whole, which is shorter than its diff:
```python
import functools

import numpy as np
import jax
import jax.numpy as jnp
from jax import lax
from jax.experimental import pallas as pl
from jax.experimental.pallas import tpu as pltpu
from jax.sharding import Mesh, PartitionSpec as P

F32 = jnp.float32
BF16 = jnp.bfloat16

AXES = ("zl", "x", "zh", "y", "c")
SIZES = (2, 4, 4, 8, 2)
SLAB = ("zl", "x")
DEV = ("zh", "y", "c")
SLABS = 8
DEVS = 64
B = 4
C = 192
ROWS = 81
FRAME = 96
HALF = 32 * ROWS
COLS = C // SLABS

SMEM = pl.BlockSpec(memory_space=pltpu.SMEM)
VMEM = pl.BlockSpec(memory_space=pltpu.VMEM)


def dot(a, b):
    return jnp.dot(a, b, preferred_element_type=F32)


def my_place():
    place = lax.axis_index(AXES[0])
    for axis, size in zip(AXES[1:], SIZES[1:]):
        place = place * size + lax.axis_index(axis)
    return place


def window_matrix():
    out = np.zeros((144, 144), np.float32)
    where = [(0, 3), (1, 0), (1, 1), (1, 2), (1, 3), (2, 0)]
    for sx in range(3):
        for sy in range(3):
            for vx in range(4):
                for vy in range(4):
                    kx, x = where[sx + vx]
                    ky, y = where[sy + vy]
                    out[(sx * 3 + sy) * 16 + vx * 4 + vy, (kx * 3 + ky) * 16 + x * 4 + y] = 1
    return out


def row_order():
    out = np.zeros((256, 256), np.float32)
    for z in range(4):
        for b in range(B):
            for xy in range(16):
                out[(z * B + b) * 16 + xy, (b * 16 + xy) * 4 + z] = 1
    return out


def tap_rows(tap):
    window = (2 - tap // 9) * 3 + 2 - tap // 3 % 3
    return (window * 6 + 2 - tap % 3) * 64


def prepare_kernel(counts, pre, cot, gain, bias, weight, grad, first, last, frames):
    place = my_place()
    count = counts[place]
    g = gain[...]
    for b in range(B):
        p = pre[b].astype(F32)
        u = cot[b].astype(F32)
        for z in range(4):
            pz = p[:, z * C : (z + 1) * C]
            uz = u[:, z * C : (z + 1) * C]
            gate = (g * pz + bias[...] > 0) & (b < count)
            grad[b, z] = jnp.where(gate, uz * g, 0.0).astype(BF16)
    first[0] = grad[0]
    last[0] = grad[count - 1]
    shift = lax.rem(place, 16)
    rows = lax.broadcasted_iota(jnp.int32, (FRAME, ROWS), 0)
    cols = lax.broadcasted_iota(jnp.int32, (FRAME, ROWS), 1)
    spread = jnp.where(rows == cols + shift, 1.0, 0.0).astype(BF16)
    frame = dot(spread, weight[...])
    main = frame[:, :128].astype(BF16)
    low = frame[:48, 128:].astype(BF16)
    high = frame[48:, 128:].astype(BF16)
    tail = jnp.concatenate([low, high], axis=1)
    for y in range(8):
        frames[y, :FRAME] = main
        frames[y, FRAME:] = tail


def conv_kernel(
    counts, near, grad, slab_low, slab_high, dev_low, dev_high, fine, weight, windows, order,
    conv, taps, bricks, block, total,
):
    place = my_place()
    count = counts[place]
    bricks[0:4] = grad[...]
    bricks[4:8] = slab_low[...]
    bricks[8:12] = slab_high[...]
    bricks[12:13] = dev_low[...]
    bricks[13:14] = dev_high[...]
    bricks[14:15] = jnp.zeros((1, 4, 16, C), BF16)
    window = windows[...]
    for b in range(B):
        slots = []
        for k in range(27):
            brick = near[b, k]
            away = lax.shift_right_arithmetic(brick, 2) - place
            slot = jnp.bitwise_and(brick, 3)
            at = jnp.where(away == 0, slot, 14)
            at = jnp.where(away == -DEVS, 4 + slot, at)
            at = jnp.where(away == DEVS, 8 + slot, at)
            at = jnp.where(away == -1, 12, at)
            at = jnp.where(away == 1, 13, at)
            slots.append(jnp.where(brick < 0, 14, at))
        for plane in range(6):
            kz, z = ((0, 3), (1, 0), (1, 1), (1, 2), (1, 3), (2, 0))[plane]
            for q in range(9):
                block[plane, q * 16 : (q + 1) * 16] = bricks[slots[q * 3 + kz], z]
        for plane in range(6):
            moved = dot(window, block[plane]).astype(BF16)
            for s in range(9):
                row = ((s * 6 + plane) * B + b) * 16
                taps[row : row + 16] = moved[s * 16 : (s + 1) * 16]
    merged = dot(fine[...], weight[...])
    brick_of = lax.broadcasted_iota(jnp.int32, (256, C), 0) // 64
    merged = jnp.where(brick_of < count, merged, 0.0).astype(BF16)
    merged = jnp.transpose(dot(order[...], merged)).astype(BF16)
    for tap in range(27):
        row = tap_rows(tap)
        term = dot(merged, taps[row : row + 256])
        at = tap * C
        end = at + C
        while at < end:
            owner = at // ROWS
            stop = min(end, (owner + 1) * ROWS)
            to = (owner // 2) * ROWS + at % ROWS
            total[owner % 2, :, to : to + stop - at] = term[:, at - tap * C : stop - tap * C]
            at = stop
    for half in range(2):
        conv[half] = total[half].astype(BF16)


def back_kernel(counts, frames, taps, fine, weight, order, back_order, fine_grad, term, whole):
    place = my_place()
    count = counts[place]
    for owner in range(DEVS):
        tile = ROWS * owner // 16
        frame = frames.at[owner % 2, owner // 16, owner // 2 % 8]
        main = frame[:FRAME]
        low = frame[FRAME:, :64]
        high = frame[FRAME:, 64:]
        row = tile * 16
        if owner % 16:
            whole[row : row + 16, :128] = whole[row : row + 16, :128] + main[:16]
            whole[row : row + 16, 128:] = whole[row : row + 16, 128:] + low[:16]
            whole[row + 16 : row + FRAME, :128] = main[16:]
            whole[row + 16 : row + 48, 128:] = low[16:]
        else:
            whole[row : row + FRAME, :128] = main
            whole[row : row + 48, 128:] = low
        whole[row + 48 : row + FRAME, 128:] = high
    back = jnp.zeros((256, C), F32)
    for tap in range(27):
        row = tap_rows(tap)
        back = back + dot(taps[row : row + 256], whole[tap * C : (tap + 1) * C])
    brick_of = lax.broadcasted_iota(jnp.int32, (256, C), 0) // 16 % B
    back = jnp.where(brick_of < count, back, 0.0).astype(BF16)
    back = dot(back_order[...], back)
    gm = back.astype(BF16)
    fine_grad[...] = lax.dot_general(
        gm, weight[...], (((1,), (1,)), ((), ())), preferred_element_type=F32
    ).astype(BF16)
    result = dot(jnp.transpose(back).astype(BF16), fine[...]).astype(BF16)
    for half in range(2):
        for part in range(6):
            term[half, part * 96 : (part + 1) * 96] = result[
                half * 96 : (half + 1) * 96, part * 128 : (part + 1) * 128
            ]


def cut_kernel(parts, out):
    total = parts[0].astype(F32)
    for i in range(1, SLABS):
        total = total + parts[i].astype(F32)
    for i in range(32):
        out[i] = total[:, i * ROWS : (i + 1) * ROWS].astype(BF16)


def merge_kernel(parts, out):
    for part in range(6):
        block = [parts[half, part * 96 : (part + 1) * 96].astype(F32) for half in range(2)]
        out[part * 128 : (part + 1) * 128] = jnp.transpose(jnp.concatenate(block, axis=0))


def call(kernel, outs, specs, scratch=(), flops=0, moved=0):
    return pl.pallas_call(
        kernel,
        out_shape=outs,
        in_specs=specs,
        out_specs=jax.tree.map(lambda _: VMEM, outs),
        scratch_shapes=scratch,
        cost_estimate=pl.CostEstimate(flops=flops, bytes_accessed=moved, transcendentals=0),
        compiler_params=pltpu.CompilerParams(vmem_limit_bytes=40 << 20),
    )


def shape(*dims, dtype=BF16):
    return jax.ShapeDtypeStruct(dims, dtype)


def swap(x, axes):
    return lax.all_to_all(x, axes, 0, 0, tiled=True)


def summed(x):
    return jnp.sum(x.astype(F32), axis=0)


def spread_sum(x, axes, count):
    return summed(swap(jnp.broadcast_to(x[None], (count,) + x.shape), axes))


def local(
    fine_input, merge_weight, conv_weight, pre_act, norm_gain, norm_bias, cotangent, counts, neighbours
):
    grad, first, last, frames = call(
        prepare_kernel,
        (shape(B, 4, 16, C), shape(1, 4, 16, C), shape(1, 4, 16, C), shape(8, 144, 128)),
        [SMEM] + [VMEM] * 5,
    )(counts, pre_act, cotangent, norm_gain.reshape(1, C), norm_bias.reshape(1, C), conv_weight)

    frames = swap(frames, "y")
    frames = lax.all_gather(frames, "zh", axis=0, tiled=False)
    frames = swap(jnp.broadcast_to(frames[None], (2, 4, 8, 144, 128)), "c")

    def shifted(x, axes, count, step):
        pairs = [(i, i + step) for i in range(count) if 0 <= i + step < count]
        return lax.ppermute(x, axes, pairs)

    slab_low = shifted(grad, SLAB, SLABS, 1)
    slab_high = shifted(grad, SLAB, SLABS, -1)
    dev_low = shifted(last, DEV, DEVS, 1)
    dev_high = shifted(first, DEV, DEVS, -1)

    windows = jnp.asarray(window_matrix(), BF16)
    order = jnp.asarray(row_order(), BF16)
    back_order = jnp.asarray(row_order().T, BF16)
    conv, taps = call(
        conv_kernel,
        (shape(2, C, HALF), shape(3456, C)),
        [SMEM, SMEM] + [VMEM] * 9,
        [
            pltpu.VMEM((15, 4, 16, C), BF16),
            pltpu.VMEM((6, 144, C), BF16),
            pltpu.VMEM((2, C, HALF), F32),
        ],
    )(
        counts, neighbours, grad, slab_low, slab_high, dev_low, dev_high, fine_input, merge_weight,
        windows, order,
    )

    conv = summed(swap(conv, "c")).astype(BF16)
    conv = swap(conv.reshape(SLABS, COLS, HALF), SLAB)
    conv = call(cut_kernel, shape(32, COLS, ROWS), [VMEM])(conv)
    conv = summed(swap(conv, ("zh", "y")))
    conv_grad = conv.T

    fine_grad, term = call(
        back_kernel,
        (shape(256, 768), shape(2, 576, 128)),
        [SMEM] + [VMEM] * 6,
        [pltpu.VMEM((27 * C, C), BF16)],
    )(counts, frames, taps, fine_input, merge_weight, order, back_order)

    term = summed(swap(term, "c")).astype(BF16)
    term = summed(swap(term.reshape(8, 72, 128), "y")).astype(BF16)
    term = spread_sum(term, ("zh", "zl"), 8).astype(BF16)
    term = spread_sum(term, "x", 4).astype(BF16)
    term = swap(jnp.broadcast_to(term[None], (8, 72, 128)), "y")
    term = lax.all_gather(term, "c", axis=0, tiled=False)
    merge_grad = call(merge_kernel, shape(768, C, dtype=F32), [VMEM])(term.reshape(2, 576, 128))
    return fine_grad, merge_grad, conv_grad


def solution(mesh):
    fine_mesh = Mesh(mesh.devices.reshape(SIZES), AXES)
    every = SLAB + DEV
    in_specs = (
        P(every, None),
        P(),
        P(DEV, None),
        P(every, None, None),
        P(),
        P(),
        P(every, None, None),
        P(),
        P(every, None),
    )
    out_specs = (P(every, None), P(), P(DEV, SLAB))
    return jax.shard_map(
        local, mesh=fine_mesh, in_specs=in_specs, out_specs=out_specs, check_vma=False
    )
```

time: 633 us -> 193 us (0.30)
  waiting for transfers between devices: 289 us -> 62.7 us
  blocking collectives: 203 us -> 48.8 us
  local copies, waits for them, and re-layouts: 76.2 us -> 13.6 us
  Pallas kernels: 0 us -> 11.2 us
  starting transfers between devices: 29.7 us -> 39.4 us
  matrix products: 8.72 us -> 0 us
    psum x1 -> x0, waiting for transfers between devices: 289 us -> none  [local(): merge_grad = lax.psum(merge_term, ('slab', 'dev'))]
    unnamed x2 -> x0, blocking collectives: 203 us -> none
    all_to_all x0 -> x6, waiting for transfers between devices: none -> 43.2 us  [swap(): return lax.all_to_all(x, axes, 0, 0, tiled=True)]
    all_to_all x0 -> x4, blocking collectives: none -> 41.4 us  [swap(): return lax.all_to_all(x, axes, 0, 0, tiled=True)]
    all_to_all x0 -> x6, starting transfers between devices: none -> 25.8 us  [swap(): return lax.all_to_all(x, axes, 0, 0, tiled=True)]
    reshape x27 -> x0, local copies, waits for them, and re-layouts: 24.7 us -> none  [unfold_taps(): columns.append(window.reshape(bricks_here * 64, channels))]
    all_gather x1, waiting for transfers between devices: 0.01 us -> 17.3 us  [local(): frames = lax.all_gather(frames, 'zh', axis=0, tiled=False)]
    unnamed x6 -> x0, starting transfers between devices: 17 us -> none
  transfers between devices with their start and end apart: 12 -> 11, of which waited for: 2 -> 8; matrix products, arithmetic and copies ran while one was open for 40% -> 2% of each run, Pallas kernels for 0% -> 4%
where the time goes in v1:
time: 193 us; the launch traced here: 192 us
  waiting for transfers between devices  62.7 us (32%)
  blocking collectives  48.8 us (25%)
  starting transfers between devices  39.4 us (20%)
  between operations  14.2 us (7%)
  local copies, waits for them, and re-layouts  13.6 us (7%)
  Pallas kernels  11.2 us (6%)
  other arithmetic  2.39 us (1%)
    all_to_all x6, waiting for transfers between devices, swap(): return lax.all_to_all(x, axes, 0, 0, tiled=True)  43.2 us
    all_to_all x4, blocking collectives, swap(): return lax.all_to_all(x, axes, 0, 0, tiled=True)  41.4 us
    all_to_all x6, starting transfers between devices, swap(): return lax.all_to_all(x, axes, 0, 0, tiled=True)  25.8 us
    all_gather x1, waiting for transfers between devices, local(): frames = lax.all_gather(frames, 'zh', axis=0, tiled=False)  17.3 us
    ppermute x4, starting transfers between devices, shifted(): return lax.ppermute(x, axes, pairs)  13.6 us
    unnamed x30, local copies, waits for them, and re-layouts  10 us
    all_gather x1, blocking collectives, local(): term = lax.all_gather(term, 'c', axis=0, tiled=False)  7.38 us
    pallas_call x1, Pallas kernels, local(): call(conv_kernel, (shape(2, C, HALF), shape(3456, C)), [SMEM, SMEM] + [VM...  6.08 us
  transfers between devices with their start and end apart: 11, of which 8 were waited for; matrix products, arithmetic and copies ran while one was open for 2% of the time, Pallas kernels for 4%

profile of v1, /device:TPU:1, one launch (start us, length us, event | category | flops | bytes accessed | tf_op | source)
XLA Modules:
  0.0 192.3 jit_solution(10863358194267719293)
XLA Ops:
  12.7 17.3 %all_to_all.50 = bf16[8,144,128]{2,1,0:T(8,128)(2,1)} all-to-all(bf16[8,144,128]{2,1,0:T(8,128)(2,1)S(1)} %get-tuple-element.11), channel_id=1, replica_groups=mesh['zl'=2,'x'=4,'zh'=4,'y'=8,'c'=2] {'y'}, dimensions={0} | all-to-all | bytes 589824 | tf_op jit(solution)/shard_map/all_to_all | solution.py:219
  31.3 4.8 %collective-permute-start = (bf16[4,4,16,192]{3,2,1,0:T(8,128)(2,1)S(1)}, bf16[4,4,16,192]{3,2,1,0:T(8,128)(2,1)S(1)}, u32[]{:S(2)}, u32[]{:S(2)}) collective-permute-start(bf16[4,4,16,192]{3,2,1,0:T(8,128)(2,1)S(1)} %get-tuple-element.12.grad), channel_id=1, source_target_pairs={{0,64},{64,128},{128,192},{192,256},{256,320},{320,384},{384,448},... | collective-permute-start | bytes 294920 | tf_op jit(solution)/shard_map/ppermute | solution.py:245
  36.2 5.6 %collective-permute-start.2 = (bf16[1,4,16,192]{3,2,1,0:T(8,128)(2,1)S(1)}, bf16[1,4,16,192]{3,2,1,0:T(8,128)(2,1)S(1)}, u32[]{:S(2)}, u32[]{:S(2)}) collective-permute-start(bf16[1,4,16,192]{3,2,1,0:T(8,128)(2,1)S(1)} %get-tuple-element.13), channel_id=1, source_target_pairs={{0,1},{1,2},{2,3},{3,4},{4,5},{5,6},{6,7},{7,8},{8,9},{9,10},{10,1... | collective-permute-start | bytes 73736 | tf_op jit(solution)/shard_map/ppermute | solution.py:245
  41.7 1.9 collective-permute-start.3
  44.8 2.2 %collective-permute-done.3.dev_high = bf16[1,4,16,192]{3,2,1,0:T(8,128)(2,1)S(1)} collective-permute-done((bf16[1,4,16,192]{3,2,1,0:T(8,128)(2,1)S(1)}, bf16[1,4,16,192]{3,2,1,0:T(8,128)(2,1)S(1)}, u32[]{:S(2)}, u32[]{:S(2)}) %collective-permute-start.3) | collective-permute-done | bytes 24608 | tf_op jit(solution)/shard_map/ppermute | solution.py:245
  50.1 6.1 %shard_map.140 = (bf16[2,192,2592]{2,1,0:T(8,128)(2,1)}, bf16[3456,192]{1,0:T(8,128)(2,1)S(1)}) custom-call(s32[512]{0:T(512)S(1)} %copy-done.9, s32[4,27]{1,0:T(4,128)S(1)} %copy-done.11, bf16[4,4,16,192]{3,2,1,0:T(8,128)(2,1)S(1)} %get-tuple-element.12.grad, bf16[4,4,16,192]{3,2,1,0:T(8,128)(2,1)S(1)} %collective-permute-done.slab_low, ...), custom_call_target="tpu_custom_call" | custom-call | tf_op jit(solution)/shard_map/pallas_call | solution.py:255
  56.2 17.3 %all-gather.4.cloned.1.call-done = bf16[32,144,128]{2,1,0:T(8,128)(2,1)} async-done(((bf16[8,144,128]{2,1,0:T(8,128)(2,1)}), bf16[32,144,128]{2,1,0:T(8,128)(2,1)}) %all-gather.4.cloned.1.call-update) | async-done | bytes 1179664 | tf_op jit(solution)/shard_map/all_gather | solution.py:240
  75.2 5.8 %all_to_all.51.frames = bf16[2,4,8,144,128]{4,3,2,1,0:T(8,128)(2,1)S(1)} all-to-all(bf16[2,4,8,144,128]{4,3,2,1,0:T(8,128)(2,1)S(1)} %broadcast_in_dim.8), channel_id=1, replica_groups=mesh['zl'=2,'x'=4,'zh'=4,'y'=8,'c'=2] {'c'}, dimensions={0} | all-to-all | bytes 4718592 | tf_op jit(solution)/shard_map/all_to_all | solution.py:219
  81.0 3.2 %shard_map.141 = (bf16[256,768]{1,0:T(8,128)(2,1)}, bf16[2,576,128]{2,1,0:T(8,128)(2,1)S(1)}) custom-call(s32[512]{0:T(512)S(1)} %copy-done.10, bf16[2,4,8,144,128]{4,3,2,1,0:T(8,128)(2,1)S(1)} %all_to_all.51.frames, bf16[3456,192]{1,0:T(8,128)(2,1)S(1)} %get-tuple-element.15.taps, bf16[256,768]{1,0:T(8,128)(2,1)S(1)} %copy-done, ...), custom_call_target="tpu_custom_call" | custom-call | tf_op jit(solution)/shard_map/pallas_call | solution.py:275
  84.2 4.0 %all_to_all.52 = bf16[2,576,128]{2,1,0:T(8,128)(2,1)S(1)} all-to-all(bf16[2,576,128]{2,1,0:T(8,128)(2,1)S(1)} %get-tuple-element.17), channel_id=1, replica_groups=mesh['zl'=2,'x'=4,'zh'=4,'y'=8,'c'=2] {'c'}, dimensions={0} | all-to-all | bytes 589824 | tf_op jit(solution)/shard_map/all_to_all | solution.py:219
  88.2 14.3 %all_to_all.53 = bf16[8,72,128]{2,1,0:T(8,128)(2,1)S(1)} all-to-all(bf16[8,72,128]{2,1,0:T(8,128)(2,1)S(1)} %bitcast.11), channel_id=1, replica_groups=mesh['zl'=2,'x'=4,'zh'=4,'y'=8,'c'=2] {'y'}, dimensions={0} | all-to-all | bytes 294912 | tf_op jit(solution)/shard_map/all_to_all | solution.py:219
  102.6 5.8 %all-to-all-start.7 = ((bf16[2,192,2592]{2,1,0:T(8,128)(2,1)}), bf16[2,192,2592]{2,1,0:T(8,128)(2,1)S(1)}, u32[]{:S(2)}, u32[]{:S(2)}) async-start(bf16[2,192,2592]{2,1,0:T(8,128)(2,1)} %get-tuple-element.18), calls=%async_computation.7 | async-start | bytes 4128768 | tf_op jit(solution)/shard_map/all_to_all | solution.py:219
  108.4 2.4 %all-to-all-done.7 = bf16[2,192,2592]{2,1,0:T(8,128)(2,1)S(1)} async-done(((bf16[2,192,2592]{2,1,0:T(8,128)(2,1)}), bf16[2,192,2592]{2,1,0:T(8,128)(2,1)S(1)}, u32[]{:S(2)}, u32[]{:S(2)}) %all-to-all-start.7) | async-done | bytes 1990688 | tf_op jit(solution)/shard_map/all_to_all | solution.py:219
  111.5 3.4 %all-to-all-start.4 = ((bf16[8,72,128]{2,1,0:T(8,128)(2,1)}), bf16[8,72,128]{2,1,0:T(8,128)(2,1)S(1)}, u32[]{:S(2)}, u32[]{:S(2)}) async-start(bf16[8,72,128]{2,1,0:T(8,128)(2,1)} %broadcast_in_dim.9), calls=%async_computation.4 | async-start | bytes 294912 | tf_op jit(solution)/shard_map/all_to_all | solution.py:219
  116.5 6.7 %all-to-all-done.4 = bf16[8,72,128]{2,1,0:T(8,128)(2,1)S(1)} async-done(((bf16[8,72,128]{2,1,0:T(8,128)(2,1)}), bf16[8,72,128]{2,1,0:T(8,128)(2,1)S(1)}, u32[]{:S(2)}, u32[]{:S(2)}) %all-to-all-start.4) | async-done | bytes 147488 | tf_op jit(solution)/shard_map/all_to_all | solution.py:219
  123.2 4.0 %all-to-all-start.8 = ((bf16[8,24,2592]{2,1,0:T(8,128)(2,1)}), bf16[8,24,2592]{2,1,0:T(8,128)(2,1)S(1)}, u32[]{:S(2)}, u32[]{:S(2)}) async-start(bf16[8,24,2592]{2,1,0:T(8,128)(2,1)} %bitcast.5), calls=%async_computation.8 | async-start | bytes 2064384 | tf_op jit(solution)/shard_map/all_to_all | solution.py:219
  127.2 11.2 %all-to-all-done.8.parts = bf16[8,24,2592]{2,1,0:T(8,128)(2,1)S(1)} async-done(((bf16[8,24,2592]{2,1,0:T(8,128)(2,1)}), bf16[8,24,2592]{2,1,0:T(8,128)(2,1)S(1)}, u32[]{:S(2)}, u32[]{:S(2)}) %all-to-all-start.8) | async-done | bytes 995360 | tf_op jit(solution)/shard_map/all_to_all | solution.py:219
  139.1 5.3 %all-to-all-start.5 = ((bf16[4,72,128]{2,1,0:T(8,128)(2,1)}), bf16[4,72,128]{2,1,0:T(8,128)(2,1)S(1)}, u32[]{:S(2)}, u32[]{:S(2)}) async-start(bf16[4,72,128]{2,1,0:T(8,128)(2,1)} %broadcast_in_dim.10), calls=%async_computation.5 | async-start | bytes 147456 | tf_op jit(solution)/shard_map/all_to_all | solution.py:219
  145.3 3.6 %all-to-all-done.5 = bf16[4,72,128]{2,1,0:T(8,128)(2,1)S(1)} async-done(((bf16[4,72,128]{2,1,0:T(8,128)(2,1)}), bf16[4,72,128]{2,1,0:T(8,128)(2,1)S(1)}, u32[]{:S(2)}, u32[]{:S(2)}) %all-to-all-start.5) | async-done | bytes 73760 | tf_op jit(solution)/shard_map/all_to_all | solution.py:219
  149.0 3.9 %all-to-all-start.9 = ((bf16[32,24,81]{2,1,0:T(8,128)(2,1)}), bf16[32,24,81]{2,1,0:T(8,128)(2,1)S(1)}, u32[]{:S(2)}, u32[]{:S(2)}) async-start(bf16[32,24,81]{2,1,0:T(8,128)(2,1)} %shard_map.143), calls=%async_computation.9 | async-start | bytes 393216 | tf_op jit(solution)/shard_map/all_to_all | solution.py:219
  152.9 11.9 %all-to-all-done.9 = bf16[32,24,81]{2,1,0:T(8,128)(2,1)S(1)} async-done(((bf16[32,24,81]{2,1,0:T(8,128)(2,1)}), bf16[32,24,81]{2,1,0:T(8,128)(2,1)S(1)}, u32[]{:S(2)}, u32[]{:S(2)}) %all-to-all-start.9) | async-done | bytes 124448 | tf_op jit(solution)/shard_map/all_to_all | solution.py:219
  165.4 3.4 %all-to-all-start.6 = ((bf16[8,72,128]{2,1,0:T(8,128)(2,1)}), bf16[8,72,128]{2,1,0:T(8,128)(2,1)S(1)}, u32[]{:S(2)}, u32[]{:S(2)}) async-start(bf16[8,72,128]{2,1,0:T(8,128)(2,1)} %broadcast_in_dim.11), calls=%async_computation.6 | async-start | bytes 294912 | tf_op jit(solution)/shard_map/all_to_all | solution.py:219
  169.5 7.4 %all-to-all-done.6 = bf16[8,72,128]{2,1,0:T(8,128)(2,1)S(1)} async-done(((bf16[8,72,128]{2,1,0:T(8,128)(2,1)}), bf16[8,72,128]{2,1,0:T(8,128)(2,1)S(1)}, u32[]{:S(2)}, u32[]{:S(2)}) %all-to-all-start.6) | async-done | bytes 147488 | tf_op jit(solution)/shard_map/all_to_all | solution.py:219
  176.8 7.4 %all-gather.1 = bf16[16,72,128]{2,1,0:T(8,128)(2,1)S(1)} all-gather(bf16[8,72,128]{2,1,0:T(8,128)(2,1)S(1)} %all-to-all-done.6), channel_id=3, replica_groups=mesh['zl'=2,'x'=4,'zh'=4,'y'=8,'c'=2] {'c'}, dimensions={0}, use_global_device_ids=true | all-gather | bytes 442368 | tf_op jit(solution)/shard_map/all_gather | solution.py:287
  (49 shorter events, 19.2 us)
Async XLA Ops:
  7.2 39.8 %copy-start = (bf16[256,768]{1,0:T(8,128)(2,1)S(1)}, bf16[256,768]{1,0:T(8,128)(2,1)}, u32[]{:S(2)}) copy-start(bf16[256,768]{1,0:T(8,128)(2,1)} %fine.3) | copy-start | bytes 1179652
  7.2 66.4 %all-gather.4.cloned.1.call-start = ((), (), s32[]{:S(2)}) async-start(), calls=%async_computation.10 | async-start | bytes 1474560 | tf_op jit(solution)/shard_map/all_gather | solution.py:240
  7.2 0.9 copy-start.4
  8.2 0.9 copy-start.5
  9.0 0.8 copy-start.7
  9.8 0.7 copy-start.8
  10.5 0.7 copy-start.12
  30.0 16.9 %collective-permute-start.1 = (bf16[4,4,16,192]{3,2,1,0:T(8,128)(2,1)S(1)}, bf16[4,4,16,192]{3,2,1,0:T(8,128)(2,1)S(1)}, u32[]{:S(2)}, u32[]{:S(2)}) collective-permute-start(bf16[4,4,16,192]{3,2,1,0:T(8,128)(2,1)S(1)} %get-tuple-element.12.grad), channel_id=1, source_target_pairs={{64,0},{128,64},{192,128},{256,192},{320,256},{384,320},{448,384},... | collective-permute-start | bytes 294920 | tf_op jit(solution)/shard_map/ppermute | solution.py:245
  31.3 15.6 %collective-permute-start = (bf16[4,4,16,192]{3,2,1,0:T(8,128)(2,1)S(1)}, bf16[4,4,16,192]{3,2,1,0:T(8,128)(2,1)S(1)}, u32[]{:S(2)}, u32[]{:S(2)}) collective-permute-start(bf16[4,4,16,192]{3,2,1,0:T(8,128)(2,1)S(1)} %get-tuple-element.12.grad), channel_id=1, source_target_pairs={{0,64},{64,128},{128,192},{192,256},{256,320},{320,384},{384,448},... | collective-permute-start | bytes 294920 | tf_op jit(solution)/shard_map/ppermute | solution.py:245
  36.2 8.6 %collective-permute-start.2 = (bf16[1,4,16,192]{3,2,1,0:T(8,128)(2,1)S(1)}, bf16[1,4,16,192]{3,2,1,0:T(8,128)(2,1)S(1)}, u32[]{:S(2)}, u32[]{:S(2)}) collective-permute-start(bf16[1,4,16,192]{3,2,1,0:T(8,128)(2,1)S(1)} %get-tuple-element.13), channel_id=1, source_target_pairs={{0,1},{1,2},{2,3},{3,4},{4,5},{5,6},{6,7},{7,8},{8,9},{9,10},{10,1... | collective-permute-start | bytes 73736 | tf_op jit(solution)/shard_map/ppermute | solution.py:245
  41.7 5.2 %collective-permute-start.3 = (bf16[1,4,16,192]{3,2,1,0:T(8,128)(2,1)S(1)}, bf16[1,4,16,192]{3,2,1,0:T(8,128)(2,1)S(1)}, u32[]{:S(2)}, u32[]{:S(2)}) collective-permute-start(bf16[1,4,16,192]{3,2,1,0:T(8,128)(2,1)S(1)} %get-tuple-element.14), channel_id=1, source_target_pairs={{1,0},{2,1},{3,2},{4,3},{5,4},{6,5},{7,6},{8,7},{9,8},{10,9},{11,1... | collective-permute-start | bytes 73736 | tf_op jit(solution)/shard_map/ppermute | solution.py:245
  47.0 0.9 copy-start.1
  47.9 0.9 copy-start.6
  48.8 0.7 copy-start.9
  49.5 0.7 copy-start.11
  75.1 5.9 %copy-start.2 = (bf16[256,256]{1,0:T(8,128)(2,1)S(1)}, bf16[256,256]{1,0:T(8,128)(2,1)}, u32[]{:S(2)}) copy-start(bf16[256,256]{1,0:T(8,128)(2,1)} %constant.15.clone.order) | copy-start | bytes 393220
  75.2 5.9 %copy-start.3 = (bf16[256,256]{1,0:T(8,128)(2,1)S(1)}, bf16[256,256]{1,0:T(8,128)(2,1)}, u32[]{:S(2)}) copy-start(bf16[256,256]{1,0:T(8,128)(2,1)} %constant.16.clone.back_order) | copy-start | bytes 393220
  75.2 5.9 %copy-start.10 = (s32[512]{0:T(512)S(1)}, s32[512]{0:T(512)}, u32[]{:S(2)}) copy-start(s32[512]{0:T(512)} %counts.5) | copy-start | bytes 6148
  102.6 8.3 %all-to-all-start.7 = ((bf16[2,192,2592]{2,1,0:T(8,128)(2,1)}), bf16[2,192,2592]{2,1,0:T(8,128)(2,1)S(1)}, u32[]{:S(2)}, u32[]{:S(2)}) async-start(bf16[2,192,2592]{2,1,0:T(8,128)(2,1)} %get-tuple-element.18), calls=%async_computation.7 | async-start | bytes 4128768 | tf_op jit(solution)/shard_map/all_to_all | solution.py:219
  111.5 11.7 %all-to-all-start.4 = ((bf16[8,72,128]{2,1,0:T(8,128)(2,1)}), bf16[8,72,128]{2,1,0:T(8,128)(2,1)S(1)}, u32[]{:S(2)}, u32[]{:S(2)}) async-start(bf16[8,72,128]{2,1,0:T(8,128)(2,1)} %broadcast_in_dim.9), calls=%async_computation.4 | async-start | bytes 294912 | tf_op jit(solution)/shard_map/all_to_all | solution.py:219
  123.2 15.3 %all-to-all-start.8 = ((bf16[8,24,2592]{2,1,0:T(8,128)(2,1)}), bf16[8,24,2592]{2,1,0:T(8,128)(2,1)S(1)}, u32[]{:S(2)}, u32[]{:S(2)}) async-start(bf16[8,24,2592]{2,1,0:T(8,128)(2,1)} %bitcast.5), calls=%async_computation.8 | async-start | bytes 2064384 | tf_op jit(solution)/shard_map/all_to_all | solution.py:219
  139.1 9.8 %all-to-all-start.5 = ((bf16[4,72,128]{2,1,0:T(8,128)(2,1)}), bf16[4,72,128]{2,1,0:T(8,128)(2,1)S(1)}, u32[]{:S(2)}, u32[]{:S(2)}) async-start(bf16[4,72,128]{2,1,0:T(8,128)(2,1)} %broadcast_in_dim.10), calls=%async_computation.5 | async-start | bytes 147456 | tf_op jit(solution)/shard_map/all_to_all | solution.py:219
  149.0 15.8 %all-to-all-start.9 = ((bf16[32,24,81]{2,1,0:T(8,128)(2,1)}), bf16[32,24,81]{2,1,0:T(8,128)(2,1)S(1)}, u32[]{:S(2)}, u32[]{:S(2)}) async-start(bf16[32,24,81]{2,1,0:T(8,128)(2,1)} %shard_map.143), calls=%async_computation.9 | async-start | bytes 393216 | tf_op jit(solution)/shard_map/all_to_all | solution.py:219
  165.4 11.4 %all-to-all-start.6 = ((bf16[8,72,128]{2,1,0:T(8,128)(2,1)}), bf16[8,72,128]{2,1,0:T(8,128)(2,1)S(1)}, u32[]{:S(2)}, u32[]{:S(2)}) async-start(bf16[8,72,128]{2,1,0:T(8,128)(2,1)} %broadcast_in_dim.11), calls=%async_computation.6 | async-start | bytes 294912 | tf_op jit(solution)/shard_map/all_to_all | solution.py:219
  (1 other events, 0.7 us)
Sparse Core Ops, SparseCore 0:
  30.2 43.3 all-gather.3

commit v2 on v1

v2 whole, which is shorter than its diff:
```python
import jax
import jax.numpy as jnp
from jax import lax
from jax.experimental import pallas as pl
from jax.experimental.pallas import tpu as pltpu
from jax.sharding import Mesh, PartitionSpec as P

F32 = jnp.float32
BF16 = jnp.bfloat16

AXES = ("zl", "x", "zh", "y", "c")
SIZES = (2, 4, 4, 8, 2)
SLAB = ("zl", "x")
DEV = ("zh", "y", "c")
SLABS = 8
DEVS = 64
B = 4
C = 192
ROWS = 81
FRAME = 96
HALF = 32 * ROWS
COLS = C // SLABS

VMEM = pl.BlockSpec(memory_space=pltpu.VMEM)
ANY = pl.BlockSpec(memory_space=pl.ANY)


def dot(a, b):
    return jnp.dot(a, b, preferred_element_type=F32)


def my_place():
    place = lax.axis_index(AXES[0])
    for axis, size in zip(AXES[1:], SIZES[1:]):
        place = place * size + lax.axis_index(axis)
    return place


def iota(rows, cols, dim):
    return lax.broadcasted_iota(jnp.int32, (rows, cols), dim)


def ones_where(condition):
    return jnp.where(condition, 1.0, 0.0).astype(BF16)


def place_in_nine(start, v):
    p = start + v
    brick = jnp.where(p == 0, 0, jnp.where(p == 5, 2, 1))
    return brick, jnp.where(p == 0, 3, jnp.where(p == 5, 0, p - 1))


def window_matrix():
    row, col = iota(144, 144, 0), iota(144, 144, 1)
    s = lax.shift_right_logical(row, 4)
    sx = jnp.where(s >= 6, 2, jnp.where(s >= 3, 1, 0))
    v = jnp.bitwise_and(row, 15)
    kx, x = place_in_nine(sx, lax.shift_right_logical(v, 2))
    ky, y = place_in_nine(s - 3 * sx, jnp.bitwise_and(v, 3))
    return ones_where(col == (kx * 3 + ky) * 16 + x * 4 + y)


def row_order(inverse):
    inner, outer = iota(256, 256, int(inverse)), iota(256, 256, int(not inverse))
    return ones_where(
        outer == jnp.bitwise_and(inner, 63) * 4 + lax.shift_right_logical(inner, 6)
    )


def fetch(sems, *pairs):
    copies = [pltpu.make_async_copy(src, dst, sems.at[i]) for i, (src, dst) in enumerate(pairs)]
    for copy in copies:
        copy.start()
    return copies


def tap_rows(tap):
    window = (2 - tap // 9) * 3 + 2 - tap // 3 % 3
    return (window * 6 + 2 - tap % 3) * 64


def prepare_kernel(
    counts_in, pre_in, cot_in, gain_in, bias_in, weight_in, grad, first, last, frames,
    counts, pre, cot, gain, bias, weight, sems,
):
    copies = fetch(
        sems, (counts_in, counts), (pre_in, pre), (cot_in, cot), (gain_in, gain), (bias_in, bias),
        (weight_in, weight),
    )
    place = my_place()
    copies[5].wait()
    shift = jnp.bitwise_and(place, 15)
    spread = ones_where(iota(FRAME, ROWS, 0) == iota(FRAME, ROWS, 1) + shift)
    frame = dot(spread, weight[...])
    main = frame[:, :128].astype(BF16)
    low = frame[:48, 128:].astype(BF16)
    high = frame[48:, 128:].astype(BF16)
    tail = jnp.concatenate([low, high], axis=1)
    for i in range(32):
        frames[i, :FRAME] = main
        frames[i, FRAME:] = tail
    for copy in copies[:5]:
        copy.wait()
    count = counts[place]
    g = gain[...]
    for b in range(B):
        p = pre[b].astype(F32)
        u = cot[b].astype(F32)
        for z in range(4):
            pz = p[:, z * C : (z + 1) * C]
            uz = u[:, z * C : (z + 1) * C]
            gate = (g * pz + bias[...] > 0) & (b < count)
            grad[b, z] = jnp.where(gate, uz * g, 0.0).astype(BF16)
    first[0] = grad[0]
    last[0] = grad[count - 1]


def conv_kernel(
    counts_in, near_in, fine_in, weight_in, grad, slab_low, slab_high, dev_low, dev_high,
    conv, taps, counts, near, fine, weight, sems, bricks, block, total,
):
    copies = fetch(
        sems, (counts_in, counts), (near_in, near), (fine_in, fine), (weight_in, weight)
    )
    place = my_place()
    bricks[0:4] = grad[...]
    bricks[4:8] = slab_low[...]
    bricks[8:12] = slab_high[...]
    bricks[12:13] = dev_low[...]
    bricks[13:14] = dev_high[...]
    bricks[14:15] = jnp.zeros((1, 4, 16, C), BF16)
    window = window_matrix()
    copies[1].wait()
    for b in range(B):
        slots = []
        for k in range(27):
            brick = near[b, k]
            away = lax.shift_right_arithmetic(brick, 2) - place
            slot = jnp.bitwise_and(brick, 3)
            at = jnp.where(away == 0, slot, 14)
            at = jnp.where(away == -DEVS, 4 + slot, at)
            at = jnp.where(away == DEVS, 8 + slot, at)
            at = jnp.where(away == -1, 12, at)
            at = jnp.where(away == 1, 13, at)
            slots.append(jnp.where(brick < 0, 14, at))
        for plane in range(6):
            kz, z = ((0, 3), (1, 0), (1, 1), (1, 2), (1, 3), (2, 0))[plane]
            for q in range(9):
                block[plane, q * 16 : (q + 1) * 16] = bricks[slots[q * 3 + kz], z]
        for plane in range(6):
            moved = dot(window, block[plane]).astype(BF16)
            for s in range(9):
                row = ((s * 6 + plane) * B + b) * 16
                taps[row : row + 16] = moved[s * 16 : (s + 1) * 16]
    for copy in (copies[0], copies[2], copies[3]):
        copy.wait()
    count = counts[place]
    merged = dot(fine[...], weight[...])
    brick_of = lax.broadcasted_iota(jnp.int32, (256, C), 0) // 64
    merged = jnp.where(brick_of < count, merged, 0.0).astype(BF16)
    merged = jnp.transpose(dot(row_order(False), merged)).astype(BF16)
    for tap in range(27):
        row = tap_rows(tap)
        term = dot(merged, taps[row : row + 256])
        at = tap * C
        end = at + C
        while at < end:
            owner = at // ROWS
            stop = min(end, (owner + 1) * ROWS)
            to = (owner // 2) * ROWS + at % ROWS
            total[owner % 2, :, to : to + stop - at] = term[:, at - tap * C : stop - tap * C]
            at = stop
    for half in range(2):
        conv[half] = total[half].astype(BF16)


def back_kernel(
    counts_in, fine_in, weight_in, mine, other, taps, fine_grad, term,
    counts, fine, weight, sems, both, whole,
):
    copies = fetch(sems, (counts_in, counts), (fine_in, fine), (weight_in, weight))
    place = my_place()
    core = jnp.bitwise_and(place, 1)
    both[core] = mine[...]
    both[1 - core] = other[...]
    for owner in range(DEVS):
        tile = ROWS * owner // 16
        frame = both.at[owner % 2, owner // 2]
        main = frame[:FRAME]
        low = frame[FRAME:, :64]
        high = frame[FRAME:, 64:]
        row = tile * 16
        if owner % 16:
            whole[row : row + 16, :128] = whole[row : row + 16, :128] + main[:16]
            whole[row : row + 16, 128:] = whole[row : row + 16, 128:] + low[:16]
            whole[row + 16 : row + FRAME, :128] = main[16:]
            whole[row + 16 : row + 48, 128:] = low[16:]
        else:
            whole[row : row + FRAME, :128] = main
            whole[row : row + 48, 128:] = low
        whole[row + 48 : row + FRAME, 128:] = high
    back = jnp.zeros((256, C), F32)
    for tap in range(27):
        row = tap_rows(tap)
        back = back + dot(taps[row : row + 256], whole[tap * C : (tap + 1) * C])
    brick_of = lax.broadcasted_iota(jnp.int32, (256, C), 0) // 16 % B
    for copy in copies:
        copy.wait()
    count = counts[place]
    back = jnp.where(brick_of < count, back, 0.0).astype(BF16)
    back = dot(row_order(True), back)
    gm = back.astype(BF16)
    fine_grad[...] = lax.dot_general(
        gm, weight[...], (((1,), (1,)), ((), ())), preferred_element_type=F32
    ).astype(BF16)
    result = dot(jnp.transpose(back).astype(BF16), fine[...]).astype(BF16)
    for part in range(6):
        term[part * C : (part + 1) * C] = result[:, part * 128 : (part + 1) * 128]
    term[6 * C :] = jnp.zeros((8 * C - 6 * C, 128), BF16)


def cut_kernel(parts, out):
    total = parts[0].astype(F32)
    for i in range(1, SLABS):
        total = total + parts[i].astype(F32)
    for i in range(32):
        out[i] = total[:, i * ROWS : (i + 1) * ROWS].astype(BF16)


def spread_kernel(parts, out):
    total = parts[0].astype(F32)
    for i in range(1, parts.shape[0]):
        total = total + parts[i].astype(F32)
    for i in range(out.shape[0]):
        out[i] = total.astype(BF16)


def merge_kernel(parts, out):
    for part in range(6):
        block = parts[part * C : (part + 1) * C].astype(F32)
        out[part * 128 : (part + 1) * 128] = jnp.transpose(block)


def call(kernel, outs, specs, scratch=()):
    return pl.pallas_call(
        kernel,
        out_shape=outs,
        in_specs=specs,
        out_specs=jax.tree.map(lambda _: VMEM, outs),
        scratch_shapes=scratch,
        compiler_params=pltpu.CompilerParams(vmem_limit_bytes=40 << 20),
    )


def shape(*dims, dtype=BF16):
    return jax.ShapeDtypeStruct(dims, dtype)


def swap(x, axes):
    return lax.all_to_all(x, axes, 0, 0, tiled=True)


def summed(x):
    return jnp.sum(x.astype(F32), axis=0)


def local(
    fine_input, merge_weight, conv_weight, pre_act, norm_gain, norm_bias, cotangent, counts, neighbours
):
    counts_scratch = pltpu.SMEM((SLABS * DEVS,), jnp.int32)
    grad, first, last, frames = call(
        prepare_kernel,
        (shape(B, 4, 16, C), shape(1, 4, 16, C), shape(1, 4, 16, C), shape(32, 144, 128)),
        [ANY] * 6,
        [
            counts_scratch,
            pltpu.VMEM((B, 16, 4 * C), BF16),
            pltpu.VMEM((B, 16, 4 * C), BF16),
            pltpu.VMEM((1, C), F32),
            pltpu.VMEM((1, C), F32),
            pltpu.VMEM((ROWS, C), BF16),
            pltpu.SemaphoreType.DMA((6,)),
        ],
    )(counts, pre_act, cotangent, norm_gain.reshape(1, C), norm_bias.reshape(1, C), conv_weight)

    frames = swap(frames, ("zh", "y"))

    def shifted(x, axes, count, step):
        pairs = [(i, i + step) for i in range(count) if 0 <= i + step < count]
        return lax.ppermute(x, axes, pairs)

    slab_low = shifted(grad, SLAB, SLABS, 1)
    slab_high = shifted(grad, SLAB, SLABS, -1)
    dev_low = shifted(last, DEV, DEVS, 1)
    dev_high = shifted(first, DEV, DEVS, -1)

    fine_scratch = pltpu.VMEM((256, 768), BF16)
    weight_scratch = pltpu.VMEM((768, C), BF16)
    conv, taps = call(
        conv_kernel,
        (shape(2, C, HALF), shape(3456, C)),
        [ANY] * 4 + [VMEM] * 5,
        [
            counts_scratch,
            pltpu.SMEM((B, 27), jnp.int32),
            fine_scratch,
            weight_scratch,
            pltpu.SemaphoreType.DMA((4,)),
            pltpu.VMEM((15, 4, 16, C), BF16),
            pltpu.VMEM((6, 144, C), BF16),
            pltpu.VMEM((2, C, HALF), F32),
        ],
    )(
        counts, neighbours, fine_input, merge_weight, grad, slab_low, slab_high, dev_low, dev_high
    )

    conv = summed(swap(conv, "c")).astype(BF16)
    conv = swap(conv.reshape(SLABS, COLS, HALF), SLAB)
    frames, conv = lax.optimization_barrier((frames, conv))

    other = lax.ppermute(frames, "c", [(0, 1), (1, 0)])
    fine_grad, term = call(
        back_kernel,
        (shape(256, 768), shape(DEVS * 24, 128)),
        [ANY] * 3 + [VMEM] * 3,
        [
            counts_scratch,
            fine_scratch,
            weight_scratch,
            pltpu.SemaphoreType.DMA((3,)),
            pltpu.VMEM((2, 32, 144, 128), BF16),
            pltpu.VMEM((27 * C, C), BF16),
        ],
    )(counts, fine_input, merge_weight, frames, other, taps)

    conv = call(cut_kernel, shape(32, COLS, ROWS), [VMEM])(conv)
    conv_grad = summed(swap(conv, ("zh", "y"))).T

    term = swap(term.reshape(DEVS, 24, 128), DEV)
    term = call(spread_kernel, shape(SLABS, 24, 128), [VMEM])(term)
    term = swap(term, SLAB)
    term = call(spread_kernel, shape(DEVS, 24, 128), [VMEM])(term)
    term = swap(term, DEV)
    merge_grad = call(merge_kernel, shape(768, C, dtype=F32), [VMEM])(term.reshape(DEVS * 24, 128))
    return fine_grad, merge_grad, conv_grad


def solution(mesh):
    fine_mesh = Mesh(mesh.devices.reshape(SIZES), AXES)
    every = SLAB + DEV
    in_specs = (
        P(every, None),
        P(),
        P(DEV, None),
        P(every, None, None),
        P(),
        P(),
        P(every, None, None),
        P(),
        P(every, None),
    )
    out_specs = (P(every, None), P(), P(DEV, SLAB))
    return jax.shard_map(
        local, mesh=fine_mesh, in_specs=in_specs, out_specs=out_specs, check_vma=False
    )
```

time: 193 us -> 194 us (level)
  blocking collectives: 48.8 us -> 93.2 us
  waiting for transfers between devices: 62.7 us -> 33.3 us
  between operations: 14.2 us -> 0.8 us
  local copies, waits for them, and re-layouts: 13.6 us -> 10.2 us
    all_to_all x4, blocking collectives: 41.4 us -> 93.2 us  [swap(): return lax.all_to_all(x, axes, 0, 0, tiled=True)]
    all_gather x1 -> x0, waiting for transfers between devices: 17.3 us -> none  [local(): frames = lax.all_gather(frames, 'zh', axis=0, tiled=False)]
    all_to_all x6 -> x3, waiting for transfers between devices: 43.2 us -> 30.8 us  [swap(): return lax.all_to_all(x, axes, 0, 0, tiled=True)]
    all_to_all x6 -> x3, starting transfers between devices: 25.8 us -> 17.8 us  [swap(): return lax.all_to_all(x, axes, 0, 0, tiled=True)]
    all_gather x1 -> x0, blocking collectives: 7.38 us -> none  [local(): term = lax.all_gather(term, 'c', axis=0, tiled=False)]
    ppermute x0 -> x1, starting transfers between devices: none -> 6.37 us  [local(): other = lax.ppermute(frames, 'c', [(0, 1), (1, 0)])]
    broadcast_in_dim x4 -> x0, local copies, waits for them, and re-layouts: 3.59 us -> none  [the longest x1 1.57 us: local(): frames = swap(jnp.broadcast_to(frames[None], (2, 4, 8, 144, 128)), 'c')]
    ppermute x0 -> x1, waiting for transfers between devices: none -> 2.45 us  [local(): other = lax.ppermute(frames, 'c', [(0, 1), (1, 0)])]
  transfers between devices with their start and end apart: 11 -> 8, of which waited for: 8 -> 4; matrix products, arithmetic and copies ran while one was open for 2% -> 1% of each run, Pallas kernels for 4% -> 1%
where the time goes in v2:
time: 194 us
  blocking collectives  93.2 us (48%)
  starting transfers between devices  40.1 us (21%)
  waiting for transfers between devices  33.3 us (17%)
  Pallas kernels  12.2 us (6%)
  local copies, waits for them, and re-layouts  10.2 us (5%)
  other arithmetic  3.82 us (2%)
    all_to_all x4, blocking collectives, swap(): return lax.all_to_all(x, axes, 0, 0, tiled=True)  93.2 us
    all_to_all x3, waiting for transfers between devices, swap(): return lax.all_to_all(x, axes, 0, 0, tiled=True)  30.8 us
    all_to_all x3, starting transfers between devices, swap(): return lax.all_to_all(x, axes, 0, 0, tiled=True)  17.8 us
    ppermute x4, starting transfers between devices, shifted(): return lax.ppermute(x, axes, pairs)  15.9 us
    unnamed x28, local copies, waits for them, and re-layouts  10.2 us
    ppermute x1, starting transfers between devices, local(): other = lax.ppermute(frames, 'c', [(0, 1), (1, 0)])  6.37 us
    pallas_call x1, Pallas kernels, local(): call(conv_kernel, (shape(2, C, HALF), shape(3456, C)), [ANY] * 4 + [VMEM]...  4.96 us
  transfers between devices with their start and end apart: 8, of which 4 were waited for; matrix products, arithmetic and copies ran while one was open for 1% of the time, Pallas kernels for 1%

profile of v2, /device:TPU:1, one launch (start us, length us, event | category | flops | bytes accessed | tf_op | source)
XLA Modules:
  0.0 193.6 jit_solution(10468423196026088807)
XLA Ops:
  1.5 0.9 copy-done.5
  6.1 1.0 copy-done.2
  7.1 1.3 collective-permute-start.1
  8.4 4.6 %collective-permute-start = (bf16[4,4,16,192]{3,2,1,0:T(8,128)(2,1)S(1)}, bf16[4,4,16,192]{3,2,1,0:T(8,128)(2,1)S(1)}, u32[]{:S(2)}, u32[]{:S(2)}) collective-permute-start(bf16[4,4,16,192]{3,2,1,0:T(8,128)(2,1)S(1)} %get-tuple-element.14.grad), channel_id=1, source_target_pairs={{0,64},{64,128},{128,192},{192,256},{256,320},{320,384},{384,448},... | collective-permute-start | bytes 294920 | tf_op jit(solution)/shard_map/ppermute | solution.py:290
  13.0 4.6 %collective-permute-start.2 = (bf16[1,4,16,192]{3,2,1,0:T(8,128)(2,1)S(1)}, bf16[1,4,16,192]{3,2,1,0:T(8,128)(2,1)S(1)}, u32[]{:S(2)}, u32[]{:S(2)}) collective-permute-start(bf16[1,4,16,192]{3,2,1,0:T(8,128)(2,1)S(1)} %get-tuple-element.15), channel_id=1, source_target_pairs={{0,1},{1,2},{2,3},{3,4},{4,5},{5,6},{6,7},{7,8},{8,9},{9,10},{10,1... | collective-permute-start | bytes 73736 | tf_op jit(solution)/shard_map/ppermute | solution.py:290
  17.5 5.5 %collective-permute-start.3 = (bf16[1,4,16,192]{3,2,1,0:T(8,128)(2,1)S(1)}, bf16[1,4,16,192]{3,2,1,0:T(8,128)(2,1)S(1)}, u32[]{:S(2)}, u32[]{:S(2)}) collective-permute-start(bf16[1,4,16,192]{3,2,1,0:T(8,128)(2,1)S(1)} %get-tuple-element.16), channel_id=1, source_target_pairs={{1,0},{2,1},{3,2},{4,3},{5,4},{6,5},{7,6},{8,7},{9,8},{10,9},{11,1... | collective-permute-start | bytes 73736 | tf_op jit(solution)/shard_map/ppermute | solution.py:290
  23.0 1.1 copy.13.weight_in
  24.2 1.0 copy-done
  26.6 5.0 %shard_map.113 = (bf16[2,192,2592]{2,1,0:T(8,128)(2,1)S(1)}, bf16[3456,192]{1,0:T(8,128)(2,1)S(1)}) custom-call(s32[512]{0:T(512)S(1)} %copy-done.8, s32[4,27]{1,0:T(4,128)S(1)} %copy-done.10, bf16[256,768]{1,0:T(8,128)(2,1)S(1)} %copy-done, bf16[768,192]{1,0:T(8,128)(2,1)S(1)} %copy.13.weight_in, bf16[4,4,16,192]{3,2,1,0:T(8,128)(2,1)S(1)} %get-tuple-element.14.grad, ...), custom_call_target="tpu_custom_call" | custom-call | tf_op jit(solution)/shard_map/pallas_call | solution.py:299
  31.5 5.9 %all_to_all.35 = bf16[2,192,2592]{2,1,0:T(8,128)(2,1)} all-to-all(bf16[2,192,2592]{2,1,0:T(8,128)(2,1)S(1)} %get-tuple-element.17), channel_id=1, replica_groups=mesh['zl'=2,'x'=4,'zh'=4,'y'=8,'c'=2] {'c'}, dimensions={0} | all-to-all | bytes 3981312 | tf_op jit(solution)/shard_map/all_to_all | solution.py:260
  37.5 3.2 %reduce_sum.21 = bf16[192,2592]{1,0:T(8,128)(2,1)} reduce(bf16[2,192,2592]{2,1,0:T(8,128)(2,1)} %all_to_all.35, bf16[]{:T(256)} %constant.2.clone.1), dimensions={0}, to_apply=%region_0.0 | reduce | flops 497664 | bytes 2985986 | tf_op jit(solution)/shard_map/reduce_sum | solution.py:264
  40.6 18.8 %all_to_all.36.parts = bf16[8,24,2592]{2,1,0:T(8,128)(2,1)S(1)} all-to-all(bf16[8,24,2592]{2,1,0:T(8,128)(2,1)} %bitcast.10), channel_id=1, replica_groups=mesh['zl'=2,'x'=4,'zh'=4,'y'=8,'c'=2] {'zl','x'}, dimensions={0} | all-to-all | bytes 1990656 | tf_op jit(solution)/shard_map/all_to_all | solution.py:260
  59.5 47.8 %all_to_all.37.mine = bf16[32,144,128]{2,1,0:T(8,128)(2,1)S(1)} all-to-all(bf16[32,144,128]{2,1,0:T(8,128)(2,1)S(1)} %copy-done.3), channel_id=1, replica_groups=mesh['zl'=2,'x'=4,'zh'=4,'y'=8,'c'=2] {'zh','y'}, dimensions={0} | all-to-all | bytes 2359296 | tf_op jit(solution)/shard_map/all_to_all | solution.py:260
  107.3 6.4 %collective-permute-start.4 = (bf16[32,144,128]{2,1,0:T(8,128)(2,1)S(1)}, bf16[32,144,128]{2,1,0:T(8,128)(2,1)S(1)}, u32[]{:S(2)}, u32[]{:S(2)}) collective-permute-start(bf16[32,144,128]{2,1,0:T(8,128)(2,1)S(1)} %all_to_all.37.mine), channel_id=1, source_target_pairs={{0,1},{1,0},{2,3},{3,2},{4,5},{5,4},{6,7},{7,6},{8,9},{9,8},{10,11... | collective-permute-start | bytes 3538952 | tf_op jit(solution)/shard_map/ppermute | solution.py:321
  113.7 2.5 %collective-permute-done.4.other = bf16[32,144,128]{2,1,0:T(8,128)(2,1)S(1)} collective-permute-done((bf16[32,144,128]{2,1,0:T(8,128)(2,1)S(1)}, bf16[32,144,128]{2,1,0:T(8,128)(2,1)S(1)}, u32[]{:S(2)}, u32[]{:S(2)}) %collective-permute-start.4) | collective-permute-done | bytes 1179680 | tf_op jit(solution)/shard_map/ppermute | solution.py:321
  116.1 3.9 %shard_map.114 = (bf16[256,768]{1,0:T(8,128)(2,1)}, bf16[1536,128]{1,0:T(8,128)(2,1)S(1)}) custom-call(s32[512]{0:T(512)S(1)} %copy-done.9, bf16[256,768]{1,0:T(8,128)(2,1)S(1)} %copy-done.1, bf16[768,192]{1,0:T(8,128)(2,1)S(1)} %copy.13.weight_in, bf16[32,144,128]{2,1,0:T(8,128)(2,1)S(1)} %all_to_all.37.mine, ...), custom_call_target="tpu_custom_call" | custom-call | tf_op jit(solution)/shard_map/pallas_call | solution.py:322
  120.0 20.6 %all_to_all.38.parts = bf16[64,24,128]{2,1,0:T(8,128)(2,1)S(1)} all-to-all(bf16[64,24,128]{2,1,0:T(8,128)(2,1)S(1)} %bitcast.7), channel_id=1, replica_groups=mesh['zl'=2,'x'=4,'zh'=4,'y'=8,'c'=2] {'zh','y','c'}, dimensions={0} | all-to-all | bytes 786432 | tf_op jit(solution)/shard_map/all_to_all | solution.py:260
  141.3 4.0 %all-to-all-start.4 = ((bf16[8,24,128]{2,1,0:T(8,128)(2,1)}), bf16[8,24,128]{2,1,0:T(8,128)(2,1)S(1)}, u32[]{:S(2)}, u32[]{:S(2)}) async-start(bf16[8,24,128]{2,1,0:T(8,128)(2,1)} %shard_map.115), calls=%async_computation.4 | async-start | bytes 98304 | tf_op jit(solution)/shard_map/all_to_all | solution.py:260
  146.3 4.3 %all-to-all-done.4.parts = bf16[8,24,128]{2,1,0:T(8,128)(2,1)S(1)} async-done(((bf16[8,24,128]{2,1,0:T(8,128)(2,1)}), bf16[8,24,128]{2,1,0:T(8,128)(2,1)S(1)}, u32[]{:S(2)}, u32[]{:S(2)}) %all-to-all-start.4) | async-done | bytes 49184 | tf_op jit(solution)/shard_map/all_to_all | solution.py:260
  150.5 6.4 %all-to-all-start.6 = ((bf16[32,24,81]{2,1,0:T(8,128)(2,1)}), bf16[32,24,81]{2,1,0:T(8,128)(2,1)S(1)}, u32[]{:S(2)}, u32[]{:S(2)}) async-start(bf16[32,24,81]{2,1,0:T(8,128)(2,1)} %shard_map.118), calls=%async_computation.6 | async-start | bytes 393216 | tf_op jit(solution)/shard_map/all_to_all | solution.py:260
  157.7 11.1 %all-to-all-done.6 = bf16[32,24,81]{2,1,0:T(8,128)(2,1)S(1)} async-done(((bf16[32,24,81]{2,1,0:T(8,128)(2,1)}), bf16[32,24,81]{2,1,0:T(8,128)(2,1)S(1)}, u32[]{:S(2)}, u32[]{:S(2)}) %all-to-all-start.6) | async-done | bytes 124448 | tf_op jit(solution)/shard_map/all_to_all | solution.py:260
  168.8 7.4 %all-to-all-start.5 = ((bf16[64,24,128]{2,1,0:T(8,128)(2,1)}), bf16[64,24,128]{2,1,0:T(8,128)(2,1)S(1)}, u32[]{:S(2)}, u32[]{:S(2)}) async-start(bf16[64,24,128]{2,1,0:T(8,128)(2,1)} %shard_map.116), calls=%async_computation.5 | async-start | bytes 786432 | tf_op jit(solution)/shard_map/all_to_all | solution.py:260
  176.9 15.4 %all-to-all-done.5 = bf16[64,24,128]{2,1,0:T(8,128)(2,1)S(1)} async-done(((bf16[64,24,128]{2,1,0:T(8,128)(2,1)}), bf16[64,24,128]{2,1,0:T(8,128)(2,1)S(1)}, u32[]{:S(2)}, u32[]{:S(2)}) %all-to-all-start.5) | async-done | bytes 393248 | tf_op jit(solution)/shard_map/all_to_all | solution.py:260
  192.5 1.1 copy.14
  (33 shorter events, 9.1 us)
Async XLA Ops:
  0.6 0.9 copy-start.4
  1.5 0.9 copy-start.5
  2.4 0.8 copy-start.6
  3.2 0.7 copy-start.7
  3.9 0.7 copy-start.11
  4.6 0.7 copy-start.12
  6.0 1.0 copy-start.2
  7.1 17.1 %collective-permute-start.1 = (bf16[4,4,16,192]{3,2,1,0:T(8,128)(2,1)S(1)}, bf16[4,4,16,192]{3,2,1,0:T(8,128)(2,1)S(1)}, u32[]{:S(2)}, u32[]{:S(2)}) collective-permute-start(bf16[4,4,16,192]{3,2,1,0:T(8,128)(2,1)S(1)} %get-tuple-element.14.grad), channel_id=1, source_target_pairs={{64,0},{128,64},{192,128},{256,192},{320,256},{384,320},{448,384},... | collective-permute-start | bytes 294920 | tf_op jit(solution)/shard_map/ppermute | solution.py:290
  8.4 15.8 %collective-permute-start = (bf16[4,4,16,192]{3,2,1,0:T(8,128)(2,1)S(1)}, bf16[4,4,16,192]{3,2,1,0:T(8,128)(2,1)S(1)}, u32[]{:S(2)}, u32[]{:S(2)}) collective-permute-start(bf16[4,4,16,192]{3,2,1,0:T(8,128)(2,1)S(1)} %get-tuple-element.14.grad), channel_id=1, source_target_pairs={{0,64},{64,128},{128,192},{192,256},{256,320},{320,384},{384,448},... | collective-permute-start | bytes 294920 | tf_op jit(solution)/shard_map/ppermute | solution.py:290
  13.0 11.2 %collective-permute-start.2 = (bf16[1,4,16,192]{3,2,1,0:T(8,128)(2,1)S(1)}, bf16[1,4,16,192]{3,2,1,0:T(8,128)(2,1)S(1)}, u32[]{:S(2)}, u32[]{:S(2)}) collective-permute-start(bf16[1,4,16,192]{3,2,1,0:T(8,128)(2,1)S(1)} %get-tuple-element.15), channel_id=1, source_target_pairs={{0,1},{1,2},{2,3},{3,4},{4,5},{5,6},{6,7},{7,8},{8,9},{9,10},{10,1... | collective-permute-start | bytes 73736 | tf_op jit(solution)/shard_map/ppermute | solution.py:290
  17.5 6.6 %collective-permute-start.3 = (bf16[1,4,16,192]{3,2,1,0:T(8,128)(2,1)S(1)}, bf16[1,4,16,192]{3,2,1,0:T(8,128)(2,1)S(1)}, u32[]{:S(2)}, u32[]{:S(2)}) collective-permute-start(bf16[1,4,16,192]{3,2,1,0:T(8,128)(2,1)S(1)} %get-tuple-element.16), channel_id=1, source_target_pairs={{1,0},{2,1},{3,2},{4,3},{5,4},{6,5},{7,6},{8,7},{9,8},{10,9},{11,1... | collective-permute-start | bytes 73736 | tf_op jit(solution)/shard_map/ppermute | solution.py:290
  24.2 1.0 copy-start
  25.2 0.7 copy-start.8
  25.9 0.7 copy-start.10
  40.6 18.9 %copy-start.3 = (bf16[32,144,128]{2,1,0:T(8,128)(2,1)S(1)}, bf16[32,144,128]{2,1,0:T(8,128)(2,1)}, u32[]{:S(2)}) copy-start(bf16[32,144,128]{2,1,0:T(8,128)(2,1)} %copy-done.2) | copy-start | bytes 3538948
  40.6 75.5 %copy-start.1 = (bf16[256,768]{1,0:T(8,128)(2,1)S(1)}, bf16[256,768]{1,0:T(8,128)(2,1)}, u32[]{:S(2)}) copy-start(bf16[256,768]{1,0:T(8,128)(2,1)} %fine_in.3) | copy-start | bytes 1179652
  40.6 75.5 %copy-start.9 = (s32[512]{0:T(512)S(1)}, s32[512]{0:T(512)}, u32[]{:S(2)}) copy-start(s32[512]{0:T(512)} %counts_in.5) | copy-start | bytes 6148
  107.3 8.8 %collective-permute-start.4 = (bf16[32,144,128]{2,1,0:T(8,128)(2,1)S(1)}, bf16[32,144,128]{2,1,0:T(8,128)(2,1)S(1)}, u32[]{:S(2)}, u32[]{:S(2)}) collective-permute-start(bf16[32,144,128]{2,1,0:T(8,128)(2,1)S(1)} %all_to_all.37.mine), channel_id=1, source_target_pairs={{0,1},{1,0},{2,3},{3,2},{4,5},{5,4},{6,7},{7,6},{8,9},{9,8},{10,11... | collective-permute-start | bytes 3538952 | tf_op jit(solution)/shard_map/ppermute | solution.py:321
  141.3 9.2 %all-to-all-start.4 = ((bf16[8,24,128]{2,1,0:T(8,128)(2,1)}), bf16[8,24,128]{2,1,0:T(8,128)(2,1)S(1)}, u32[]{:S(2)}, u32[]{:S(2)}) async-start(bf16[8,24,128]{2,1,0:T(8,128)(2,1)} %shard_map.115), calls=%async_computation.4 | async-start | bytes 98304 | tf_op jit(solution)/shard_map/all_to_all | solution.py:260
  150.5 18.3 %all-to-all-start.6 = ((bf16[32,24,81]{2,1,0:T(8,128)(2,1)}), bf16[32,24,81]{2,1,0:T(8,128)(2,1)S(1)}, u32[]{:S(2)}, u32[]{:S(2)}) async-start(bf16[32,24,81]{2,1,0:T(8,128)(2,1)} %shard_map.118), calls=%async_computation.6 | async-start | bytes 393216 | tf_op jit(solution)/shard_map/all_to_all | solution.py:260
  168.8 23.5 %all-to-all-start.5 = ((bf16[64,24,128]{2,1,0:T(8,128)(2,1)}), bf16[64,24,128]{2,1,0:T(8,128)(2,1)S(1)}, u32[]{:S(2)}, u32[]{:S(2)}) async-start(bf16[64,24,128]{2,1,0:T(8,128)(2,1)} %shard_map.116), calls=%async_computation.5 | async-start | bytes 786432 | tf_op jit(solution)/shard_map/all_to_all | solution.py:260

commit v3 on v2

--- a/solution.py
+++ b/solution.py
@@ -22,7 +22,7 @@
 COLS = C // SLABS
 
 VMEM = pl.BlockSpec(memory_space=pltpu.VMEM)
-ANY = pl.BlockSpec(memory_space=pl.ANY)
+HBM = pl.BlockSpec(memory_space=pltpu.HBM)
 
 
 def dot(a, b):
@@ -117,7 +117,7 @@
 
 def conv_kernel(
     counts_in, near_in, fine_in, weight_in, grad, slab_low, slab_high, dev_low, dev_high,
-    conv, taps, counts, near, fine, weight, sems, bricks, block, total,
+    keep, send, taps, counts, near, fine, weight, sems, bricks, block, total,
 ):
     copies = fetch(
         sems, (counts_in, counts), (near_in, near), (fine_in, fine), (weight_in, weight)
@@ -155,7 +155,9 @@
     for copy in (copies[0], copies[2], copies[3]):
         copy.wait()
     count = counts[place]
-    merged = dot(fine[...], weight[...])
+    merged = lax.dot_general(
+        fine[...], weight[...], (((1,), (1,)), ((), ())), preferred_element_type=F32
+    )
     brick_of = lax.broadcasted_iota(jnp.int32, (256, C), 0) // 64
     merged = jnp.where(brick_of < count, merged, 0.0).astype(BF16)
     merged = jnp.transpose(dot(row_order(False), merged)).astype(BF16)
@@ -170,13 +172,26 @@
             to = (owner // 2) * ROWS + at % ROWS
             total[owner % 2, :, to : to + stop - at] = term[:, at - tap * C : stop - tap * C]
             at = stop
-    for half in range(2):
-        conv[half] = total[half].astype(BF16)
+    core = jnp.bitwise_and(place, 1)
+    for out, half in ((keep, core), (send, 1 - core)):
+        for slab in range(SLABS):
+            out[slab] = total[half, slab * COLS : (slab + 1) * COLS].astype(BF16)
+
+
+def slab_partners():
+    return [(dz, dx) for dz in range(2) for dx in range(4) if dz or dx]
+
+
+def split_kernel(keep, received, *outs):
+    zl, x = lax.axis_index("zl"), lax.axis_index("x")
+    for out, (dz, dx) in zip(outs, [(0, 0)] + slab_partners()):
+        slab = jnp.bitwise_xor(zl, dz) * 4 + jnp.bitwise_and(x + dx, 3)
+        out[...] = (keep[slab].astype(F32) + received[slab].astype(F32)).astype(BF16)
 
 
 def back_kernel(
-    counts_in, fine_in, weight_in, mine, other, taps, fine_grad, term,
-    counts, fine, weight, sems, both, whole,
+    counts_in, fine_in, weight_in, mine, other, taps, fine_grad, keep, send,
+    counts, fine, weight, sems, both, whole, term,
 ):
     copies = fetch(sems, (counts_in, counts), (fine_in, fine), (weight_in, weight))
     place = my_place()
@@ -210,21 +225,37 @@
     back = jnp.where(brick_of < count, back, 0.0).astype(BF16)
     back = dot(row_order(True), back)
     gm = back.astype(BF16)
-    fine_grad[...] = lax.dot_general(
-        gm, weight[...], (((1,), (1,)), ((), ())), preferred_element_type=F32
-    ).astype(BF16)
+    fine_grad[...] = dot(gm, weight[...]).astype(BF16)
     result = dot(jnp.transpose(back).astype(BF16), fine[...]).astype(BF16)
     for part in range(6):
-        term[part * C : (part + 1) * C] = result[:, part * 128 : (part + 1) * 128]
-    term[6 * C :] = jnp.zeros((8 * C - 6 * C, 128), BF16)
-
-
-def cut_kernel(parts, out):
-    total = parts[0].astype(F32)
-    for i in range(1, SLABS):
-        total = total + parts[i].astype(F32)
+        row = part % 3 * C
+        term[part // 3, row : row + C] = result[:, part * 128 : (part + 1) * 128]
+    keep[...] = term[core]
+    send[...] = term[1 - core]
+
+
+def join_kernel(keep, received, *refs):
+    parts, out = refs[:-1], refs[-1]
+    total = parts[0][...].astype(F32)
+    for part in parts[1:]:
+        total = total + part[...].astype(F32)
+    pad = jnp.zeros((COLS, 128 - ROWS), BF16)
     for i in range(32):
-        out[i] = total[:, i * ROWS : (i + 1) * ROWS].astype(BF16)
+        piece = total[:, i * ROWS : (i + 1) * ROWS].astype(BF16)
+        out[i, 0] = jnp.concatenate([piece, pad], axis=1)
+    for i in range(24):
+        out[i, 1] = (keep[i].astype(F32) + received[i].astype(F32)).astype(BF16)
+    for i in range(24, 32):
+        out[i, 1] = jnp.zeros((24, 128), BF16)
+
+
+def part_kernel(parts, conv_grad, out):
+    total = [parts[0, kind].astype(F32) for kind in range(2)]
+    for i in range(1, 32):
+        total = [total[kind] + parts[i, kind].astype(F32) for kind in range(2)]
+    conv_grad[...] = jnp.transpose(total[0])[:ROWS]
+    for i in range(SLABS):
+        out[i] = total[1].astype(BF16)
 
 
 def spread_kernel(parts, out):
@@ -235,20 +266,25 @@
         out[i] = total.astype(BF16)
 
 
-def merge_kernel(parts, out):
+def merge_kernel(parts, out, held, sems):
     for part in range(6):
-        block = parts[part * C : (part + 1) * C].astype(F32)
-        out[part * 128 : (part + 1) * 128] = jnp.transpose(block)
-
-
-def call(kernel, outs, specs, scratch=()):
+        row = part % 3 * C
+        block = parts[part // 3, row : row + C]
+        held[:, part * 128 : (part + 1) * 128] = block.astype(F32)
+    copy = pltpu.make_async_copy(held, out, sems.at[0])
+    copy.start()
+    copy.wait()
+
+
+def call(kernel, outs, specs, scratch=(), flops=0, out_spec=VMEM, vmem=40):
     return pl.pallas_call(
         kernel,
         out_shape=outs,
         in_specs=specs,
-        out_specs=jax.tree.map(lambda _: VMEM, outs),
+        out_specs=jax.tree.map(lambda _: out_spec, outs),
         scratch_shapes=scratch,
-        compiler_params=pltpu.CompilerParams(vmem_limit_bytes=40 << 20),
+        cost_estimate=pl.CostEstimate(flops=flops, bytes_accessed=0, transcendentals=0),
+        compiler_params=pltpu.CompilerParams(vmem_limit_bytes=vmem << 20),
     )
 
 
@@ -258,10 +294,6 @@
 
 def swap(x, axes):
     return lax.all_to_all(x, axes, 0, 0, tiled=True)
-
-
-def summed(x):
-    return jnp.sum(x.astype(F32), axis=0)
 
 
 def local(
@@ -271,7 +303,7 @@
     grad, first, last, frames = call(
         prepare_kernel,
         (shape(B, 4, 16, C), shape(1, 4, 16, C), shape(1, 4, 16, C), shape(32, 144, 128)),
-        [ANY] * 6,
+        [HBM] * 6,
         [
             counts_scratch,
             pltpu.VMEM((B, 16, 4 * C), BF16),
@@ -281,6 +313,7 @@
             pltpu.VMEM((ROWS, C), BF16),
             pltpu.SemaphoreType.DMA((6,)),
         ],
+        vmem=60,
     )(counts, pre_act, cotangent, norm_gain.reshape(1, C), norm_bias.reshape(1, C), conv_weight)
 
     frames = swap(frames, ("zh", "y"))
@@ -288,6 +321,9 @@
     def shifted(x, axes, count, step):
         pairs = [(i, i + step) for i in range(count) if 0 <= i + step < count]
         return lax.ppermute(x, axes, pairs)
+
+    def flipped(x):
+        return lax.ppermute(x, "c", [(0, 1), (1, 0)])
 
     slab_low = shifted(grad, SLAB, SLABS, 1)
     slab_high = shifted(grad, SLAB, SLABS, -1)
@@ -295,11 +331,12 @@
     dev_high = shifted(first, DEV, DEVS, -1)
 
     fine_scratch = pltpu.VMEM((256, 768), BF16)
-    weight_scratch = pltpu.VMEM((768, C), BF16)
-    conv, taps = call(
+    weight_scratch = pltpu.VMEM((C, 768), BF16)
+    merge_weight = merge_weight.T
+    keep, send, taps = call(
         conv_kernel,
-        (shape(2, C, HALF), shape(3456, C)),
-        [ANY] * 4 + [VMEM] * 5,
+        (shape(SLABS, COLS, HALF), shape(SLABS, COLS, HALF), shape(3456, C)),
+        [HBM] * 4 + [VMEM] * 5,
         [
             counts_scratch,
             pltpu.SMEM((B, 27), jnp.int32),
@@ -310,19 +347,23 @@
             pltpu.VMEM((6, 144, C), BF16),
             pltpu.VMEM((2, C, HALF), F32),
         ],
+        flops=6 * 10**9,
     )(
         counts, neighbours, fine_input, merge_weight, grad, slab_low, slab_high, dev_low, dev_high
     )
 
-    conv = summed(swap(conv, "c")).astype(BF16)
-    conv = swap(conv.reshape(SLABS, COLS, HALF), SLAB)
-    frames, conv = lax.optimization_barrier((frames, conv))
-
-    other = lax.ppermute(frames, "c", [(0, 1), (1, 0)])
-    fine_grad, term = call(
+    conv = call(split_kernel, (shape(COLS, HALF),) * SLABS, [VMEM] * 2)(keep, flipped(send))
+    moved = [conv[0]]
+    for block, (dz, dx) in zip(conv[1:], slab_partners()):
+        pairs = [(i, (i // 4 ^ dz) * 4 + (i + dx) % 4) for i in range(SLABS)]
+        moved.append(lax.ppermute(block, SLAB, pairs))
+    frames, moved = lax.optimization_barrier((frames, moved))
+
+    other = flipped(frames)
+    fine_grad, keep, send = call(
         back_kernel,
-        (shape(256, 768), shape(DEVS * 24, 128)),
-        [ANY] * 3 + [VMEM] * 3,
+        (shape(256, 768), shape(576, 128), shape(576, 128)),
+        [HBM] * 3 + [VMEM] * 3,
         [
             counts_scratch,
             fine_scratch,
@@ -330,18 +371,30 @@
             pltpu.SemaphoreType.DMA((3,)),
             pltpu.VMEM((2, 32, 144, 128), BF16),
             pltpu.VMEM((27 * C, C), BF16),
+            pltpu.VMEM((2, 576, 128), BF16),
         ],
+        flops=4 * 10**9,
+        vmem=48,
     )(counts, fine_input, merge_weight, frames, other, taps)
 
-    conv = call(cut_kernel, shape(32, COLS, ROWS), [VMEM])(conv)
-    conv_grad = summed(swap(conv, ("zh", "y"))).T
-
-    term = swap(term.reshape(DEVS, 24, 128), DEV)
-    term = call(spread_kernel, shape(SLABS, 24, 128), [VMEM])(term)
+    joined = call(join_kernel, shape(32, 2, 24, 128), [VMEM] * (2 + SLABS))(
+        keep.reshape(24, 24, 128), flipped(send).reshape(24, 24, 128), *moved
+    )
+    joined = swap(joined, ("zh", "y"))
+    conv_grad, term = call(
+        part_kernel, (shape(ROWS, COLS, dtype=F32), shape(SLABS, 24, 128)), [VMEM]
+    )(joined)
     term = swap(term, SLAB)
-    term = call(spread_kernel, shape(DEVS, 24, 128), [VMEM])(term)
-    term = swap(term, DEV)
-    merge_grad = call(merge_kernel, shape(768, C, dtype=F32), [VMEM])(term.reshape(DEVS * 24, 128))
+    term = call(spread_kernel, shape(32, 24, 128), [VMEM])(term)
+    term = swap(term, ("zh", "y"))
+    term = lax.all_gather(term, "c", axis=0, tiled=False)
+    merge_grad = call(
+        merge_kernel,
+        shape(C, 768, dtype=F32),
+        [VMEM],
+        [pltpu.VMEM((C, 768), F32), pltpu.SemaphoreType.DMA((1,))],
+        out_spec=HBM,
+    )(term.reshape(2, 768, 128)).T
     return fine_grad, merge_grad, conv_grad
 
 

time: 194 us -> 167 us (0.86)
  blocking collectives: 93.2 us -> 40.2 us
  starting transfers between devices: 40.1 us -> 72.4 us
  local copies, waits for them, and re-layouts: 10.2 us -> 3.42 us
  other arithmetic: 3.82 us -> 0 us
  waiting for transfers between devices: 33.3 us -> 35.5 us
    all_to_all x4 -> x2, blocking collectives: 93.2 us -> 34.6 us  [swap(): return lax.all_to_all(x, axes, 0, 0, tiled=True)]
    ppermute x1 -> x10, starting transfers between devices: 6.37 us -> 36.9 us  [the longest x7 28.1 us: local(): moved.append(lax.ppermute(block, SLAB, pairs))]
    all_to_all x3 -> x2, waiting for transfers between devices: 30.8 us -> 11.2 us  [swap(): return lax.all_to_all(x, axes, 0, 0, tiled=True)]
    ppermute x4, waiting for transfers between devices: 0.01 us -> 15.8 us  [shifted(): return lax.ppermute(x, axes, pairs)]
    unnamed x28 -> x19, local copies, waits for them, and re-layouts: 10.2 us -> 3.42 us
    ppermute x1 -> x10, waiting for transfers between devices: 2.45 us -> 8.47 us  [the longest x3 6.07 us: flipped(): return lax.ppermute(x, 'c', [(0, 1), (1, 0)])]
    all_to_all x3 -> x2, starting transfers between devices: 17.8 us -> 23.5 us  [swap(): return lax.all_to_all(x, axes, 0, 0, tiled=True)]
    all_gather x0 -> x1, blocking collectives: none -> 5.56 us  [local(): term = lax.all_gather(term, 'c', axis=0, tiled=False)]
  transfers between devices with their start and end apart: 8 -> 16, of which waited for: 4 -> 7; matrix products, arithmetic and copies ran while one was open for 1% -> 0% of each run, Pallas kernels for 1% -> 3%
where the time goes in v3:
time: 167 us; the launch traced here: 166 us
  starting transfers between devices  72.4 us (43%)
  blocking collectives  40.2 us (24%)
  waiting for transfers between devices  35.5 us (21%)
  Pallas kernels  13.5 us (8%)
  local copies, waits for them, and re-layouts  3.42 us (2%)
    all_to_all x2, blocking collectives, swap(): return lax.all_to_all(x, axes, 0, 0, tiled=True)  34.6 us
    ppermute x7, starting transfers between devices, local(): moved.append(lax.ppermute(block, SLAB, pairs))  28.1 us
    all_to_all x2, starting transfers between devices, swap(): return lax.all_to_all(x, axes, 0, 0, tiled=True)  23.5 us
    ppermute x4, waiting for transfers between devices, shifted(): return lax.ppermute(x, axes, pairs)  15.8 us
    ppermute x4, starting transfers between devices, shifted(): return lax.ppermute(x, axes, pairs)  12 us
    all_to_all x2, waiting for transfers between devices, swap(): return lax.all_to_all(x, axes, 0, 0, tiled=True)  11.2 us
    ppermute x3, starting transfers between devices, flipped(): return lax.ppermute(x, 'c', [(0, 1), (1, 0)])  8.82 us
    ppermute x3, waiting for transfers between devices, flipped(): return lax.ppermute(x, 'c', [(0, 1), (1, 0)])  6.07 us
  transfers between devices with their start and end apart: 16, of which 7 were waited for; matrix products, arithmetic and copies ran while one was open for 0% of the time, Pallas kernels for 3%

profile of v3, /device:TPU:1, one launch (start us, length us, event | category | flops | bytes accessed | tf_op | source)
XLA Modules:
  0.0 165.9 jit_solution(3728616246293881810)
XLA Ops:
  0.6 2.3 %shard_map.112 = (bf16[4,4,16,192]{3,2,1,0:T(8,128)(2,1)}, bf16[1,4,16,192]{3,2,1,0:T(8,128)(2,1)}, bf16[1,4,16,192]{3,2,1,0:T(8,128)(2,1)}, bf16[32,144,128]{2,1,0:T(8,128)(2,1)}) custom-call(s32[512]{0:T(512)} %counts_in.5, bf16[4,16,768]{2,1,0:T(8,128)(2,1)} %pre_in.1, bf16[4,16,768]{2,1,0:T(8,128)(2,1)} %cot_in.1, f32[1,192]{1,0:T(1,128)} %bitcast.13, ...), custom_call_target="tpu_custom_call" | custom-call | tf_op jit(solution)/shard_map/pallas_call | solution.py:303
  3.0 16.6 %all-to-all-start = ((bf16[32,144,128]{2,1,0:T(8,128)(2,1)}), bf16[32,144,128]{2,1,0:T(8,128)(2,1)S(1)}, u32[]{:S(2)}, u32[]{:S(2)}) async-start(bf16[32,144,128]{2,1,0:T(8,128)(2,1)} %get-tuple-element.32), calls=%async_computation | async-start | bytes 2359296 | tf_op jit(solution)/shard_map/all_to_all | solution.py:296
  21.0 4.0 %collective-permute-start = (bf16[4,4,16,192]{3,2,1,0:T(8,128)(2,1)S(1)}, bf16[4,4,16,192]{3,2,1,0:T(8,128)(2,1)S(1)}, u32[]{:S(2)}, u32[]{:S(2)}) collective-permute-start(bf16[4,4,16,192]{3,2,1,0:T(8,128)(2,1)S(1)} %copy-done.3), channel_id=1, source_target_pairs={{0,64},{64,128},{128,192},{192,256},{256,320},{320,384},{384,448},... | collective-permute-start | bytes 294920 | tf_op jit(solution)/shard_map/ppermute | solution.py:323
  25.0 4.8 %collective-permute-start.2 = (bf16[1,4,16,192]{3,2,1,0:T(8,128)(2,1)S(1)}, bf16[1,4,16,192]{3,2,1,0:T(8,128)(2,1)S(1)}, u32[]{:S(2)}, u32[]{:S(2)}) collective-permute-start(bf16[1,4,16,192]{3,2,1,0:T(8,128)(2,1)S(1)} %copy-done.8), channel_id=1, source_target_pairs={{0,1},{1,2},{2,3},{3,4},{4,5},{5,6},{6,7},{7,8},{8,9},{9,10},{10,1... | collective-permute-start | bytes 73736 | tf_op jit(solution)/shard_map/ppermute | solution.py:323
  31.8 10.9 %collective-permute-done.2.dev_low = bf16[1,4,16,192]{3,2,1,0:T(8,128)(2,1)S(1)} collective-permute-done((bf16[1,4,16,192]{3,2,1,0:T(8,128)(2,1)S(1)}, bf16[1,4,16,192]{3,2,1,0:T(8,128)(2,1)S(1)}, u32[]{:S(2)}, u32[]{:S(2)}) %collective-permute-start.2) | collective-permute-done | bytes 24608 | tf_op jit(solution)/shard_map/ppermute | solution.py:323
  42.7 4.9 %collective-permute-done.3.dev_high = bf16[1,4,16,192]{3,2,1,0:T(8,128)(2,1)S(1)} collective-permute-done((bf16[1,4,16,192]{3,2,1,0:T(8,128)(2,1)S(1)}, bf16[1,4,16,192]{3,2,1,0:T(8,128)(2,1)S(1)}, u32[]{:S(2)}, u32[]{:S(2)}) %collective-permute-start.3) | collective-permute-done | bytes 24608 | tf_op jit(solution)/shard_map/ppermute | solution.py:323
  47.6 5.3 %shard_map.113 = (bf16[8,24,2592]{2,1,0:T(8,128)(2,1)S(1)}, bf16[8,24,2592]{2,1,0:T(8,128)(2,1)S(1)}, bf16[3456,192]{1,0:T(8,128)(2,1)S(1)}) custom-call(s32[512]{0:T(512)S(1)} %copy-done, s32[4,27]{1,0:T(4,128)S(1)} %copy-done.4, bf16[256,768]{1,0:T(8,128)(2,1)S(1)} %copy-done.1, bf16[192,768]{1,0:T(8,128)(2,1)S(1)} %bitcast.10, ...), custom_call_target="tpu_custom_call" | custom-call | flops 6000000000 | tf_op jit(solution)/shard_map/pallas_call | solution.py:336
  56.1 2.6 %collective-permute-done.4.received = bf16[8,24,2592]{2,1,0:T(8,128)(2,1)S(1)} collective-permute-done((bf16[8,24,2592]{2,1,0:T(8,128)(2,1)S(1)}, bf16[8,24,2592]{2,1,0:T(8,128)(2,1)S(1)}, u32[]{:S(2)}, u32[]{:S(2)}) %collective-permute-start.4) | collective-permute-done | bytes 995360 | tf_op jit(solution)/shard_map/ppermute | solution.py:326
  58.9 3.1 %collective-permute-start.5 = (bf16[24,2592]{1,0:T(8,128)(2,1)S(1)}, bf16[24,2592]{1,0:T(8,128)(2,1)S(1)}, u32[]{:S(2)}, u32[]{:S(2)}) collective-permute-start(bf16[24,2592]{1,0:T(8,128)(2,1)S(1)} %get-tuple-element.39), channel_id=1, source_target_pairs={{0,64},{64,128},{128,192},{192,0},{256,320},{320,384},{384,448},{4... | collective-permute-start | bytes 373256 | tf_op jit(solution)/shard_map/ppermute | solution.py:359
  62.0 7.7 %collective-permute-start.6 = (bf16[24,2592]{1,0:T(8,128)(2,1)S(1)}, bf16[24,2592]{1,0:T(8,128)(2,1)S(1)}, u32[]{:S(2)}, u32[]{:S(2)}) collective-permute-start(bf16[24,2592]{1,0:T(8,128)(2,1)S(1)} %get-tuple-element.40), channel_id=1, source_target_pairs={{0,128},{64,192},{128,0},{192,64},{256,384},{320,448},{384,256},{4... | collective-permute-start | bytes 373256 | tf_op jit(solution)/shard_map/ppermute | solution.py:359
  71.7 4.6 %collective-permute-start.8 = (bf16[24,2592]{1,0:T(8,128)(2,1)S(1)}, bf16[24,2592]{1,0:T(8,128)(2,1)S(1)}, u32[]{:S(2)}, u32[]{:S(2)}) collective-permute-start(bf16[24,2592]{1,0:T(8,128)(2,1)S(1)} %get-tuple-element.42), channel_id=1, source_target_pairs={{0,256},{64,320},{128,384},{192,448},{256,0},{320,64},{384,128},{4... | collective-permute-start | bytes 373256 | tf_op jit(solution)/shard_map/ppermute | solution.py:359
  76.3 2.2 %collective-permute-start.9 = (bf16[24,2592]{1,0:T(8,128)(2,1)S(1)}, bf16[24,2592]{1,0:T(8,128)(2,1)S(1)}, u32[]{:S(2)}, u32[]{:S(2)}) collective-permute-start(bf16[24,2592]{1,0:T(8,128)(2,1)S(1)} %get-tuple-element.43), channel_id=1, source_target_pairs={{0,320},{64,384},{128,448},{192,256},{256,64},{320,128},{384,192},... | collective-permute-start | bytes 373256 | tf_op jit(solution)/shard_map/ppermute | solution.py:359
  78.5 4.3 %collective-permute-start.10 = (bf16[24,2592]{1,0:T(8,128)(2,1)S(1)}, bf16[24,2592]{1,0:T(8,128)(2,1)S(1)}, u32[]{:S(2)}, u32[]{:S(2)}) collective-permute-start(bf16[24,2592]{1,0:T(8,128)(2,1)S(1)} %get-tuple-element.44), channel_id=1, source_target_pairs={{0,384},{64,448},{128,256},{192,320},{256,128},{320,192},{384,0},{... | collective-permute-start | bytes 373256 | tf_op jit(solution)/shard_map/ppermute | solution.py:359
  82.8 4.3 %collective-permute-start.11 = (bf16[24,2592]{1,0:T(8,128)(2,1)S(1)}, bf16[24,2592]{1,0:T(8,128)(2,1)S(1)}, u32[]{:S(2)}, u32[]{:S(2)}) collective-permute-start(bf16[24,2592]{1,0:T(8,128)(2,1)S(1)} %get-tuple-element.45), channel_id=1, source_target_pairs={{0,448},{64,256},{128,320},{192,384},{256,192},{320,0},{384,64},{4... | collective-permute-start | bytes 373256 | tf_op jit(solution)/shard_map/ppermute | solution.py:359
  87.1 2.4 %collective-permute-done.11.refs_7_ = bf16[24,2592]{1,0:T(8,128)(2,1)S(1)} collective-permute-done((bf16[24,2592]{1,0:T(8,128)(2,1)S(1)}, bf16[24,2592]{1,0:T(8,128)(2,1)S(1)}, u32[]{:S(2)}, u32[]{:S(2)}) %collective-permute-start.11) | collective-permute-done | bytes 124448 | tf_op jit(solution)/shard_map/ppermute | solution.py:359
  89.5 4.7 %collective-permute-start.12 = (bf16[32,144,128]{2,1,0:T(8,128)(2,1)S(1)}, bf16[32,144,128]{2,1,0:T(8,128)(2,1)S(1)}, u32[]{:S(2)}, u32[]{:S(2)}) collective-permute-start(bf16[32,144,128]{2,1,0:T(8,128)(2,1)S(1)} %all-to-all-done.mine), channel_id=1, source_target_pairs={{0,1},{1,0},{2,3},{3,2},{4,5},{5,4},{6,7},{7,6},{8,9},{9,8},{10,11... | collective-permute-start | bytes 3538952 | tf_op jit(solution)/shard_map/ppermute | solution.py:326
  94.2 2.5 %collective-permute-done.12.other = bf16[32,144,128]{2,1,0:T(8,128)(2,1)S(1)} collective-permute-done((bf16[32,144,128]{2,1,0:T(8,128)(2,1)S(1)}, bf16[32,144,128]{2,1,0:T(8,128)(2,1)S(1)}, u32[]{:S(2)}, u32[]{:S(2)}) %collective-permute-start.12) | collective-permute-done | bytes 1179680 | tf_op jit(solution)/shard_map/ppermute | solution.py:326
  98.1 3.7 %shard_map.115 = (bf16[256,768]{1,0:T(8,128)(2,1)}, bf16[576,128]{1,0:T(8,128)(2,1)S(1)}, bf16[576,128]{1,0:T(8,128)(2,1)S(1)}) custom-call(s32[512]{0:T(512)S(1)} %copy-done, bf16[256,768]{1,0:T(8,128)(2,1)S(1)} %copy-done.1, bf16[192,768]{1,0:T(8,128)(2,1)S(1)} %bitcast.11, bf16[32,144,128]{2,1,0:T(8,128)(2,1)S(1)} %all-to-all-done.mine, ...), custom_call_target="tpu_custom_call" | custom-call | flops 4000000000 | tf_op jit(solution)/shard_map/pallas_call | solution.py:363
  101.9 2.2 %collective-permute-start.13 = (bf16[576,128]{1,0:T(8,128)(2,1)S(1)}, bf16[576,128]{1,0:T(8,128)(2,1)S(1)}, u32[]{:S(2)}, u32[]{:S(2)}) collective-permute-start(bf16[576,128]{1,0:T(8,128)(2,1)S(1)} %get-tuple-element.50), channel_id=1, source_target_pairs={{0,1},{1,0},{2,3},{3,2},{4,5},{5,4},{6,7},{7,6},{8,9},{9,8},{10,11... | collective-permute-start | bytes 442376 | tf_op jit(solution)/shard_map/ppermute | solution.py:326
  105.4 24.6 %all_to_all.20.parts = bf16[32,2,24,128]{3,2,1,0:T(8,128)(2,1)S(1)} all-to-all(bf16[32,2,24,128]{3,2,1,0:T(8,128)(2,1)S(1)} %shard_map.116), channel_id=1, replica_groups=mesh['zl'=2,'x'=4,'zh'=4,'y'=8,'c'=2] {'zh','y'}, dimensions={0} | all-to-all | bytes 786432 | tf_op jit(solution)/shard_map/all_to_all | solution.py:296
  130.1 10.0 %all_to_all.21.parts = bf16[8,24,128]{2,1,0:T(8,128)(2,1)S(1)} all-to-all(bf16[8,24,128]{2,1,0:T(8,128)(2,1)S(1)} %get-tuple-element.59), channel_id=1, replica_groups=mesh['zl'=2,'x'=4,'zh'=4,'y'=8,'c'=2] {'zl','x'}, dimensions={0} | all-to-all | bytes 98304 | tf_op jit(solution)/shard_map/all_to_all | solution.py:296
  140.8 6.8 %all-to-all-start.3 = ((bf16[32,24,128]{2,1,0:T(8,128)(2,1)}), bf16[32,24,128]{2,1,0:T(8,128)(2,1)S(1)}, u32[]{:S(2)}, u32[]{:S(2)}) async-start(bf16[32,24,128]{2,1,0:T(8,128)(2,1)} %shard_map.118), calls=%async_computation.3 | async-start | bytes 393216 | tf_op jit(solution)/shard_map/all_to_all | solution.py:296
  148.3 11.2 %all-to-all-done.3 = bf16[32,24,128]{2,1,0:T(8,128)(2,1)S(1)} async-done(((bf16[32,24,128]{2,1,0:T(8,128)(2,1)}), bf16[32,24,128]{2,1,0:T(8,128)(2,1)S(1)}, u32[]{:S(2)}, u32[]{:S(2)}) %all-to-all-start.3) | async-done | bytes 196640 | tf_op jit(solution)/shard_map/all_to_all | solution.py:296
  159.5 5.6 %all-gather = bf16[64,24,128]{2,1,0:T(8,128)(2,1)S(1)} all-gather(bf16[32,24,128]{2,1,0:T(8,128)(2,1)S(1)} %all-to-all-done.3), channel_id=2, replica_groups=mesh['zl'=2,'x'=4,'zh'=4,'y'=8,'c'=2] {'c'}, dimensions={0}, use_global_device_ids=true | all-gather | bytes 589824 | tf_op jit(solution)/shard_map/all_gather | solution.py:390
  (38 shorter events, 13.7 us)
Async XLA Ops:
  2.9 16.7 %copy-start.3 = (bf16[4,4,16,192]{3,2,1,0:T(8,128)(2,1)S(1)}, bf16[4,4,16,192]{3,2,1,0:T(8,128)(2,1)}, u32[]{:S(2)}) copy-start(bf16[4,4,16,192]{3,2,1,0:T(8,128)(2,1)} %get-tuple-element.33.grad) | copy-start | bytes 294916
  2.9 22.0 %copy-start.8 = (bf16[1,4,16,192]{3,2,1,0:T(8,128)(2,1)S(1)}, bf16[1,4,16,192]{3,2,1,0:T(8,128)(2,1)}, u32[]{:S(2)}) copy-start(bf16[1,4,16,192]{3,2,1,0:T(8,128)(2,1)} %get-tuple-element.34) | copy-start | bytes 73732
  3.0 26.9 %copy-start.7 = (bf16[1,4,16,192]{3,2,1,0:T(8,128)(2,1)S(1)}, bf16[1,4,16,192]{3,2,1,0:T(8,128)(2,1)}, u32[]{:S(2)}) copy-start(bf16[1,4,16,192]{3,2,1,0:T(8,128)(2,1)} %get-tuple-element.35) | copy-start | bytes 73732
  3.0 44.6 %copy-start = (s32[512]{0:T(512)S(1)}, s32[512]{0:T(512)}, u32[]{:S(2)}) copy-start(s32[512]{0:T(512)} %counts_in.5) | copy-start | bytes 6148
  3.0 44.6 %copy-start.1 = (bf16[256,768]{1,0:T(8,128)(2,1)S(1)}, bf16[256,768]{1,0:T(8,128)(2,1)}, u32[]{:S(2)}) copy-start(bf16[256,768]{1,0:T(8,128)(2,1)} %fine_in.3) | copy-start | bytes 1179652
  3.0 44.6 %copy-start.2 = (bf16[768,192]{0,1:T(8,128)(2,1)S(1)}, bf16[768,192]{0,1:T(8,128)(2,1)}, u32[]{:S(2)}) copy-start(bf16[768,192]{0,1:T(8,128)(2,1)} %param.10) | copy-start | bytes 884740
  3.0 44.6 %copy-start.4 = (s32[4,27]{1,0:T(4,128)S(1)}, s32[4,27]{1,0:T(4,128)}, u32[]{:S(2)}) copy-start(s32[4,27]{1,0:T(4,128)} %near_in.1) | copy-start | bytes 1300
  3.0 86.5 %all-to-all-start = ((bf16[32,144,128]{2,1,0:T(8,128)(2,1)}), bf16[32,144,128]{2,1,0:T(8,128)(2,1)S(1)}, u32[]{:S(2)}, u32[]{:S(2)}) async-start(bf16[32,144,128]{2,1,0:T(8,128)(2,1)} %get-tuple-element.32), calls=%async_computation | async-start | bytes 2359296 | tf_op jit(solution)/shard_map/all_to_all | solution.py:296
  19.7 27.9 %collective-permute-start.1 = (bf16[4,4,16,192]{3,2,1,0:T(8,128)(2,1)S(1)}, bf16[4,4,16,192]{3,2,1,0:T(8,128)(2,1)S(1)}, u32[]{:S(2)}, u32[]{:S(2)}) collective-permute-start(bf16[4,4,16,192]{3,2,1,0:T(8,128)(2,1)S(1)} %copy-done.3), channel_id=1, source_target_pairs={{64,0},{128,64},{192,128},{256,192},{320,256},{384,320},{448,384},... | collective-permute-start | bytes 294920 | tf_op jit(solution)/shard_map/ppermute | solution.py:323
  21.0 26.6 %collective-permute-start = (bf16[4,4,16,192]{3,2,1,0:T(8,128)(2,1)S(1)}, bf16[4,4,16,192]{3,2,1,0:T(8,128)(2,1)S(1)}, u32[]{:S(2)}, u32[]{:S(2)}) collective-permute-start(bf16[4,4,16,192]{3,2,1,0:T(8,128)(2,1)S(1)} %copy-done.3), channel_id=1, source_target_pairs={{0,64},{64,128},{128,192},{192,256},{256,320},{320,384},{384,448},... | collective-permute-start | bytes 294920 | tf_op jit(solution)/shard_map/ppermute | solution.py:323
  25.0 17.7 %collective-permute-start.2 = (bf16[1,4,16,192]{3,2,1,0:T(8,128)(2,1)S(1)}, bf16[1,4,16,192]{3,2,1,0:T(8,128)(2,1)S(1)}, u32[]{:S(2)}, u32[]{:S(2)}) collective-permute-start(bf16[1,4,16,192]{3,2,1,0:T(8,128)(2,1)S(1)} %copy-done.8), channel_id=1, source_target_pairs={{0,1},{1,2},{2,3},{3,4},{4,5},{5,6},{6,7},{7,8},{8,9},{9,10},{10,1... | collective-permute-start | bytes 73736 | tf_op jit(solution)/shard_map/ppermute | solution.py:323
  29.8 17.7 %collective-permute-start.3 = (bf16[1,4,16,192]{3,2,1,0:T(8,128)(2,1)S(1)}, bf16[1,4,16,192]{3,2,1,0:T(8,128)(2,1)S(1)}, u32[]{:S(2)}, u32[]{:S(2)}) collective-permute-start(bf16[1,4,16,192]{3,2,1,0:T(8,128)(2,1)S(1)} %copy-done.7), channel_id=1, source_target_pairs={{1,0},{2,1},{3,2},{4,3},{5,4},{6,5},{7,6},{8,7},{9,8},{10,9},{11,1... | collective-permute-start | bytes 73736 | tf_op jit(solution)/shard_map/ppermute | solution.py:323
  54.2 4.5 %collective-permute-start.4 = (bf16[8,24,2592]{2,1,0:T(8,128)(2,1)S(1)}, bf16[8,24,2592]{2,1,0:T(8,128)(2,1)S(1)}, u32[]{:S(2)}, u32[]{:S(2)}) collective-permute-start(bf16[8,24,2592]{2,1,0:T(8,128)(2,1)S(1)} %get-tuple-element.37), channel_id=1, source_target_pairs={{0,1},{1,0},{2,3},{3,2},{4,5},{5,4},{6,7},{7,6},{8,9},{9,8},{10,11... | collective-permute-start | bytes 2985992 | tf_op jit(solution)/shard_map/ppermute | solution.py:326
  58.9 19.6 %collective-permute-start.5 = (bf16[24,2592]{1,0:T(8,128)(2,1)S(1)}, bf16[24,2592]{1,0:T(8,128)(2,1)S(1)}, u32[]{:S(2)}, u32[]{:S(2)}) collective-permute-start(bf16[24,2592]{1,0:T(8,128)(2,1)S(1)} %get-tuple-element.39), channel_id=1, source_target_pairs={{0,64},{64,128},{128,192},{192,0},{256,320},{320,384},{384,448},{4... | collective-permute-start | bytes 373256 | tf_op jit(solution)/shard_map/ppermute | solution.py:359
  62.0 20.7 %collective-permute-start.6 = (bf16[24,2592]{1,0:T(8,128)(2,1)S(1)}, bf16[24,2592]{1,0:T(8,128)(2,1)S(1)}, u32[]{:S(2)}, u32[]{:S(2)}) collective-permute-start(bf16[24,2592]{1,0:T(8,128)(2,1)S(1)} %get-tuple-element.40), channel_id=1, source_target_pairs={{0,128},{64,192},{128,0},{192,64},{256,384},{320,448},{384,256},{4... | collective-permute-start | bytes 373256 | tf_op jit(solution)/shard_map/ppermute | solution.py:359
  69.8 17.3 %collective-permute-start.7 = (bf16[24,2592]{1,0:T(8,128)(2,1)S(1)}, bf16[24,2592]{1,0:T(8,128)(2,1)S(1)}, u32[]{:S(2)}, u32[]{:S(2)}) collective-permute-start(bf16[24,2592]{1,0:T(8,128)(2,1)S(1)} %get-tuple-element.41), channel_id=1, source_target_pairs={{0,192},{64,0},{128,64},{192,128},{256,448},{320,256},{384,320},{4... | collective-permute-start | bytes 373256 | tf_op jit(solution)/shard_map/ppermute | solution.py:359
  71.7 15.4 %collective-permute-start.8 = (bf16[24,2592]{1,0:T(8,128)(2,1)S(1)}, bf16[24,2592]{1,0:T(8,128)(2,1)S(1)}, u32[]{:S(2)}, u32[]{:S(2)}) collective-permute-start(bf16[24,2592]{1,0:T(8,128)(2,1)S(1)} %get-tuple-element.42), channel_id=1, source_target_pairs={{0,256},{64,320},{128,384},{192,448},{256,0},{320,64},{384,128},{4... | collective-permute-start | bytes 373256 | tf_op jit(solution)/shard_map/ppermute | solution.py:359
  76.3 10.8 %collective-permute-start.9 = (bf16[24,2592]{1,0:T(8,128)(2,1)S(1)}, bf16[24,2592]{1,0:T(8,128)(2,1)S(1)}, u32[]{:S(2)}, u32[]{:S(2)}) collective-permute-start(bf16[24,2592]{1,0:T(8,128)(2,1)S(1)} %get-tuple-element.43), channel_id=1, source_target_pairs={{0,320},{64,384},{128,448},{192,256},{256,64},{320,128},{384,192},... | collective-permute-start | bytes 373256 | tf_op jit(solution)/shard_map/ppermute | solution.py:359
  78.5 8.6 %collective-permute-start.10 = (bf16[24,2592]{1,0:T(8,128)(2,1)S(1)}, bf16[24,2592]{1,0:T(8,128)(2,1)S(1)}, u32[]{:S(2)}, u32[]{:S(2)}) collective-permute-start(bf16[24,2592]{1,0:T(8,128)(2,1)S(1)} %get-tuple-element.44), channel_id=1, source_target_pairs={{0,384},{64,448},{128,256},{192,320},{256,128},{320,192},{384,0},{... | collective-permute-start | bytes 373256 | tf_op jit(solution)/shard_map/ppermute | solution.py:359
  82.8 6.7 %collective-permute-start.11 = (bf16[24,2592]{1,0:T(8,128)(2,1)S(1)}, bf16[24,2592]{1,0:T(8,128)(2,1)S(1)}, u32[]{:S(2)}, u32[]{:S(2)}) collective-permute-start(bf16[24,2592]{1,0:T(8,128)(2,1)S(1)} %get-tuple-element.45), channel_id=1, source_target_pairs={{0,448},{64,256},{128,320},{192,384},{256,192},{320,0},{384,64},{4... | collective-permute-start | bytes 373256 | tf_op jit(solution)/shard_map/ppermute | solution.py:359
  89.5 7.1 %collective-permute-start.12 = (bf16[32,144,128]{2,1,0:T(8,128)(2,1)S(1)}, bf16[32,144,128]{2,1,0:T(8,128)(2,1)S(1)}, u32[]{:S(2)}, u32[]{:S(2)}) collective-permute-start(bf16[32,144,128]{2,1,0:T(8,128)(2,1)S(1)} %all-to-all-done.mine), channel_id=1, source_target_pairs={{0,1},{1,0},{2,3},{3,2},{4,5},{5,4},{6,7},{7,6},{8,9},{9,8},{10,11... | collective-permute-start | bytes 3538952 | tf_op jit(solution)/shard_map/ppermute | solution.py:326
  96.7 1.5 copy-start.6
  101.9 3.3 %collective-permute-start.13 = (bf16[576,128]{1,0:T(8,128)(2,1)S(1)}, bf16[576,128]{1,0:T(8,128)(2,1)S(1)}, u32[]{:S(2)}, u32[]{:S(2)}) collective-permute-start(bf16[576,128]{1,0:T(8,128)(2,1)S(1)} %get-tuple-element.50), channel_id=1, source_target_pairs={{0,1},{1,0},{2,3},{3,2},{4,5},{5,4},{6,7},{7,6},{8,9},{9,8},{10,11... | collective-permute-start | bytes 442376 | tf_op jit(solution)/shard_map/ppermute | solution.py:326
  140.8 18.7 %all-to-all-start.3 = ((bf16[32,24,128]{2,1,0:T(8,128)(2,1)}), bf16[32,24,128]{2,1,0:T(8,128)(2,1)S(1)}, u32[]{:S(2)}, u32[]{:S(2)}) async-start(bf16[32,24,128]{2,1,0:T(8,128)(2,1)} %shard_map.118), calls=%async_computation.3 | async-start | bytes 393216 | tf_op jit(solution)/shard_map/all_to_all | solution.py:296
  (1 other events, 1.2 us)

commit v4 on v3

--- a/solution.py
+++ b/solution.py
@@ -117,7 +117,7 @@
 
 def conv_kernel(
     counts_in, near_in, fine_in, weight_in, grad, slab_low, slab_high, dev_low, dev_high,
-    keep, send, taps, counts, near, fine, weight, sems, bricks, block, total,
+    keep, send, taps_out, counts, near, fine, weight, sems, bricks, block, total, taps,
 ):
     copies = fetch(
         sems, (counts_in, counts), (near_in, near), (fine_in, fine), (weight_in, weight)
@@ -152,6 +152,8 @@
             for s in range(9):
                 row = ((s * 6 + plane) * B + b) * 16
                 taps[row : row + 16] = moved[s * 16 : (s + 1) * 16]
+    leave = pltpu.make_async_copy(taps, taps_out, sems.at[4])
+    leave.start()
     for copy in (copies[0], copies[2], copies[3]):
         copy.wait()
     count = counts[place]
@@ -176,24 +178,31 @@
     for out, half in ((keep, core), (send, 1 - core)):
         for slab in range(SLABS):
             out[slab] = total[half, slab * COLS : (slab + 1) * COLS].astype(BF16)
-
-
-def slab_partners():
-    return [(dz, dx) for dz in range(2) for dx in range(4) if dz or dx]
+    leave.wait()
 
 
 def split_kernel(keep, received, *outs):
-    zl, x = lax.axis_index("zl"), lax.axis_index("x")
-    for out, (dz, dx) in zip(outs, [(0, 0)] + slab_partners()):
-        slab = jnp.bitwise_xor(zl, dz) * 4 + jnp.bitwise_and(x + dx, 3)
-        out[...] = (keep[slab].astype(F32) + received[slab].astype(F32)).astype(BF16)
+    x = lax.axis_index("x")
+    for dx, out in enumerate(outs):
+        for zl in range(2):
+            slab = zl * 4 + jnp.bitwise_and(x + dx, 3)
+            out[zl] = (keep[slab].astype(F32) + received[slab].astype(F32)).astype(BF16)
+
+
+def halve_kernel(a, b, c, d, keep, send):
+    zl = lax.axis_index("zl")
+    for out, half in ((keep, zl), (send, 1 - zl)):
+        total = a[half].astype(F32) + b[half].astype(F32) + c[half].astype(F32)
+        out[...] = (total + d[half].astype(F32)).astype(BF16)
 
 
 def back_kernel(
-    counts_in, fine_in, weight_in, mine, other, taps, fine_grad, keep, send,
-    counts, fine, weight, sems, both, whole, term,
+    counts_in, fine_in, weight_in, taps_in, mine, other, fine_grad, keep, send,
+    counts, fine, weight, taps, sems, both, whole, term,
 ):
-    copies = fetch(sems, (counts_in, counts), (fine_in, fine), (weight_in, weight))
+    copies = fetch(
+        sems, (counts_in, counts), (fine_in, fine), (weight_in, weight), (taps_in, taps)
+    )
     place = my_place()
     core = jnp.bitwise_and(place, 1)
     both[core] = mine[...]
@@ -214,12 +223,13 @@
             whole[row : row + FRAME, :128] = main
             whole[row : row + 48, 128:] = low
         whole[row + 48 : row + FRAME, 128:] = high
+    copies[3].wait()
     back = jnp.zeros((256, C), F32)
     for tap in range(27):
         row = tap_rows(tap)
         back = back + dot(taps[row : row + 256], whole[tap * C : (tap + 1) * C])
     brick_of = lax.broadcasted_iota(jnp.int32, (256, C), 0) // 16 % B
-    for copy in copies:
+    for copy in copies[:3]:
         copy.wait()
     count = counts[place]
     back = jnp.where(brick_of < count, back, 0.0).astype(BF16)
@@ -234,11 +244,8 @@
     send[...] = term[1 - core]
 
 
-def join_kernel(keep, received, *refs):
-    parts, out = refs[:-1], refs[-1]
-    total = parts[0][...].astype(F32)
-    for part in parts[1:]:
-        total = total + part[...].astype(F32)
+def join_kernel(keep, received, conv_keep, conv_received, out):
+    total = conv_keep[...].astype(F32) + conv_received[...].astype(F32)
     pad = jnp.zeros((COLS, 128 - ROWS), BF16)
     for i in range(32):
         piece = total[:, i * ROWS : (i + 1) * ROWS].astype(BF16)
@@ -276,12 +283,12 @@
     copy.wait()
 
 
-def call(kernel, outs, specs, scratch=(), flops=0, out_spec=VMEM, vmem=40):
+def call(kernel, outs, specs, scratch=(), flops=0, out_spec=None, vmem=40):
     return pl.pallas_call(
         kernel,
         out_shape=outs,
         in_specs=specs,
-        out_specs=jax.tree.map(lambda _: out_spec, outs),
+        out_specs=out_spec or jax.tree.map(lambda _: VMEM, outs),
         scratch_shapes=scratch,
         cost_estimate=pl.CostEstimate(flops=flops, bytes_accessed=0, transcendentals=0),
         compiler_params=pltpu.CompilerParams(vmem_limit_bytes=vmem << 20),
@@ -316,8 +323,6 @@
         vmem=60,
     )(counts, pre_act, cotangent, norm_gain.reshape(1, C), norm_bias.reshape(1, C), conv_weight)
 
-    frames = swap(frames, ("zh", "y"))
-
     def shifted(x, axes, count, step):
         pairs = [(i, i + step) for i in range(count) if 0 <= i + step < count]
         return lax.ppermute(x, axes, pairs)
@@ -330,7 +335,13 @@
     dev_low = shifted(last, DEV, DEVS, 1)
     dev_high = shifted(first, DEV, DEVS, -1)
 
+    frames, slab_low, slab_high, dev_low, dev_high = lax.optimization_barrier(
+        (frames, slab_low, slab_high, dev_low, dev_high)
+    )
+    frames = swap(frames, ("zh", "y"))
+
     fine_scratch = pltpu.VMEM((256, 768), BF16)
+    taps_scratch = pltpu.VMEM((3456, C), BF16)
     weight_scratch = pltpu.VMEM((C, 768), BF16)
     merge_weight = merge_weight.T
     keep, send, taps = call(
@@ -342,43 +353,47 @@
             pltpu.SMEM((B, 27), jnp.int32),
             fine_scratch,
             weight_scratch,
-            pltpu.SemaphoreType.DMA((4,)),
+            pltpu.SemaphoreType.DMA((5,)),
             pltpu.VMEM((15, 4, 16, C), BF16),
             pltpu.VMEM((6, 144, C), BF16),
             pltpu.VMEM((2, C, HALF), F32),
+            taps_scratch,
         ],
         flops=6 * 10**9,
+        out_spec=(VMEM, VMEM, HBM),
     )(
         counts, neighbours, fine_input, merge_weight, grad, slab_low, slab_high, dev_low, dev_high
     )
 
-    conv = call(split_kernel, (shape(COLS, HALF),) * SLABS, [VMEM] * 2)(keep, flipped(send))
-    moved = [conv[0]]
-    for block, (dz, dx) in zip(conv[1:], slab_partners()):
-        pairs = [(i, (i // 4 ^ dz) * 4 + (i + dx) % 4) for i in range(SLABS)]
-        moved.append(lax.ppermute(block, SLAB, pairs))
-    frames, moved = lax.optimization_barrier((frames, moved))
+    conv = call(split_kernel, (shape(2, COLS, HALF),) * 4, [VMEM] * 2)(keep, flipped(send))
+    conv = [conv[0]] + [
+        lax.ppermute(conv[dx], "x", [(i, (i + dx) % 4) for i in range(4)]) for dx in (1, 2, 3)
+    ]
+    keep, send = call(halve_kernel, (shape(COLS, HALF),) * 2, [VMEM] * 4)(*conv)
+    conv = (keep, lax.ppermute(send, "zl", [(0, 1), (1, 0)]))
+    frames, conv = lax.optimization_barrier((frames, conv))
 
     other = flipped(frames)
     fine_grad, keep, send = call(
         back_kernel,
         (shape(256, 768), shape(576, 128), shape(576, 128)),
-        [HBM] * 3 + [VMEM] * 3,
+        [HBM] * 4 + [VMEM] * 2,
         [
             counts_scratch,
             fine_scratch,
             weight_scratch,
-            pltpu.SemaphoreType.DMA((3,)),
+            taps_scratch,
+            pltpu.SemaphoreType.DMA((4,)),
             pltpu.VMEM((2, 32, 144, 128), BF16),
             pltpu.VMEM((27 * C, C), BF16),
             pltpu.VMEM((2, 576, 128), BF16),
         ],
         flops=4 * 10**9,
         vmem=48,
-    )(counts, fine_input, merge_weight, frames, other, taps)
-
-    joined = call(join_kernel, shape(32, 2, 24, 128), [VMEM] * (2 + SLABS))(
-        keep.reshape(24, 24, 128), flipped(send).reshape(24, 24, 128), *moved
+    )(counts, fine_input, merge_weight, taps, frames, other)
+
+    joined = call(join_kernel, shape(32, 2, 24, 128), [VMEM] * 4)(
+        keep.reshape(24, 24, 128), flipped(send).reshape(24, 24, 128), *conv
     )
     joined = swap(joined, ("zh", "y"))
     conv_grad, term = call(

time: 167 us -> 150 us (0.90)
  starting transfers between devices: 72.4 us -> 59.9 us
  waiting for transfers between devices: 35.5 us -> 31.3 us
    ppermute x4, waiting for transfers between devices: 15.8 us -> 1.05 us  [shifted(): return lax.ppermute(x, axes, pairs)]
    ppermute x7 -> x4, starting transfers between devices: 28.1 us -> 13.4 us  [the longest x3 11.5 us: local(): lax.ppermute(conv[dx], 'x', [(i, (i + dx) % 4) for i in range(4)])]
    ppermute x7 -> x4, waiting for transfers between devices: 2.41 us -> 13 us  [the longest x3 9.24 us: local(): lax.ppermute(conv[dx], 'x', [(i, (i + dx) % 4) for i in range(4)])]
    ppermute x4, starting transfers between devices: 12 us -> 15.9 us  [shifted(): return lax.ppermute(x, axes, pairs)]
    unnamed x19 -> x15, local copies, waits for them, and re-layouts: 3.42 us -> 2.18 us
  transfers between devices with their start and end apart: 16 -> 13, of which waited for: 7 -> 9; matrix products, arithmetic and copies ran while one was open for 0% -> 0% of each run, Pallas kernels for 3% -> 4%
where the time goes in v4:
time: 150 us; the launch traced here: 149 us
  starting transfers between devices  59.9 us (40%)
  blocking collectives  40.6 us (27%)
  waiting for transfers between devices  31.3 us (21%)
  Pallas kernels  14.5 us (10%)
  local copies, waits for them, and re-layouts  2.18 us (1%)
    all_to_all x2, blocking collectives, swap(): return lax.all_to_all(x, axes, 0, 0, tiled=True)  35 us
    all_to_all x2, starting transfers between devices, swap(): return lax.all_to_all(x, axes, 0, 0, tiled=True)  22.3 us
    ppermute x4, starting transfers between devices, shifted(): return lax.ppermute(x, axes, pairs)  15.9 us
    ppermute x3, starting transfers between devices, local(): lax.ppermute(conv[dx], 'x', [(i, (i + dx) % 4) for i in range(4)])  11.5 us
    all_to_all x2, waiting for transfers between devices, swap(): return lax.all_to_all(x, axes, 0, 0, tiled=True)  11.2 us
    ppermute x3, waiting for transfers between devices, local(): lax.ppermute(conv[dx], 'x', [(i, (i + dx) % 4) for i in range(4)])  9.24 us
    ppermute x3, starting transfers between devices, flipped(): return lax.ppermute(x, 'c', [(0, 1), (1, 0)])  8.19 us
    ppermute x3, waiting for transfers between devices, flipped(): return lax.ppermute(x, 'c', [(0, 1), (1, 0)])  6.04 us
  transfers between devices with their start and end apart: 13, of which 9 were waited for; matrix products, arithmetic and copies ran while one was open for 0% of the time, Pallas kernels for 4%

profile of v4, /device:TPU:1, one launch (start us, length us, event | category | flops | bytes accessed | tf_op | source)
XLA Modules:
  0.0 149.3 jit_solution(14726796179381509620)
XLA Ops:
  0.6 2.3 %shard_map.112 = (bf16[4,4,16,192]{3,2,1,0:T(8,128)(2,1)}, bf16[1,4,16,192]{3,2,1,0:T(8,128)(2,1)}, bf16[1,4,16,192]{3,2,1,0:T(8,128)(2,1)}, bf16[32,144,128]{2,1,0:T(8,128)(2,1)}) custom-call(s32[512]{0:T(512)} %counts_in.5, bf16[4,16,768]{2,1,0:T(8,128)(2,1)} %pre_in.1, bf16[4,16,768]{2,1,0:T(8,128)(2,1)} %cot_in.1, f32[1,192]{1,0:T(1,128)} %bitcast.13, ...), custom_call_target="tpu_custom_call" | custom-call | tf_op jit(solution)/shard_map/pallas_call | solution.py:310
  4.2 4.6 %collective-permute-start = (bf16[4,4,16,192]{3,2,1,0:T(8,128)(2,1)}, bf16[4,4,16,192]{3,2,1,0:T(8,128)(2,1)S(1)}, u32[]{:S(2)}, u32[]{:S(2)}) collective-permute-start(bf16[4,4,16,192]{3,2,1,0:T(8,128)(2,1)} %get-tuple-element.29.grad), channel_id=1, source_target_pairs={{0,64},{64,128},{128,192},{192,256},{256,320},{320,384},{384,448},... | collective-permute-start | bytes 294920 | tf_op jit(solution)/shard_map/ppermute | solution.py:328
  8.8 4.6 %collective-permute-start.2 = (bf16[1,4,16,192]{3,2,1,0:T(8,128)(2,1)}, bf16[1,4,16,192]{3,2,1,0:T(8,128)(2,1)S(1)}, u32[]{:S(2)}, u32[]{:S(2)}) collective-permute-start(bf16[1,4,16,192]{3,2,1,0:T(8,128)(2,1)} %get-tuple-element.31), channel_id=1, source_target_pairs={{0,1},{1,2},{2,3},{3,4},{4,5},{5,6},{6,7},{7,8},{8,9},{9,10},{10,1... | collective-permute-start | bytes 73736 | tf_op jit(solution)/shard_map/ppermute | solution.py:328
  13.4 5.5 %collective-permute-start.3 = (bf16[1,4,16,192]{3,2,1,0:T(8,128)(2,1)}, bf16[1,4,16,192]{3,2,1,0:T(8,128)(2,1)S(1)}, u32[]{:S(2)}, u32[]{:S(2)}) collective-permute-start(bf16[1,4,16,192]{3,2,1,0:T(8,128)(2,1)} %get-tuple-element.32), channel_id=1, source_target_pairs={{1,0},{2,1},{3,2},{4,3},{5,4},{6,5},{7,6},{8,7},{9,8},{10,9},{11,1... | collective-permute-start | bytes 73736 | tf_op jit(solution)/shard_map/ppermute | solution.py:328
  20.0 15.4 %all-to-all-start = ((bf16[32,144,128]{2,1,0:T(8,128)(2,1)}), bf16[32,144,128]{2,1,0:T(8,128)(2,1)S(1)}, u32[]{:S(2)}, u32[]{:S(2)}) async-start(bf16[32,144,128]{2,1,0:T(8,128)(2,1)} %get-tuple-element.38), calls=%async_computation | async-start | bytes 2359296 | tf_op jit(solution)/shard_map/all_to_all | solution.py:303
  35.4 5.6 %shard_map.113 = (bf16[8,24,2592]{2,1,0:T(8,128)(2,1)S(1)}, bf16[8,24,2592]{2,1,0:T(8,128)(2,1)S(1)}, bf16[3456,192]{1,0:T(8,128)(2,1)S(1)}) custom-call(s32[512]{0:T(512)S(1)} %copy-done, s32[4,27]{1,0:T(4,128)S(1)} %copy-done.4, bf16[256,768]{1,0:T(8,128)(2,1)S(1)} %copy-done.1, bf16[192,768]{1,0:T(8,128)(2,1)S(1)} %bitcast.10, ...), custom_call_target="tpu_custom_call" | custom-call | flops 6000000000 | tf_op jit(solution)/shard_map/pallas_call | solution.py:347
  41.0 1.9 %collective-permute-start.4 = (bf16[8,24,2592]{2,1,0:T(8,128)(2,1)S(1)}, bf16[8,24,2592]{2,1,0:T(8,128)(2,1)S(1)}, u32[]{:S(2)}, u32[]{:S(2)}) collective-permute-start(bf16[8,24,2592]{2,1,0:T(8,128)(2,1)S(1)} %get-tuple-element.40), channel_id=1, source_target_pairs={{0,1},{1,0},{2,3},{3,2},{4,5},{5,4},{6,7},{7,6},{8,9},{9,8},{10,11... | collective-permute-start | bytes 2985992 | tf_op jit(solution)/shard_map/ppermute | solution.py:331
  43.0 2.6 %collective-permute-done.4.received = bf16[8,24,2592]{2,1,0:T(8,128)(2,1)S(1)} collective-permute-done((bf16[8,24,2592]{2,1,0:T(8,128)(2,1)S(1)}, bf16[8,24,2592]{2,1,0:T(8,128)(2,1)S(1)}, u32[]{:S(2)}, u32[]{:S(2)}) %collective-permute-start.4) | collective-permute-done | bytes 995360 | tf_op jit(solution)/shard_map/ppermute | solution.py:331
  45.8 3.2 %collective-permute-start.5 = (bf16[2,24,2592]{2,1,0:T(8,128)(2,1)S(1)}, bf16[2,24,2592]{2,1,0:T(8,128)(2,1)S(1)}, u32[]{:S(2)}, u32[]{:S(2)}) collective-permute-start(bf16[2,24,2592]{2,1,0:T(8,128)(2,1)S(1)} %get-tuple-element.42), channel_id=1, source_target_pairs={{0,64},{64,128},{128,192},{192,0},{1,65},{65,129},{129,193},{193,1... | collective-permute-start | bytes 746504 | tf_op jit(solution)/shard_map/ppermute | solution.py:370
  49.0 6.4 %collective-permute-start.6 = (bf16[2,24,2592]{2,1,0:T(8,128)(2,1)S(1)}, bf16[2,24,2592]{2,1,0:T(8,128)(2,1)S(1)}, u32[]{:S(2)}, u32[]{:S(2)}) collective-permute-start(bf16[2,24,2592]{2,1,0:T(8,128)(2,1)S(1)} %get-tuple-element.43), channel_id=1, source_target_pairs={{0,128},{64,192},{128,0},{192,64},{1,129},{65,193},{129,1},{193,65... | collective-permute-start | bytes 746504 | tf_op jit(solution)/shard_map/ppermute | solution.py:370
  55.4 1.9 %collective-permute-start.7 = (bf16[2,24,2592]{2,1,0:T(8,128)(2,1)S(1)}, bf16[2,24,2592]{2,1,0:T(8,128)(2,1)S(1)}, u32[]{:S(2)}, u32[]{:S(2)}) collective-permute-start(bf16[2,24,2592]{2,1,0:T(8,128)(2,1)S(1)} %get-tuple-element.44), channel_id=1, source_target_pairs={{0,192},{64,0},{128,64},{192,128},{1,193},{65,1},{129,65},{193,129... | collective-permute-start | bytes 746504 | tf_op jit(solution)/shard_map/ppermute | solution.py:370
  58.8 6.5 %collective-permute-done.6.c = bf16[2,24,2592]{2,1,0:T(8,128)(2,1)S(1)} collective-permute-done((bf16[2,24,2592]{2,1,0:T(8,128)(2,1)S(1)}, bf16[2,24,2592]{2,1,0:T(8,128)(2,1)S(1)}, u32[]{:S(2)}, u32[]{:S(2)}) %collective-permute-start.6) | collective-permute-done | bytes 248864 | tf_op jit(solution)/shard_map/ppermute | solution.py:370
  66.7 1.9 %collective-permute-start.8 = (bf16[24,2592]{1,0:T(8,128)(2,1)S(1)}, bf16[24,2592]{1,0:T(8,128)(2,1)S(1)}, u32[]{:S(2)}, u32[]{:S(2)}) collective-permute-start(bf16[24,2592]{1,0:T(8,128)(2,1)S(1)} %get-tuple-element.46), channel_id=1, source_target_pairs={{0,256},{256,0},{1,257},{257,1},{2,258},{258,2},{3,259},{259,3},{4... | collective-permute-start | bytes 373256 | tf_op jit(solution)/shard_map/ppermute | solution.py:373
  68.7 3.8 %collective-permute-done.8.conv_received = bf16[24,2592]{1,0:T(8,128)(2,1)S(1)} collective-permute-done((bf16[24,2592]{1,0:T(8,128)(2,1)S(1)}, bf16[24,2592]{1,0:T(8,128)(2,1)S(1)}, u32[]{:S(2)}, u32[]{:S(2)}) %collective-permute-start.8) | collective-permute-done | bytes 124448 | tf_op jit(solution)/shard_map/ppermute | solution.py:373
  72.4 4.0 %collective-permute-start.9 = (bf16[32,144,128]{2,1,0:T(8,128)(2,1)S(1)}, bf16[32,144,128]{2,1,0:T(8,128)(2,1)S(1)}, u32[]{:S(2)}, u32[]{:S(2)}) collective-permute-start(bf16[32,144,128]{2,1,0:T(8,128)(2,1)S(1)} %all-to-all-done.mine), channel_id=1, source_target_pairs={{0,1},{1,0},{2,3},{3,2},{4,5},{5,4},{6,7},{7,6},{8,9},{9,8},{10,11... | collective-permute-start | bytes 3538952 | tf_op jit(solution)/shard_map/ppermute | solution.py:331
  76.4 2.5 %collective-permute-done.9.other = bf16[32,144,128]{2,1,0:T(8,128)(2,1)S(1)} collective-permute-done((bf16[32,144,128]{2,1,0:T(8,128)(2,1)S(1)}, bf16[32,144,128]{2,1,0:T(8,128)(2,1)S(1)}, u32[]{:S(2)}, u32[]{:S(2)}) %collective-permute-start.9) | collective-permute-done | bytes 1179680 | tf_op jit(solution)/shard_map/ppermute | solution.py:331
  78.9 1.5 copy-done.6
  80.4 4.3 %shard_map.116 = (bf16[256,768]{1,0:T(8,128)(2,1)}, bf16[576,128]{1,0:T(8,128)(2,1)S(1)}, bf16[576,128]{1,0:T(8,128)(2,1)S(1)}) custom-call(s32[512]{0:T(512)S(1)} %copy-done, bf16[256,768]{1,0:T(8,128)(2,1)S(1)} %copy-done.1, bf16[192,768]{1,0:T(8,128)(2,1)S(1)} %bitcast.11, bf16[3456,192]{1,0:T(8,128)(2,1)S(1)} %copy-done.6, ...), custom_call_target="tpu_custom_call" | custom-call | flops 4000000000 | tf_op jit(solution)/shard_map/pallas_call | solution.py:377
  84.7 2.3 %collective-permute-start.10 = (bf16[576,128]{1,0:T(8,128)(2,1)S(1)}, bf16[576,128]{1,0:T(8,128)(2,1)S(1)}, u32[]{:S(2)}, u32[]{:S(2)}) collective-permute-start(bf16[576,128]{1,0:T(8,128)(2,1)S(1)} %get-tuple-element.50), channel_id=1, source_target_pairs={{0,1},{1,0},{2,3},{3,2},{4,5},{5,4},{6,7},{7,6},{8,9},{9,8},{10,11... | collective-permute-start | bytes 442376 | tf_op jit(solution)/shard_map/ppermute | solution.py:331
  88.2 26.0 %all_to_all.20.parts = bf16[32,2,24,128]{3,2,1,0:T(8,128)(2,1)S(1)} all-to-all(bf16[32,2,24,128]{3,2,1,0:T(8,128)(2,1)S(1)} %shard_map.117), channel_id=1, replica_groups=mesh['zl'=2,'x'=4,'zh'=4,'y'=8,'c'=2] {'zh','y'}, dimensions={0} | all-to-all | bytes 786432 | tf_op jit(solution)/shard_map/all_to_all | solution.py:303
  114.3 9.0 %all_to_all.21.parts = bf16[8,24,128]{2,1,0:T(8,128)(2,1)S(1)} all-to-all(bf16[8,24,128]{2,1,0:T(8,128)(2,1)S(1)} %get-tuple-element.53), channel_id=1, replica_groups=mesh['zl'=2,'x'=4,'zh'=4,'y'=8,'c'=2] {'zl','x'}, dimensions={0} | all-to-all | bytes 98304 | tf_op jit(solution)/shard_map/all_to_all | solution.py:303
  124.0 7.0 %all-to-all-start.3 = ((bf16[32,24,128]{2,1,0:T(8,128)(2,1)}), bf16[32,24,128]{2,1,0:T(8,128)(2,1)S(1)}, u32[]{:S(2)}, u32[]{:S(2)}) async-start(bf16[32,24,128]{2,1,0:T(8,128)(2,1)} %shard_map.119), calls=%async_computation.3 | async-start | bytes 393216 | tf_op jit(solution)/shard_map/all_to_all | solution.py:303
  131.6 11.2 %all-to-all-done.3 = bf16[32,24,128]{2,1,0:T(8,128)(2,1)S(1)} async-done(((bf16[32,24,128]{2,1,0:T(8,128)(2,1)}), bf16[32,24,128]{2,1,0:T(8,128)(2,1)S(1)}, u32[]{:S(2)}, u32[]{:S(2)}) %all-to-all-start.3) | async-done | bytes 196640 | tf_op jit(solution)/shard_map/all_to_all | solution.py:303
  142.8 5.6 %all-gather = bf16[64,24,128]{2,1,0:T(8,128)(2,1)S(1)} all-gather(bf16[32,24,128]{2,1,0:T(8,128)(2,1)S(1)} %all-to-all-done.3), channel_id=2, replica_groups=mesh['zl'=2,'x'=4,'zh'=4,'y'=8,'c'=2] {'c'}, dimensions={0}, use_global_device_ids=true | all-gather | bytes 589824 | tf_op jit(solution)/shard_map/all_gather | solution.py:405
  (29 shorter events, 9.1 us)
Async XLA Ops:
  2.9 17.0 %collective-permute-start.1 = (bf16[4,4,16,192]{3,2,1,0:T(8,128)(2,1)}, bf16[4,4,16,192]{3,2,1,0:T(8,128)(2,1)S(1)}, u32[]{:S(2)}, u32[]{:S(2)}) collective-permute-start(bf16[4,4,16,192]{3,2,1,0:T(8,128)(2,1)} %get-tuple-element.29.grad), channel_id=1, source_target_pairs={{64,0},{128,64},{192,128},{256,192},{320,256},{384,320},{448,384},... | collective-permute-start | bytes 294920 | tf_op jit(solution)/shard_map/ppermute | solution.py:328
  4.2 15.7 %collective-permute-start = (bf16[4,4,16,192]{3,2,1,0:T(8,128)(2,1)}, bf16[4,4,16,192]{3,2,1,0:T(8,128)(2,1)S(1)}, u32[]{:S(2)}, u32[]{:S(2)}) collective-permute-start(bf16[4,4,16,192]{3,2,1,0:T(8,128)(2,1)} %get-tuple-element.29.grad), channel_id=1, source_target_pairs={{0,64},{64,128},{128,192},{192,256},{256,320},{320,384},{384,448},... | collective-permute-start | bytes 294920 | tf_op jit(solution)/shard_map/ppermute | solution.py:328
  8.8 10.1 %collective-permute-start.2 = (bf16[1,4,16,192]{3,2,1,0:T(8,128)(2,1)}, bf16[1,4,16,192]{3,2,1,0:T(8,128)(2,1)S(1)}, u32[]{:S(2)}, u32[]{:S(2)}) collective-permute-start(bf16[1,4,16,192]{3,2,1,0:T(8,128)(2,1)} %get-tuple-element.31), channel_id=1, source_target_pairs={{0,1},{1,2},{2,3},{3,4},{4,5},{5,6},{6,7},{7,8},{8,9},{9,10},{10,1... | collective-permute-start | bytes 73736 | tf_op jit(solution)/shard_map/ppermute | solution.py:328
  13.4 6.5 %collective-permute-start.3 = (bf16[1,4,16,192]{3,2,1,0:T(8,128)(2,1)}, bf16[1,4,16,192]{3,2,1,0:T(8,128)(2,1)S(1)}, u32[]{:S(2)}, u32[]{:S(2)}) collective-permute-start(bf16[1,4,16,192]{3,2,1,0:T(8,128)(2,1)} %get-tuple-element.32), channel_id=1, source_target_pairs={{1,0},{2,1},{3,2},{4,3},{5,4},{6,5},{7,6},{8,7},{9,8},{10,9},{11,1... | collective-permute-start | bytes 73736 | tf_op jit(solution)/shard_map/ppermute | solution.py:328
  19.9 15.4 %copy-start = (s32[512]{0:T(512)S(1)}, s32[512]{0:T(512)}, u32[]{:S(2)}) copy-start(s32[512]{0:T(512)} %counts_in.5) | copy-start | bytes 6148
  19.9 15.4 %copy-start.1 = (bf16[256,768]{1,0:T(8,128)(2,1)S(1)}, bf16[256,768]{1,0:T(8,128)(2,1)}, u32[]{:S(2)}) copy-start(bf16[256,768]{1,0:T(8,128)(2,1)} %fine_in.3) | copy-start | bytes 1179652
  19.9 15.4 %copy-start.2 = (bf16[768,192]{0,1:T(8,128)(2,1)S(1)}, bf16[768,192]{0,1:T(8,128)(2,1)}, u32[]{:S(2)}) copy-start(bf16[768,192]{0,1:T(8,128)(2,1)} %param.10) | copy-start | bytes 884740
  20.0 15.4 %copy-start.3 = (bf16[4,4,16,192]{3,2,1,0:T(8,128)(2,1)S(1)}, bf16[4,4,16,192]{3,2,1,0:T(8,128)(2,1)}, u32[]{:S(2)}) copy-start(bf16[4,4,16,192]{3,2,1,0:T(8,128)(2,1)} %get-tuple-element.29.grad) | copy-start | bytes 294916
  20.0 15.4 %copy-start.4 = (s32[4,27]{1,0:T(4,128)S(1)}, s32[4,27]{1,0:T(4,128)}, u32[]{:S(2)}) copy-start(s32[4,27]{1,0:T(4,128)} %near_in.1) | copy-start | bytes 1300
  20.0 52.4 %all-to-all-start = ((bf16[32,144,128]{2,1,0:T(8,128)(2,1)}), bf16[32,144,128]{2,1,0:T(8,128)(2,1)S(1)}, u32[]{:S(2)}, u32[]{:S(2)}) async-start(bf16[32,144,128]{2,1,0:T(8,128)(2,1)} %get-tuple-element.38), calls=%async_computation | async-start | bytes 2359296 | tf_op jit(solution)/shard_map/all_to_all | solution.py:303
  41.0 25.7 %copy-start.5 = (bf16[3456,192]{1,0:T(8,128)(2,1)}, bf16[3456,192]{1,0:T(8,128)(2,1)S(1)}, u32[]{:S(2)}) copy-start(bf16[3456,192]{1,0:T(8,128)(2,1)S(1)} %get-tuple-element.37.taps_in) | copy-start | bytes 3981316
  41.0 4.5 %collective-permute-start.4 = (bf16[8,24,2592]{2,1,0:T(8,128)(2,1)S(1)}, bf16[8,24,2592]{2,1,0:T(8,128)(2,1)S(1)}, u32[]{:S(2)}, u32[]{:S(2)}) collective-permute-start(bf16[8,24,2592]{2,1,0:T(8,128)(2,1)S(1)} %get-tuple-element.40), channel_id=1, source_target_pairs={{0,1},{1,0},{2,3},{3,2},{4,5},{5,4},{6,7},{7,6},{8,9},{9,8},{10,11... | collective-permute-start | bytes 2985992 | tf_op jit(solution)/shard_map/ppermute | solution.py:331
  45.8 12.9 %collective-permute-start.5 = (bf16[2,24,2592]{2,1,0:T(8,128)(2,1)S(1)}, bf16[2,24,2592]{2,1,0:T(8,128)(2,1)S(1)}, u32[]{:S(2)}, u32[]{:S(2)}) collective-permute-start(bf16[2,24,2592]{2,1,0:T(8,128)(2,1)S(1)} %get-tuple-element.42), channel_id=1, source_target_pairs={{0,64},{64,128},{128,192},{192,0},{1,65},{65,129},{129,193},{193,1... | collective-permute-start | bytes 746504 | tf_op jit(solution)/shard_map/ppermute | solution.py:370
  49.0 16.2 %collective-permute-start.6 = (bf16[2,24,2592]{2,1,0:T(8,128)(2,1)S(1)}, bf16[2,24,2592]{2,1,0:T(8,128)(2,1)S(1)}, u32[]{:S(2)}, u32[]{:S(2)}) collective-permute-start(bf16[2,24,2592]{2,1,0:T(8,128)(2,1)S(1)} %get-tuple-element.43), channel_id=1, source_target_pairs={{0,128},{64,192},{128,0},{192,64},{1,129},{65,193},{129,1},{193,65... | collective-permute-start | bytes 746504 | tf_op jit(solution)/shard_map/ppermute | solution.py:370
  55.4 11.2 %collective-permute-start.7 = (bf16[2,24,2592]{2,1,0:T(8,128)(2,1)S(1)}, bf16[2,24,2592]{2,1,0:T(8,128)(2,1)S(1)}, u32[]{:S(2)}, u32[]{:S(2)}) collective-permute-start(bf16[2,24,2592]{2,1,0:T(8,128)(2,1)S(1)} %get-tuple-element.44), channel_id=1, source_target_pairs={{0,192},{64,0},{128,64},{192,128},{1,193},{65,1},{129,65},{193,129... | collective-permute-start | bytes 746504 | tf_op jit(solution)/shard_map/ppermute | solution.py:370
  66.7 5.7 %collective-permute-start.8 = (bf16[24,2592]{1,0:T(8,128)(2,1)S(1)}, bf16[24,2592]{1,0:T(8,128)(2,1)S(1)}, u32[]{:S(2)}, u32[]{:S(2)}) collective-permute-start(bf16[24,2592]{1,0:T(8,128)(2,1)S(1)} %get-tuple-element.46), channel_id=1, source_target_pairs={{0,256},{256,0},{1,257},{257,1},{2,258},{258,2},{3,259},{259,3},{4... | collective-permute-start | bytes 373256 | tf_op jit(solution)/shard_map/ppermute | solution.py:373
  72.4 6.5 %collective-permute-start.9 = (bf16[32,144,128]{2,1,0:T(8,128)(2,1)S(1)}, bf16[32,144,128]{2,1,0:T(8,128)(2,1)S(1)}, u32[]{:S(2)}, u32[]{:S(2)}) collective-permute-start(bf16[32,144,128]{2,1,0:T(8,128)(2,1)S(1)} %all-to-all-done.mine), channel_id=1, source_target_pairs={{0,1},{1,0},{2,3},{3,2},{4,5},{5,4},{6,7},{7,6},{8,9},{9,8},{10,11... | collective-permute-start | bytes 3538952 | tf_op jit(solution)/shard_map/ppermute | solution.py:331
  78.9 1.5 copy-start.6
  84.7 3.3 %collective-permute-start.10 = (bf16[576,128]{1,0:T(8,128)(2,1)S(1)}, bf16[576,128]{1,0:T(8,128)(2,1)S(1)}, u32[]{:S(2)}, u32[]{:S(2)}) collective-permute-start(bf16[576,128]{1,0:T(8,128)(2,1)S(1)} %get-tuple-element.50), channel_id=1, source_target_pairs={{0,1},{1,0},{2,3},{3,2},{4,5},{5,4},{6,7},{7,6},{8,9},{9,8},{10,11... | collective-permute-start | bytes 442376 | tf_op jit(solution)/shard_map/ppermute | solution.py:331
  124.0 18.8 %all-to-all-start.3 = ((bf16[32,24,128]{2,1,0:T(8,128)(2,1)}), bf16[32,24,128]{2,1,0:T(8,128)(2,1)S(1)}, u32[]{:S(2)}, u32[]{:S(2)}) async-start(bf16[32,24,128]{2,1,0:T(8,128)(2,1)} %shard_map.119), calls=%async_computation.3 | async-start | bytes 393216 | tf_op jit(solution)/shard_map/all_to_all | solution.py:303

commit v5 on v4

--- a/solution.py
+++ b/solution.py
@@ -117,7 +117,7 @@
 
 def conv_kernel(
     counts_in, near_in, fine_in, weight_in, grad, slab_low, slab_high, dev_low, dev_high,
-    keep, send, taps_out, counts, near, fine, weight, sems, bricks, block, total, taps,
+    keep, send, taps, counts, near, fine, weight, sems, bricks, block, total,
 ):
     copies = fetch(
         sems, (counts_in, counts), (near_in, near), (fine_in, fine), (weight_in, weight)
@@ -152,8 +152,6 @@
             for s in range(9):
                 row = ((s * 6 + plane) * B + b) * 16
                 taps[row : row + 16] = moved[s * 16 : (s + 1) * 16]
-    leave = pltpu.make_async_copy(taps, taps_out, sems.at[4])
-    leave.start()
     for copy in (copies[0], copies[2], copies[3]):
         copy.wait()
     count = counts[place]
@@ -178,7 +176,6 @@
     for out, half in ((keep, core), (send, 1 - core)):
         for slab in range(SLABS):
             out[slab] = total[half, slab * COLS : (slab + 1) * COLS].astype(BF16)
-    leave.wait()
 
 
 def split_kernel(keep, received, *outs):
@@ -197,12 +194,10 @@
 
 
 def back_kernel(
-    counts_in, fine_in, weight_in, taps_in, mine, other, fine_grad, keep, send,
-    counts, fine, weight, taps, sems, both, whole, term,
+    counts_in, fine_in, weight_in, taps, mine, other, fine_grad, keep, send,
+    counts, fine, weight, sems, both, whole, term,
 ):
-    copies = fetch(
-        sems, (counts_in, counts), (fine_in, fine), (weight_in, weight), (taps_in, taps)
-    )
+    copies = fetch(sems, (counts_in, counts), (fine_in, fine), (weight_in, weight))
     place = my_place()
     core = jnp.bitwise_and(place, 1)
     both[core] = mine[...]
@@ -223,13 +218,12 @@
             whole[row : row + FRAME, :128] = main
             whole[row : row + 48, 128:] = low
         whole[row + 48 : row + FRAME, 128:] = high
-    copies[3].wait()
     back = jnp.zeros((256, C), F32)
     for tap in range(27):
         row = tap_rows(tap)
         back = back + dot(taps[row : row + 256], whole[tap * C : (tap + 1) * C])
     brick_of = lax.broadcasted_iota(jnp.int32, (256, C), 0) // 16 % B
-    for copy in copies[:3]:
+    for copy in copies:
         copy.wait()
     count = counts[place]
     back = jnp.where(brick_of < count, back, 0.0).astype(BF16)
@@ -244,25 +238,11 @@
     send[...] = term[1 - core]
 
 
-def join_kernel(keep, received, conv_keep, conv_received, out):
-    total = conv_keep[...].astype(F32) + conv_received[...].astype(F32)
-    pad = jnp.zeros((COLS, 128 - ROWS), BF16)
-    for i in range(32):
-        piece = total[:, i * ROWS : (i + 1) * ROWS].astype(BF16)
-        out[i, 0] = jnp.concatenate([piece, pad], axis=1)
+def join_kernel(keep, received, out):
     for i in range(24):
-        out[i, 1] = (keep[i].astype(F32) + received[i].astype(F32)).astype(BF16)
+        out[i] = (keep[i].astype(F32) + received[i].astype(F32)).astype(BF16)
     for i in range(24, 32):
-        out[i, 1] = jnp.zeros((24, 128), BF16)
-
-
-def part_kernel(parts, conv_grad, out):
-    total = [parts[0, kind].astype(F32) for kind in range(2)]
-    for i in range(1, 32):
-        total = [total[kind] + parts[i, kind].astype(F32) for kind in range(2)]
-    conv_grad[...] = jnp.transpose(total[0])[:ROWS]
-    for i in range(SLABS):
-        out[i] = total[1].astype(BF16)
+        out[i] = jnp.zeros((24, 128), BF16)
 
 
 def spread_kernel(parts, out):
@@ -271,6 +251,27 @@
         total = total + parts[i].astype(F32)
     for i in range(out.shape[0]):
         out[i] = total.astype(BF16)
+
+
+def both_kernel(parts, keep, received, out):
+    merge = parts[0].astype(F32)
+    for i in range(1, SLABS):
+        merge = merge + parts[i].astype(F32)
+    conv = keep[...].astype(F32) + received[...].astype(F32)
+    pad = jnp.zeros((COLS, 128 - ROWS), BF16)
+    for i in range(32):
+        piece = conv[:, i * ROWS : (i + 1) * ROWS].astype(BF16)
+        out[i, 0] = jnp.concatenate([piece, pad], axis=1)
+        out[i, 1] = merge.astype(BF16)
+
+
+def part_kernel(parts, conv_grad, merge):
+    conv = parts[0, 0].astype(F32)
+    for i in range(1, 32):
+        conv = conv + parts[i, 0].astype(F32)
+    conv_grad[...] = jnp.transpose(conv)[:ROWS]
+    for i in range(32):
+        merge[i] = parts[i, 1]
 
 
 def merge_kernel(parts, out, held, sems):
@@ -283,7 +284,7 @@
     copy.wait()
 
 
-def call(kernel, outs, specs, scratch=(), flops=0, out_spec=None, vmem=40):
+def call(kernel, outs, specs, scratch=(), flops=0, out_spec=None, vmem=20):
     return pl.pallas_call(
         kernel,
         out_shape=outs,
@@ -335,13 +336,10 @@
     dev_low = shifted(last, DEV, DEVS, 1)
     dev_high = shifted(first, DEV, DEVS, -1)
 
-    frames, slab_low, slab_high, dev_low, dev_high = lax.optimization_barrier(
-        (frames, slab_low, slab_high, dev_low, dev_high)
-    )
+    frames, dev_low, dev_high = lax.optimization_barrier((frames, dev_low, dev_high))
     frames = swap(frames, ("zh", "y"))
 
     fine_scratch = pltpu.VMEM((256, 768), BF16)
-    taps_scratch = pltpu.VMEM((3456, C), BF16)
     weight_scratch = pltpu.VMEM((C, 768), BF16)
     merge_weight = merge_weight.T
     keep, send, taps = call(
@@ -353,55 +351,53 @@
             pltpu.SMEM((B, 27), jnp.int32),
             fine_scratch,
             weight_scratch,
-            pltpu.SemaphoreType.DMA((5,)),
+            pltpu.SemaphoreType.DMA((4,)),
             pltpu.VMEM((15, 4, 16, C), BF16),
             pltpu.VMEM((6, 144, C), BF16),
             pltpu.VMEM((2, C, HALF), F32),
-            taps_scratch,
         ],
         flops=6 * 10**9,
-        out_spec=(VMEM, VMEM, HBM),
+        vmem=20,
     )(
         counts, neighbours, fine_input, merge_weight, grad, slab_low, slab_high, dev_low, dev_high
     )
 
-    conv = call(split_kernel, (shape(2, COLS, HALF),) * 4, [VMEM] * 2)(keep, flipped(send))
+    frames, received = lax.optimization_barrier((frames, flipped(send)))
+    conv = call(split_kernel, (shape(2, COLS, HALF),) * 4, [VMEM] * 2)(keep, received)
     conv = [conv[0]] + [
         lax.ppermute(conv[dx], "x", [(i, (i + dx) % 4) for i in range(4)]) for dx in (1, 2, 3)
     ]
     keep, send = call(halve_kernel, (shape(COLS, HALF),) * 2, [VMEM] * 4)(*conv)
     conv = (keep, lax.ppermute(send, "zl", [(0, 1), (1, 0)]))
-    frames, conv = lax.optimization_barrier((frames, conv))
-
     other = flipped(frames)
     fine_grad, keep, send = call(
         back_kernel,
         (shape(256, 768), shape(576, 128), shape(576, 128)),
-        [HBM] * 4 + [VMEM] * 2,
+        [HBM] * 3 + [VMEM] * 3,
         [
             counts_scratch,
             fine_scratch,
             weight_scratch,
-            taps_scratch,
-            pltpu.SemaphoreType.DMA((4,)),
+            pltpu.SemaphoreType.DMA((3,)),
             pltpu.VMEM((2, 32, 144, 128), BF16),
             pltpu.VMEM((27 * C, C), BF16),
             pltpu.VMEM((2, 576, 128), BF16),
         ],
         flops=4 * 10**9,
-        vmem=48,
+        vmem=20,
     )(counts, fine_input, merge_weight, taps, frames, other)
 
-    joined = call(join_kernel, shape(32, 2, 24, 128), [VMEM] * 4)(
-        keep.reshape(24, 24, 128), flipped(send).reshape(24, 24, 128), *conv
-    )
+    term = call(join_kernel, shape(32, 24, 128), [VMEM] * 2)(
+        keep.reshape(24, 24, 128), flipped(send).reshape(24, 24, 128)
+    )
+    term = swap(term, ("zh", "y"))
+    term = call(spread_kernel, shape(SLABS, 24, 128), [VMEM])(term)
+    term = swap(term, SLAB)
+    joined = call(both_kernel, shape(32, 2, 24, 128), [VMEM] * 3)(term, *conv)
     joined = swap(joined, ("zh", "y"))
     conv_grad, term = call(
-        part_kernel, (shape(ROWS, COLS, dtype=F32), shape(SLABS, 24, 128)), [VMEM]
+        part_kernel, (shape(ROWS, COLS, dtype=F32), shape(32, 24, 128)), [VMEM]
     )(joined)
-    term = swap(term, SLAB)
-    term = call(spread_kernel, shape(32, 24, 128), [VMEM])(term)
-    term = swap(term, ("zh", "y"))
     term = lax.all_gather(term, "c", axis=0, tiled=False)
     merge_grad = call(
         merge_kernel,

time: 150 us -> 167 us (1.11)
  starting transfers between devices: 59.9 us -> 79.4 us
  blocking collectives: 40.6 us -> 31.1 us
  waiting for transfers between devices: 31.3 us -> 36.7 us
  local copies, waits for them, and re-layouts: 2.18 us -> 4.39 us
    all_to_all x2 -> x1, blocking collectives: 35 us -> 24.5 us  [swap(): return lax.all_to_all(x, axes, 0, 0, tiled=True)]
    ppermute x3, starting transfers between devices: 11.5 us -> 21.1 us  [local(): lax.ppermute(conv[dx], 'x', [(i, (i + dx) % 4) for i in range(4)])]
    all_to_all x2 -> x3, waiting for transfers between devices: 11.2 us -> 18.4 us  [swap(): return lax.all_to_all(x, axes, 0, 0, tiled=True)]
    all_to_all x2 -> x3, starting transfers between devices: 22.3 us -> 28.9 us  [swap(): return lax.all_to_all(x, axes, 0, 0, tiled=True)]
    ppermute x1, starting transfers between devices: 1.92 us -> 6.46 us  [local(): conv = (keep, lax.ppermute(send, 'zl', [(0, 1), (1, 0)]))]
    ppermute x1, waiting for transfers between devices: 3.76 us -> 0.01 us  [local(): conv = (keep, lax.ppermute(send, 'zl', [(0, 1), (1, 0)]))]
    ppermute x4, waiting for transfers between devices: 1.05 us -> 3.95 us  [shifted(): return lax.ppermute(x, axes, pairs)]
    unnamed x15 -> x17, local copies, waits for them, and re-layouts: 2.18 us -> 4.39 us
  transfers between devices with their start and end apart: 13 -> 14, of which waited for: 9 -> 11; matrix products, arithmetic and copies ran while one was open for 0% -> 0% of each run, Pallas kernels for 4% -> 4%
where the time goes in v5:
time: 167 us
  starting transfers between devices  79.4 us (48%)
  waiting for transfers between devices  36.7 us (22%)
  blocking collectives  31.1 us (19%)
  Pallas kernels  14.2 us (9%)
  local copies, waits for them, and re-layouts  4.39 us (3%)
    all_to_all x3, starting transfers between devices, swap(): return lax.all_to_all(x, axes, 0, 0, tiled=True)  28.9 us
    all_to_all x1, blocking collectives, swap(): return lax.all_to_all(x, axes, 0, 0, tiled=True)  24.5 us
    ppermute x3, starting transfers between devices, local(): lax.ppermute(conv[dx], 'x', [(i, (i + dx) % 4) for i in range(4)])  21.1 us
    all_to_all x3, waiting for transfers between devices, swap(): return lax.all_to_all(x, axes, 0, 0, tiled=True)  18.4 us
    ppermute x4, starting transfers between devices, shifted(): return lax.ppermute(x, axes, pairs)  15.4 us
    ppermute x3, waiting for transfers between devices, local(): lax.ppermute(conv[dx], 'x', [(i, (i + dx) % 4) for i in range(4)])  8.68 us
    ppermute x3, starting transfers between devices, flipped(): return lax.ppermute(x, 'c', [(0, 1), (1, 0)])  7.56 us
    all_gather x1, blocking collectives, local(): term = lax.all_gather(term, 'c', axis=0, tiled=False)  6.59 us
  transfers between devices with their start and end apart: 14, of which 11 were waited for; matrix products, arithmetic and copies ran while one was open for 0% of the time, Pallas kernels for 4%

profile of v5, /device:TPU:1, one launch (start us, length us, event | category | flops | bytes accessed | tf_op | source)
XLA Modules:
  0.0 166.7 jit_solution(8335528106280491353)
XLA Ops:
  0.6 2.3 %shard_map.112 = (bf16[4,4,16,192]{3,2,1,0:T(8,128)(2,1)}, bf16[1,4,16,192]{3,2,1,0:T(8,128)(2,1)}, bf16[1,4,16,192]{3,2,1,0:T(8,128)(2,1)}, bf16[32,144,128]{2,1,0:T(8,128)(2,1)}) custom-call(s32[512]{0:T(512)} %counts_in.5, bf16[4,16,768]{2,1,0:T(8,128)(2,1)} %pre_in.1, bf16[4,16,768]{2,1,0:T(8,128)(2,1)} %cot_in.1, f32[1,192]{1,0:T(1,128)} %bitcast.13, ...), custom_call_target="tpu_custom_call" | custom-call | tf_op jit(solution)/shard_map/pallas_call | solution.py:311
  2.9 4.6 %collective-permute-start.2 = (bf16[1,4,16,192]{3,2,1,0:T(8,128)(2,1)}, bf16[1,4,16,192]{3,2,1,0:T(8,128)(2,1)S(1)}, u32[]{:S(2)}, u32[]{:S(2)}) collective-permute-start(bf16[1,4,16,192]{3,2,1,0:T(8,128)(2,1)} %get-tuple-element.28), channel_id=1, source_target_pairs={{0,1},{1,2},{2,3},{3,4},{4,5},{5,6},{6,7},{7,8},{8,9},{9,10},{10,1... | collective-permute-start | bytes 73736 | tf_op jit(solution)/shard_map/ppermute | solution.py:329
  7.5 5.5 %collective-permute-start.3 = (bf16[1,4,16,192]{3,2,1,0:T(8,128)(2,1)}, bf16[1,4,16,192]{3,2,1,0:T(8,128)(2,1)S(1)}, u32[]{:S(2)}, u32[]{:S(2)}) collective-permute-start(bf16[1,4,16,192]{3,2,1,0:T(8,128)(2,1)} %get-tuple-element.29), channel_id=1, source_target_pairs={{1,0},{2,1},{3,2},{4,3},{5,4},{6,5},{7,6},{8,7},{9,8},{10,9},{11,1... | collective-permute-start | bytes 73736 | tf_op jit(solution)/shard_map/ppermute | solution.py:329
  14.1 15.4 %all-to-all-start = ((bf16[32,144,128]{2,1,0:T(8,128)(2,1)}), bf16[32,144,128]{2,1,0:T(8,128)(2,1)S(1)}, u32[]{:S(2)}, u32[]{:S(2)}) async-start(bf16[32,144,128]{2,1,0:T(8,128)(2,1)} %get-tuple-element.33), calls=%async_computation | async-start | bytes 2359296 | tf_op jit(solution)/shard_map/all_to_all | solution.py:304
  30.8 4.0 %collective-permute-start = (bf16[4,4,16,192]{3,2,1,0:T(8,128)(2,1)S(1)}, bf16[4,4,16,192]{3,2,1,0:T(8,128)(2,1)S(1)}, u32[]{:S(2)}, u32[]{:S(2)}) collective-permute-start(bf16[4,4,16,192]{3,2,1,0:T(8,128)(2,1)S(1)} %copy-done.4), channel_id=1, source_target_pairs={{0,64},{64,128},{128,192},{192,256},{256,320},{320,384},{384,448},... | collective-permute-start | bytes 294920 | tf_op jit(solution)/shard_map/ppermute | solution.py:329
  34.8 1.9 %collective-permute-done.1.slab_high = bf16[4,4,16,192]{3,2,1,0:T(8,128)(2,1)S(1)} collective-permute-done((bf16[4,4,16,192]{3,2,1,0:T(8,128)(2,1)S(1)}, bf16[4,4,16,192]{3,2,1,0:T(8,128)(2,1)S(1)}, u32[]{:S(2)}, u32[]{:S(2)}) %collective-permute-start.1) | collective-permute-done | bytes 98336 | tf_op jit(solution)/shard_map/ppermute | solution.py:329
  37.8 5.2 %shard_map.113 = (bf16[8,24,2592]{2,1,0:T(8,128)(2,1)S(1)}, bf16[8,24,2592]{2,1,0:T(8,128)(2,1)S(1)}, bf16[3456,192]{1,0:T(8,128)(2,1)S(1)}) custom-call(s32[512]{0:T(512)S(1)} %copy-done, s32[4,27]{1,0:T(4,128)S(1)} %copy-done.5, bf16[256,768]{1,0:T(8,128)(2,1)S(1)} %copy-done.1, bf16[192,768]{1,0:T(8,128)(2,1)S(1)} %bitcast.10, ...), custom_call_target="tpu_custom_call" | custom-call | flops 6000000000 | tf_op jit(solution)/shard_map/pallas_call | solution.py:345
  44.2 2.7 %collective-permute-start.4 = (bf16[8,24,2592]{2,1,0:T(8,128)(2,1)S(1)}, bf16[8,24,2592]{2,1,0:T(8,128)(2,1)S(1)}, u32[]{:S(2)}, u32[]{:S(2)}) collective-permute-start(bf16[8,24,2592]{2,1,0:T(8,128)(2,1)S(1)} %get-tuple-element.34), channel_id=1, source_target_pairs={{0,1},{1,0},{2,3},{3,2},{4,5},{5,4},{6,7},{7,6},{8,9},{9,8},{10,11... | collective-permute-start | bytes 2985992 | tf_op jit(solution)/shard_map/ppermute | solution.py:332
  46.9 2.2 %collective-permute-done.4.received = bf16[8,24,2592]{2,1,0:T(8,128)(2,1)S(1)} collective-permute-done((bf16[8,24,2592]{2,1,0:T(8,128)(2,1)S(1)}, bf16[8,24,2592]{2,1,0:T(8,128)(2,1)S(1)}, u32[]{:S(2)}, u32[]{:S(2)}) %collective-permute-start.4) | collective-permute-done | bytes 995360 | tf_op jit(solution)/shard_map/ppermute | solution.py:332
  49.2 13.3 %all-to-all-done.mine = bf16[32,144,128]{2,1,0:T(8,128)(2,1)S(1)} async-done(((bf16[32,144,128]{2,1,0:T(8,128)(2,1)}), bf16[32,144,128]{2,1,0:T(8,128)(2,1)S(1)}, u32[]{:S(2)}, u32[]{:S(2)}) %all-to-all-start) | async-done | bytes 1179680 | tf_op jit(solution)/shard_map/all_to_all | solution.py:304
  62.4 2.7 %collective-permute-start.5 = (bf16[32,144,128]{2,1,0:T(8,128)(2,1)S(1)}, bf16[32,144,128]{2,1,0:T(8,128)(2,1)S(1)}, u32[]{:S(2)}, u32[]{:S(2)}) collective-permute-start(bf16[32,144,128]{2,1,0:T(8,128)(2,1)S(1)} %all-to-all-done.mine), channel_id=1, source_target_pairs={{0,1},{1,0},{2,3},{3,2},{4,5},{5,4},{6,7},{7,6},{8,9},{9,8},{10,11... | collective-permute-start | bytes 3538952 | tf_op jit(solution)/shard_map/ppermute | solution.py:332
  65.1 2.5 %collective-permute-done.5.other = bf16[32,144,128]{2,1,0:T(8,128)(2,1)S(1)} collective-permute-done((bf16[32,144,128]{2,1,0:T(8,128)(2,1)S(1)}, bf16[32,144,128]{2,1,0:T(8,128)(2,1)S(1)}, u32[]{:S(2)}, u32[]{:S(2)}) %collective-permute-start.5) | collective-permute-done | bytes 1179680 | tf_op jit(solution)/shard_map/ppermute | solution.py:332
  70.0 3.7 %shard_map.114 = (bf16[256,768]{1,0:T(8,128)(2,1)}, bf16[576,128]{1,0:T(8,128)(2,1)S(1)}, bf16[576,128]{1,0:T(8,128)(2,1)S(1)}) custom-call(s32[512]{0:T(512)S(1)} %copy-done, bf16[256,768]{1,0:T(8,128)(2,1)S(1)} %copy-done.2, bf16[192,768]{1,0:T(8,128)(2,1)S(1)} %bitcast.11, bf16[3456,192]{1,0:T(8,128)(2,1)S(1)} %copy-done.7, ...), custom_call_target="tpu_custom_call" | custom-call | flops 4000000000 | tf_op jit(solution)/shard_map/pallas_call | solution.py:373
  73.7 2.2 %collective-permute-start.6 = (bf16[576,128]{1,0:T(8,128)(2,1)S(1)}, bf16[576,128]{1,0:T(8,128)(2,1)S(1)}, u32[]{:S(2)}, u32[]{:S(2)}) collective-permute-start(bf16[576,128]{1,0:T(8,128)(2,1)S(1)} %get-tuple-element.38), channel_id=1, source_target_pairs={{0,1},{1,0},{2,3},{3,2},{4,5},{5,4},{6,7},{7,6},{8,9},{9,8},{10,11... | collective-permute-start | bytes 442376 | tf_op jit(solution)/shard_map/ppermute | solution.py:332
  77.7 8.8 %all-to-all-start.1 = ((bf16[32,24,128]{2,1,0:T(8,128)(2,1)}), bf16[32,24,128]{2,1,0:T(8,128)(2,1)S(1)}, u32[]{:S(2)}, u32[]{:S(2)}) async-start(bf16[32,24,128]{2,1,0:T(8,128)(2,1)} %shard_map.115), calls=%async_computation.1 | async-start | bytes 393216 | tf_op jit(solution)/shard_map/all_to_all | solution.py:304
  86.8 3.1 %collective-permute-start.7 = (bf16[2,24,2592]{2,1,0:T(8,128)(2,1)S(1)}, bf16[2,24,2592]{2,1,0:T(8,128)(2,1)S(1)}, u32[]{:S(2)}, u32[]{:S(2)}) collective-permute-start(bf16[2,24,2592]{2,1,0:T(8,128)(2,1)S(1)} %get-tuple-element.42), channel_id=1, source_target_pairs={{0,64},{64,128},{128,192},{192,0},{1,65},{65,129},{129,193},{193,1... | collective-permute-start | bytes 746504 | tf_op jit(solution)/shard_map/ppermute | solution.py:368
  89.9 16.0 %collective-permute-start.8 = (bf16[2,24,2592]{2,1,0:T(8,128)(2,1)S(1)}, bf16[2,24,2592]{2,1,0:T(8,128)(2,1)S(1)}, u32[]{:S(2)}, u32[]{:S(2)}) collective-permute-start(bf16[2,24,2592]{2,1,0:T(8,128)(2,1)S(1)} %get-tuple-element.43), channel_id=1, source_target_pairs={{0,128},{64,192},{128,0},{192,64},{1,129},{65,193},{129,1},{193,65... | collective-permute-start | bytes 746504 | tf_op jit(solution)/shard_map/ppermute | solution.py:368
  106.0 1.9 %collective-permute-start.9 = (bf16[2,24,2592]{2,1,0:T(8,128)(2,1)S(1)}, bf16[2,24,2592]{2,1,0:T(8,128)(2,1)S(1)}, u32[]{:S(2)}, u32[]{:S(2)}) collective-permute-start(bf16[2,24,2592]{2,1,0:T(8,128)(2,1)S(1)} %get-tuple-element.44), channel_id=1, source_target_pairs={{0,192},{64,0},{128,64},{192,128},{1,193},{65,1},{129,65},{193,129... | collective-permute-start | bytes 746504 | tf_op jit(solution)/shard_map/ppermute | solution.py:368
  108.9 6.4 %collective-permute-done.8.c = bf16[2,24,2592]{2,1,0:T(8,128)(2,1)S(1)} collective-permute-done((bf16[2,24,2592]{2,1,0:T(8,128)(2,1)S(1)}, bf16[2,24,2592]{2,1,0:T(8,128)(2,1)S(1)}, u32[]{:S(2)}, u32[]{:S(2)}) %collective-permute-start.8) | collective-permute-done | bytes 248864 | tf_op jit(solution)/shard_map/ppermute | solution.py:368
  116.7 6.5 %collective-permute-start.10 = (bf16[24,2592]{1,0:T(8,128)(2,1)S(1)}, bf16[24,2592]{1,0:T(8,128)(2,1)S(1)}, u32[]{:S(2)}, u32[]{:S(2)}) collective-permute-start(bf16[24,2592]{1,0:T(8,128)(2,1)S(1)} %get-tuple-element.46), channel_id=1, source_target_pairs={{0,256},{256,0},{1,257},{257,1},{2,258},{258,2},{3,259},{259,3},{4... | collective-permute-start | bytes 373256 | tf_op jit(solution)/shard_map/ppermute | solution.py:371
  123.8 4.7 %all-to-all-start.2 = ((bf16[8,24,128]{2,1,0:T(8,128)(2,1)}), bf16[8,24,128]{2,1,0:T(8,128)(2,1)S(1)}, u32[]{:S(2)}, u32[]{:S(2)}) async-start(bf16[8,24,128]{2,1,0:T(8,128)(2,1)} %shard_map.116), calls=%async_computation.2 | async-start | bytes 98304 | tf_op jit(solution)/shard_map/all_to_all | solution.py:304
  128.5 5.1 %all-to-all-done.2.parts = bf16[8,24,128]{2,1,0:T(8,128)(2,1)S(1)} async-done(((bf16[8,24,128]{2,1,0:T(8,128)(2,1)}), bf16[8,24,128]{2,1,0:T(8,128)(2,1)S(1)}, u32[]{:S(2)}, u32[]{:S(2)}) %all-to-all-start.2) | async-done | bytes 49184 | tf_op jit(solution)/shard_map/all_to_all | solution.py:304
  133.9 24.5 %all_to_all.20.parts = bf16[32,2,24,128]{3,2,1,0:T(8,128)(2,1)S(1)} all-to-all(bf16[32,2,24,128]{3,2,1,0:T(8,128)(2,1)S(1)} %shard_map.119), channel_id=1, replica_groups=mesh['zl'=2,'x'=4,'zh'=4,'y'=8,'c'=2] {'zh','y'}, dimensions={0} | all-to-all | bytes 786432 | tf_op jit(solution)/shard_map/all_to_all | solution.py:304
  159.2 6.6 %all-gather = bf16[64,24,128]{2,1,0:T(8,128)(2,1)S(1)} all-gather(bf16[32,24,128]{2,1,0:T(8,128)(2,1)S(1)} %get-tuple-element.47), channel_id=2, replica_groups=mesh['zl'=2,'x'=4,'zh'=4,'y'=8,'c'=2] {'c'}, dimensions={0}, use_global_device_ids=true | all-gather | bytes 589824 | tf_op jit(solution)/shard_map/all_gather | solution.py:401
  (33 shorter events, 14.0 us)
Async XLA Ops:
  2.9 10.1 %collective-permute-start.2 = (bf16[1,4,16,192]{3,2,1,0:T(8,128)(2,1)}, bf16[1,4,16,192]{3,2,1,0:T(8,128)(2,1)S(1)}, u32[]{:S(2)}, u32[]{:S(2)}) collective-permute-start(bf16[1,4,16,192]{3,2,1,0:T(8,128)(2,1)} %get-tuple-element.28), channel_id=1, source_target_pairs={{0,1},{1,2},{2,3},{3,4},{4,5},{5,6},{6,7},{7,8},{8,9},{9,10},{10,1... | collective-permute-start | bytes 73736 | tf_op jit(solution)/shard_map/ppermute | solution.py:329
  7.5 6.5 %collective-permute-start.3 = (bf16[1,4,16,192]{3,2,1,0:T(8,128)(2,1)}, bf16[1,4,16,192]{3,2,1,0:T(8,128)(2,1)S(1)}, u32[]{:S(2)}, u32[]{:S(2)}) collective-permute-start(bf16[1,4,16,192]{3,2,1,0:T(8,128)(2,1)} %get-tuple-element.29), channel_id=1, source_target_pairs={{1,0},{2,1},{3,2},{4,3},{5,4},{6,5},{7,6},{8,7},{9,8},{10,9},{11,1... | collective-permute-start | bytes 73736 | tf_op jit(solution)/shard_map/ppermute | solution.py:329
  14.1 15.4 %copy-start.4 = (bf16[4,4,16,192]{3,2,1,0:T(8,128)(2,1)S(1)}, bf16[4,4,16,192]{3,2,1,0:T(8,128)(2,1)}, u32[]{:S(2)}) copy-start(bf16[4,4,16,192]{3,2,1,0:T(8,128)(2,1)} %get-tuple-element.26.grad) | copy-start | bytes 294916
  14.1 23.7 %copy-start = (s32[512]{0:T(512)S(1)}, s32[512]{0:T(512)}, u32[]{:S(2)}) copy-start(s32[512]{0:T(512)} %counts_in.5) | copy-start | bytes 6148
  14.1 23.7 %copy-start.1 = (bf16[256,768]{1,0:T(8,128)(2,1)S(1)}, bf16[256,768]{1,0:T(8,128)(2,1)}, u32[]{:S(2)}) copy-start(bf16[256,768]{1,0:T(8,128)(2,1)} %fine_in.3) | copy-start | bytes 1179652
  14.1 23.7 %copy-start.3 = (bf16[768,192]{0,1:T(8,128)(2,1)S(1)}, bf16[768,192]{0,1:T(8,128)(2,1)}, u32[]{:S(2)}) copy-start(bf16[768,192]{0,1:T(8,128)(2,1)} %param.10) | copy-start | bytes 884740
  14.1 23.7 %copy-start.5 = (s32[4,27]{1,0:T(4,128)S(1)}, s32[4,27]{1,0:T(4,128)}, u32[]{:S(2)}) copy-start(s32[4,27]{1,0:T(4,128)} %near_in.1) | copy-start | bytes 1300
  14.1 48.3 %all-to-all-start = ((bf16[32,144,128]{2,1,0:T(8,128)(2,1)}), bf16[32,144,128]{2,1,0:T(8,128)(2,1)S(1)}, u32[]{:S(2)}, u32[]{:S(2)}) async-start(bf16[32,144,128]{2,1,0:T(8,128)(2,1)} %get-tuple-element.33), calls=%async_computation | async-start | bytes 2359296 | tf_op jit(solution)/shard_map/all_to_all | solution.py:304
  29.5 7.2 %collective-permute-start.1 = (bf16[4,4,16,192]{3,2,1,0:T(8,128)(2,1)S(1)}, bf16[4,4,16,192]{3,2,1,0:T(8,128)(2,1)S(1)}, u32[]{:S(2)}, u32[]{:S(2)}) collective-permute-start(bf16[4,4,16,192]{3,2,1,0:T(8,128)(2,1)S(1)} %copy-done.4), channel_id=1, source_target_pairs={{64,0},{128,64},{192,128},{256,192},{320,256},{384,320},{448,384},... | collective-permute-start | bytes 294920 | tf_op jit(solution)/shard_map/ppermute | solution.py:329
  30.8 6.9 %collective-permute-start = (bf16[4,4,16,192]{3,2,1,0:T(8,128)(2,1)S(1)}, bf16[4,4,16,192]{3,2,1,0:T(8,128)(2,1)S(1)}, u32[]{:S(2)}, u32[]{:S(2)}) collective-permute-start(bf16[4,4,16,192]{3,2,1,0:T(8,128)(2,1)S(1)} %copy-done.4), channel_id=1, source_target_pairs={{0,64},{64,128},{128,192},{192,256},{256,320},{320,384},{384,448},... | collective-permute-start | bytes 294920 | tf_op jit(solution)/shard_map/ppermute | solution.py:329
  43.0 1.2 copy-start.6
  44.2 4.9 %collective-permute-start.4 = (bf16[8,24,2592]{2,1,0:T(8,128)(2,1)S(1)}, bf16[8,24,2592]{2,1,0:T(8,128)(2,1)S(1)}, u32[]{:S(2)}, u32[]{:S(2)}) collective-permute-start(bf16[8,24,2592]{2,1,0:T(8,128)(2,1)S(1)} %get-tuple-element.34), channel_id=1, source_target_pairs={{0,1},{1,0},{2,3},{3,2},{4,5},{5,4},{6,7},{7,6},{8,9},{9,8},{10,11... | collective-permute-start | bytes 2985992 | tf_op jit(solution)/shard_map/ppermute | solution.py:332
  62.4 5.1 %collective-permute-start.5 = (bf16[32,144,128]{2,1,0:T(8,128)(2,1)S(1)}, bf16[32,144,128]{2,1,0:T(8,128)(2,1)S(1)}, u32[]{:S(2)}, u32[]{:S(2)}) collective-permute-start(bf16[32,144,128]{2,1,0:T(8,128)(2,1)S(1)} %all-to-all-done.mine), channel_id=1, source_target_pairs={{0,1},{1,0},{2,3},{3,2},{4,5},{5,4},{6,7},{7,6},{8,9},{9,8},{10,11... | collective-permute-start | bytes 3538952 | tf_op jit(solution)/shard_map/ppermute | solution.py:332
  67.5 1.0 copy-start.2
  68.5 1.5 copy-start.7
  73.7 3.3 %collective-permute-start.6 = (bf16[576,128]{1,0:T(8,128)(2,1)S(1)}, bf16[576,128]{1,0:T(8,128)(2,1)S(1)}, u32[]{:S(2)}, u32[]{:S(2)}) collective-permute-start(bf16[576,128]{1,0:T(8,128)(2,1)S(1)} %get-tuple-element.38), channel_id=1, source_target_pairs={{0,1},{1,0},{2,3},{3,2},{4,5},{5,4},{6,7},{7,6},{8,9},{9,8},{10,11... | collective-permute-start | bytes 442376 | tf_op jit(solution)/shard_map/ppermute | solution.py:332
  77.7 45.5 %all-to-all-start.1 = ((bf16[32,24,128]{2,1,0:T(8,128)(2,1)}), bf16[32,24,128]{2,1,0:T(8,128)(2,1)S(1)}, u32[]{:S(2)}, u32[]{:S(2)}) async-start(bf16[32,24,128]{2,1,0:T(8,128)(2,1)} %shard_map.115), calls=%async_computation.1 | async-start | bytes 393216 | tf_op jit(solution)/shard_map/all_to_all | solution.py:304
  86.8 22.1 %collective-permute-start.7 = (bf16[2,24,2592]{2,1,0:T(8,128)(2,1)S(1)}, bf16[2,24,2592]{2,1,0:T(8,128)(2,1)S(1)}, u32[]{:S(2)}, u32[]{:S(2)}) collective-permute-start(bf16[2,24,2592]{2,1,0:T(8,128)(2,1)S(1)} %get-tuple-element.42), channel_id=1, source_target_pairs={{0,64},{64,128},{128,192},{192,0},{1,65},{65,129},{129,193},{193,1... | collective-permute-start | bytes 746504 | tf_op jit(solution)/shard_map/ppermute | solution.py:368
  89.9 25.3 %collective-permute-start.8 = (bf16[2,24,2592]{2,1,0:T(8,128)(2,1)S(1)}, bf16[2,24,2592]{2,1,0:T(8,128)(2,1)S(1)}, u32[]{:S(2)}, u32[]{:S(2)}) collective-permute-start(bf16[2,24,2592]{2,1,0:T(8,128)(2,1)S(1)} %get-tuple-element.43), channel_id=1, source_target_pairs={{0,128},{64,192},{128,0},{192,64},{1,129},{65,193},{129,1},{193,65... | collective-permute-start | bytes 746504 | tf_op jit(solution)/shard_map/ppermute | solution.py:368
  106.0 10.6 %collective-permute-start.9 = (bf16[2,24,2592]{2,1,0:T(8,128)(2,1)S(1)}, bf16[2,24,2592]{2,1,0:T(8,128)(2,1)S(1)}, u32[]{:S(2)}, u32[]{:S(2)}) collective-permute-start(bf16[2,24,2592]{2,1,0:T(8,128)(2,1)S(1)} %get-tuple-element.44), channel_id=1, source_target_pairs={{0,192},{64,0},{128,64},{192,128},{1,193},{65,1},{129,65},{193,129... | collective-permute-start | bytes 746504 | tf_op jit(solution)/shard_map/ppermute | solution.py:368
  116.7 11.8 %collective-permute-start.10 = (bf16[24,2592]{1,0:T(8,128)(2,1)S(1)}, bf16[24,2592]{1,0:T(8,128)(2,1)S(1)}, u32[]{:S(2)}, u32[]{:S(2)}) collective-permute-start(bf16[24,2592]{1,0:T(8,128)(2,1)S(1)} %get-tuple-element.46), channel_id=1, source_target_pairs={{0,256},{256,0},{1,257},{257,1},{2,258},{258,2},{3,259},{259,3},{4... | collective-permute-start | bytes 373256 | tf_op jit(solution)/shard_map/ppermute | solution.py:371
  123.8 9.8 %all-to-all-start.2 = ((bf16[8,24,128]{2,1,0:T(8,128)(2,1)}), bf16[8,24,128]{2,1,0:T(8,128)(2,1)S(1)}, u32[]{:S(2)}, u32[]{:S(2)}) async-start(bf16[8,24,128]{2,1,0:T(8,128)(2,1)} %shard_map.116), calls=%async_computation.2 | async-start | bytes 98304 | tf_op jit(solution)/shard_map/all_to_all | solution.py:304

commit v6 on v5

--- a/solution.py
+++ b/solution.py
@@ -17,7 +17,7 @@
 B = 4
 C = 192
 ROWS = 81
-FRAME = 96
+FRAME = 80
 HALF = 32 * ROWS
 COLS = C // SLABS
 
@@ -34,6 +34,11 @@
     for axis, size in zip(AXES[1:], SIZES[1:]):
         place = place * size + lax.axis_index(axis)
     return place
+
+
+def repeat_kernel(block, out):
+    for i in range(out.shape[0]):
+        out[i] = block[...]
 
 
 def iota(rows, cols, dim):
@@ -81,7 +86,7 @@
 
 def prepare_kernel(
     counts_in, pre_in, cot_in, gain_in, bias_in, weight_in, grad, first, last, frames,
-    counts, pre, cot, gain, bias, weight, sems,
+    counts, pre, cot, gain, bias, weight, tiles, sems,
 ):
     copies = fetch(
         sems, (counts_in, counts), (pre_in, pre), (cot_in, cot), (gain_in, gain), (bias_in, bias),
@@ -90,15 +95,24 @@
     place = my_place()
     copies[5].wait()
     shift = jnp.bitwise_and(place, 15)
-    spread = ones_where(iota(FRAME, ROWS, 0) == iota(FRAME, ROWS, 1) + shift)
-    frame = dot(spread, weight[...])
-    main = frame[:, :128].astype(BF16)
-    low = frame[:48, 128:].astype(BF16)
-    high = frame[48:, 128:].astype(BF16)
-    tail = jnp.concatenate([low, high], axis=1)
+    at = iota(FRAME, ROWS, 1) + shift
+    turned = jnp.where(at >= FRAME, at - FRAME, at)
+    spread = ones_where((iota(FRAME, ROWS, 0) == turned) & (iota(FRAME, ROWS, 1) < FRAME))
+    turned = dot(spread, weight[...])
+    for i in range(5):
+        tiles[i] = turned[i * 16 : (i + 1) * 16, :128].astype(BF16)
+    extra = dot(ones_where(iota(16, ROWS, 1) == ROWS - 1), weight[...])
+    row = iota(16, 64, 0)
+    extra = jnp.where(
+        row == 0, extra[:, :64], jnp.where(row == 1, extra[:, 64:128], extra[:, 128:])
+    )
+    tails = [turned[i * 16 : (i + 1) * 16, 128:] for i in range(5)] + [extra]
+    for i in range(3):
+        pair = jnp.concatenate([tails[2 * i], tails[2 * i + 1]], axis=1)
+        tiles[5 + i] = pair.astype(BF16)
+    mine = tiles[lax.shift_right_logical(place, 6)]
     for i in range(32):
-        frames[i, :FRAME] = main
-        frames[i, FRAME:] = tail
+        frames[i] = mine
     for copy in copies[:5]:
         copy.wait()
     count = counts[place]
@@ -202,22 +216,33 @@
     core = jnp.bitwise_and(place, 1)
     both[core] = mine[...]
     both[1 - core] = other[...]
+    row = iota(16, 128, 0)
+    held = None
     for owner in range(DEVS):
-        tile = ROWS * owner // 16
-        frame = both.at[owner % 2, owner // 2]
-        main = frame[:FRAME]
-        low = frame[FRAME:, :64]
-        high = frame[FRAME:, 64:]
-        row = tile * 16
-        if owner % 16:
-            whole[row : row + 16, :128] = whole[row : row + 16, :128] + main[:16]
-            whole[row : row + 16, 128:] = whole[row : row + 16, 128:] + low[:16]
-            whole[row + 16 : row + FRAME, :128] = main[16:]
-            whole[row + 16 : row + 48, 128:] = low[16:]
-        else:
-            whole[row : row + FRAME, :128] = main
-            whole[row : row + 48, 128:] = low
-        whole[row + 48 : row + FRAME, 128:] = high
+        first = ROWS * owner // 16 * 16
+        shift = owner % 16
+        tiles = [both[owner % 2, i, owner // 2] for i in range(SLABS)]
+        for i in range(1, 5):
+            whole[first + i * 16 : first + (i + 1) * 16, :128] = tiles[i]
+            half = i % 2 * 64
+            whole[first + i * 16 : first + (i + 1) * 16, 128:] = tiles[5 + i // 2][
+                :, half : half + 64
+            ]
+        main, tail = tiles[0].astype(F32), tiles[5][:, :64].astype(F32)
+        extra = tiles[7][:, 64:].astype(F32)
+        long = jnp.concatenate([extra[0:1], extra[1:2]], axis=1)
+        ends = [jnp.where(row < shift, main, jnp.where(row == shift, long, 0.0))]
+        short = row[:, :64]
+        ends.append(jnp.where(short < shift, tail, jnp.where(short == shift, extra[2:3], 0.0)))
+        if shift:
+            main = jnp.where(row >= shift, main, held[0])
+            tail = jnp.where(short >= shift, tail, held[1])
+        whole[first : first + 16, :128] = main.astype(BF16)
+        whole[first : first + 16, 128:] = tail.astype(BF16)
+        if shift == 15:
+            whole[first + 80 : first + 96, :128] = ends[0].astype(BF16)
+            whole[first + 80 : first + 96, 128:] = ends[1].astype(BF16)
+        held = ends
     back = jnp.zeros((256, C), F32)
     for tap in range(27):
         row = tap_rows(tap)
@@ -310,7 +335,7 @@
     counts_scratch = pltpu.SMEM((SLABS * DEVS,), jnp.int32)
     grad, first, last, frames = call(
         prepare_kernel,
-        (shape(B, 4, 16, C), shape(1, 4, 16, C), shape(1, 4, 16, C), shape(32, 144, 128)),
+        (shape(B, 4, 16, C), shape(1, 4, 16, C), shape(1, 4, 16, C), shape(32, 16, 128)),
         [HBM] * 6,
         [
             counts_scratch,
@@ -319,6 +344,7 @@
             pltpu.VMEM((1, C), F32),
             pltpu.VMEM((1, C), F32),
             pltpu.VMEM((ROWS, C), BF16),
+            pltpu.VMEM((SLABS, 16, 128), BF16),
             pltpu.SemaphoreType.DMA((6,)),
         ],
         vmem=60,
@@ -336,8 +362,12 @@
     dev_low = shifted(last, DEV, DEVS, 1)
     dev_high = shifted(first, DEV, DEVS, -1)
 
-    frames, dev_low, dev_high = lax.optimization_barrier((frames, dev_low, dev_high))
     frames = swap(frames, ("zh", "y"))
+    frames, slab_low, slab_high, dev_low, dev_high = lax.optimization_barrier(
+        (frames, slab_low, slab_high, dev_low, dev_high)
+    )
+    frames = call(repeat_kernel, shape(SLABS, 32, 16, 128), [VMEM])(frames)
+    frames = swap(frames, SLAB)
 
     fine_scratch = pltpu.VMEM((256, 768), BF16)
     weight_scratch = pltpu.VMEM((C, 768), BF16)
@@ -379,7 +409,7 @@
             fine_scratch,
             weight_scratch,
             pltpu.SemaphoreType.DMA((3,)),
-            pltpu.VMEM((2, 32, 144, 128), BF16),
+            pltpu.VMEM((2, SLABS, 32, 16, 128), BF16),
             pltpu.VMEM((27 * C, C), BF16),
             pltpu.VMEM((2, 576, 128), BF16),
         ],

time: 167 us -> 149 us (0.89)
  waiting for transfers between devices: 36.7 us -> 26.3 us
  starting transfers between devices: 79.4 us -> 70.2 us
    ppermute x3, starting transfers between devices: 21.1 us -> 9.32 us  [local(): lax.ppermute(conv[dx], 'x', [(i, (i + dx) % 4) for i in range(4)])]
    all_to_all x3 -> x4, starting transfers between devices: 28.9 us -> 39.6 us  [swap(): return lax.all_to_all(x, axes, 0, 0, tiled=True)]
    all_to_all x3 -> x4, waiting for transfers between devices: 18.4 us -> 7.8 us  [swap(): return lax.all_to_all(x, axes, 0, 0, tiled=True)]
    ppermute x1, starting transfers between devices: 6.46 us -> 3.1 us  [local(): conv = (keep, lax.ppermute(send, 'zl', [(0, 1), (1, 0)]))]
    ppermute x4, starting transfers between devices: 15.4 us -> 12 us  [shifted(): return lax.ppermute(x, axes, pairs)]
  transfers between devices with their start and end apart: 14 -> 15, of which waited for: 11 -> 9; matrix products, arithmetic and copies ran while one was open for 0% -> 0% of each run, Pallas kernels for 4% -> 4%
where the time goes in v6:
time: 149 us; the launch traced here: 148 us
  starting transfers between devices  70.2 us (47%)
  blocking collectives  31.1 us (21%)
  waiting for transfers between devices  26.3 us (18%)
  Pallas kernels  15 us (10%)
  local copies, waits for them, and re-layouts  4.37 us (3%)
    all_to_all x4, starting transfers between devices, swap(): return lax.all_to_all(x, axes, 0, 0, tiled=True)  39.6 us
    all_to_all x1, blocking collectives, swap(): return lax.all_to_all(x, axes, 0, 0, tiled=True)  24.5 us
    ppermute x4, starting transfers between devices, shifted(): return lax.ppermute(x, axes, pairs)  12 us
    ppermute x3, starting transfers between devices, local(): lax.ppermute(conv[dx], 'x', [(i, (i + dx) % 4) for i in range(4)])  9.32 us
    ppermute x3, waiting for transfers between devices, local(): lax.ppermute(conv[dx], 'x', [(i, (i + dx) % 4) for i in range(4)])  8.9 us
    all_to_all x4, waiting for transfers between devices, swap(): return lax.all_to_all(x, axes, 0, 0, tiled=True)  7.8 us
    all_gather x1, blocking collectives, local(): term = lax.all_gather(term, 'c', axis=0, tiled=False)  6.59 us
    ppermute x3, starting transfers between devices, flipped(): return lax.ppermute(x, 'c', [(0, 1), (1, 0)])  6.17 us
  transfers between devices with their start and end apart: 15, of which 9 were waited for; matrix products, arithmetic and copies ran while one was open for 0% of the time, Pallas kernels for 4%

profile of v6, /device:TPU:1, one launch (start us, length us, event | category | flops | bytes accessed | tf_op | source)
XLA Modules:
  0.0 147.9 jit_solution(7397868202040514875)
XLA Ops:
  0.6 2.2 %shard_map.112 = (bf16[4,4,16,192]{3,2,1,0:T(8,128)(2,1)}, bf16[1,4,16,192]{3,2,1,0:T(8,128)(2,1)}, bf16[1,4,16,192]{3,2,1,0:T(8,128)(2,1)}, bf16[32,16,128]{2,1,0:T(8,128)(2,1)}) custom-call(s32[512]{0:T(512)} %counts_in.5, bf16[4,16,768]{2,1,0:T(8,128)(2,1)} %pre_in.1, bf16[4,16,768]{2,1,0:T(8,128)(2,1)} %cot_in.1, f32[1,192]{1,0:T(1,128)} %bitcast.13, ...), custom_call_target="tpu_custom_call" | custom-call | tf_op jit(solution)/shard_map/pallas_call | solution.py:336
  2.9 16.6 %all-to-all-start = ((bf16[32,16,128]{2,1,0:T(8,128)(2,1)}), bf16[32,16,128]{2,1,0:T(8,128)(2,1)S(1)}, u32[]{:S(2)}, u32[]{:S(2)}) async-start(bf16[32,16,128]{2,1,0:T(8,128)(2,1)} %get-tuple-element.29), calls=%async_computation | async-start | bytes 262144 | tf_op jit(solution)/shard_map/all_to_all | solution.py:329
  20.8 4.0 %collective-permute-start = (bf16[4,4,16,192]{3,2,1,0:T(8,128)(2,1)}, bf16[4,4,16,192]{3,2,1,0:T(8,128)(2,1)S(1)}, u32[]{:S(2)}, u32[]{:S(2)}) collective-permute-start(bf16[4,4,16,192]{3,2,1,0:T(8,128)(2,1)} %get-tuple-element.28.grad), channel_id=1, source_target_pairs={{0,64},{64,128},{128,192},{192,256},{256,320},{320,384},{384,448},... | collective-permute-start | bytes 294920 | tf_op jit(solution)/shard_map/ppermute | solution.py:355
  24.8 4.8 %collective-permute-start.2 = (bf16[1,4,16,192]{3,2,1,0:T(8,128)(2,1)}, bf16[1,4,16,192]{3,2,1,0:T(8,128)(2,1)S(1)}, u32[]{:S(2)}, u32[]{:S(2)}) collective-permute-start(bf16[1,4,16,192]{3,2,1,0:T(8,128)(2,1)} %get-tuple-element.30), channel_id=1, source_target_pairs={{0,1},{1,2},{2,3},{3,4},{4,5},{5,6},{6,7},{7,8},{8,9},{9,10},{10,1... | collective-permute-start | bytes 73736 | tf_op jit(solution)/shard_map/ppermute | solution.py:355
  31.6 3.5 %collective-permute-done.3.dev_high = bf16[1,4,16,192]{3,2,1,0:T(8,128)(2,1)S(1)} collective-permute-done((bf16[1,4,16,192]{3,2,1,0:T(8,128)(2,1)}, bf16[1,4,16,192]{3,2,1,0:T(8,128)(2,1)S(1)}, u32[]{:S(2)}, u32[]{:S(2)}) %collective-permute-start.3) | collective-permute-done | bytes 24608 | tf_op jit(solution)/shard_map/ppermute | solution.py:355
  36.2 5.9 %all-to-all-start.1 = ((bf16[8,32,16,128]{3,2,1,0:T(8,128)(2,1)}), bf16[8,32,16,128]{3,2,1,0:T(8,128)(2,1)S(1)}, u32[]{:S(2)}, u32[]{:S(2)}) async-start(bf16[8,32,16,128]{3,2,1,0:T(8,128)(2,1)} %shard_map.114), calls=%async_computation.1 | async-start | bytes 2097152 | tf_op jit(solution)/shard_map/all_to_all | solution.py:329
  42.1 5.2 %shard_map.113 = (bf16[8,24,2592]{2,1,0:T(8,128)(2,1)S(1)}, bf16[8,24,2592]{2,1,0:T(8,128)(2,1)S(1)}, bf16[3456,192]{1,0:T(8,128)(2,1)S(1)}) custom-call(s32[512]{0:T(512)S(1)} %copy-done, s32[4,27]{1,0:T(4,128)S(1)} %copy-done.5, bf16[256,768]{1,0:T(8,128)(2,1)S(1)} %copy-done.1, bf16[192,768]{1,0:T(8,128)(2,1)S(1)} %bitcast.10, ...), custom_call_target="tpu_custom_call" | custom-call | flops 6000000000 | tf_op jit(solution)/shard_map/pallas_call | solution.py:375
  50.5 2.6 %collective-permute-done.4.received = bf16[8,24,2592]{2,1,0:T(8,128)(2,1)S(1)} collective-permute-done((bf16[8,24,2592]{2,1,0:T(8,128)(2,1)S(1)}, bf16[8,24,2592]{2,1,0:T(8,128)(2,1)S(1)}, u32[]{:S(2)}, u32[]{:S(2)}) %collective-permute-start.4) | collective-permute-done | bytes 995360 | tf_op jit(solution)/shard_map/ppermute | solution.py:358
  53.1 2.6 %all-to-all-done.1.mine = bf16[8,32,16,128]{3,2,1,0:T(8,128)(2,1)S(1)} async-done(((bf16[8,32,16,128]{3,2,1,0:T(8,128)(2,1)}), bf16[8,32,16,128]{3,2,1,0:T(8,128)(2,1)S(1)}, u32[]{:S(2)}, u32[]{:S(2)}) %all-to-all-start.1) | async-done | bytes 1048608 | tf_op jit(solution)/shard_map/all_to_all | solution.py:329
  55.8 2.1 %collective-permute-start.5 = (bf16[8,32,16,128]{3,2,1,0:T(8,128)(2,1)S(1)}, bf16[8,32,16,128]{3,2,1,0:T(8,128)(2,1)S(1)}, u32[]{:S(2)}, u32[]{:S(2)}) collective-permute-start(bf16[8,32,16,128]{3,2,1,0:T(8,128)(2,1)S(1)} %all-to-all-done.1.mine), channel_id=1, source_target_pairs={{0,1},{1,0},{2,3},{3,2},{4,5},{5,4},{6,7},{7,6},{8,9},{9,8},{10,11... | collective-permute-start | bytes 3145736 | tf_op jit(solution)/shard_map/ppermute | solution.py:358
  57.9 2.4 %collective-permute-done.5.other = bf16[8,32,16,128]{3,2,1,0:T(8,128)(2,1)S(1)} collective-permute-done((bf16[8,32,16,128]{3,2,1,0:T(8,128)(2,1)S(1)}, bf16[8,32,16,128]{3,2,1,0:T(8,128)(2,1)S(1)}, u32[]{:S(2)}, u32[]{:S(2)}) %collective-permute-start.5) | collective-permute-done | bytes 1048608 | tf_op jit(solution)/shard_map/ppermute | solution.py:358
  62.7 3.5 %shard_map.115 = (bf16[256,768]{1,0:T(8,128)(2,1)}, bf16[576,128]{1,0:T(8,128)(2,1)S(1)}, bf16[576,128]{1,0:T(8,128)(2,1)S(1)}) custom-call(s32[512]{0:T(512)S(1)} %copy-done, bf16[256,768]{1,0:T(8,128)(2,1)S(1)} %copy-done.1, bf16[192,768]{1,0:T(8,128)(2,1)S(1)} %bitcast.11, bf16[3456,192]{1,0:T(8,128)(2,1)S(1)} %copy-done.7, ...), custom_call_target="tpu_custom_call" | custom-call | flops 4000000000 | tf_op jit(solution)/shard_map/pallas_call | solution.py:403
  66.3 2.1 %collective-permute-start.6 = (bf16[576,128]{1,0:T(8,128)(2,1)S(1)}, bf16[576,128]{1,0:T(8,128)(2,1)S(1)}, u32[]{:S(2)}, u32[]{:S(2)}) collective-permute-start(bf16[576,128]{1,0:T(8,128)(2,1)S(1)} %get-tuple-element.42), channel_id=1, source_target_pairs={{0,1},{1,0},{2,3},{3,2},{4,5},{5,4},{6,7},{7,6},{8,9},{9,8},{10,11... | collective-permute-start | bytes 442376 | tf_op jit(solution)/shard_map/ppermute | solution.py:358
  70.3 12.4 %all-to-all-start.2 = ((bf16[32,24,128]{2,1,0:T(8,128)(2,1)}), bf16[32,24,128]{2,1,0:T(8,128)(2,1)S(1)}, u32[]{:S(2)}, u32[]{:S(2)}) async-start(bf16[32,24,128]{2,1,0:T(8,128)(2,1)} %shard_map.116), calls=%async_computation.2 | async-start | bytes 393216 | tf_op jit(solution)/shard_map/all_to_all | solution.py:329
  82.9 2.5 %collective-permute-start.7 = (bf16[2,24,2592]{2,1,0:T(8,128)(2,1)S(1)}, bf16[2,24,2592]{2,1,0:T(8,128)(2,1)S(1)}, u32[]{:S(2)}, u32[]{:S(2)}) collective-permute-start(bf16[2,24,2592]{2,1,0:T(8,128)(2,1)S(1)} %get-tuple-element.46), channel_id=1, source_target_pairs={{0,64},{64,128},{128,192},{192,0},{1,65},{65,129},{129,193},{193,1... | collective-permute-start | bytes 746504 | tf_op jit(solution)/shard_map/ppermute | solution.py:398
  85.4 3.7 %collective-permute-start.8 = (bf16[2,24,2592]{2,1,0:T(8,128)(2,1)S(1)}, bf16[2,24,2592]{2,1,0:T(8,128)(2,1)S(1)}, u32[]{:S(2)}, u32[]{:S(2)}) collective-permute-start(bf16[2,24,2592]{2,1,0:T(8,128)(2,1)S(1)} %get-tuple-element.47), channel_id=1, source_target_pairs={{0,128},{64,192},{128,0},{192,64},{1,129},{65,193},{129,1},{193,65... | collective-permute-start | bytes 746504 | tf_op jit(solution)/shard_map/ppermute | solution.py:398
  89.2 3.1 %collective-permute-start.9 = (bf16[2,24,2592]{2,1,0:T(8,128)(2,1)S(1)}, bf16[2,24,2592]{2,1,0:T(8,128)(2,1)S(1)}, u32[]{:S(2)}, u32[]{:S(2)}) collective-permute-start(bf16[2,24,2592]{2,1,0:T(8,128)(2,1)S(1)} %get-tuple-element.48), channel_id=1, source_target_pairs={{0,192},{64,0},{128,64},{192,128},{1,193},{65,1},{129,65},{193,129... | collective-permute-start | bytes 746504 | tf_op jit(solution)/shard_map/ppermute | solution.py:398
  93.4 5.1 %collective-permute-done.8.c = bf16[2,24,2592]{2,1,0:T(8,128)(2,1)S(1)} collective-permute-done((bf16[2,24,2592]{2,1,0:T(8,128)(2,1)S(1)}, bf16[2,24,2592]{2,1,0:T(8,128)(2,1)S(1)}, u32[]{:S(2)}, u32[]{:S(2)}) %collective-permute-start.8) | collective-permute-done | bytes 248864 | tf_op jit(solution)/shard_map/ppermute | solution.py:398
  98.5 2.7 %collective-permute-done.9.d = bf16[2,24,2592]{2,1,0:T(8,128)(2,1)S(1)} collective-permute-done((bf16[2,24,2592]{2,1,0:T(8,128)(2,1)S(1)}, bf16[2,24,2592]{2,1,0:T(8,128)(2,1)S(1)}, u32[]{:S(2)}, u32[]{:S(2)}) %collective-permute-start.9) | collective-permute-done | bytes 248864 | tf_op jit(solution)/shard_map/ppermute | solution.py:398
  101.3 3.1 %collective-permute-start.10 = (bf16[24,2592]{1,0:T(8,128)(2,1)S(1)}, bf16[24,2592]{1,0:T(8,128)(2,1)S(1)}, u32[]{:S(2)}, u32[]{:S(2)}) collective-permute-start(bf16[24,2592]{1,0:T(8,128)(2,1)S(1)} %get-tuple-element.50), channel_id=1, source_target_pairs={{0,256},{256,0},{1,257},{257,1},{2,258},{258,2},{3,259},{259,3},{4... | collective-permute-start | bytes 373256 | tf_op jit(solution)/shard_map/ppermute | solution.py:401
  105.1 4.7 %all-to-all-start.3 = ((bf16[8,24,128]{2,1,0:T(8,128)(2,1)}), bf16[8,24,128]{2,1,0:T(8,128)(2,1)S(1)}, u32[]{:S(2)}, u32[]{:S(2)}) async-start(bf16[8,24,128]{2,1,0:T(8,128)(2,1)} %shard_map.117), calls=%async_computation.3 | async-start | bytes 98304 | tf_op jit(solution)/shard_map/all_to_all | solution.py:329
  109.8 5.1 %all-to-all-done.3.parts = bf16[8,24,128]{2,1,0:T(8,128)(2,1)S(1)} async-done(((bf16[8,24,128]{2,1,0:T(8,128)(2,1)}), bf16[8,24,128]{2,1,0:T(8,128)(2,1)S(1)}, u32[]{:S(2)}, u32[]{:S(2)}) %all-to-all-start.3) | async-done | bytes 49184 | tf_op jit(solution)/shard_map/all_to_all | solution.py:329
  115.1 24.5 %all_to_all.25.parts = bf16[32,2,24,128]{3,2,1,0:T(8,128)(2,1)S(1)} all-to-all(bf16[32,2,24,128]{3,2,1,0:T(8,128)(2,1)S(1)} %shard_map.120), channel_id=1, replica_groups=mesh['zl'=2,'x'=4,'zh'=4,'y'=8,'c'=2] {'zh','y'}, dimensions={0} | all-to-all | bytes 786432 | tf_op jit(solution)/shard_map/all_to_all | solution.py:329
  140.4 6.6 %all-gather = bf16[64,24,128]{2,1,0:T(8,128)(2,1)S(1)} all-gather(bf16[32,24,128]{2,1,0:T(8,128)(2,1)S(1)} %get-tuple-element.51), channel_id=2, replica_groups=mesh['zl'=2,'x'=4,'zh'=4,'y'=8,'c'=2] {'c'}, dimensions={0}, use_global_device_ids=true | all-gather | bytes 589824 | tf_op jit(solution)/shard_map/all_gather | solution.py:431
  (36 shorter events, 15.8 us)
Async XLA Ops:
  2.8 39.3 %copy-start = (s32[512]{0:T(512)S(1)}, s32[512]{0:T(512)}, u32[]{:S(2)}) copy-start(s32[512]{0:T(512)} %counts_in.5) | copy-start | bytes 6148
  2.8 39.3 %copy-start.1 = (bf16[256,768]{1,0:T(8,128)(2,1)S(1)}, bf16[256,768]{1,0:T(8,128)(2,1)}, u32[]{:S(2)}) copy-start(bf16[256,768]{1,0:T(8,128)(2,1)} %fine_in.3) | copy-start | bytes 1179652
  2.8 39.3 %copy-start.2 = (bf16[768,192]{0,1:T(8,128)(2,1)S(1)}, bf16[768,192]{0,1:T(8,128)(2,1)}, u32[]{:S(2)}) copy-start(bf16[768,192]{0,1:T(8,128)(2,1)} %param.10) | copy-start | bytes 884740
  2.8 39.3 %copy-start.4 = (bf16[4,4,16,192]{3,2,1,0:T(8,128)(2,1)S(1)}, bf16[4,4,16,192]{3,2,1,0:T(8,128)(2,1)}, u32[]{:S(2)}) copy-start(bf16[4,4,16,192]{3,2,1,0:T(8,128)(2,1)} %get-tuple-element.28.grad) | copy-start | bytes 294916
  2.9 39.3 %copy-start.5 = (s32[4,27]{1,0:T(4,128)S(1)}, s32[4,27]{1,0:T(4,128)}, u32[]{:S(2)}) copy-start(s32[4,27]{1,0:T(4,128)} %near_in.1) | copy-start | bytes 1300
  2.9 32.2 %all-to-all-start = ((bf16[32,16,128]{2,1,0:T(8,128)(2,1)}), bf16[32,16,128]{2,1,0:T(8,128)(2,1)S(1)}, u32[]{:S(2)}, u32[]{:S(2)}) async-start(bf16[32,16,128]{2,1,0:T(8,128)(2,1)} %get-tuple-element.29), calls=%async_computation | async-start | bytes 262144 | tf_op jit(solution)/shard_map/all_to_all | solution.py:329
  19.5 15.6 %collective-permute-start.1 = (bf16[4,4,16,192]{3,2,1,0:T(8,128)(2,1)}, bf16[4,4,16,192]{3,2,1,0:T(8,128)(2,1)S(1)}, u32[]{:S(2)}, u32[]{:S(2)}) collective-permute-start(bf16[4,4,16,192]{3,2,1,0:T(8,128)(2,1)} %get-tuple-element.28.grad), channel_id=1, source_target_pairs={{64,0},{128,64},{192,128},{256,192},{320,256},{384,320},{448,384},... | collective-permute-start | bytes 294920 | tf_op jit(solution)/shard_map/ppermute | solution.py:355
  20.8 14.3 %collective-permute-start = (bf16[4,4,16,192]{3,2,1,0:T(8,128)(2,1)}, bf16[4,4,16,192]{3,2,1,0:T(8,128)(2,1)S(1)}, u32[]{:S(2)}, u32[]{:S(2)}) collective-permute-start(bf16[4,4,16,192]{3,2,1,0:T(8,128)(2,1)} %get-tuple-element.28.grad), channel_id=1, source_target_pairs={{0,64},{64,128},{128,192},{192,256},{256,320},{320,384},{384,448},... | collective-permute-start | bytes 294920 | tf_op jit(solution)/shard_map/ppermute | solution.py:355
  24.8 6.8 %collective-permute-start.2 = (bf16[1,4,16,192]{3,2,1,0:T(8,128)(2,1)}, bf16[1,4,16,192]{3,2,1,0:T(8,128)(2,1)S(1)}, u32[]{:S(2)}, u32[]{:S(2)}) collective-permute-start(bf16[1,4,16,192]{3,2,1,0:T(8,128)(2,1)} %get-tuple-element.30), channel_id=1, source_target_pairs={{0,1},{1,2},{2,3},{3,4},{4,5},{5,6},{6,7},{7,8},{8,9},{9,10},{10,1... | collective-permute-start | bytes 73736 | tf_op jit(solution)/shard_map/ppermute | solution.py:355
  29.6 5.4 %collective-permute-start.3 = (bf16[1,4,16,192]{3,2,1,0:T(8,128)(2,1)}, bf16[1,4,16,192]{3,2,1,0:T(8,128)(2,1)S(1)}, u32[]{:S(2)}, u32[]{:S(2)}) collective-permute-start(bf16[1,4,16,192]{3,2,1,0:T(8,128)(2,1)} %get-tuple-element.31), channel_id=1, source_target_pairs={{1,0},{2,1},{3,2},{4,3},{5,4},{6,5},{7,6},{8,7},{9,8},{10,9},{11,1... | collective-permute-start | bytes 73736 | tf_op jit(solution)/shard_map/ppermute | solution.py:355
  36.2 19.5 %all-to-all-start.1 = ((bf16[8,32,16,128]{3,2,1,0:T(8,128)(2,1)}), bf16[8,32,16,128]{3,2,1,0:T(8,128)(2,1)S(1)}, u32[]{:S(2)}, u32[]{:S(2)}) async-start(bf16[8,32,16,128]{3,2,1,0:T(8,128)(2,1)} %shard_map.114), calls=%async_computation.1 | async-start | bytes 2097152 | tf_op jit(solution)/shard_map/all_to_all | solution.py:329
  47.4 1.2 copy-start.6
  48.6 4.5 %collective-permute-start.4 = (bf16[8,24,2592]{2,1,0:T(8,128)(2,1)S(1)}, bf16[8,24,2592]{2,1,0:T(8,128)(2,1)S(1)}, u32[]{:S(2)}, u32[]{:S(2)}) collective-permute-start(bf16[8,24,2592]{2,1,0:T(8,128)(2,1)S(1)} %get-tuple-element.38), channel_id=1, source_target_pairs={{0,1},{1,0},{2,3},{3,2},{4,5},{5,4},{6,7},{7,6},{8,9},{9,8},{10,11... | collective-permute-start | bytes 2985992 | tf_op jit(solution)/shard_map/ppermute | solution.py:358
  55.8 4.5 %collective-permute-start.5 = (bf16[8,32,16,128]{3,2,1,0:T(8,128)(2,1)S(1)}, bf16[8,32,16,128]{3,2,1,0:T(8,128)(2,1)S(1)}, u32[]{:S(2)}, u32[]{:S(2)}) collective-permute-start(bf16[8,32,16,128]{3,2,1,0:T(8,128)(2,1)S(1)} %all-to-all-done.1.mine), channel_id=1, source_target_pairs={{0,1},{1,0},{2,3},{3,2},{4,5},{5,4},{6,7},{7,6},{8,9},{9,8},{10,11... | collective-permute-start | bytes 3145736 | tf_op jit(solution)/shard_map/ppermute | solution.py:358
  60.3 1.0 copy-start.3
  61.3 1.5 copy-start.7
  66.3 3.3 %collective-permute-start.6 = (bf16[576,128]{1,0:T(8,128)(2,1)S(1)}, bf16[576,128]{1,0:T(8,128)(2,1)S(1)}, u32[]{:S(2)}, u32[]{:S(2)}) collective-permute-start(bf16[576,128]{1,0:T(8,128)(2,1)S(1)} %get-tuple-element.42), channel_id=1, source_target_pairs={{0,1},{1,0},{2,3},{3,2},{4,5},{5,4},{6,7},{7,6},{8,9},{9,8},{10,11... | collective-permute-start | bytes 442376 | tf_op jit(solution)/shard_map/ppermute | solution.py:358
  70.3 34.1 %all-to-all-start.2 = ((bf16[32,24,128]{2,1,0:T(8,128)(2,1)}), bf16[32,24,128]{2,1,0:T(8,128)(2,1)S(1)}, u32[]{:S(2)}, u32[]{:S(2)}) async-start(bf16[32,24,128]{2,1,0:T(8,128)(2,1)} %shard_map.116), calls=%async_computation.2 | async-start | bytes 393216 | tf_op jit(solution)/shard_map/all_to_all | solution.py:329
  82.9 10.5 %collective-permute-start.7 = (bf16[2,24,2592]{2,1,0:T(8,128)(2,1)S(1)}, bf16[2,24,2592]{2,1,0:T(8,128)(2,1)S(1)}, u32[]{:S(2)}, u32[]{:S(2)}) collective-permute-start(bf16[2,24,2592]{2,1,0:T(8,128)(2,1)S(1)} %get-tuple-element.46), channel_id=1, source_target_pairs={{0,64},{64,128},{128,192},{192,0},{1,65},{65,129},{129,193},{193,1... | collective-permute-start | bytes 746504 | tf_op jit(solution)/shard_map/ppermute | solution.py:398
  85.4 13.1 %collective-permute-start.8 = (bf16[2,24,2592]{2,1,0:T(8,128)(2,1)S(1)}, bf16[2,24,2592]{2,1,0:T(8,128)(2,1)S(1)}, u32[]{:S(2)}, u32[]{:S(2)}) collective-permute-start(bf16[2,24,2592]{2,1,0:T(8,128)(2,1)S(1)} %get-tuple-element.47), channel_id=1, source_target_pairs={{0,128},{64,192},{128,0},{192,64},{1,129},{65,193},{129,1},{193,65... | collective-permute-start | bytes 746504 | tf_op jit(solution)/shard_map/ppermute | solution.py:398
  89.2 12.0 %collective-permute-start.9 = (bf16[2,24,2592]{2,1,0:T(8,128)(2,1)S(1)}, bf16[2,24,2592]{2,1,0:T(8,128)(2,1)S(1)}, u32[]{:S(2)}, u32[]{:S(2)}) collective-permute-start(bf16[2,24,2592]{2,1,0:T(8,128)(2,1)S(1)} %get-tuple-element.48), channel_id=1, source_target_pairs={{0,192},{64,0},{128,64},{192,128},{1,193},{65,1},{129,65},{193,129... | collective-permute-start | bytes 746504 | tf_op jit(solution)/shard_map/ppermute | solution.py:398
  101.3 8.5 %collective-permute-start.10 = (bf16[24,2592]{1,0:T(8,128)(2,1)S(1)}, bf16[24,2592]{1,0:T(8,128)(2,1)S(1)}, u32[]{:S(2)}, u32[]{:S(2)}) collective-permute-start(bf16[24,2592]{1,0:T(8,128)(2,1)S(1)} %get-tuple-element.50), channel_id=1, source_target_pairs={{0,256},{256,0},{1,257},{257,1},{2,258},{258,2},{3,259},{259,3},{4... | collective-permute-start | bytes 373256 | tf_op jit(solution)/shard_map/ppermute | solution.py:401
  105.1 9.8 %all-to-all-start.3 = ((bf16[8,24,128]{2,1,0:T(8,128)(2,1)}), bf16[8,24,128]{2,1,0:T(8,128)(2,1)S(1)}, u32[]{:S(2)}, u32[]{:S(2)}) async-start(bf16[8,24,128]{2,1,0:T(8,128)(2,1)} %shard_map.117), calls=%async_computation.3 | async-start | bytes 98304 | tf_op jit(solution)/shard_map/all_to_all | solution.py:329

commit v7 on v6

--- a/solution.py
+++ b/solution.py
@@ -20,6 +20,7 @@
 FRAME = 80
 HALF = 32 * ROWS
 COLS = C // SLABS
+WIDE = 2688
 
 VMEM = pl.BlockSpec(memory_space=pltpu.VMEM)
 HBM = pl.BlockSpec(memory_space=pltpu.HBM)
@@ -131,20 +132,19 @@
 
 def conv_kernel(
     counts_in, near_in, fine_in, weight_in, grad, slab_low, slab_high, dev_low, dev_high,
-    keep, send, taps, counts, near, fine, weight, sems, bricks, block, total,
+    keep_out, send_out, taps_out, counts, near, fine, weight, sems, bricks, block, total, taps,
+    keep, send,
 ):
     copies = fetch(
-        sems, (counts_in, counts), (near_in, near), (fine_in, fine), (weight_in, weight)
+        sems, (near_in, near), (grad, bricks.at[0:4]), (slab_low, bricks.at[4:8]),
+        (slab_high, bricks.at[8:12]), (dev_low, bricks.at[12:13]), (dev_high, bricks.at[13:14]),
+        (counts_in, counts), (fine_in, fine), (weight_in, weight),
     )
     place = my_place()
-    bricks[0:4] = grad[...]
-    bricks[4:8] = slab_low[...]
-    bricks[8:12] = slab_high[...]
-    bricks[12:13] = dev_low[...]
-    bricks[13:14] = dev_high[...]
     bricks[14:15] = jnp.zeros((1, 4, 16, C), BF16)
     window = window_matrix()
-    copies[1].wait()
+    for copy in copies[:6]:
+        copy.wait()
     for b in range(B):
         slots = []
         for k in range(27):
@@ -166,7 +166,9 @@
             for s in range(9):
                 row = ((s * 6 + plane) * B + b) * 16
                 taps[row : row + 16] = moved[s * 16 : (s + 1) * 16]
-    for copy in (copies[0], copies[2], copies[3]):
+    leave = [pltpu.make_async_copy(taps, taps_out, sems.at[9])]
+    leave[0].start()
+    for copy in copies[6:]:
         copy.wait()
     count = counts[place]
     merged = lax.dot_general(
@@ -187,35 +189,27 @@
             total[owner % 2, :, to : to + stop - at] = term[:, at - tap * C : stop - tap * C]
             at = stop
     core = jnp.bitwise_and(place, 1)
-    for out, half in ((keep, core), (send, 1 - core)):
+    for i, (held, out, half) in enumerate(((send, send_out, 1 - core), (keep, keep_out, core))):
         for slab in range(SLABS):
-            out[slab] = total[half, slab * COLS : (slab + 1) * COLS].astype(BF16)
-
-
-def split_kernel(keep, received, *outs):
-    x = lax.axis_index("x")
-    for dx, out in enumerate(outs):
-        for zl in range(2):
-            slab = zl * 4 + jnp.bitwise_and(x + dx, 3)
-            out[zl] = (keep[slab].astype(F32) + received[slab].astype(F32)).astype(BF16)
-
-
-def halve_kernel(a, b, c, d, keep, send):
-    zl = lax.axis_index("zl")
-    for out, half in ((keep, zl), (send, 1 - zl)):
-        total = a[half].astype(F32) + b[half].astype(F32) + c[half].astype(F32)
-        out[...] = (total + d[half].astype(F32)).astype(BF16)
+            held[slab] = total[half, slab * COLS : (slab + 1) * COLS].astype(BF16)
+        leave.append(pltpu.make_async_copy(held, out, sems.at[10 + i]))
+        leave[-1].start()
+    for copy in leave:
+        copy.wait()
 
 
 def back_kernel(
-    counts_in, fine_in, weight_in, taps, mine, other, fine_grad, keep, send,
-    counts, fine, weight, sems, both, whole, term,
+    counts_in, fine_in, weight_in, taps_in, mine, other, fine_grad, keep, send,
+    counts, fine, weight, taps, sems, both, whole, term,
 ):
-    copies = fetch(sems, (counts_in, counts), (fine_in, fine), (weight_in, weight))
     place = my_place()
     core = jnp.bitwise_and(place, 1)
-    both[core] = mine[...]
-    both[1 - core] = other[...]
+    copies = fetch(
+        sems, (mine, both.at[core]), (other, both.at[1 - core]), (taps_in, taps),
+        (fine_in, fine), (weight_in, weight), (counts_in, counts),
+    )
+    for copy in copies[:2]:
+        copy.wait()
     row = iota(16, 128, 0)
     held = None
     for owner in range(DEVS):
@@ -243,13 +237,13 @@
             whole[first + 80 : first + 96, :128] = ends[0].astype(BF16)
             whole[first + 80 : first + 96, 128:] = ends[1].astype(BF16)
         held = ends
+    for copy in copies[2:]:
+        copy.wait()
     back = jnp.zeros((256, C), F32)
     for tap in range(27):
         row = tap_rows(tap)
         back = back + dot(taps[row : row + 256], whole[tap * C : (tap + 1) * C])
     brick_of = lax.broadcasted_iota(jnp.int32, (256, C), 0) // 16 % B
-    for copy in copies:
-        copy.wait()
     count = counts[place]
     back = jnp.where(brick_of < count, back, 0.0).astype(BF16)
     back = dot(row_order(True), back)
@@ -270,24 +264,26 @@
         out[i] = jnp.zeros((24, 128), BF16)
 
 
-def spread_kernel(parts, out):
+def spread_kernel(parts, keep, received, out):
+    merge = parts[0].astype(F32)
+    for i in range(1, 32):
+        merge = merge + parts[i].astype(F32)
+    for i in range(SLABS):
+        out[i, :, :HALF] = (keep[i].astype(F32) + received[i].astype(F32)).astype(BF16)
+        out[i, :, HALF:WIDE] = jnp.zeros((COLS, WIDE - HALF), BF16)
+        out[i, :, WIDE:] = merge.astype(BF16)
+
+
+def both_kernel(parts, out):
     total = parts[0].astype(F32)
-    for i in range(1, parts.shape[0]):
+    for i in range(1, SLABS):
         total = total + parts[i].astype(F32)
-    for i in range(out.shape[0]):
-        out[i] = total.astype(BF16)
-
-
-def both_kernel(parts, keep, received, out):
-    merge = parts[0].astype(F32)
-    for i in range(1, SLABS):
-        merge = merge + parts[i].astype(F32)
-    conv = keep[...].astype(F32) + received[...].astype(F32)
+    merge = total[:, WIDE:].astype(BF16)
     pad = jnp.zeros((COLS, 128 - ROWS), BF16)
     for i in range(32):
-        piece = conv[:, i * ROWS : (i + 1) * ROWS].astype(BF16)
+        piece = total[:, i * ROWS : (i + 1) * ROWS].astype(BF16)
         out[i, 0] = jnp.concatenate([piece, pad], axis=1)
-        out[i, 1] = merge.astype(BF16)
+        out[i, 1] = merge
 
 
 def part_kernel(parts, conv_grad, merge):
@@ -359,13 +355,12 @@
 
     slab_low = shifted(grad, SLAB, SLABS, 1)
     slab_high = shifted(grad, SLAB, SLABS, -1)
+    frames = swap(frames, ("zh", "y"))
+    frames, slab_low, slab_high, first, last = lax.optimization_barrier(
+        (frames, slab_low, slab_high, first, last)
+    )
     dev_low = shifted(last, DEV, DEVS, 1)
     dev_high = shifted(first, DEV, DEVS, -1)
-
-    frames = swap(frames, ("zh", "y"))
-    frames, slab_low, slab_high, dev_low, dev_high = lax.optimization_barrier(
-        (frames, slab_low, slab_high, dev_low, dev_high)
-    )
     frames = call(repeat_kernel, shape(SLABS, 32, 16, 128), [VMEM])(frames)
     frames = swap(frames, SLAB)
 
@@ -375,55 +370,58 @@
     keep, send, taps = call(
         conv_kernel,
         (shape(SLABS, COLS, HALF), shape(SLABS, COLS, HALF), shape(3456, C)),
-        [HBM] * 4 + [VMEM] * 5,
+        [HBM] * 9,
         [
             counts_scratch,
             pltpu.SMEM((B, 27), jnp.int32),
             fine_scratch,
             weight_scratch,
-            pltpu.SemaphoreType.DMA((4,)),
+            pltpu.SemaphoreType.DMA((12,)),
             pltpu.VMEM((15, 4, 16, C), BF16),
             pltpu.VMEM((6, 144, C), BF16),
             pltpu.VMEM((2, C, HALF), F32),
+            pltpu.VMEM((3456, C), BF16),
+            pltpu.VMEM((SLABS, COLS, HALF), BF16),
+            pltpu.VMEM((SLABS, COLS, HALF), BF16),
         ],
         flops=6 * 10**9,
-        vmem=20,
+        out_spec=(HBM, HBM, HBM),
+        vmem=60,
     )(
         counts, neighbours, fine_input, merge_weight, grad, slab_low, slab_high, dev_low, dev_high
     )
 
-    frames, received = lax.optimization_barrier((frames, flipped(send)))
-    conv = call(split_kernel, (shape(2, COLS, HALF),) * 4, [VMEM] * 2)(keep, received)
-    conv = [conv[0]] + [
-        lax.ppermute(conv[dx], "x", [(i, (i + dx) % 4) for i in range(4)]) for dx in (1, 2, 3)
-    ]
-    keep, send = call(halve_kernel, (shape(COLS, HALF),) * 2, [VMEM] * 4)(*conv)
-    conv = (keep, lax.ppermute(send, "zl", [(0, 1), (1, 0)]))
+    frames, taps = lax.optimization_barrier((frames, taps))
+    conv_keep, conv_send = keep, send
+
     other = flipped(frames)
     fine_grad, keep, send = call(
         back_kernel,
         (shape(256, 768), shape(576, 128), shape(576, 128)),
-        [HBM] * 3 + [VMEM] * 3,
+        [HBM] * 6,
         [
             counts_scratch,
             fine_scratch,
             weight_scratch,
-            pltpu.SemaphoreType.DMA((3,)),
+            pltpu.VMEM((3456, C), BF16),
+            pltpu.SemaphoreType.DMA((6,)),
             pltpu.VMEM((2, SLABS, 32, 16, 128), BF16),
             pltpu.VMEM((27 * C, C), BF16),
             pltpu.VMEM((2, 576, 128), BF16),
         ],
         flops=4 * 10**9,
-        vmem=20,
+        vmem=60,
     )(counts, fine_input, merge_weight, taps, frames, other)
 
     term = call(join_kernel, shape(32, 24, 128), [VMEM] * 2)(
         keep.reshape(24, 24, 128), flipped(send).reshape(24, 24, 128)
     )
     term = swap(term, ("zh", "y"))
-    term = call(spread_kernel, shape(SLABS, 24, 128), [VMEM])(term)
+    term = call(spread_kernel, shape(SLABS, COLS, WIDE + 128), [VMEM] * 3)(
+        term, conv_keep, flipped(conv_send)
+    )
     term = swap(term, SLAB)
-    joined = call(both_kernel, shape(32, 2, 24, 128), [VMEM] * 3)(term, *conv)
+    joined = call(both_kernel, shape(32, 2, 24, 128), [VMEM])(term)
     joined = swap(joined, ("zh", "y"))
     conv_grad, term = call(
         part_kernel, (shape(ROWS, COLS, dtype=F32), shape(32, 24, 128)), [VMEM]

time: 149 us -> 141 us (0.946)
  starting transfers between devices: 70.2 us -> 51.4 us
  blocking collectives: 31.1 us -> 45 us
  waiting for transfers between devices: 26.3 us -> 23.5 us
  Pallas kernels: 15 us -> 17.6 us
  local copies, waits for them, and re-layouts: 4.37 us -> 2.21 us
    all_to_all x1 -> x2, blocking collectives: 24.5 us -> 38.4 us  [swap(): return lax.all_to_all(x, axes, 0, 0, tiled=True)]
    ppermute x4 -> x0, starting transfers between devices: 12.4 us -> none  [the longest x3 9.32 us: local(): lax.ppermute(conv[dx], 'x', [(i, (i + dx) % 4) for i in range(4)])]
    ppermute x4 -> x0, waiting for transfers between devices: 8.91 us -> none  [the longest x3 8.9 us: local(): lax.ppermute(conv[dx], 'x', [(i, (i + dx) % 4) for i in range(4)])]
    all_to_all x4 -> x3, waiting for transfers between devices: 7.8 us -> 15.9 us  [swap(): return lax.all_to_all(x, axes, 0, 0, tiled=True)]
    all_to_all x4 -> x3, starting transfers between devices: 39.6 us -> 32.6 us  [swap(): return lax.all_to_all(x, axes, 0, 0, tiled=True)]
    ppermute x3, waiting for transfers between devices: 6.13 us -> 1.78 us  [flipped(): return lax.ppermute(x, 'c', [(0, 1), (1, 0)])]
    ppermute x4, waiting for transfers between devices: 3.51 us -> 5.82 us  [shifted(): return lax.ppermute(x, axes, pairs)]
    unnamed x17 -> x19, local copies, waits for them, and re-layouts: 4.37 us -> 2.21 us
  transfers between devices with their start and end apart: 15 -> 10, of which waited for: 9 -> 7; matrix products, arithmetic and copies ran while one was open for 0% -> 0% of each run, Pallas kernels for 4% -> 9%
where the time goes in v7:
time: 141 us; the launch traced here: 140 us
  starting transfers between devices  51.4 us (36%)
  blocking collectives  45 us (32%)
  waiting for transfers between devices  23.5 us (17%)
  Pallas kernels  17.6 us (12%)
  local copies, waits for them, and re-layouts  2.21 us (2%)
    all_to_all x2, blocking collectives, swap(): return lax.all_to_all(x, axes, 0, 0, tiled=True)  38.4 us
    all_to_all x3, starting transfers between devices, swap(): return lax.all_to_all(x, axes, 0, 0, tiled=True)  32.6 us
    all_to_all x3, waiting for transfers between devices, swap(): return lax.all_to_all(x, axes, 0, 0, tiled=True)  15.9 us
    ppermute x4, starting transfers between devices, shifted(): return lax.ppermute(x, axes, pairs)  12.4 us
    pallas_call x1, Pallas kernels, local(): call(conv_kernel, (shape(SLABS, COLS, HALF), shape(SLABS, COLS, HALF), sh...  7.03 us
    all_gather x1, blocking collectives, local(): term = lax.all_gather(term, 'c', axis=0, tiled=False)  6.58 us
    ppermute x3, starting transfers between devices, flipped(): return lax.ppermute(x, 'c', [(0, 1), (1, 0)])  6.36 us
    ppermute x4, waiting for transfers between devices, shifted(): return lax.ppermute(x, axes, pairs)  5.82 us
  transfers between devices with their start and end apart: 10, of which 7 were waited for; matrix products, arithmetic and copies ran while one was open for 0% of the time, Pallas kernels for 9%

profile of v7, /device:TPU:1, one launch (start us, length us, event | category | flops | bytes accessed | tf_op | source)
XLA Modules:
  0.0 140.4 jit_solution(7787373613517682069)
XLA Ops:
  0.6 2.2 %shard_map.112 = (bf16[4,4,16,192]{3,2,1,0:T(8,128)(2,1)}, bf16[1,4,16,192]{3,2,1,0:T(8,128)(2,1)}, bf16[1,4,16,192]{3,2,1,0:T(8,128)(2,1)}, bf16[32,16,128]{2,1,0:T(8,128)(2,1)}) custom-call(s32[512]{0:T(512)} %counts_in.5, bf16[4,16,768]{2,1,0:T(8,128)(2,1)} %pre_in.1, bf16[4,16,768]{2,1,0:T(8,128)(2,1)} %cot_in.1, f32[1,192]{1,0:T(1,128)} %bitcast.11, ...), custom_call_target="tpu_custom_call" | custom-call | tf_op jit(solution)/shard_map/pallas_call | solution.py:332
  2.8 16.5 %all-to-all-start = ((bf16[32,16,128]{2,1,0:T(8,128)(2,1)}), bf16[32,16,128]{2,1,0:T(8,128)(2,1)S(1)}, u32[]{:S(2)}, u32[]{:S(2)}) async-start(bf16[32,16,128]{2,1,0:T(8,128)(2,1)} %get-tuple-element.22), calls=%async_computation | async-start | bytes 262144 | tf_op jit(solution)/shard_map/all_to_all | solution.py:325
  19.3 1.3 collective-permute-start.1
  20.6 4.0 %collective-permute-start = (bf16[4,4,16,192]{3,2,1,0:T(8,128)(2,1)}, bf16[4,4,16,192]{3,2,1,0:T(8,128)(2,1)S(1)}, u32[]{:S(2)}, u32[]{:S(2)}) collective-permute-start(bf16[4,4,16,192]{3,2,1,0:T(8,128)(2,1)} %get-tuple-element.23.grad), channel_id=1, source_target_pairs={{0,64},{64,128},{128,192},{192,256},{256,320},{320,384},{384,448},... | collective-permute-start | bytes 294920 | tf_op jit(solution)/shard_map/ppermute | solution.py:351
  24.6 0.9 collective-permute-done.1.slab_high
  25.5 1.3 collective-permute-done.slab_low
  26.9 4.0 %all-to-all-done.block = bf16[32,16,128]{2,1,0:T(8,128)(2,1)S(1)} async-done(((bf16[32,16,128]{2,1,0:T(8,128)(2,1)}), bf16[32,16,128]{2,1,0:T(8,128)(2,1)S(1)}, u32[]{:S(2)}, u32[]{:S(2)}) %all-to-all-start) | async-done | bytes 131104 | tf_op jit(solution)/shard_map/all_to_all | solution.py:325
  30.9 1.1 shard_map.113
  32.1 5.0 %all-to-all-start.1 = ((bf16[8,32,16,128]{3,2,1,0:T(8,128)(2,1)}), bf16[8,32,16,128]{3,2,1,0:T(8,128)(2,1)S(1)}, u32[]{:S(2)}, u32[]{:S(2)}) async-start(bf16[8,32,16,128]{3,2,1,0:T(8,128)(2,1)} %shard_map.113), calls=%async_computation.1 | async-start | bytes 2097152 | tf_op jit(solution)/shard_map/all_to_all | solution.py:325
  37.1 5.2 %collective-permute-start.2 = (bf16[1,4,16,192]{3,2,1,0:T(8,128)(2,1)S(1)}, bf16[1,4,16,192]{3,2,1,0:T(8,128)(2,1)S(1)}, u32[]{:S(2)}, u32[]{:S(2)}) collective-permute-start(bf16[1,4,16,192]{3,2,1,0:T(8,128)(2,1)S(1)} %copy-done.6), channel_id=1, source_target_pairs={{0,1},{1,2},{2,3},{3,4},{4,5},{5,6},{6,7},{7,8},{8,9},{9,10},{10,1... | collective-permute-start | bytes 73736 | tf_op jit(solution)/shard_map/ppermute | solution.py:351
  42.3 1.9 %collective-permute-start.3 = (bf16[1,4,16,192]{3,2,1,0:T(8,128)(2,1)S(1)}, bf16[1,4,16,192]{3,2,1,0:T(8,128)(2,1)S(1)}, u32[]{:S(2)}, u32[]{:S(2)}) collective-permute-start(bf16[1,4,16,192]{3,2,1,0:T(8,128)(2,1)S(1)} %copy-done.5), channel_id=1, source_target_pairs={{1,0},{2,1},{3,2},{4,3},{5,4},{6,5},{7,6},{8,7},{9,8},{10,9},{11,1... | collective-permute-start | bytes 73736 | tf_op jit(solution)/shard_map/ppermute | solution.py:351
  44.2 3.6 %collective-permute-done.3.dev_high = bf16[1,4,16,192]{3,2,1,0:T(8,128)(2,1)S(1)} collective-permute-done((bf16[1,4,16,192]{3,2,1,0:T(8,128)(2,1)S(1)}, bf16[1,4,16,192]{3,2,1,0:T(8,128)(2,1)S(1)}, u32[]{:S(2)}, u32[]{:S(2)}) %collective-permute-start.3) | collective-permute-done | bytes 24608 | tf_op jit(solution)/shard_map/ppermute | solution.py:351
  48.4 7.0 %shard_map.114 = (bf16[8,24,2592]{2,1,0:T(8,128)(2,1)}, bf16[8,24,2592]{2,1,0:T(8,128)(2,1)}, bf16[3456,192]{1,0:T(8,128)(2,1)}) custom-call(s32[512]{0:T(512)} %counts_in.5, s32[4,27]{1,0:T(4,128)} %near_in.1, bf16[256,768]{1,0:T(8,128)(2,1)} %fine_in.3, bf16[192,768]{1,0:T(8,128)(2,1)} %bitcast.13, bf16[4,4,16,192]{3,2,1,0:T(8,128)(2,1)} %get-tuple-element.23.grad, ...), custom_call_target="tpu_custom_call" | custom-call | flops 6000000000 | tf_op jit(solution)/shard_map/pallas_call | solution.py:370
  55.5 1.9 %collective-permute-start.4 = (bf16[8,32,16,128]{3,2,1,0:T(8,128)(2,1)S(1)}, bf16[8,32,16,128]{3,2,1,0:T(8,128)(2,1)}, u32[]{:S(2)}, u32[]{:S(2)}) collective-permute-start(bf16[8,32,16,128]{3,2,1,0:T(8,128)(2,1)S(1)} %all-to-all-done.1.mine), channel_id=1, source_target_pairs={{0,1},{1,0},{2,3},{3,2},{4,5},{5,4},{6,7},{7,6},{8,9},{9,8},{10,11... | collective-permute-start | bytes 3145736 | tf_op jit(solution)/shard_map/ppermute | solution.py:354
  57.4 2.4 %collective-permute-start.6 = (bf16[8,24,2592]{2,1,0:T(8,128)(2,1)}, bf16[8,24,2592]{2,1,0:T(8,128)(2,1)S(1)}, u32[]{:S(2)}, u32[]{:S(2)}) collective-permute-start(bf16[8,24,2592]{2,1,0:T(8,128)(2,1)} %get-tuple-element.38), channel_id=1, source_target_pairs={{0,1},{1,0},{2,3},{3,2},{4,5},{5,4},{6,7},{7,6},{8,9},{9,8},{10,11... | collective-permute-start | bytes 2985992 | tf_op jit(solution)/shard_map/ppermute | solution.py:354
  60.2 5.0 %shard_map.115 = (bf16[256,768]{1,0:T(8,128)(2,1)}, bf16[576,128]{1,0:T(8,128)(2,1)}, bf16[576,128]{1,0:T(8,128)(2,1)}) custom-call(s32[512]{0:T(512)} %counts_in.5, bf16[256,768]{1,0:T(8,128)(2,1)} %fine_in.3, bf16[192,768]{1,0:T(8,128)(2,1)} %bitcast.14, bf16[3456,192]{1,0:T(8,128)(2,1)} %get-tuple-element.32.taps_in, bf16[8,32,16,128]{3,2,1,0:T(8,128)(2,1)} %copy-done.2, ...), custom_call_target="tpu_custom_call" | custom-call | flops 4000000000 | tf_op jit(solution)/shard_map/pallas_call | solution.py:398
  65.2 2.0 %collective-permute-start.5 = (bf16[576,128]{1,0:T(8,128)(2,1)}, bf16[576,128]{1,0:T(8,128)(2,1)S(1)}, u32[]{:S(2)}, u32[]{:S(2)}) collective-permute-start(bf16[576,128]{1,0:T(8,128)(2,1)} %get-tuple-element.36), channel_id=1, source_target_pairs={{0,1},{1,0},{2,3},{3,2},{4,5},{5,4},{6,7},{7,6},{8,9},{9,8},{10,11... | collective-permute-start | bytes 442376 | tf_op jit(solution)/shard_map/ppermute | solution.py:354
  67.3 1.4 %collective-permute-done.5 = bf16[576,128]{1,0:T(8,128)(2,1)S(1)} collective-permute-done((bf16[576,128]{1,0:T(8,128)(2,1)}, bf16[576,128]{1,0:T(8,128)(2,1)S(1)}, u32[]{:S(2)}, u32[]{:S(2)}) %collective-permute-start.5) | collective-permute-done | bytes 147488 | tf_op jit(solution)/shard_map/ppermute | solution.py:354
  68.7 0.9 copy-done.1
  70.3 11.1 %all-to-all-start.2 = ((bf16[32,24,128]{2,1,0:T(8,128)(2,1)}), bf16[32,24,128]{2,1,0:T(8,128)(2,1)S(1)}, u32[]{:S(2)}, u32[]{:S(2)}) async-start(bf16[32,24,128]{2,1,0:T(8,128)(2,1)} %shard_map.116), calls=%async_computation.2 | async-start | bytes 393216 | tf_op jit(solution)/shard_map/all_to_all | solution.py:325
  81.4 11.8 %all-to-all-done.2.parts = bf16[32,24,128]{2,1,0:T(8,128)(2,1)S(1)} async-done(((bf16[32,24,128]{2,1,0:T(8,128)(2,1)}), bf16[32,24,128]{2,1,0:T(8,128)(2,1)S(1)}, u32[]{:S(2)}, u32[]{:S(2)}) %all-to-all-start.2) | async-done | bytes 196640 | tf_op jit(solution)/shard_map/all_to_all | solution.py:325
  93.5 18.1 %all_to_all.25.parts = bf16[8,24,2816]{2,1,0:T(8,128)(2,1)S(1)} all-to-all(bf16[8,24,2816]{2,1,0:T(8,128)(2,1)S(1)} %shard_map.117), channel_id=1, replica_groups=mesh['zl'=2,'x'=4,'zh'=4,'y'=8,'c'=2] {'zl','x'}, dimensions={0} | all-to-all | bytes 2162688 | tf_op jit(solution)/shard_map/all_to_all | solution.py:325
  111.9 20.3 %all_to_all.26.parts = bf16[32,2,24,128]{3,2,1,0:T(8,128)(2,1)S(1)} all-to-all(bf16[32,2,24,128]{3,2,1,0:T(8,128)(2,1)S(1)} %shard_map.118), channel_id=1, replica_groups=mesh['zl'=2,'x'=4,'zh'=4,'y'=8,'c'=2] {'zh','y'}, dimensions={0} | all-to-all | bytes 786432 | tf_op jit(solution)/shard_map/all_to_all | solution.py:325
  133.0 6.6 %all-gather = bf16[64,24,128]{2,1,0:T(8,128)(2,1)S(1)} all-gather(bf16[32,24,128]{2,1,0:T(8,128)(2,1)S(1)} %get-tuple-element.39), channel_id=2, replica_groups=mesh['zl'=2,'x'=4,'zh'=4,'y'=8,'c'=2] {'c'}, dimensions={0}, use_global_device_ids=true | all-gather | bytes 589824 | tf_op jit(solution)/shard_map/all_gather | solution.py:429
  (27 shorter events, 3.9 us)
Async XLA Ops:
  2.8 28.1 %all-to-all-start = ((bf16[32,16,128]{2,1,0:T(8,128)(2,1)}), bf16[32,16,128]{2,1,0:T(8,128)(2,1)S(1)}, u32[]{:S(2)}, u32[]{:S(2)}) async-start(bf16[32,16,128]{2,1,0:T(8,128)(2,1)} %get-tuple-element.22), calls=%async_computation | async-start | bytes 262144 | tf_op jit(solution)/shard_map/all_to_all | solution.py:325
  19.3 6.2 %collective-permute-start.1 = (bf16[4,4,16,192]{3,2,1,0:T(8,128)(2,1)}, bf16[4,4,16,192]{3,2,1,0:T(8,128)(2,1)S(1)}, u32[]{:S(2)}, u32[]{:S(2)}) collective-permute-start(bf16[4,4,16,192]{3,2,1,0:T(8,128)(2,1)} %get-tuple-element.23.grad), channel_id=1, source_target_pairs={{64,0},{128,64},{192,128},{256,192},{320,256},{384,320},{448,384},... | collective-permute-start | bytes 294920 | tf_op jit(solution)/shard_map/ppermute | solution.py:351
  20.6 6.2 %collective-permute-start = (bf16[4,4,16,192]{3,2,1,0:T(8,128)(2,1)}, bf16[4,4,16,192]{3,2,1,0:T(8,128)(2,1)S(1)}, u32[]{:S(2)}, u32[]{:S(2)}) collective-permute-start(bf16[4,4,16,192]{3,2,1,0:T(8,128)(2,1)} %get-tuple-element.23.grad), channel_id=1, source_target_pairs={{0,64},{64,128},{128,192},{192,256},{256,320},{320,384},{384,448},... | collective-permute-start | bytes 294920 | tf_op jit(solution)/shard_map/ppermute | solution.py:351
  25.5 6.5 %copy-start.3 = (bf16[4,4,16,192]{3,2,1,0:T(8,128)(2,1)}, bf16[4,4,16,192]{3,2,1,0:T(8,128)(2,1)S(1)}, u32[]{:S(2)}) copy-start(bf16[4,4,16,192]{3,2,1,0:T(8,128)(2,1)S(1)} %collective-permute-done.1.slab_high) | copy-start | bytes 294916
  26.9 5.2 %copy-start.4 = (bf16[4,4,16,192]{3,2,1,0:T(8,128)(2,1)}, bf16[4,4,16,192]{3,2,1,0:T(8,128)(2,1)S(1)}, u32[]{:S(2)}) copy-start(bf16[4,4,16,192]{3,2,1,0:T(8,128)(2,1)S(1)} %collective-permute-done.slab_low) | copy-start | bytes 294916
  32.0 5.1 %copy-start.6 = (bf16[1,4,16,192]{3,2,1,0:T(8,128)(2,1)S(1)}, bf16[1,4,16,192]{3,2,1,0:T(8,128)(2,1)}, u32[]{:S(2)}) copy-start(bf16[1,4,16,192]{3,2,1,0:T(8,128)(2,1)} %get-tuple-element.29) | copy-start | bytes 73732
  32.0 10.2 %copy-start.5 = (bf16[1,4,16,192]{3,2,1,0:T(8,128)(2,1)S(1)}, bf16[1,4,16,192]{3,2,1,0:T(8,128)(2,1)}, u32[]{:S(2)}) copy-start(bf16[1,4,16,192]{3,2,1,0:T(8,128)(2,1)} %get-tuple-element.30) | copy-start | bytes 73732
  32.1 23.4 %all-to-all-start.1 = ((bf16[8,32,16,128]{3,2,1,0:T(8,128)(2,1)}), bf16[8,32,16,128]{3,2,1,0:T(8,128)(2,1)S(1)}, u32[]{:S(2)}, u32[]{:S(2)}) async-start(bf16[8,32,16,128]{3,2,1,0:T(8,128)(2,1)} %shard_map.113), calls=%async_computation.1 | async-start | bytes 2097152 | tf_op jit(solution)/shard_map/all_to_all | solution.py:325
  37.1 7.1 %collective-permute-start.2 = (bf16[1,4,16,192]{3,2,1,0:T(8,128)(2,1)S(1)}, bf16[1,4,16,192]{3,2,1,0:T(8,128)(2,1)S(1)}, u32[]{:S(2)}, u32[]{:S(2)}) collective-permute-start(bf16[1,4,16,192]{3,2,1,0:T(8,128)(2,1)S(1)} %copy-done.6), channel_id=1, source_target_pairs={{0,1},{1,2},{2,3},{3,4},{4,5},{5,6},{6,7},{7,8},{8,9},{9,10},{10,1... | collective-permute-start | bytes 73736 | tf_op jit(solution)/shard_map/ppermute | solution.py:351
  42.3 5.5 %collective-permute-start.3 = (bf16[1,4,16,192]{3,2,1,0:T(8,128)(2,1)S(1)}, bf16[1,4,16,192]{3,2,1,0:T(8,128)(2,1)S(1)}, u32[]{:S(2)}, u32[]{:S(2)}) collective-permute-start(bf16[1,4,16,192]{3,2,1,0:T(8,128)(2,1)S(1)} %copy-done.5), channel_id=1, source_target_pairs={{1,0},{2,1},{3,2},{4,3},{5,4},{6,5},{7,6},{8,7},{9,8},{10,9},{11,1... | collective-permute-start | bytes 73736 | tf_op jit(solution)/shard_map/ppermute | solution.py:351
  44.2 3.6 %copy-start.7 = (bf16[1,4,16,192]{3,2,1,0:T(8,128)(2,1)}, bf16[1,4,16,192]{3,2,1,0:T(8,128)(2,1)S(1)}, u32[]{:S(2)}) copy-start(bf16[1,4,16,192]{3,2,1,0:T(8,128)(2,1)S(1)} %collective-permute-done.2.dev_low) | copy-start | bytes 73732
  47.8 0.6 copy-start.8
  55.5 4.7 %copy-start.2 = (bf16[8,32,16,128]{3,2,1,0:T(8,128)(2,1)}, bf16[8,32,16,128]{3,2,1,0:T(8,128)(2,1)S(1)}, u32[]{:S(2)}) copy-start(bf16[8,32,16,128]{3,2,1,0:T(8,128)(2,1)S(1)} %all-to-all-done.1.mine) | copy-start | bytes 3145732
  55.5 4.7 %collective-permute-start.4 = (bf16[8,32,16,128]{3,2,1,0:T(8,128)(2,1)S(1)}, bf16[8,32,16,128]{3,2,1,0:T(8,128)(2,1)}, u32[]{:S(2)}, u32[]{:S(2)}) collective-permute-start(bf16[8,32,16,128]{3,2,1,0:T(8,128)(2,1)S(1)} %all-to-all-done.1.mine), channel_id=1, source_target_pairs={{0,1},{1,0},{2,3},{3,2},{4,5},{5,4},{6,7},{7,6},{8,9},{9,8},{10,11... | collective-permute-start | bytes 3145736 | tf_op jit(solution)/shard_map/ppermute | solution.py:354
  57.4 24.0 %collective-permute-start.6 = (bf16[8,24,2592]{2,1,0:T(8,128)(2,1)}, bf16[8,24,2592]{2,1,0:T(8,128)(2,1)S(1)}, u32[]{:S(2)}, u32[]{:S(2)}) collective-permute-start(bf16[8,24,2592]{2,1,0:T(8,128)(2,1)} %get-tuple-element.38), channel_id=1, source_target_pairs={{0,1},{1,0},{2,3},{3,2},{4,5},{5,4},{6,7},{7,6},{8,9},{9,8},{10,11... | collective-permute-start | bytes 2985992 | tf_op jit(solution)/shard_map/ppermute | solution.py:354
  60.2 33.1 %copy-start = (bf16[8,24,2592]{2,1,0:T(8,128)(2,1)S(1)}, bf16[8,24,2592]{2,1,0:T(8,128)(2,1)}, u32[]{:S(2)}) copy-start(bf16[8,24,2592]{2,1,0:T(8,128)(2,1)} %get-tuple-element.37.keep) | copy-start | bytes 2985988
  65.2 3.5 %collective-permute-start.5 = (bf16[576,128]{1,0:T(8,128)(2,1)}, bf16[576,128]{1,0:T(8,128)(2,1)S(1)}, u32[]{:S(2)}, u32[]{:S(2)}) collective-permute-start(bf16[576,128]{1,0:T(8,128)(2,1)} %get-tuple-element.36), channel_id=1, source_target_pairs={{0,1},{1,0},{2,3},{3,2},{4,5},{5,4},{6,7},{7,6},{8,9},{9,8},{10,11... | collective-permute-start | bytes 442376 | tf_op jit(solution)/shard_map/ppermute | solution.py:354
  68.7 0.9 copy-start.1
  70.3 22.9 %all-to-all-start.2 = ((bf16[32,24,128]{2,1,0:T(8,128)(2,1)}), bf16[32,24,128]{2,1,0:T(8,128)(2,1)S(1)}, u32[]{:S(2)}, u32[]{:S(2)}) async-start(bf16[32,24,128]{2,1,0:T(8,128)(2,1)} %shard_map.116), calls=%async_computation.2 | async-start | bytes 393216 | tf_op jit(solution)/shard_map/all_to_all | solution.py:325

commit v8 on v7

--- a/solution.py
+++ b/solution.py
@@ -20,6 +20,7 @@
 FRAME = 80
 HALF = 32 * ROWS
 COLS = C // SLABS
+PIECES = 48
 WIDE = 2688
 
 VMEM = pl.BlockSpec(memory_space=pltpu.VMEM)
@@ -86,7 +87,7 @@
 
 
 def prepare_kernel(
-    counts_in, pre_in, cot_in, gain_in, bias_in, weight_in, grad, first, last, frames,
+    counts_in, pre_in, cot_in, gain_in, bias_in, weight_in, grad, near, far, frames,
     counts, pre, cot, gain, bias, weight, tiles, sems,
 ):
     copies = fetch(
@@ -126,21 +127,24 @@
             uz = u[:, z * C : (z + 1) * C]
             gate = (g * pz + bias[...] > 0) & (b < count)
             grad[b, z] = jnp.where(gate, uz * g, 0.0).astype(BF16)
-    first[0] = grad[0]
-    last[0] = grad[count - 1]
+    core = jnp.bitwise_and(place, 1)
+    near[0] = grad[jnp.where(core == 0, count - 1, 0)]
+    far[0] = grad[jnp.where(core == 0, 0, count - 1)]
 
 
 def conv_kernel(
-    counts_in, near_in, fine_in, weight_in, grad, slab_low, slab_high, dev_low, dev_high,
+    counts_in, near_in, fine_in, weight_in, grad, slab_low, slab_high, dev_near, dev_far,
     keep_out, send_out, taps_out, counts, near, fine, weight, sems, bricks, block, total, taps,
     keep, send,
 ):
+    place = my_place()
+    core = jnp.bitwise_and(place, 1)
     copies = fetch(
         sems, (near_in, near), (grad, bricks.at[0:4]), (slab_low, bricks.at[4:8]),
-        (slab_high, bricks.at[8:12]), (dev_low, bricks.at[12:13]), (dev_high, bricks.at[13:14]),
+        (slab_high, bricks.at[8:12]), (dev_near, bricks.at[pl.ds(13 - core, 1)]),
+        (dev_far, bricks.at[pl.ds(12 + core, 1)]),
         (counts_in, counts), (fine_in, fine), (weight_in, weight),
     )
-    place = my_place()
     bricks[14:15] = jnp.zeros((1, 4, 16, C), BF16)
     window = window_matrix()
     for copy in copies[:6]:
@@ -188,7 +192,6 @@
             to = (owner // 2) * ROWS + at % ROWS
             total[owner % 2, :, to : to + stop - at] = term[:, at - tap * C : stop - tap * C]
             at = stop
-    core = jnp.bitwise_and(place, 1)
     for i, (held, out, half) in enumerate(((send, send_out, 1 - core), (keep, keep_out, core))):
         for slab in range(SLABS):
             held[slab] = total[half, slab * COLS : (slab + 1) * COLS].astype(BF16)
@@ -199,8 +202,8 @@
 
 
 def back_kernel(
-    counts_in, fine_in, weight_in, taps_in, mine, other, fine_grad, keep, send,
-    counts, fine, weight, taps, sems, both, whole, term,
+    counts_in, fine_in, weight_in, taps_in, mine, other, fine_grad, term,
+    counts, fine, weight, taps, sems, both, whole,
 ):
     place = my_place()
     core = jnp.bitwise_and(place, 1)
@@ -249,24 +252,18 @@
     back = dot(row_order(True), back)
     gm = back.astype(BF16)
     fine_grad[...] = dot(gm, weight[...]).astype(BF16)
-    result = dot(jnp.transpose(back).astype(BF16), fine[...]).astype(BF16)
-    for part in range(6):
-        row = part % 3 * C
-        term[part // 3, row : row + C] = result[:, part * 128 : (part + 1) * 128]
-    keep[...] = term[core]
-    send[...] = term[1 - core]
-
-
-def join_kernel(keep, received, out):
-    for i in range(24):
-        out[i] = (keep[i].astype(F32) + received[i].astype(F32)).astype(BF16)
-    for i in range(24, 32):
-        out[i] = jnp.zeros((24, 128), BF16)
+    result = dot(jnp.transpose(back).astype(BF16), fine[...])
+    for i in range(DEVS):
+        if i < PIECES:
+            piece = result[i % 8 * 24 : i % 8 * 24 + 24, i // 8 * 128 : i // 8 * 128 + 128]
+            term[i] = piece.astype(BF16)
+        else:
+            term[i] = jnp.zeros((24, 128), BF16)
 
 
 def spread_kernel(parts, keep, received, out):
     merge = parts[0].astype(F32)
-    for i in range(1, 32):
+    for i in range(1, DEVS):
         merge = merge + parts[i].astype(F32)
     for i in range(SLABS):
         out[i, :, :HALF] = (keep[i].astype(F32) + received[i].astype(F32)).astype(BF16)
@@ -286,23 +283,19 @@
         out[i, 1] = merge
 
 
-def part_kernel(parts, conv_grad, merge):
-    conv = parts[0, 0].astype(F32)
+def last_kernel(parts, merge_out, conv_out, merge, conv, sems):
+    core = jnp.bitwise_and(my_place(), 1)
+    for i in range(PIECES):
+        row, col = i % 8 * 24, i // 8 * 128
+        merge[row : row + 24, col : col + 128] = parts[i % 2, i // 2, 1].astype(F32)
+    copies = fetch(sems, (merge, merge_out))
+    total = parts[core, 0, 0].astype(F32)
     for i in range(1, 32):
-        conv = conv + parts[i, 0].astype(F32)
-    conv_grad[...] = jnp.transpose(conv)[:ROWS]
-    for i in range(32):
-        merge[i] = parts[i, 1]
-
-
-def merge_kernel(parts, out, held, sems):
-    for part in range(6):
-        row = part % 3 * C
-        block = parts[part // 3, row : row + C]
-        held[:, part * 128 : (part + 1) * 128] = block.astype(F32)
-    copy = pltpu.make_async_copy(held, out, sems.at[0])
-    copy.start()
-    copy.wait()
+        total = total + parts[core, i, 0].astype(F32)
+    conv[...] = total[:, :ROWS]
+    copies += fetch(sems.at[1:], (conv, conv_out))
+    for copy in copies:
+        copy.wait()
 
 
 def call(kernel, outs, specs, scratch=(), flops=0, out_spec=None, vmem=20):
@@ -329,7 +322,7 @@
     fine_input, merge_weight, conv_weight, pre_act, norm_gain, norm_bias, cotangent, counts, neighbours
 ):
     counts_scratch = pltpu.SMEM((SLABS * DEVS,), jnp.int32)
-    grad, first, last, frames = call(
+    grad, near, far, frames = call(
         prepare_kernel,
         (shape(B, 4, 16, C), shape(1, 4, 16, C), shape(1, 4, 16, C), shape(32, 16, 128)),
         [HBM] * 6,
@@ -356,11 +349,12 @@
     slab_low = shifted(grad, SLAB, SLABS, 1)
     slab_high = shifted(grad, SLAB, SLABS, -1)
     frames = swap(frames, ("zh", "y"))
-    frames, slab_low, slab_high, first, last = lax.optimization_barrier(
-        (frames, slab_low, slab_high, first, last)
-    )
-    dev_low = shifted(last, DEV, DEVS, 1)
-    dev_high = shifted(first, DEV, DEVS, -1)
+    frames, slab_low, slab_high, near, far = lax.optimization_barrier(
+        (frames, slab_low, slab_high, near, far)
+    )
+    dev_near = flipped(near)
+    ups = [(i, i + 1) for i in range(1, DEVS - 1, 2)]
+    dev_far = lax.ppermute(far, DEV, ups + [(j, i) for i, j in ups])
     frames = call(repeat_kernel, shape(SLABS, 32, 16, 128), [VMEM])(frames)
     frames = swap(frames, SLAB)
 
@@ -388,16 +382,14 @@
         out_spec=(HBM, HBM, HBM),
         vmem=60,
     )(
-        counts, neighbours, fine_input, merge_weight, grad, slab_low, slab_high, dev_low, dev_high
+        counts, neighbours, fine_input, merge_weight, grad, slab_low, slab_high, dev_near, dev_far
     )
 
     frames, taps = lax.optimization_barrier((frames, taps))
-    conv_keep, conv_send = keep, send
-
     other = flipped(frames)
-    fine_grad, keep, send = call(
+    fine_grad, term = call(
         back_kernel,
-        (shape(256, 768), shape(576, 128), shape(576, 128)),
+        (shape(256, 768), shape(DEVS, 24, 128)),
         [HBM] * 6,
         [
             counts_scratch,
@@ -407,34 +399,30 @@
             pltpu.SemaphoreType.DMA((6,)),
             pltpu.VMEM((2, SLABS, 32, 16, 128), BF16),
             pltpu.VMEM((27 * C, C), BF16),
-            pltpu.VMEM((2, 576, 128), BF16),
         ],
         flops=4 * 10**9,
         vmem=60,
     )(counts, fine_input, merge_weight, taps, frames, other)
 
-    term = call(join_kernel, shape(32, 24, 128), [VMEM] * 2)(
-        keep.reshape(24, 24, 128), flipped(send).reshape(24, 24, 128)
-    )
+    term, received = lax.optimization_barrier((term, flipped(send)))
+    term = swap(term, DEV)
+    term = call(spread_kernel, shape(SLABS, COLS, WIDE + 128), [VMEM] * 3)(term, keep, received)
+    term = swap(term, SLAB)
+    term = call(both_kernel, shape(32, 2, 24, 128), [VMEM])(term)
     term = swap(term, ("zh", "y"))
-    term = call(spread_kernel, shape(SLABS, COLS, WIDE + 128), [VMEM] * 3)(
-        term, conv_keep, flipped(conv_send)
-    )
-    term = swap(term, SLAB)
-    joined = call(both_kernel, shape(32, 2, 24, 128), [VMEM])(term)
-    joined = swap(joined, ("zh", "y"))
-    conv_grad, term = call(
-        part_kernel, (shape(ROWS, COLS, dtype=F32), shape(32, 24, 128)), [VMEM]
-    )(joined)
     term = lax.all_gather(term, "c", axis=0, tiled=False)
-    merge_grad = call(
-        merge_kernel,
-        shape(C, 768, dtype=F32),
+    merge_grad, conv_grad = call(
+        last_kernel,
+        (shape(C, 768, dtype=F32), shape(COLS, ROWS, dtype=F32)),
         [VMEM],
-        [pltpu.VMEM((C, 768), F32), pltpu.SemaphoreType.DMA((1,))],
-        out_spec=HBM,
-    )(term.reshape(2, 768, 128)).T
-    return fine_grad, merge_grad, conv_grad
+        [
+            pltpu.VMEM((C, 768), F32),
+            pltpu.VMEM((COLS, ROWS), F32),
+            pltpu.SemaphoreType.DMA((2,)),
+        ],
+        out_spec=(HBM, HBM),
+    )(term)
+    return fine_grad, merge_grad.T, conv_grad.T
 
 
 def solution(mesh):

time: 141 us -> 141 us (level)
  blocking collectives: 45 us -> 74.5 us
  waiting for transfers between devices: 23.5 us -> 9.3 us
  starting transfers between devices: 51.4 us -> 38.3 us
  local copies, waits for them, and re-layouts: 2.21 us -> 0.64 us
    all_to_all x2 -> x3, blocking collectives: 38.4 us -> 67.7 us  [swap(): return lax.all_to_all(x, axes, 0, 0, tiled=True)]
    all_to_all x3 -> x2, waiting for transfers between devices: 15.9 us -> 4.05 us  [swap(): return lax.all_to_all(x, axes, 0, 0, tiled=True)]
    all_to_all x3 -> x2, starting transfers between devices: 32.6 us -> 21.6 us  [swap(): return lax.all_to_all(x, axes, 0, 0, tiled=True)]
    ppermute x4 -> x2, starting transfers between devices: 12.4 us -> 5.28 us  [shifted(): return lax.ppermute(x, axes, pairs)]
    ppermute x4 -> x2, waiting for transfers between devices: 5.82 us -> 2.24 us  [shifted(): return lax.ppermute(x, axes, pairs)]
    ppermute x0 -> x1, starting transfers between devices: none -> 2.83 us  [local(): dev_far = lax.ppermute(far, DEV, ups + [(j, i) for i, j in ups])]
    ppermute x0 -> x1, waiting for transfers between devices: none -> 2.67 us  [local(): dev_far = lax.ppermute(far, DEV, ups + [(j, i) for i, j in ups])]
    ppermute x3, starting transfers between devices: 6.36 us -> 8.59 us  [flipped(): return lax.ppermute(x, 'c', [(0, 1), (1, 0)])]
  transfers between devices with their start and end apart: 10 -> 8, of which waited for: 7 -> 5; matrix products, arithmetic and copies ran while one was open for 0% -> 0% of each run, Pallas kernels for 9% -> 9%
where the time goes in v8:
time: 141 us; the launch traced here: 140 us
  blocking collectives  74.5 us (53%)
  starting transfers between devices  38.3 us (27%)
  Pallas kernels  16.7 us (12%)
  waiting for transfers between devices  9.3 us (7%)
    all_to_all x3, blocking collectives, swap(): return lax.all_to_all(x, axes, 0, 0, tiled=True)  67.7 us
    all_to_all x2, starting transfers between devices, swap(): return lax.all_to_all(x, axes, 0, 0, tiled=True)  21.6 us
    ppermute x3, starting transfers between devices, flipped(): return lax.ppermute(x, 'c', [(0, 1), (1, 0)])  8.59 us
    pallas_call x1, Pallas kernels, local(): call(conv_kernel, (shape(SLABS, COLS, HALF), shape(SLABS, COLS, HALF), sh...  7.04 us
    all_gather x1, blocking collectives, local(): term = lax.all_gather(term, 'c', axis=0, tiled=False)  6.74 us
    ppermute x2, starting transfers between devices, shifted(): return lax.ppermute(x, axes, pairs)  5.28 us
    pallas_call x1, Pallas kernels, local(): call(back_kernel, (shape(256, 768), shape(DEVS, 24, 128)), [HBM] * 6, [co...  5 us
    all_to_all x2, waiting for transfers between devices, swap(): return lax.all_to_all(x, axes, 0, 0, tiled=True)  4.05 us
  transfers between devices with their start and end apart: 8, of which 5 were waited for; matrix products, arithmetic and copies ran while one was open for 0% of the time, Pallas kernels for 9%

profile of v8, /device:TPU:1, one launch (start us, length us, event | category | flops | bytes accessed | tf_op | source)
XLA Modules:
  0.0 140.2 jit_solution(3276221087369660896)
XLA Ops:
  0.6 2.2 %shard_map.112 = (bf16[4,4,16,192]{3,2,1,0:T(8,128)(2,1)}, bf16[1,4,16,192]{3,2,1,0:T(8,128)(2,1)}, bf16[1,4,16,192]{3,2,1,0:T(8,128)(2,1)}, bf16[32,16,128]{2,1,0:T(8,128)(2,1)}) custom-call(s32[512]{0:T(512)} %counts_in.5, bf16[4,16,768]{2,1,0:T(8,128)(2,1)} %pre_in.1, bf16[4,16,768]{2,1,0:T(8,128)(2,1)} %cot_in.1, f32[1,192]{1,0:T(1,128)} %bitcast.7, ...), custom_call_target="tpu_custom_call" | custom-call | tf_op jit(solution)/shard_map/pallas_call | solution.py:325
  2.8 16.5 %all-to-all-start = ((bf16[32,16,128]{2,1,0:T(8,128)(2,1)}), bf16[32,16,128]{2,1,0:T(8,128)(2,1)S(1)}, u32[]{:S(2)}, u32[]{:S(2)}) async-start(bf16[32,16,128]{2,1,0:T(8,128)(2,1)} %get-tuple-element.23), calls=%async_computation | async-start | bytes 262144 | tf_op jit(solution)/shard_map/all_to_all | solution.py:318
  19.3 1.3 collective-permute-start.1
  20.6 4.0 %collective-permute-start = (bf16[4,4,16,192]{3,2,1,0:T(8,128)(2,1)}, bf16[4,4,16,192]{3,2,1,0:T(8,128)(2,1)S(1)}, u32[]{:S(2)}, u32[]{:S(2)}) collective-permute-start(bf16[4,4,16,192]{3,2,1,0:T(8,128)(2,1)} %get-tuple-element.24.grad), channel_id=1, source_target_pairs={{0,64},{64,128},{128,192},{192,256},{256,320},{320,384},{384,448},... | collective-permute-start | bytes 294920 | tf_op jit(solution)/shard_map/ppermute | solution.py:344
  24.6 0.9 collective-permute-done.1.slab_high
  25.5 1.3 collective-permute-done.slab_low
  26.9 4.0 %all-to-all-done.block = bf16[32,16,128]{2,1,0:T(8,128)(2,1)S(1)} async-done(((bf16[32,16,128]{2,1,0:T(8,128)(2,1)}), bf16[32,16,128]{2,1,0:T(8,128)(2,1)S(1)}, u32[]{:S(2)}, u32[]{:S(2)}) %all-to-all-start) | async-done | bytes 131104 | tf_op jit(solution)/shard_map/all_to_all | solution.py:318
  30.9 1.1 shard_map.113
  32.1 5.0 %all-to-all-start.1 = ((bf16[8,32,16,128]{3,2,1,0:T(8,128)(2,1)}), bf16[8,32,16,128]{3,2,1,0:T(8,128)(2,1)S(1)}, u32[]{:S(2)}, u32[]{:S(2)}) async-start(bf16[8,32,16,128]{3,2,1,0:T(8,128)(2,1)} %shard_map.113), calls=%async_computation.1 | async-start | bytes 2097152 | tf_op jit(solution)/shard_map/all_to_all | solution.py:318
  37.1 4.3 %collective-permute-start.2 = (bf16[1,4,16,192]{3,2,1,0:T(8,128)(2,1)S(1)}, bf16[1,4,16,192]{3,2,1,0:T(8,128)(2,1)S(1)}, u32[]{:S(2)}, u32[]{:S(2)}) collective-permute-start(bf16[1,4,16,192]{3,2,1,0:T(8,128)(2,1)S(1)} %copy-done.5), channel_id=1, source_target_pairs={{0,1},{1,0},{2,3},{3,2},{4,5},{5,4},{6,7},{7,6},{8,9},{9,8},{10,11... | collective-permute-start | bytes 73736 | tf_op jit(solution)/shard_map/ppermute | solution.py:347
  41.4 2.8 %collective-permute-start.3 = (bf16[1,4,16,192]{3,2,1,0:T(8,128)(2,1)S(1)}, bf16[1,4,16,192]{3,2,1,0:T(8,128)(2,1)S(1)}, u32[]{:S(2)}, u32[]{:S(2)}) collective-permute-start(bf16[1,4,16,192]{3,2,1,0:T(8,128)(2,1)S(1)} %copy-done.4), channel_id=1, source_target_pairs={{1,2},{3,4},{5,6},{7,8},{9,10},{11,12},{13,14},{15,16},{17,18},{19... | collective-permute-start | bytes 73736 | tf_op jit(solution)/shard_map/ppermute | solution.py:357
  44.2 2.7 %collective-permute-done.3.dev_far = bf16[1,4,16,192]{3,2,1,0:T(8,128)(2,1)S(1)} collective-permute-done((bf16[1,4,16,192]{3,2,1,0:T(8,128)(2,1)S(1)}, bf16[1,4,16,192]{3,2,1,0:T(8,128)(2,1)S(1)}, u32[]{:S(2)}, u32[]{:S(2)}) %collective-permute-start.3) | collective-permute-done | bytes 24608 | tf_op jit(solution)/shard_map/ppermute | solution.py:357
  46.9 0.6 copy-done.7
  47.5 7.0 %shard_map.114 = (bf16[8,24,2592]{2,1,0:T(8,128)(2,1)}, bf16[8,24,2592]{2,1,0:T(8,128)(2,1)}, bf16[3456,192]{1,0:T(8,128)(2,1)}) custom-call(s32[512]{0:T(512)} %counts_in.5, s32[4,27]{1,0:T(4,128)} %near_in.1, bf16[256,768]{1,0:T(8,128)(2,1)} %fine_in.3, bf16[192,768]{1,0:T(8,128)(2,1)} %bitcast.10, bf16[4,4,16,192]{3,2,1,0:T(8,128)(2,1)} %get-tuple-element.24.grad, ...), custom_call_target="tpu_custom_call" | custom-call | flops 6000000000 | tf_op jit(solution)/shard_map/pallas_call | solution.py:364
  54.6 1.9 %collective-permute-start.4 = (bf16[8,32,16,128]{3,2,1,0:T(8,128)(2,1)S(1)}, bf16[8,32,16,128]{3,2,1,0:T(8,128)(2,1)}, u32[]{:S(2)}, u32[]{:S(2)}) collective-permute-start(bf16[8,32,16,128]{3,2,1,0:T(8,128)(2,1)S(1)} %all-to-all-done.1.mine), channel_id=1, source_target_pairs={{0,1},{1,0},{2,3},{3,2},{4,5},{5,4},{6,7},{7,6},{8,9},{9,8},{10,11... | collective-permute-start | bytes 3145736 | tf_op jit(solution)/shard_map/ppermute | solution.py:347
  56.5 2.4 %collective-permute-start.5 = (bf16[8,24,2592]{2,1,0:T(8,128)(2,1)}, bf16[8,24,2592]{2,1,0:T(8,128)(2,1)S(1)}, u32[]{:S(2)}, u32[]{:S(2)}) collective-permute-start(bf16[8,24,2592]{2,1,0:T(8,128)(2,1)} %get-tuple-element.37), channel_id=1, source_target_pairs={{0,1},{1,0},{2,3},{3,2},{4,5},{5,4},{6,7},{7,6},{8,9},{9,8},{10,11... | collective-permute-start | bytes 2985992 | tf_op jit(solution)/shard_map/ppermute | solution.py:347
  58.9 0.3 collective-permute-done.4.other
  59.3 5.0 %shard_map.115 = (bf16[256,768]{1,0:T(8,128)(2,1)}, bf16[64,24,128]{2,1,0:T(8,128)(2,1)}) custom-call(s32[512]{0:T(512)} %counts_in.5, bf16[256,768]{1,0:T(8,128)(2,1)} %fine_in.3, bf16[192,768]{1,0:T(8,128)(2,1)} %bitcast.11, bf16[3456,192]{1,0:T(8,128)(2,1)} %get-tuple-element.33.taps_in, bf16[8,32,16,128]{3,2,1,0:T(8,128)(2,1)} %copy-done.1, ...), custom_call_target="tpu_custom_call" | custom-call | flops 4000000000 | tf_op jit(solution)/shard_map/pallas_call | solution.py:390
  64.3 28.2 %all_to_all.25.parts = bf16[64,24,128]{2,1,0:T(8,128)(2,1)S(1)} all-to-all(bf16[64,24,128]{2,1,0:T(8,128)(2,1)} %get-tuple-element.38), channel_id=1, replica_groups=mesh['zl'=2,'x'=4,'zh'=4,'y'=8,'c'=2] {'zh','y','c'}, dimensions={0} | all-to-all | bytes 786432 | tf_op jit(solution)/shard_map/all_to_all | solution.py:318
  92.5 0.3 shard_map.116
  92.8 19.2 %all_to_all.26.parts = bf16[8,24,2816]{2,1,0:T(8,128)(2,1)S(1)} all-to-all(bf16[8,24,2816]{2,1,0:T(8,128)(2,1)S(1)} %shard_map.116), channel_id=1, replica_groups=mesh['zl'=2,'x'=4,'zh'=4,'y'=8,'c'=2] {'zl','x'}, dimensions={0} | all-to-all | bytes 2162688 | tf_op jit(solution)/shard_map/all_to_all | solution.py:318
  112.2 20.3 %all_to_all.27 = bf16[32,2,24,128]{3,2,1,0:T(8,128)(2,1)S(1)} all-to-all(bf16[32,2,24,128]{3,2,1,0:T(8,128)(2,1)S(1)} %shard_map.117), channel_id=1, replica_groups=mesh['zl'=2,'x'=4,'zh'=4,'y'=8,'c'=2] {'zh','y'}, dimensions={0} | all-to-all | bytes 786432 | tf_op jit(solution)/shard_map/all_to_all | solution.py:318
  132.6 6.7 %all-gather = bf16[64,2,24,128]{3,2,1,0:T(8,128)(2,1)S(1)} all-gather(bf16[32,2,24,128]{3,2,1,0:T(8,128)(2,1)S(1)} %all_to_all.27), channel_id=2, replica_groups=mesh['zl'=2,'x'=4,'zh'=4,'y'=8,'c'=2] {'c'}, dimensions={0}, use_global_device_ids=true | all-gather | bytes 1179648 | tf_op jit(solution)/shard_map/all_gather | solution.py:413
  139.3 0.9 shard_map.118
  (19 shorter events, 0.3 us)
Async XLA Ops:
  2.8 28.1 %all-to-all-start = ((bf16[32,16,128]{2,1,0:T(8,128)(2,1)}), bf16[32,16,128]{2,1,0:T(8,128)(2,1)S(1)}, u32[]{:S(2)}, u32[]{:S(2)}) async-start(bf16[32,16,128]{2,1,0:T(8,128)(2,1)} %get-tuple-element.23), calls=%async_computation | async-start | bytes 262144 | tf_op jit(solution)/shard_map/all_to_all | solution.py:318
  19.3 6.2 %collective-permute-start.1 = (bf16[4,4,16,192]{3,2,1,0:T(8,128)(2,1)}, bf16[4,4,16,192]{3,2,1,0:T(8,128)(2,1)S(1)}, u32[]{:S(2)}, u32[]{:S(2)}) collective-permute-start(bf16[4,4,16,192]{3,2,1,0:T(8,128)(2,1)} %get-tuple-element.24.grad), channel_id=1, source_target_pairs={{64,0},{128,64},{192,128},{256,192},{320,256},{384,320},{448,384},... | collective-permute-start | bytes 294920 | tf_op jit(solution)/shard_map/ppermute | solution.py:344
  20.6 6.2 %collective-permute-start = (bf16[4,4,16,192]{3,2,1,0:T(8,128)(2,1)}, bf16[4,4,16,192]{3,2,1,0:T(8,128)(2,1)S(1)}, u32[]{:S(2)}, u32[]{:S(2)}) collective-permute-start(bf16[4,4,16,192]{3,2,1,0:T(8,128)(2,1)} %get-tuple-element.24.grad), channel_id=1, source_target_pairs={{0,64},{64,128},{128,192},{192,256},{256,320},{320,384},{384,448},... | collective-permute-start | bytes 294920 | tf_op jit(solution)/shard_map/ppermute | solution.py:344
  25.5 6.5 %copy-start.2 = (bf16[4,4,16,192]{3,2,1,0:T(8,128)(2,1)}, bf16[4,4,16,192]{3,2,1,0:T(8,128)(2,1)S(1)}, u32[]{:S(2)}) copy-start(bf16[4,4,16,192]{3,2,1,0:T(8,128)(2,1)S(1)} %collective-permute-done.1.slab_high) | copy-start | bytes 294916
  26.9 5.2 %copy-start.3 = (bf16[4,4,16,192]{3,2,1,0:T(8,128)(2,1)}, bf16[4,4,16,192]{3,2,1,0:T(8,128)(2,1)S(1)}, u32[]{:S(2)}) copy-start(bf16[4,4,16,192]{3,2,1,0:T(8,128)(2,1)S(1)} %collective-permute-done.slab_low) | copy-start | bytes 294916
  32.0 5.1 %copy-start.5 = (bf16[1,4,16,192]{3,2,1,0:T(8,128)(2,1)S(1)}, bf16[1,4,16,192]{3,2,1,0:T(8,128)(2,1)}, u32[]{:S(2)}) copy-start(bf16[1,4,16,192]{3,2,1,0:T(8,128)(2,1)} %get-tuple-element.30) | copy-start | bytes 73732
  32.0 9.3 %copy-start.4 = (bf16[1,4,16,192]{3,2,1,0:T(8,128)(2,1)S(1)}, bf16[1,4,16,192]{3,2,1,0:T(8,128)(2,1)}, u32[]{:S(2)}) copy-start(bf16[1,4,16,192]{3,2,1,0:T(8,128)(2,1)} %get-tuple-element.31) | copy-start | bytes 73732
  32.1 22.5 %all-to-all-start.1 = ((bf16[8,32,16,128]{3,2,1,0:T(8,128)(2,1)}), bf16[8,32,16,128]{3,2,1,0:T(8,128)(2,1)S(1)}, u32[]{:S(2)}, u32[]{:S(2)}) async-start(bf16[8,32,16,128]{3,2,1,0:T(8,128)(2,1)} %shard_map.113), calls=%async_computation.1 | async-start | bytes 2097152 | tf_op jit(solution)/shard_map/all_to_all | solution.py:318
  37.1 7.1 %collective-permute-start.2 = (bf16[1,4,16,192]{3,2,1,0:T(8,128)(2,1)S(1)}, bf16[1,4,16,192]{3,2,1,0:T(8,128)(2,1)S(1)}, u32[]{:S(2)}, u32[]{:S(2)}) collective-permute-start(bf16[1,4,16,192]{3,2,1,0:T(8,128)(2,1)S(1)} %copy-done.5), channel_id=1, source_target_pairs={{0,1},{1,0},{2,3},{3,2},{4,5},{5,4},{6,7},{7,6},{8,9},{9,8},{10,11... | collective-permute-start | bytes 73736 | tf_op jit(solution)/shard_map/ppermute | solution.py:347
  41.4 5.5 %collective-permute-start.3 = (bf16[1,4,16,192]{3,2,1,0:T(8,128)(2,1)S(1)}, bf16[1,4,16,192]{3,2,1,0:T(8,128)(2,1)S(1)}, u32[]{:S(2)}, u32[]{:S(2)}) collective-permute-start(bf16[1,4,16,192]{3,2,1,0:T(8,128)(2,1)S(1)} %copy-done.4), channel_id=1, source_target_pairs={{1,2},{3,4},{5,6},{7,8},{9,10},{11,12},{13,14},{15,16},{17,18},{19... | collective-permute-start | bytes 73736 | tf_op jit(solution)/shard_map/ppermute | solution.py:357
  44.2 2.7 %copy-start.6 = (bf16[1,4,16,192]{3,2,1,0:T(8,128)(2,1)}, bf16[1,4,16,192]{3,2,1,0:T(8,128)(2,1)S(1)}, u32[]{:S(2)}) copy-start(bf16[1,4,16,192]{3,2,1,0:T(8,128)(2,1)S(1)} %collective-permute-done.2.dev_near) | copy-start | bytes 73732
  46.9 0.6 copy-start.7
  54.6 4.7 %copy-start.1 = (bf16[8,32,16,128]{3,2,1,0:T(8,128)(2,1)}, bf16[8,32,16,128]{3,2,1,0:T(8,128)(2,1)S(1)}, u32[]{:S(2)}) copy-start(bf16[8,32,16,128]{3,2,1,0:T(8,128)(2,1)S(1)} %all-to-all-done.1.mine) | copy-start | bytes 3145732
  54.6 4.7 %collective-permute-start.4 = (bf16[8,32,16,128]{3,2,1,0:T(8,128)(2,1)S(1)}, bf16[8,32,16,128]{3,2,1,0:T(8,128)(2,1)}, u32[]{:S(2)}, u32[]{:S(2)}) collective-permute-start(bf16[8,32,16,128]{3,2,1,0:T(8,128)(2,1)S(1)} %all-to-all-done.1.mine), channel_id=1, source_target_pairs={{0,1},{1,0},{2,3},{3,2},{4,5},{5,4},{6,7},{7,6},{8,9},{9,8},{10,11... | collective-permute-start | bytes 3145736 | tf_op jit(solution)/shard_map/ppermute | solution.py:347
  56.5 7.8 %collective-permute-start.5 = (bf16[8,24,2592]{2,1,0:T(8,128)(2,1)}, bf16[8,24,2592]{2,1,0:T(8,128)(2,1)S(1)}, u32[]{:S(2)}, u32[]{:S(2)}) collective-permute-start(bf16[8,24,2592]{2,1,0:T(8,128)(2,1)} %get-tuple-element.37), channel_id=1, source_target_pairs={{0,1},{1,0},{2,3},{3,2},{4,5},{5,4},{6,7},{7,6},{8,9},{9,8},{10,11... | collective-permute-start | bytes 2985992 | tf_op jit(solution)/shard_map/ppermute | solution.py:347
  59.3 33.2 %copy-start = (bf16[8,24,2592]{2,1,0:T(8,128)(2,1)S(1)}, bf16[8,24,2592]{2,1,0:T(8,128)(2,1)}, u32[]{:S(2)}) copy-start(bf16[8,24,2592]{2,1,0:T(8,128)(2,1)} %get-tuple-element.39.keep) | copy-start | bytes 2985988

commit v9 on v8

--- a/solution.py
+++ b/solution.py
@@ -132,10 +132,8 @@
     far[0] = grad[jnp.where(core == 0, 0, count - 1)]
 
 
-def conv_kernel(
-    counts_in, near_in, fine_in, weight_in, grad, slab_low, slab_high, dev_near, dev_far,
-    keep_out, send_out, taps_out, counts, near, fine, weight, sems, bricks, block, total, taps,
-    keep, send,
+def taps_kernel(
+    near_in, grad, slab_low, slab_high, dev_near, dev_far, taps_out, near, sems, bricks, block, taps
 ):
     place = my_place()
     core = jnp.bitwise_and(place, 1)
@@ -143,11 +141,10 @@
         sems, (near_in, near), (grad, bricks.at[0:4]), (slab_low, bricks.at[4:8]),
         (slab_high, bricks.at[8:12]), (dev_near, bricks.at[pl.ds(13 - core, 1)]),
         (dev_far, bricks.at[pl.ds(12 + core, 1)]),
-        (counts_in, counts), (fine_in, fine), (weight_in, weight),
     )
     bricks[14:15] = jnp.zeros((1, 4, 16, C), BF16)
     window = window_matrix()
-    for copy in copies[:6]:
+    for copy in copies:
         copy.wait()
     for b in range(B):
         slots = []
@@ -170,9 +167,21 @@
             for s in range(9):
                 row = ((s * 6 + plane) * B + b) * 16
                 taps[row : row + 16] = moved[s * 16 : (s + 1) * 16]
-    leave = [pltpu.make_async_copy(taps, taps_out, sems.at[9])]
-    leave[0].start()
-    for copy in copies[6:]:
+    leave = pltpu.make_async_copy(taps, taps_out, sems.at[6])
+    leave.start()
+    leave.wait()
+
+
+def conv_kernel(
+    counts_in, fine_in, weight_in, taps_in, keep_out, send_out,
+    counts, fine, weight, taps, sems, total, keep, send,
+):
+    place = my_place()
+    core = jnp.bitwise_and(place, 1)
+    copies = fetch(
+        sems, (counts_in, counts), (fine_in, fine), (weight_in, weight), (taps_in, taps)
+    )
+    for copy in copies[:3]:
         copy.wait()
     count = counts[place]
     merged = lax.dot_general(
@@ -181,6 +190,7 @@
     brick_of = lax.broadcasted_iota(jnp.int32, (256, C), 0) // 64
     merged = jnp.where(brick_of < count, merged, 0.0).astype(BF16)
     merged = jnp.transpose(dot(row_order(False), merged)).astype(BF16)
+    copies[3].wait()
     for tap in range(27):
         row = tap_rows(tap)
         term = dot(merged, taps[row : row + 256])
@@ -192,10 +202,11 @@
             to = (owner // 2) * ROWS + at % ROWS
             total[owner % 2, :, to : to + stop - at] = term[:, at - tap * C : stop - tap * C]
             at = stop
+    leave = []
     for i, (held, out, half) in enumerate(((send, send_out, 1 - core), (keep, keep_out, core))):
         for slab in range(SLABS):
             held[slab] = total[half, slab * COLS : (slab + 1) * COLS].astype(BF16)
-        leave.append(pltpu.make_async_copy(held, out, sems.at[10 + i]))
+        leave.append(pltpu.make_async_copy(held, out, sems.at[4 + i]))
         leave[-1].start()
     for copy in leave:
         copy.wait()
@@ -253,17 +264,22 @@
     gm = back.astype(BF16)
     fine_grad[...] = dot(gm, weight[...]).astype(BF16)
     result = dot(jnp.transpose(back).astype(BF16), fine[...])
-    for i in range(DEVS):
-        if i < PIECES:
-            piece = result[i % 8 * 24 : i % 8 * 24 + 24, i // 8 * 128 : i // 8 * 128 + 128]
-            term[i] = piece.astype(BF16)
-        else:
-            term[i] = jnp.zeros((24, 128), BF16)
+    for i in range(PIECES):
+        piece = result[i % 8 * 24 : i % 8 * 24 + 24, i // 8 * 128 : i // 8 * 128 + 128]
+        term[i // 24, i % 24] = piece.astype(BF16)
+
+
+def join_kernel(parts, out):
+    core = lax.axis_index("c")
+    for i in range(24):
+        out[i] = (parts[0, core, i].astype(F32) + parts[1, core, i].astype(F32)).astype(BF16)
+    for i in range(24, 32):
+        out[i] = jnp.zeros((24, 128), BF16)
 
 
 def spread_kernel(parts, keep, received, out):
     merge = parts[0].astype(F32)
-    for i in range(1, DEVS):
+    for i in range(1, 32):
         merge = merge + parts[i].astype(F32)
     for i in range(SLABS):
         out[i, :, :HALF] = (keep[i].astype(F32) + received[i].astype(F32)).astype(BF16)
@@ -287,7 +303,7 @@
     core = jnp.bitwise_and(my_place(), 1)
     for i in range(PIECES):
         row, col = i % 8 * 24, i // 8 * 128
-        merge[row : row + 24, col : col + 128] = parts[i % 2, i // 2, 1].astype(F32)
+        merge[row : row + 24, col : col + 128] = parts[i // 24, i % 24, 1].astype(F32)
     copies = fetch(sems, (merge, merge_out))
     total = parts[core, 0, 0].astype(F32)
     for i in range(1, 32):
@@ -361,41 +377,52 @@
     fine_scratch = pltpu.VMEM((256, 768), BF16)
     weight_scratch = pltpu.VMEM((C, 768), BF16)
     merge_weight = merge_weight.T
-    keep, send, taps = call(
+    taps_scratch = pltpu.VMEM((3456, C), BF16)
+    half_scratch = pltpu.VMEM((SLABS, COLS, HALF), BF16)
+    taps = call(
+        taps_kernel,
+        shape(3456, C),
+        [HBM] * 6,
+        [
+            pltpu.SMEM((B, 27), jnp.int32),
+            pltpu.SemaphoreType.DMA((7,)),
+            pltpu.VMEM((15, 4, 16, C), BF16),
+            pltpu.VMEM((6, 144, C), BF16),
+            taps_scratch,
+        ],
+        flops=3 * 10**9,
+        out_spec=HBM,
+        vmem=60,
+    )(neighbours, grad, slab_low, slab_high, dev_near, dev_far)
+    frames, taps = lax.optimization_barrier((frames, taps))
+    other = flipped(frames)
+    keep, send = call(
         conv_kernel,
-        (shape(SLABS, COLS, HALF), shape(SLABS, COLS, HALF), shape(3456, C)),
-        [HBM] * 9,
+        (shape(SLABS, COLS, HALF), shape(SLABS, COLS, HALF)),
+        [HBM] * 4,
         [
             counts_scratch,
-            pltpu.SMEM((B, 27), jnp.int32),
             fine_scratch,
             weight_scratch,
-            pltpu.SemaphoreType.DMA((12,)),
-            pltpu.VMEM((15, 4, 16, C), BF16),
-            pltpu.VMEM((6, 144, C), BF16),
+            taps_scratch,
+            pltpu.SemaphoreType.DMA((6,)),
             pltpu.VMEM((2, C, HALF), F32),
-            pltpu.VMEM((3456, C), BF16),
-            pltpu.VMEM((SLABS, COLS, HALF), BF16),
-            pltpu.VMEM((SLABS, COLS, HALF), BF16),
+            half_scratch,
+            half_scratch,
         ],
-        flops=6 * 10**9,
-        out_spec=(HBM, HBM, HBM),
+        flops=4 * 10**9,
+        out_spec=(HBM, HBM),
         vmem=60,
-    )(
-        counts, neighbours, fine_input, merge_weight, grad, slab_low, slab_high, dev_near, dev_far
-    )
-
-    frames, taps = lax.optimization_barrier((frames, taps))
-    other = flipped(frames)
+    )(counts, fine_input, merge_weight, taps)
     fine_grad, term = call(
         back_kernel,
-        (shape(256, 768), shape(DEVS, 24, 128)),
+        (shape(256, 768), shape(2, 24, 24, 128)),
         [HBM] * 6,
         [
             counts_scratch,
             fine_scratch,
             weight_scratch,
-            pltpu.VMEM((3456, C), BF16),
+            taps_scratch,
             pltpu.SemaphoreType.DMA((6,)),
             pltpu.VMEM((2, SLABS, 32, 16, 128), BF16),
             pltpu.VMEM((27 * C, C), BF16),
@@ -404,8 +431,10 @@
         vmem=60,
     )(counts, fine_input, merge_weight, taps, frames, other)
 
+    term = lax.all_gather(term, "c", axis=0, tiled=False)
     term, received = lax.optimization_barrier((term, flipped(send)))
-    term = swap(term, DEV)
+    term = call(join_kernel, shape(32, 24, 128), [VMEM])(term)
+    term = swap(term, ("zh", "y"))
     term = call(spread_kernel, shape(SLABS, COLS, WIDE + 128), [VMEM] * 3)(term, keep, received)
     term = swap(term, SLAB)
     term = call(both_kernel, shape(32, 2, 24, 128), [VMEM])(term)

time: 141 us -> 139 us (0.986)
  blocking collectives: 74.5 us -> 68.4 us
  Pallas kernels: 16.7 us -> 19.1 us
  starting transfers between devices: 38.3 us -> 39.8 us
    all_to_all x3, blocking collectives: 67.7 us -> 58.9 us  [swap(): return lax.all_to_all(x, axes, 0, 0, tiled=True)]
    all_gather x1 -> x2, blocking collectives: 6.74 us -> 9.55 us  [local(): term = lax.all_gather(term, 'c', axis=0, tiled=False)]
    pallas_call x2 -> x4, Pallas kernels: 12 us -> 14.5 us  [the longest x1 6.25 us: local(): call(conv_kernel, (shape(SLABS, COLS, HALF), shape(SLABS, COLS, HALF)), [...]
    ppermute x3, starting transfers between devices: 8.59 us -> 10.1 us  [flipped(): return lax.ppermute(x, 'c', [(0, 1), (1, 0)])]
  transfers between devices with their start and end apart: 8 -> 8, of which waited for: 5 -> 4; matrix products, arithmetic and copies ran while one was open for 0% -> 0% of each run, Pallas kernels for 9% -> 10%
where the time goes in v9:
time: 139 us
  blocking collectives  68.4 us (49%)
  starting transfers between devices  39.8 us (29%)
  Pallas kernels  19.1 us (14%)
  waiting for transfers between devices  8.96 us (6%)
  local copies, waits for them, and re-layouts  1.61 us (1%)
    all_to_all x3, blocking collectives, swap(): return lax.all_to_all(x, axes, 0, 0, tiled=True)  58.9 us
    all_to_all x2, starting transfers between devices, swap(): return lax.all_to_all(x, axes, 0, 0, tiled=True)  21.6 us
    ppermute x3, starting transfers between devices, flipped(): return lax.ppermute(x, 'c', [(0, 1), (1, 0)])  10.1 us
    all_gather x2, blocking collectives, local(): term = lax.all_gather(term, 'c', axis=0, tiled=False)  9.55 us
    pallas_call x1, Pallas kernels, local(): call(conv_kernel, (shape(SLABS, COLS, HALF), shape(SLABS, COLS, HALF)), [...  6.25 us
    ppermute x2, starting transfers between devices, shifted(): return lax.ppermute(x, axes, pairs)  5.28 us
    pallas_call x1, Pallas kernels, local(): call(back_kernel, (shape(256, 768), shape(2, 24, 24, 128)), [HBM] * 6, [c...  4.88 us
    all_to_all x2, waiting for transfers between devices, swap(): return lax.all_to_all(x, axes, 0, 0, tiled=True)  4.05 us
  transfers between devices with their start and end apart: 8, of which 4 were waited for; matrix products, arithmetic and copies ran while one was open for 0% of the time, Pallas kernels for 10%

profile of v9, /device:TPU:1, one launch (start us, length us, event | category | flops | bytes accessed | tf_op | source)
XLA Modules:
  0.0 138.8 jit_solution(9230088527070602818)
XLA Ops:
  0.6 2.2 %shard_map.112 = (bf16[4,4,16,192]{3,2,1,0:T(8,128)(2,1)}, bf16[1,4,16,192]{3,2,1,0:T(8,128)(2,1)}, bf16[1,4,16,192]{3,2,1,0:T(8,128)(2,1)}, bf16[32,16,128]{2,1,0:T(8,128)(2,1)}) custom-call(s32[512]{0:T(512)} %counts_in.5, bf16[4,16,768]{2,1,0:T(8,128)(2,1)} %pre_in.1, bf16[4,16,768]{2,1,0:T(8,128)(2,1)} %cot_in.1, f32[1,192]{1,0:T(1,128)} %bitcast.9, ...), custom_call_target="tpu_custom_call" | custom-call | tf_op jit(solution)/shard_map/pallas_call | solution.py:341
  2.8 16.5 %all-to-all-start = ((bf16[32,16,128]{2,1,0:T(8,128)(2,1)}), bf16[32,16,128]{2,1,0:T(8,128)(2,1)S(1)}, u32[]{:S(2)}, u32[]{:S(2)}) async-start(bf16[32,16,128]{2,1,0:T(8,128)(2,1)} %get-tuple-element.22), calls=%async_computation | async-start | bytes 262144 | tf_op jit(solution)/shard_map/all_to_all | solution.py:334
  19.3 1.3 collective-permute-start.1
  20.6 4.0 %collective-permute-start = (bf16[4,4,16,192]{3,2,1,0:T(8,128)(2,1)}, bf16[4,4,16,192]{3,2,1,0:T(8,128)(2,1)S(1)}, u32[]{:S(2)}, u32[]{:S(2)}) collective-permute-start(bf16[4,4,16,192]{3,2,1,0:T(8,128)(2,1)} %get-tuple-element.23.grad), channel_id=1, source_target_pairs={{0,64},{64,128},{128,192},{192,256},{256,320},{320,384},{384,448},... | collective-permute-start | bytes 294920 | tf_op jit(solution)/shard_map/ppermute | solution.py:360
  24.6 0.9 collective-permute-done.1.slab_high
  25.6 1.3 collective-permute-done.slab_low
  26.9 4.0 %all-to-all-done.block = bf16[32,16,128]{2,1,0:T(8,128)(2,1)S(1)} async-done(((bf16[32,16,128]{2,1,0:T(8,128)(2,1)}), bf16[32,16,128]{2,1,0:T(8,128)(2,1)S(1)}, u32[]{:S(2)}, u32[]{:S(2)}) %all-to-all-start) | async-done | bytes 131104 | tf_op jit(solution)/shard_map/all_to_all | solution.py:334
  30.9 1.1 shard_map.113
  32.1 5.0 %all-to-all-start.1 = ((bf16[8,32,16,128]{3,2,1,0:T(8,128)(2,1)}), bf16[8,32,16,128]{3,2,1,0:T(8,128)(2,1)S(1)}, u32[]{:S(2)}, u32[]{:S(2)}) async-start(bf16[8,32,16,128]{3,2,1,0:T(8,128)(2,1)} %shard_map.113), calls=%async_computation.1 | async-start | bytes 2097152 | tf_op jit(solution)/shard_map/all_to_all | solution.py:334
  37.1 4.3 %collective-permute-start.2 = (bf16[1,4,16,192]{3,2,1,0:T(8,128)(2,1)S(1)}, bf16[1,4,16,192]{3,2,1,0:T(8,128)(2,1)S(1)}, u32[]{:S(2)}, u32[]{:S(2)}) collective-permute-start(bf16[1,4,16,192]{3,2,1,0:T(8,128)(2,1)S(1)} %copy-done.6), channel_id=1, source_target_pairs={{0,1},{1,0},{2,3},{3,2},{4,5},{5,4},{6,7},{7,6},{8,9},{9,8},{10,11... | collective-permute-start | bytes 73736 | tf_op jit(solution)/shard_map/ppermute | solution.py:363
  41.4 2.8 %collective-permute-start.3 = (bf16[1,4,16,192]{3,2,1,0:T(8,128)(2,1)S(1)}, bf16[1,4,16,192]{3,2,1,0:T(8,128)(2,1)S(1)}, u32[]{:S(2)}, u32[]{:S(2)}) collective-permute-start(bf16[1,4,16,192]{3,2,1,0:T(8,128)(2,1)S(1)} %copy-done.5), channel_id=1, source_target_pairs={{1,2},{3,4},{5,6},{7,8},{9,10},{11,12},{13,14},{15,16},{17,18},{19... | collective-permute-start | bytes 73736 | tf_op jit(solution)/shard_map/ppermute | solution.py:373
  44.3 2.7 %collective-permute-done.3.dev_far = bf16[1,4,16,192]{3,2,1,0:T(8,128)(2,1)S(1)} collective-permute-done((bf16[1,4,16,192]{3,2,1,0:T(8,128)(2,1)S(1)}, bf16[1,4,16,192]{3,2,1,0:T(8,128)(2,1)S(1)}, u32[]{:S(2)}, u32[]{:S(2)}) %collective-permute-start.3) | collective-permute-done | bytes 24608 | tf_op jit(solution)/shard_map/ppermute | solution.py:373
  47.6 3.3 %shard_map.114.taps_in = bf16[3456,192]{1,0:T(8,128)(2,1)} custom-call(s32[4,27]{1,0:T(4,128)} %near_in.1, bf16[4,4,16,192]{3,2,1,0:T(8,128)(2,1)} %get-tuple-element.23.grad, bf16[4,4,16,192]{3,2,1,0:T(8,128)(2,1)} %copy-done.4, bf16[4,4,16,192]{3,2,1,0:T(8,128)(2,1)} %copy-done.3, bf16[1,4,16,192]{3,2,1,0:T(8,128)(2,1)} %copy-done.7, ...), custom_call_target="tpu_custom_call" | custom-call | flops 3000000000 | tf_op jit(solution)/shard_map/pallas_call | solution.py:382
  50.9 3.9 %collective-permute-start.4 = (bf16[8,32,16,128]{3,2,1,0:T(8,128)(2,1)S(1)}, bf16[8,32,16,128]{3,2,1,0:T(8,128)(2,1)S(1)}, u32[]{:S(2)}, u32[]{:S(2)}) collective-permute-start(bf16[8,32,16,128]{3,2,1,0:T(8,128)(2,1)S(1)} %all-to-all-done.1.mine), channel_id=1, source_target_pairs={{0,1},{1,0},{2,3},{3,2},{4,5},{5,4},{6,7},{7,6},{8,9},{9,8},{10,11... | collective-permute-start | bytes 3145736 | tf_op jit(solution)/shard_map/ppermute | solution.py:363
  54.8 6.3 %shard_map.116 = (bf16[8,24,2592]{2,1,0:T(8,128)(2,1)}, bf16[8,24,2592]{2,1,0:T(8,128)(2,1)}) custom-call(s32[512]{0:T(512)} %counts_in.5, bf16[256,768]{1,0:T(8,128)(2,1)} %fine_in.3, bf16[192,768]{1,0:T(8,128)(2,1)} %bitcast.12, bf16[3456,192]{1,0:T(8,128)(2,1)} %shard_map.114.taps_in), custom_call_target="tpu_custom_call" | custom-call | flops 4000000000 | tf_op jit(solution)/shard_map/pallas_call | solution.py:399
  61.1 1.9 %collective-permute-start.5 = (bf16[8,24,2592]{2,1,0:T(8,128)(2,1)}, bf16[8,24,2592]{2,1,0:T(8,128)(2,1)S(1)}, u32[]{:S(2)}, u32[]{:S(2)}) collective-permute-start(bf16[8,24,2592]{2,1,0:T(8,128)(2,1)} %get-tuple-element.35), channel_id=1, source_target_pairs={{0,1},{1,0},{2,3},{3,2},{4,5},{5,4},{6,7},{7,6},{8,9},{9,8},{10,11... | collective-permute-start | bytes 2985992 | tf_op jit(solution)/shard_map/ppermute | solution.py:363
  63.0 1.0 copy-done.2
  64.0 4.9 %shard_map.115 = (bf16[256,768]{1,0:T(8,128)(2,1)}, bf16[2,24,24,128]{3,2,1,0:T(8,128)(2,1)}) custom-call(s32[512]{0:T(512)} %counts_in.5, bf16[256,768]{1,0:T(8,128)(2,1)} %fine_in.3, bf16[192,768]{1,0:T(8,128)(2,1)} %bitcast.13, bf16[3456,192]{1,0:T(8,128)(2,1)} %shard_map.114.taps_in, bf16[8,32,16,128]{3,2,1,0:T(8,128)(2,1)} %copy-done.1, ...), custom_call_target="tpu_custom_call" | custom-call | flops 4000000000 | tf_op jit(solution)/shard_map/pallas_call | solution.py:417
  68.9 2.7 %all-gather = bf16[4,24,24,128]{3,2,1,0:T(8,128)(2,1)S(1)} all-gather(bf16[2,24,24,128]{3,2,1,0:T(8,128)(2,1)} %get-tuple-element.34), channel_id=2, replica_groups=mesh['zl'=2,'x'=4,'zh'=4,'y'=8,'c'=2] {'c'}, dimensions={0}, use_global_device_ids=true | all-gather | bytes 884736 | tf_op jit(solution)/shard_map/all_gather | solution.py:434
  71.6 21.7 %all_to_all.25.parts = bf16[32,24,128]{2,1,0:T(8,128)(2,1)S(1)} all-to-all(bf16[32,24,128]{2,1,0:T(8,128)(2,1)S(1)} %shard_map.117), channel_id=1, replica_groups=mesh['zl'=2,'x'=4,'zh'=4,'y'=8,'c'=2] {'zh','y'}, dimensions={0} | all-to-all | bytes 393216 | tf_op jit(solution)/shard_map/all_to_all | solution.py:334
  93.6 17.7 %all_to_all.26.parts = bf16[8,24,2816]{2,1,0:T(8,128)(2,1)S(1)} all-to-all(bf16[8,24,2816]{2,1,0:T(8,128)(2,1)S(1)} %shard_map.118), channel_id=1, replica_groups=mesh['zl'=2,'x'=4,'zh'=4,'y'=8,'c'=2] {'zl','x'}, dimensions={0} | all-to-all | bytes 2162688 | tf_op jit(solution)/shard_map/all_to_all | solution.py:334
  111.5 19.5 %all_to_all.27 = bf16[32,2,24,128]{3,2,1,0:T(8,128)(2,1)S(1)} all-to-all(bf16[32,2,24,128]{3,2,1,0:T(8,128)(2,1)S(1)} %shard_map.119), channel_id=1, replica_groups=mesh['zl'=2,'x'=4,'zh'=4,'y'=8,'c'=2] {'zh','y'}, dimensions={0} | all-to-all | bytes 786432 | tf_op jit(solution)/shard_map/all_to_all | solution.py:334
  131.0 6.9 %all-gather.1 = bf16[64,2,24,128]{3,2,1,0:T(8,128)(2,1)S(1)} all-gather(bf16[32,2,24,128]{3,2,1,0:T(8,128)(2,1)S(1)} %all_to_all.27), channel_id=3, replica_groups=mesh['zl'=2,'x'=4,'zh'=4,'y'=8,'c'=2] {'c'}, dimensions={0}, use_global_device_ids=true | all-gather | bytes 1179648 | tf_op jit(solution)/shard_map/all_gather | solution.py:442
  137.9 0.9 shard_map.120
  (24 shorter events, 1.2 us)
Async XLA Ops:
  2.8 28.1 %all-to-all-start = ((bf16[32,16,128]{2,1,0:T(8,128)(2,1)}), bf16[32,16,128]{2,1,0:T(8,128)(2,1)S(1)}, u32[]{:S(2)}, u32[]{:S(2)}) async-start(bf16[32,16,128]{2,1,0:T(8,128)(2,1)} %get-tuple-element.22), calls=%async_computation | async-start | bytes 262144 | tf_op jit(solution)/shard_map/all_to_all | solution.py:334
  19.3 6.2 %collective-permute-start.1 = (bf16[4,4,16,192]{3,2,1,0:T(8,128)(2,1)}, bf16[4,4,16,192]{3,2,1,0:T(8,128)(2,1)S(1)}, u32[]{:S(2)}, u32[]{:S(2)}) collective-permute-start(bf16[4,4,16,192]{3,2,1,0:T(8,128)(2,1)} %get-tuple-element.23.grad), channel_id=1, source_target_pairs={{64,0},{128,64},{192,128},{256,192},{320,256},{384,320},{448,384},... | collective-permute-start | bytes 294920 | tf_op jit(solution)/shard_map/ppermute | solution.py:360
  20.6 6.2 %collective-permute-start = (bf16[4,4,16,192]{3,2,1,0:T(8,128)(2,1)}, bf16[4,4,16,192]{3,2,1,0:T(8,128)(2,1)S(1)}, u32[]{:S(2)}, u32[]{:S(2)}) collective-permute-start(bf16[4,4,16,192]{3,2,1,0:T(8,128)(2,1)} %get-tuple-element.23.grad), channel_id=1, source_target_pairs={{0,64},{64,128},{128,192},{192,256},{256,320},{320,384},{384,448},... | collective-permute-start | bytes 294920 | tf_op jit(solution)/shard_map/ppermute | solution.py:360
  25.6 6.5 %copy-start.3 = (bf16[4,4,16,192]{3,2,1,0:T(8,128)(2,1)}, bf16[4,4,16,192]{3,2,1,0:T(8,128)(2,1)S(1)}, u32[]{:S(2)}) copy-start(bf16[4,4,16,192]{3,2,1,0:T(8,128)(2,1)S(1)} %collective-permute-done.1.slab_high) | copy-start | bytes 294916
  26.9 5.2 %copy-start.4 = (bf16[4,4,16,192]{3,2,1,0:T(8,128)(2,1)}, bf16[4,4,16,192]{3,2,1,0:T(8,128)(2,1)S(1)}, u32[]{:S(2)}) copy-start(bf16[4,4,16,192]{3,2,1,0:T(8,128)(2,1)S(1)} %collective-permute-done.slab_low) | copy-start | bytes 294916
  32.1 5.1 %copy-start.6 = (bf16[1,4,16,192]{3,2,1,0:T(8,128)(2,1)S(1)}, bf16[1,4,16,192]{3,2,1,0:T(8,128)(2,1)}, u32[]{:S(2)}) copy-start(bf16[1,4,16,192]{3,2,1,0:T(8,128)(2,1)} %get-tuple-element.29) | copy-start | bytes 73732
  32.1 9.3 %copy-start.5 = (bf16[1,4,16,192]{3,2,1,0:T(8,128)(2,1)S(1)}, bf16[1,4,16,192]{3,2,1,0:T(8,128)(2,1)}, u32[]{:S(2)}) copy-start(bf16[1,4,16,192]{3,2,1,0:T(8,128)(2,1)} %get-tuple-element.30) | copy-start | bytes 73732
  32.1 18.8 %all-to-all-start.1 = ((bf16[8,32,16,128]{3,2,1,0:T(8,128)(2,1)}), bf16[8,32,16,128]{3,2,1,0:T(8,128)(2,1)S(1)}, u32[]{:S(2)}, u32[]{:S(2)}) async-start(bf16[8,32,16,128]{3,2,1,0:T(8,128)(2,1)} %shard_map.113), calls=%async_computation.1 | async-start | bytes 2097152 | tf_op jit(solution)/shard_map/all_to_all | solution.py:334
  37.1 7.1 %collective-permute-start.2 = (bf16[1,4,16,192]{3,2,1,0:T(8,128)(2,1)S(1)}, bf16[1,4,16,192]{3,2,1,0:T(8,128)(2,1)S(1)}, u32[]{:S(2)}, u32[]{:S(2)}) collective-permute-start(bf16[1,4,16,192]{3,2,1,0:T(8,128)(2,1)S(1)} %copy-done.6), channel_id=1, source_target_pairs={{0,1},{1,0},{2,3},{3,2},{4,5},{5,4},{6,7},{7,6},{8,9},{9,8},{10,11... | collective-permute-start | bytes 73736 | tf_op jit(solution)/shard_map/ppermute | solution.py:363
  41.4 5.5 %collective-permute-start.3 = (bf16[1,4,16,192]{3,2,1,0:T(8,128)(2,1)S(1)}, bf16[1,4,16,192]{3,2,1,0:T(8,128)(2,1)S(1)}, u32[]{:S(2)}, u32[]{:S(2)}) collective-permute-start(bf16[1,4,16,192]{3,2,1,0:T(8,128)(2,1)S(1)} %copy-done.5), channel_id=1, source_target_pairs={{1,2},{3,4},{5,6},{7,8},{9,10},{11,12},{13,14},{15,16},{17,18},{19... | collective-permute-start | bytes 73736 | tf_op jit(solution)/shard_map/ppermute | solution.py:373
  44.3 2.7 %copy-start.7 = (bf16[1,4,16,192]{3,2,1,0:T(8,128)(2,1)}, bf16[1,4,16,192]{3,2,1,0:T(8,128)(2,1)S(1)}, u32[]{:S(2)}) copy-start(bf16[1,4,16,192]{3,2,1,0:T(8,128)(2,1)S(1)} %collective-permute-done.2.dev_near) | copy-start | bytes 73732
  46.9 0.6 copy-start.8
  50.8 10.2 %copy-start.1 = (bf16[8,32,16,128]{3,2,1,0:T(8,128)(2,1)}, bf16[8,32,16,128]{3,2,1,0:T(8,128)(2,1)S(1)}, u32[]{:S(2)}) copy-start(bf16[8,32,16,128]{3,2,1,0:T(8,128)(2,1)S(1)} %all-to-all-done.1.mine) | copy-start | bytes 3145732
  50.9 12.1 %collective-permute-start.4 = (bf16[8,32,16,128]{3,2,1,0:T(8,128)(2,1)S(1)}, bf16[8,32,16,128]{3,2,1,0:T(8,128)(2,1)S(1)}, u32[]{:S(2)}, u32[]{:S(2)}) collective-permute-start(bf16[8,32,16,128]{3,2,1,0:T(8,128)(2,1)S(1)} %all-to-all-done.1.mine), channel_id=1, source_target_pairs={{0,1},{1,0},{2,3},{3,2},{4,5},{5,4},{6,7},{7,6},{8,9},{9,8},{10,11... | collective-permute-start | bytes 3145736 | tf_op jit(solution)/shard_map/ppermute | solution.py:363
  61.1 10.5 %collective-permute-start.5 = (bf16[8,24,2592]{2,1,0:T(8,128)(2,1)}, bf16[8,24,2592]{2,1,0:T(8,128)(2,1)S(1)}, u32[]{:S(2)}, u32[]{:S(2)}) collective-permute-start(bf16[8,24,2592]{2,1,0:T(8,128)(2,1)} %get-tuple-element.35), channel_id=1, source_target_pairs={{0,1},{1,0},{2,3},{3,2},{4,5},{5,4},{6,7},{7,6},{8,9},{9,8},{10,11... | collective-permute-start | bytes 2985992 | tf_op jit(solution)/shard_map/ppermute | solution.py:363
  63.0 1.0 copy-start.2
  68.9 24.4 %copy-start = (bf16[8,24,2592]{2,1,0:T(8,128)(2,1)S(1)}, bf16[8,24,2592]{2,1,0:T(8,128)(2,1)}, u32[]{:S(2)}) copy-start(bf16[8,24,2592]{2,1,0:T(8,128)(2,1)} %get-tuple-element.37.keep) | copy-start | bytes 2985988

commit v10 on v8

--- a/solution.py
+++ b/solution.py
@@ -202,14 +202,13 @@
 
 
 def back_kernel(
-    counts_in, fine_in, weight_in, taps_in, mine, other, fine_grad, term,
-    counts, fine, weight, taps, sems, both, whole,
+    counts_in, fine_in, taps_in, mine, other, gm, term, counts, fine, taps, sems, both, whole,
 ):
     place = my_place()
     core = jnp.bitwise_and(place, 1)
     copies = fetch(
         sems, (mine, both.at[core]), (other, both.at[1 - core]), (taps_in, taps),
-        (fine_in, fine), (weight_in, weight), (counts_in, counts),
+        (fine_in, fine), (counts_in, counts),
     )
     for copy in copies[:2]:
         copy.wait()
@@ -250,20 +249,32 @@
     count = counts[place]
     back = jnp.where(brick_of < count, back, 0.0).astype(BF16)
     back = dot(row_order(True), back)
-    gm = back.astype(BF16)
-    fine_grad[...] = dot(gm, weight[...]).astype(BF16)
+    gm[...] = back.astype(BF16)
     result = dot(jnp.transpose(back).astype(BF16), fine[...])
-    for i in range(DEVS):
-        if i < PIECES:
-            piece = result[i % 8 * 24 : i % 8 * 24 + 24, i // 8 * 128 : i // 8 * 128 + 128]
-            term[i] = piece.astype(BF16)
-        else:
-            term[i] = jnp.zeros((24, 128), BF16)
+    for i in range(PIECES):
+        piece = result[i % 8 * 24 : i % 8 * 24 + 24, i // 8 * 128 : i // 8 * 128 + 128]
+        term[i // 24, i % 24] = piece.astype(BF16)
+
+
+def fine_kernel(gm_in, weight_in, fine_out, gm, weight, fine_grad, sems):
+    for copy in fetch(sems, (gm_in, gm), (weight_in, weight)):
+        copy.wait()
+    fine_grad[...] = dot(gm[...], weight[...]).astype(BF16)
+    for copy in fetch(sems.at[2:], (fine_grad, fine_out)):
+        copy.wait()
+
+
+def join_kernel(parts, out):
+    core = lax.axis_index("c")
+    for i in range(24):
+        out[i] = (parts[0, core, i].astype(F32) + parts[1, core, i].astype(F32)).astype(BF16)
+    for i in range(24, 32):
+        out[i] = jnp.zeros((24, 128), BF16)
 
 
 def spread_kernel(parts, keep, received, out):
     merge = parts[0].astype(F32)
-    for i in range(1, DEVS):
+    for i in range(1, 32):
         merge = merge + parts[i].astype(F32)
     for i in range(SLABS):
         out[i, :, :HALF] = (keep[i].astype(F32) + received[i].astype(F32)).astype(BF16)
@@ -287,7 +298,7 @@
     core = jnp.bitwise_and(my_place(), 1)
     for i in range(PIECES):
         row, col = i % 8 * 24, i // 8 * 128
-        merge[row : row + 24, col : col + 128] = parts[i % 2, i // 2, 1].astype(F32)
+        merge[row : row + 24, col : col + 128] = parts[i // 24, i % 24, 1].astype(F32)
     copies = fetch(sems, (merge, merge_out))
     total = parts[core, 0, 0].astype(F32)
     for i in range(1, 32):
@@ -387,26 +398,41 @@
 
     frames, taps = lax.optimization_barrier((frames, taps))
     other = flipped(frames)
-    fine_grad, term = call(
+    gm, term = call(
         back_kernel,
-        (shape(256, 768), shape(DEVS, 24, 128)),
-        [HBM] * 6,
+        (shape(256, C), shape(2, 24, 24, 128)),
+        [HBM] * 5,
         [
             counts_scratch,
             fine_scratch,
-            weight_scratch,
             pltpu.VMEM((3456, C), BF16),
-            pltpu.SemaphoreType.DMA((6,)),
+            pltpu.SemaphoreType.DMA((5,)),
             pltpu.VMEM((2, SLABS, 32, 16, 128), BF16),
             pltpu.VMEM((27 * C, C), BF16),
         ],
         flops=4 * 10**9,
         vmem=60,
-    )(counts, fine_input, merge_weight, taps, frames, other)
-
-    term, received = lax.optimization_barrier((term, flipped(send)))
-    term = swap(term, DEV)
-    term = call(spread_kernel, shape(SLABS, COLS, WIDE + 128), [VMEM] * 3)(term, keep, received)
+    )(counts, fine_input, taps, frames, other)
+    fine_grad = call(
+        fine_kernel,
+        shape(256, 768),
+        [HBM] * 2,
+        [
+            pltpu.VMEM((256, C), BF16),
+            weight_scratch,
+            fine_scratch,
+            pltpu.SemaphoreType.DMA((3,)),
+        ],
+        flops=10**9,
+        out_spec=HBM,
+    )(gm, merge_weight)
+
+    term = lax.all_gather(term, "c", axis=0, tiled=False)
+    term = call(join_kernel, shape(32, 24, 128), [VMEM])(term)
+    term = swap(term, ("zh", "y"))
+    term = call(spread_kernel, shape(SLABS, COLS, WIDE + 128), [VMEM] * 3)(
+        term, keep, flipped(send)
+    )
     term = swap(term, SLAB)
     term = call(both_kernel, shape(32, 2, 24, 128), [VMEM])(term)
     term = swap(term, ("zh", "y"))

time: 141 us -> 139 us (0.986)
  blocking collectives: 74.5 us -> 27.6 us
  waiting for transfers between devices: 9.3 us -> 32.8 us
  starting transfers between devices: 38.3 us -> 56.1 us
  Pallas kernels: 16.7 us -> 19 us
    all_to_all x3 -> x1, blocking collectives: 67.7 us -> 18.2 us  [swap(): return lax.all_to_all(x, axes, 0, 0, tiled=True)]
    all_to_all x2 -> x4, waiting for transfers between devices: 4.05 us -> 27.7 us  [swap(): return lax.all_to_all(x, axes, 0, 0, tiled=True)]
    all_to_all x2 -> x4, starting transfers between devices: 21.6 us -> 39.4 us  [swap(): return lax.all_to_all(x, axes, 0, 0, tiled=True)]
    all_gather x1 -> x2, blocking collectives: 6.74 us -> 9.44 us  [local(): term = lax.all_gather(term, 'c', axis=0, tiled=False)]
    pallas_call x1 -> x3, Pallas kernels: 5 us -> 6.61 us  [the longest x1 4.63 us: local(): call(back_kernel, (shape(256, C), shape(2, 24, 24, 128)), [HBM] * 5, [cou...]
  transfers between devices with their start and end apart: 8 -> 10, of which waited for: 5 -> 7; matrix products, arithmetic and copies ran while one was open for 0% -> 0% of each run, Pallas kernels for 9% -> 10%
where the time goes in v10:
time: 139 us; the launch traced here: 138 us
  starting transfers between devices  56.1 us (40%)
  waiting for transfers between devices  32.8 us (24%)
  blocking collectives  27.6 us (20%)
  Pallas kernels  19 us (14%)
  local copies, waits for them, and re-layouts  1.63 us (1%)
    all_to_all x4, starting transfers between devices, swap(): return lax.all_to_all(x, axes, 0, 0, tiled=True)  39.4 us
    all_to_all x4, waiting for transfers between devices, swap(): return lax.all_to_all(x, axes, 0, 0, tiled=True)  27.7 us
    all_to_all x1, blocking collectives, swap(): return lax.all_to_all(x, axes, 0, 0, tiled=True)  18.2 us
    all_gather x2, blocking collectives, local(): term = lax.all_gather(term, 'c', axis=0, tiled=False)  9.44 us
    ppermute x3, starting transfers between devices, flipped(): return lax.ppermute(x, 'c', [(0, 1), (1, 0)])  8.59 us
    pallas_call x1, Pallas kernels, local(): call(conv_kernel, (shape(SLABS, COLS, HALF), shape(SLABS, COLS, HALF), sh...  7.01 us
    ppermute x2, starting transfers between devices, shifted(): return lax.ppermute(x, axes, pairs)  5.28 us
    pallas_call x1, Pallas kernels, local(): call(back_kernel, (shape(256, C), shape(2, 24, 24, 128)), [HBM] * 5, [cou...  4.63 us
  transfers between devices with their start and end apart: 10, of which 7 were waited for; matrix products, arithmetic and copies ran while one was open for 0% of the time, Pallas kernels for 10%

profile of v10, /device:TPU:1, one launch (start us, length us, event | category | flops | bytes accessed | tf_op | source)
XLA Modules:
  0.0 138.0 jit_solution(6070277953935988362)
XLA Ops:
  0.6 2.2 %shard_map.112 = (bf16[4,4,16,192]{3,2,1,0:T(8,128)(2,1)}, bf16[1,4,16,192]{3,2,1,0:T(8,128)(2,1)}, bf16[1,4,16,192]{3,2,1,0:T(8,128)(2,1)}, bf16[32,16,128]{2,1,0:T(8,128)(2,1)}) custom-call(s32[512]{0:T(512)} %counts_in.5, bf16[4,16,768]{2,1,0:T(8,128)(2,1)} %pre_in.1, bf16[4,16,768]{2,1,0:T(8,128)(2,1)} %cot_in.1, f32[1,192]{1,0:T(1,128)} %bitcast.11, ...), custom_call_target="tpu_custom_call" | custom-call | tf_op jit(solution)/shard_map/pallas_call | solution.py:336
  2.8 16.5 %all-to-all-start = ((bf16[32,16,128]{2,1,0:T(8,128)(2,1)}), bf16[32,16,128]{2,1,0:T(8,128)(2,1)S(1)}, u32[]{:S(2)}, u32[]{:S(2)}) async-start(bf16[32,16,128]{2,1,0:T(8,128)(2,1)} %get-tuple-element.21), calls=%async_computation | async-start | bytes 262144 | tf_op jit(solution)/shard_map/all_to_all | solution.py:329
  19.3 1.3 collective-permute-start.1
  20.6 4.0 %collective-permute-start = (bf16[4,4,16,192]{3,2,1,0:T(8,128)(2,1)}, bf16[4,4,16,192]{3,2,1,0:T(8,128)(2,1)S(1)}, u32[]{:S(2)}, u32[]{:S(2)}) collective-permute-start(bf16[4,4,16,192]{3,2,1,0:T(8,128)(2,1)} %get-tuple-element.22.grad), channel_id=1, source_target_pairs={{0,64},{64,128},{128,192},{192,256},{256,320},{320,384},{384,448},... | collective-permute-start | bytes 294920 | tf_op jit(solution)/shard_map/ppermute | solution.py:355
  25.5 1.3 collective-permute-done.slab_low
  26.9 4.0 %all-to-all-done.block = bf16[32,16,128]{2,1,0:T(8,128)(2,1)S(1)} async-done(((bf16[32,16,128]{2,1,0:T(8,128)(2,1)}), bf16[32,16,128]{2,1,0:T(8,128)(2,1)S(1)}, u32[]{:S(2)}, u32[]{:S(2)}) %all-to-all-start) | async-done | bytes 131104 | tf_op jit(solution)/shard_map/all_to_all | solution.py:329
  30.9 1.1 shard_map.113
  32.0 5.0 %all-to-all-start.1 = ((bf16[8,32,16,128]{3,2,1,0:T(8,128)(2,1)}), bf16[8,32,16,128]{3,2,1,0:T(8,128)(2,1)S(1)}, u32[]{:S(2)}, u32[]{:S(2)}) async-start(bf16[8,32,16,128]{3,2,1,0:T(8,128)(2,1)} %shard_map.113), calls=%async_computation.1 | async-start | bytes 2097152 | tf_op jit(solution)/shard_map/all_to_all | solution.py:329
  37.1 4.3 %collective-permute-start.2 = (bf16[1,4,16,192]{3,2,1,0:T(8,128)(2,1)S(1)}, bf16[1,4,16,192]{3,2,1,0:T(8,128)(2,1)S(1)}, u32[]{:S(2)}, u32[]{:S(2)}) collective-permute-start(bf16[1,4,16,192]{3,2,1,0:T(8,128)(2,1)S(1)} %copy-done.8), channel_id=1, source_target_pairs={{0,1},{1,0},{2,3},{3,2},{4,5},{5,4},{6,7},{7,6},{8,9},{9,8},{10,11... | collective-permute-start | bytes 73736 | tf_op jit(solution)/shard_map/ppermute | solution.py:358
  41.4 2.8 %collective-permute-start.3 = (bf16[1,4,16,192]{3,2,1,0:T(8,128)(2,1)S(1)}, bf16[1,4,16,192]{3,2,1,0:T(8,128)(2,1)S(1)}, u32[]{:S(2)}, u32[]{:S(2)}) collective-permute-start(bf16[1,4,16,192]{3,2,1,0:T(8,128)(2,1)S(1)} %copy-done.7), channel_id=1, source_target_pairs={{1,2},{3,4},{5,6},{7,8},{9,10},{11,12},{13,14},{15,16},{17,18},{19... | collective-permute-start | bytes 73736 | tf_op jit(solution)/shard_map/ppermute | solution.py:368
  44.2 2.7 %collective-permute-done.3.dev_far = bf16[1,4,16,192]{3,2,1,0:T(8,128)(2,1)S(1)} collective-permute-done((bf16[1,4,16,192]{3,2,1,0:T(8,128)(2,1)S(1)}, bf16[1,4,16,192]{3,2,1,0:T(8,128)(2,1)S(1)}, u32[]{:S(2)}, u32[]{:S(2)}) %collective-permute-start.3) | collective-permute-done | bytes 24608 | tf_op jit(solution)/shard_map/ppermute | solution.py:368
  47.5 7.0 %shard_map.114 = (bf16[8,24,2592]{2,1,0:T(8,128)(2,1)}, bf16[8,24,2592]{2,1,0:T(8,128)(2,1)}, bf16[3456,192]{1,0:T(8,128)(2,1)}) custom-call(s32[512]{0:T(512)} %counts_in.5, s32[4,27]{1,0:T(4,128)} %near_in.1, bf16[256,768]{1,0:T(8,128)(2,1)} %fine_in.3, bf16[192,768]{1,0:T(8,128)(2,1)} %bitcast.9, bf16[4,4,16,192]{3,2,1,0:T(8,128)(2,1)} %get-tuple-element.22.grad, ...), custom_call_target="tpu_custom_call" | custom-call | flops 6000000000 | tf_op jit(solution)/shard_map/pallas_call | solution.py:375
  54.6 1.9 %collective-permute-start.4 = (bf16[8,32,16,128]{3,2,1,0:T(8,128)(2,1)S(1)}, bf16[8,32,16,128]{3,2,1,0:T(8,128)(2,1)S(1)}, u32[]{:S(2)}, u32[]{:S(2)}) collective-permute-start(bf16[8,32,16,128]{3,2,1,0:T(8,128)(2,1)S(1)} %all-to-all-done.1.mine), channel_id=1, source_target_pairs={{0,1},{1,0},{2,3},{3,2},{4,5},{5,4},{6,7},{7,6},{8,9},{9,8},{10,11... | collective-permute-start | bytes 3145736 | tf_op jit(solution)/shard_map/ppermute | solution.py:358
  56.5 2.4 %collective-permute-start.5 = (bf16[8,24,2592]{2,1,0:T(8,128)(2,1)}, bf16[8,24,2592]{2,1,0:T(8,128)(2,1)S(1)}, u32[]{:S(2)}, u32[]{:S(2)}) collective-permute-start(bf16[8,24,2592]{2,1,0:T(8,128)(2,1)} %get-tuple-element.36), channel_id=1, source_target_pairs={{0,1},{1,0},{2,3},{3,2},{4,5},{5,4},{6,7},{7,6},{8,9},{9,8},{10,11... | collective-permute-start | bytes 2985992 | tf_op jit(solution)/shard_map/ppermute | solution.py:358
  59.1 1.0 copy-done.4
  60.1 4.6 %shard_map.115 = (bf16[256,192]{1,0:T(8,128)(2,1)}, bf16[2,24,24,128]{3,2,1,0:T(8,128)(2,1)}) custom-call(s32[512]{0:T(512)} %counts_in.5, bf16[256,768]{1,0:T(8,128)(2,1)} %fine_in.3, bf16[3456,192]{1,0:T(8,128)(2,1)} %get-tuple-element.31.taps_in, bf16[8,32,16,128]{3,2,1,0:T(8,128)(2,1)} %copy-done.3, bf16[8,32,16,128]{3,2,1,0:T(8,128)(2,1)} %copy-done.4), custom_call_target="tpu_custom_call" | custom-call | flops 4000000000 | tf_op jit(solution)/shard_map/pallas_call | solution.py:401
  64.7 2.6 %all-gather = bf16[4,24,24,128]{3,2,1,0:T(8,128)(2,1)S(1)} all-gather(bf16[2,24,24,128]{3,2,1,0:T(8,128)(2,1)} %get-tuple-element.34), channel_id=2, replica_groups=mesh['zl'=2,'x'=4,'zh'=4,'y'=8,'c'=2] {'c'}, dimensions={0}, use_global_device_ids=true | all-gather | bytes 884736 | tf_op jit(solution)/shard_map/all_gather | solution.py:430
  68.0 11.2 %all-to-all-start.2 = ((bf16[32,24,128]{2,1,0:T(8,128)(2,1)}), bf16[32,24,128]{2,1,0:T(8,128)(2,1)S(1)}, u32[]{:S(2)}, u32[]{:S(2)}) async-start(bf16[32,24,128]{2,1,0:T(8,128)(2,1)} %shard_map.117), calls=%async_computation.2 | async-start | bytes 393216 | tf_op jit(solution)/shard_map/all_to_all | solution.py:329
  79.2 11.9 %all-to-all-done.2.parts = bf16[32,24,128]{2,1,0:T(8,128)(2,1)S(1)} async-done(((bf16[32,24,128]{2,1,0:T(8,128)(2,1)}), bf16[32,24,128]{2,1,0:T(8,128)(2,1)S(1)}, u32[]{:S(2)}, u32[]{:S(2)}) %all-to-all-start.2) | async-done | bytes 196640 | tf_op jit(solution)/shard_map/all_to_all | solution.py:329
  91.4 18.2 %all_to_all.25.parts = bf16[8,24,2816]{2,1,0:T(8,128)(2,1)S(1)} all-to-all(bf16[8,24,2816]{2,1,0:T(8,128)(2,1)S(1)} %shard_map.118), channel_id=1, replica_groups=mesh['zl'=2,'x'=4,'zh'=4,'y'=8,'c'=2] {'zl','x'}, dimensions={0} | all-to-all | bytes 2162688 | tf_op jit(solution)/shard_map/all_to_all | solution.py:329
  110.5 6.7 %all-to-all-start.4 = ((bf16[32,2,24,128]{3,2,1,0:T(8,128)(2,1)}), bf16[32,2,24,128]{3,2,1,0:T(8,128)(2,1)S(1)}, u32[]{:S(2)}, u32[]{:S(2)}) async-start(bf16[32,2,24,128]{3,2,1,0:T(8,128)(2,1)} %shard_map.119), calls=%async_computation.4 | async-start | bytes 786432 | tf_op jit(solution)/shard_map/all_to_all | solution.py:329
  117.2 1.3 shard_map.116
  118.5 11.8 %all-to-all-done.4 = bf16[32,2,24,128]{3,2,1,0:T(8,128)(2,1)S(1)} async-done(((bf16[32,2,24,128]{3,2,1,0:T(8,128)(2,1)}), bf16[32,2,24,128]{3,2,1,0:T(8,128)(2,1)S(1)}, u32[]{:S(2)}, u32[]{:S(2)}) %all-to-all-start.4) | async-done | bytes 393248 | tf_op jit(solution)/shard_map/all_to_all | solution.py:329
  130.3 6.9 %all-gather.1 = bf16[64,2,24,128]{3,2,1,0:T(8,128)(2,1)S(1)} all-gather(bf16[32,2,24,128]{3,2,1,0:T(8,128)(2,1)S(1)} %all-to-all-done.4), channel_id=3, replica_groups=mesh['zl'=2,'x'=4,'zh'=4,'y'=8,'c'=2] {'c'}, dimensions={0}, use_global_device_ids=true | all-gather | bytes 1179648 | tf_op jit(solution)/shard_map/all_gather | solution.py:439
  (30 shorter events, 4.6 us)
Async XLA Ops:
  2.8 28.1 %all-to-all-start = ((bf16[32,16,128]{2,1,0:T(8,128)(2,1)}), bf16[32,16,128]{2,1,0:T(8,128)(2,1)S(1)}, u32[]{:S(2)}, u32[]{:S(2)}) async-start(bf16[32,16,128]{2,1,0:T(8,128)(2,1)} %get-tuple-element.21), calls=%async_computation | async-start | bytes 262144 | tf_op jit(solution)/shard_map/all_to_all | solution.py:329
  19.3 6.2 %collective-permute-start.1 = (bf16[4,4,16,192]{3,2,1,0:T(8,128)(2,1)}, bf16[4,4,16,192]{3,2,1,0:T(8,128)(2,1)S(1)}, u32[]{:S(2)}, u32[]{:S(2)}) collective-permute-start(bf16[4,4,16,192]{3,2,1,0:T(8,128)(2,1)} %get-tuple-element.22.grad), channel_id=1, source_target_pairs={{64,0},{128,64},{192,128},{256,192},{320,256},{384,320},{448,384},... | collective-permute-start | bytes 294920 | tf_op jit(solution)/shard_map/ppermute | solution.py:355
  20.6 6.2 %collective-permute-start = (bf16[4,4,16,192]{3,2,1,0:T(8,128)(2,1)}, bf16[4,4,16,192]{3,2,1,0:T(8,128)(2,1)S(1)}, u32[]{:S(2)}, u32[]{:S(2)}) collective-permute-start(bf16[4,4,16,192]{3,2,1,0:T(8,128)(2,1)} %get-tuple-element.22.grad), channel_id=1, source_target_pairs={{0,64},{64,128},{128,192},{192,256},{256,320},{320,384},{384,448},... | collective-permute-start | bytes 294920 | tf_op jit(solution)/shard_map/ppermute | solution.py:355
  25.5 6.5 %copy-start.5 = (bf16[4,4,16,192]{3,2,1,0:T(8,128)(2,1)}, bf16[4,4,16,192]{3,2,1,0:T(8,128)(2,1)S(1)}, u32[]{:S(2)}) copy-start(bf16[4,4,16,192]{3,2,1,0:T(8,128)(2,1)S(1)} %collective-permute-done.1.slab_high) | copy-start | bytes 294916
  26.9 5.2 %copy-start.6 = (bf16[4,4,16,192]{3,2,1,0:T(8,128)(2,1)}, bf16[4,4,16,192]{3,2,1,0:T(8,128)(2,1)S(1)}, u32[]{:S(2)}) copy-start(bf16[4,4,16,192]{3,2,1,0:T(8,128)(2,1)S(1)} %collective-permute-done.slab_low) | copy-start | bytes 294916
  32.0 5.1 %copy-start.8 = (bf16[1,4,16,192]{3,2,1,0:T(8,128)(2,1)S(1)}, bf16[1,4,16,192]{3,2,1,0:T(8,128)(2,1)}, u32[]{:S(2)}) copy-start(bf16[1,4,16,192]{3,2,1,0:T(8,128)(2,1)} %get-tuple-element.28) | copy-start | bytes 73732
  32.0 9.3 %copy-start.7 = (bf16[1,4,16,192]{3,2,1,0:T(8,128)(2,1)S(1)}, bf16[1,4,16,192]{3,2,1,0:T(8,128)(2,1)}, u32[]{:S(2)}) copy-start(bf16[1,4,16,192]{3,2,1,0:T(8,128)(2,1)} %get-tuple-element.29) | copy-start | bytes 73732
  32.0 22.5 %all-to-all-start.1 = ((bf16[8,32,16,128]{3,2,1,0:T(8,128)(2,1)}), bf16[8,32,16,128]{3,2,1,0:T(8,128)(2,1)S(1)}, u32[]{:S(2)}, u32[]{:S(2)}) async-start(bf16[8,32,16,128]{3,2,1,0:T(8,128)(2,1)} %shard_map.113), calls=%async_computation.1 | async-start | bytes 2097152 | tf_op jit(solution)/shard_map/all_to_all | solution.py:329
  37.1 7.1 %collective-permute-start.2 = (bf16[1,4,16,192]{3,2,1,0:T(8,128)(2,1)S(1)}, bf16[1,4,16,192]{3,2,1,0:T(8,128)(2,1)S(1)}, u32[]{:S(2)}, u32[]{:S(2)}) collective-permute-start(bf16[1,4,16,192]{3,2,1,0:T(8,128)(2,1)S(1)} %copy-done.8), channel_id=1, source_target_pairs={{0,1},{1,0},{2,3},{3,2},{4,5},{5,4},{6,7},{7,6},{8,9},{9,8},{10,11... | collective-permute-start | bytes 73736 | tf_op jit(solution)/shard_map/ppermute | solution.py:358
  41.4 5.5 %collective-permute-start.3 = (bf16[1,4,16,192]{3,2,1,0:T(8,128)(2,1)S(1)}, bf16[1,4,16,192]{3,2,1,0:T(8,128)(2,1)S(1)}, u32[]{:S(2)}, u32[]{:S(2)}) collective-permute-start(bf16[1,4,16,192]{3,2,1,0:T(8,128)(2,1)S(1)} %copy-done.7), channel_id=1, source_target_pairs={{1,2},{3,4},{5,6},{7,8},{9,10},{11,12},{13,14},{15,16},{17,18},{19... | collective-permute-start | bytes 73736 | tf_op jit(solution)/shard_map/ppermute | solution.py:368
  44.2 2.7 %copy-start.9 = (bf16[1,4,16,192]{3,2,1,0:T(8,128)(2,1)}, bf16[1,4,16,192]{3,2,1,0:T(8,128)(2,1)S(1)}, u32[]{:S(2)}) copy-start(bf16[1,4,16,192]{3,2,1,0:T(8,128)(2,1)S(1)} %collective-permute-done.2.dev_near) | copy-start | bytes 73732
  46.9 0.6 copy-start.10
  54.5 4.6 %copy-start.3 = (bf16[8,32,16,128]{3,2,1,0:T(8,128)(2,1)}, bf16[8,32,16,128]{3,2,1,0:T(8,128)(2,1)S(1)}, u32[]{:S(2)}) copy-start(bf16[8,32,16,128]{3,2,1,0:T(8,128)(2,1)S(1)} %all-to-all-done.1.mine) | copy-start | bytes 3145732
  54.6 4.6 %collective-permute-start.4 = (bf16[8,32,16,128]{3,2,1,0:T(8,128)(2,1)S(1)}, bf16[8,32,16,128]{3,2,1,0:T(8,128)(2,1)S(1)}, u32[]{:S(2)}, u32[]{:S(2)}) collective-permute-start(bf16[8,32,16,128]{3,2,1,0:T(8,128)(2,1)S(1)} %all-to-all-done.1.mine), channel_id=1, source_target_pairs={{0,1},{1,0},{2,3},{3,2},{4,5},{5,4},{6,7},{7,6},{8,9},{9,8},{10,11... | collective-permute-start | bytes 3145736 | tf_op jit(solution)/shard_map/ppermute | solution.py:358
  56.5 22.7 %collective-permute-start.5 = (bf16[8,24,2592]{2,1,0:T(8,128)(2,1)}, bf16[8,24,2592]{2,1,0:T(8,128)(2,1)S(1)}, u32[]{:S(2)}, u32[]{:S(2)}) collective-permute-start(bf16[8,24,2592]{2,1,0:T(8,128)(2,1)} %get-tuple-element.36), channel_id=1, source_target_pairs={{0,1},{1,0},{2,3},{3,2},{4,5},{5,4},{6,7},{7,6},{8,9},{9,8},{10,11... | collective-permute-start | bytes 2985992 | tf_op jit(solution)/shard_map/ppermute | solution.py:358
  59.1 1.0 copy-start.4
  64.7 26.4 %copy-start = (bf16[8,24,2592]{2,1,0:T(8,128)(2,1)S(1)}, bf16[8,24,2592]{2,1,0:T(8,128)(2,1)}, u32[]{:S(2)}) copy-start(bf16[8,24,2592]{2,1,0:T(8,128)(2,1)} %get-tuple-element.35.keep) | copy-start | bytes 2985988
  68.0 23.1 %all-to-all-start.2 = ((bf16[32,24,128]{2,1,0:T(8,128)(2,1)}), bf16[32,24,128]{2,1,0:T(8,128)(2,1)S(1)}, u32[]{:S(2)}, u32[]{:S(2)}) async-start(bf16[32,24,128]{2,1,0:T(8,128)(2,1)} %shard_map.117), calls=%async_computation.2 | async-start | bytes 393216 | tf_op jit(solution)/shard_map/all_to_all | solution.py:329
  109.5 7.7 %copy-start.1 = (bf16[768,192]{0,1:T(8,128)(2,1)S(1)}, bf16[768,192]{0,1:T(8,128)(2,1)}, u32[]{:S(2)}) copy-start(bf16[768,192]{0,1:T(8,128)(2,1)} %param.10) | copy-start | bytes 884740
  109.5 7.7 %copy-start.2 = (bf16[256,192]{1,0:T(8,128)(2,1)S(1)}, bf16[256,192]{1,0:T(8,128)(2,1)}, u32[]{:S(2)}) copy-start(bf16[256,192]{1,0:T(8,128)(2,1)} %get-tuple-element.33.gm_in) | copy-start | bytes 294916
  110.5 19.8 %all-to-all-start.4 = ((bf16[32,2,24,128]{3,2,1,0:T(8,128)(2,1)}), bf16[32,2,24,128]{3,2,1,0:T(8,128)(2,1)S(1)}, u32[]{:S(2)}, u32[]{:S(2)}) async-start(bf16[32,2,24,128]{3,2,1,0:T(8,128)(2,1)} %shard_map.119), calls=%async_computation.4 | async-start | bytes 786432 | tf_op jit(solution)/shard_map/all_to_all | solution.py:329

commit v11 on v10

--- a/solution.py
+++ b/solution.py
@@ -21,7 +21,6 @@
 HALF = 32 * ROWS
 COLS = C // SLABS
 PIECES = 48
-WIDE = 2688
 
 VMEM = pl.BlockSpec(memory_space=pltpu.VMEM)
 HBM = pl.BlockSpec(memory_space=pltpu.HBM)
@@ -272,24 +271,38 @@
         out[i] = jnp.zeros((24, 128), BF16)
 
 
-def spread_kernel(parts, keep, received, out):
+def spread_kernel(parts, out):
+    total = parts[0].astype(F32)
+    for i in range(1, 32):
+        total = total + parts[i].astype(F32)
+    for i in range(SLABS):
+        out[i] = total.astype(BF16)
+
+
+def split_kernel(keep, received, *outs):
+    x = lax.axis_index("x")
+    for dx, out in enumerate(outs):
+        for zl in range(2):
+            slab = zl * 4 + jnp.bitwise_and(x + dx, 3)
+            out[zl] = (keep[slab].astype(F32) + received[slab].astype(F32)).astype(BF16)
+
+
+def halve_kernel(a, b, c, d, keep, send):
+    zl = lax.axis_index("zl")
+    for out, half in ((keep, zl), (send, 1 - zl)):
+        total = a[half].astype(F32) + b[half].astype(F32) + c[half].astype(F32)
+        out[...] = (total + d[half].astype(F32)).astype(BF16)
+
+
+def both_kernel(parts, keep, received, out):
     merge = parts[0].astype(F32)
-    for i in range(1, 32):
+    for i in range(1, SLABS):
         merge = merge + parts[i].astype(F32)
-    for i in range(SLABS):
-        out[i, :, :HALF] = (keep[i].astype(F32) + received[i].astype(F32)).astype(BF16)
-        out[i, :, HALF:WIDE] = jnp.zeros((COLS, WIDE - HALF), BF16)
-        out[i, :, WIDE:] = merge.astype(BF16)
-
-
-def both_kernel(parts, out):
-    total = parts[0].astype(F32)
-    for i in range(1, SLABS):
-        total = total + parts[i].astype(F32)
-    merge = total[:, WIDE:].astype(BF16)
+    merge = merge.astype(BF16)
+    conv = keep[...].astype(F32) + received[...].astype(F32)
     pad = jnp.zeros((COLS, 128 - ROWS), BF16)
     for i in range(32):
-        piece = total[:, i * ROWS : (i + 1) * ROWS].astype(BF16)
+        piece = conv[:, i * ROWS : (i + 1) * ROWS].astype(BF16)
         out[i, 0] = jnp.concatenate([piece, pad], axis=1)
         out[i, 1] = merge
 
@@ -360,10 +373,10 @@
     slab_low = shifted(grad, SLAB, SLABS, 1)
     slab_high = shifted(grad, SLAB, SLABS, -1)
     frames = swap(frames, ("zh", "y"))
-    frames, slab_low, slab_high, near, far = lax.optimization_barrier(
-        (frames, slab_low, slab_high, near, far)
-    )
     dev_near = flipped(near)
+    frames, slab_low, slab_high, dev_near, far = lax.optimization_barrier(
+        (frames, slab_low, slab_high, dev_near, far)
+    )
     ups = [(i, i + 1) for i in range(1, DEVS - 1, 2)]
     dev_far = lax.ppermute(far, DEV, ups + [(j, i) for i, j in ups])
     frames = call(repeat_kernel, shape(SLABS, 32, 16, 128), [VMEM])(frames)
@@ -430,11 +443,16 @@
     term = lax.all_gather(term, "c", axis=0, tiled=False)
     term = call(join_kernel, shape(32, 24, 128), [VMEM])(term)
     term = swap(term, ("zh", "y"))
-    term = call(spread_kernel, shape(SLABS, COLS, WIDE + 128), [VMEM] * 3)(
-        term, keep, flipped(send)
-    )
+    term = call(spread_kernel, shape(SLABS, 24, 128), [VMEM])(term)
+    conv = call(split_kernel, (shape(2, COLS, HALF),) * 4, [VMEM] * 2)(keep, flipped(send))
+    moved = [
+        lax.ppermute(conv[dx], "x", [(i, (i + dx) % 4) for i in range(4)]) for dx in (1, 2, 3)
+    ]
+    term, moved = lax.optimization_barrier((term, moved))
     term = swap(term, SLAB)
-    term = call(both_kernel, shape(32, 2, 24, 128), [VMEM])(term)
+    keep, send = call(halve_kernel, (shape(COLS, HALF),) * 2, [VMEM] * 4)(conv[0], *moved)
+    received = lax.ppermute(send, "zl", [(0, 1), (1, 0)])
+    term = call(both_kernel, shape(32, 2, 24, 128), [VMEM] * 3)(term, keep, received)
     term = swap(term, ("zh", "y"))
     term = lax.all_gather(term, "c", axis=0, tiled=False)
     merge_grad, conv_grad = call(

time: 139 us -> 143 us (1.029)
  starting transfers between devices: 56.1 us -> 76.1 us
  blocking collectives: 27.6 us -> 19.2 us
  waiting for transfers between devices: 32.8 us -> 25.3 us
    ppermute x0 -> x4, starting transfers between devices: none -> 14.2 us  [the longest x3 11.2 us: local(): lax.ppermute(conv[dx], 'x', [(i, (i + dx) % 4) for i in range(4)])]
    all_to_all x4, waiting for transfers between devices: 27.7 us -> 14.3 us  [swap(): return lax.all_to_all(x, axes, 0, 0, tiled=True)]
    all_to_all x1, blocking collectives: 18.2 us -> 9.65 us  [swap(): return lax.all_to_all(x, axes, 0, 0, tiled=True)]
    ppermute x0 -> x4, waiting for transfers between devices: none -> 7.02 us  [the longest x3 7.01 us: local(): lax.ppermute(conv[dx], 'x', [(i, (i + dx) % 4) for i in range(4)])]
    all_to_all x4, starting transfers between devices: 39.4 us -> 44.3 us  [swap(): return lax.all_to_all(x, axes, 0, 0, tiled=True)]
    ppermute x1, starting transfers between devices: 2.83 us -> 5.17 us  [local(): dev_far = lax.ppermute(far, DEV, ups + [(j, i) for i, j in ups])]
    ppermute x2, waiting for transfers between devices: 2.24 us -> 0.71 us  [shifted(): return lax.ppermute(x, axes, pairs)]
  transfers between devices with their start and end apart: 10 -> 14, of which waited for: 7 -> 9; matrix products, arithmetic and copies ran while one was open for 0% -> 0% of each run, Pallas kernels for 10% -> 10%
where the time goes in v11:
time: 143 us; the launch traced here: 142 us
  starting transfers between devices  76.1 us (53%)
  waiting for transfers between devices  25.3 us (18%)
  blocking collectives  19.2 us (13%)
  Pallas kernels  19.1 us (13%)
  local copies, waits for them, and re-layouts  1.63 us (1%)
    all_to_all x4, starting transfers between devices, swap(): return lax.all_to_all(x, axes, 0, 0, tiled=True)  44.3 us
    all_to_all x4, waiting for transfers between devices, swap(): return lax.all_to_all(x, axes, 0, 0, tiled=True)  14.3 us
    ppermute x3, starting transfers between devices, local(): lax.ppermute(conv[dx], 'x', [(i, (i + dx) % 4) for i in range(4)])  11.2 us
    all_to_all x1, blocking collectives, swap(): return lax.all_to_all(x, axes, 0, 0, tiled=True)  9.65 us
    all_gather x2, blocking collectives, local(): term = lax.all_gather(term, 'c', axis=0, tiled=False)  9.56 us
    ppermute x3, starting transfers between devices, flipped(): return lax.ppermute(x, 'c', [(0, 1), (1, 0)])  7.99 us
    pallas_call x1, Pallas kernels, local(): call(conv_kernel, (shape(SLABS, COLS, HALF), shape(SLABS, COLS, HALF), sh...  7.02 us
    ppermute x3, waiting for transfers between devices, local(): lax.ppermute(conv[dx], 'x', [(i, (i + dx) % 4) for i in range(4)])  7.01 us
  transfers between devices with their start and end apart: 14, of which 9 were waited for; matrix products, arithmetic and copies ran while one was open for 0% of the time, Pallas kernels for 10%

profile of v11, /device:TPU:1, one launch (start us, length us, event | category | flops | bytes accessed | tf_op | source)
XLA Modules:
  0.0 142.3 jit_solution(141885028733794309)
XLA Ops:
  0.6 2.2 %shard_map.112 = (bf16[4,4,16,192]{3,2,1,0:T(8,128)(2,1)}, bf16[1,4,16,192]{3,2,1,0:T(8,128)(2,1)}, bf16[1,4,16,192]{3,2,1,0:T(8,128)(2,1)}, bf16[32,16,128]{2,1,0:T(8,128)(2,1)}) custom-call(s32[512]{0:T(512)} %counts_in.5, bf16[4,16,768]{2,1,0:T(8,128)(2,1)} %pre_in.1, bf16[4,16,768]{2,1,0:T(8,128)(2,1)} %cot_in.1, f32[1,192]{1,0:T(1,128)} %bitcast.11, ...), custom_call_target="tpu_custom_call" | custom-call | tf_op jit(solution)/shard_map/pallas_call | solution.py:349
  2.8 16.5 %all-to-all-start = ((bf16[32,16,128]{2,1,0:T(8,128)(2,1)}), bf16[32,16,128]{2,1,0:T(8,128)(2,1)S(1)}, u32[]{:S(2)}, u32[]{:S(2)}) async-start(bf16[32,16,128]{2,1,0:T(8,128)(2,1)} %get-tuple-element.31), calls=%async_computation | async-start | bytes 262144 | tf_op jit(solution)/shard_map/all_to_all | solution.py:342
  19.3 3.1 %collective-permute-start = (bf16[4,4,16,192]{3,2,1,0:T(8,128)(2,1)}, bf16[4,4,16,192]{3,2,1,0:T(8,128)(2,1)S(1)}, u32[]{:S(2)}, u32[]{:S(2)}) collective-permute-start(bf16[4,4,16,192]{3,2,1,0:T(8,128)(2,1)} %get-tuple-element.32.grad), channel_id=1, source_target_pairs={{0,64},{64,128},{128,192},{192,256},{256,320},{320,384},{384,448},... | collective-permute-start | bytes 294920 | tf_op jit(solution)/shard_map/ppermute | solution.py:368
  23.8 3.1 %collective-permute-start.2 = (bf16[1,4,16,192]{3,2,1,0:T(8,128)(2,1)}, bf16[1,4,16,192]{3,2,1,0:T(8,128)(2,1)S(1)}, u32[]{:S(2)}, u32[]{:S(2)}) collective-permute-start(bf16[1,4,16,192]{3,2,1,0:T(8,128)(2,1)} %get-tuple-element.33), channel_id=1, source_target_pairs={{0,1},{1,0},{2,3},{3,2},{4,5},{5,4},{6,7},{7,6},{8,9},{9,8},{10,11... | collective-permute-start | bytes 73736 | tf_op jit(solution)/shard_map/ppermute | solution.py:371
  28.7 2.2 %all-to-all-done.block = bf16[32,16,128]{2,1,0:T(8,128)(2,1)S(1)} async-done(((bf16[32,16,128]{2,1,0:T(8,128)(2,1)}), bf16[32,16,128]{2,1,0:T(8,128)(2,1)S(1)}, u32[]{:S(2)}, u32[]{:S(2)}) %all-to-all-start) | async-done | bytes 131104 | tf_op jit(solution)/shard_map/all_to_all | solution.py:342
  32.0 4.9 %all-to-all-start.1 = ((bf16[8,32,16,128]{3,2,1,0:T(8,128)(2,1)}), bf16[8,32,16,128]{3,2,1,0:T(8,128)(2,1)S(1)}, u32[]{:S(2)}, u32[]{:S(2)}) async-start(bf16[8,32,16,128]{3,2,1,0:T(8,128)(2,1)} %shard_map.113), calls=%async_computation.1 | async-start | bytes 2097152 | tf_op jit(solution)/shard_map/all_to_all | solution.py:342
  36.9 5.2 %collective-permute-start.3 = (bf16[1,4,16,192]{3,2,1,0:T(8,128)(2,1)S(1)}, bf16[1,4,16,192]{3,2,1,0:T(8,128)(2,1)S(1)}, u32[]{:S(2)}, u32[]{:S(2)}) collective-permute-start(bf16[1,4,16,192]{3,2,1,0:T(8,128)(2,1)S(1)} %copy-done.7), channel_id=1, source_target_pairs={{1,2},{3,4},{5,6},{7,8},{9,10},{11,12},{13,14},{15,16},{17,18},{19... | collective-permute-start | bytes 73736 | tf_op jit(solution)/shard_map/ppermute | solution.py:381
  42.1 1.9 %collective-permute-done.3.dev_far = bf16[1,4,16,192]{3,2,1,0:T(8,128)(2,1)S(1)} collective-permute-done((bf16[1,4,16,192]{3,2,1,0:T(8,128)(2,1)S(1)}, bf16[1,4,16,192]{3,2,1,0:T(8,128)(2,1)S(1)}, u32[]{:S(2)}, u32[]{:S(2)}) %collective-permute-start.3) | collective-permute-done | bytes 24608 | tf_op jit(solution)/shard_map/ppermute | solution.py:381
  44.6 7.0 %shard_map.114 = (bf16[8,24,2592]{2,1,0:T(8,128)(2,1)}, bf16[8,24,2592]{2,1,0:T(8,128)(2,1)}, bf16[3456,192]{1,0:T(8,128)(2,1)}) custom-call(s32[512]{0:T(512)} %counts_in.5, s32[4,27]{1,0:T(4,128)} %near_in.1, bf16[256,768]{1,0:T(8,128)(2,1)} %fine_in.3, bf16[192,768]{1,0:T(8,128)(2,1)} %bitcast.9, bf16[4,4,16,192]{3,2,1,0:T(8,128)(2,1)} %get-tuple-element.32.grad, ...), custom_call_target="tpu_custom_call" | custom-call | flops 6000000000 | tf_op jit(solution)/shard_map/pallas_call | solution.py:388
  51.7 2.9 %collective-permute-start.4 = (bf16[8,32,16,128]{3,2,1,0:T(8,128)(2,1)S(1)}, bf16[8,32,16,128]{3,2,1,0:T(8,128)(2,1)S(1)}, u32[]{:S(2)}, u32[]{:S(2)}) collective-permute-start(bf16[8,32,16,128]{3,2,1,0:T(8,128)(2,1)S(1)} %all-to-all-done.1.mine), channel_id=1, source_target_pairs={{0,1},{1,0},{2,3},{3,2},{4,5},{5,4},{6,7},{7,6},{8,9},{9,8},{10,11... | collective-permute-start | bytes 3145736 | tf_op jit(solution)/shard_map/ppermute | solution.py:371
  54.6 1.9 %collective-permute-start.5 = (bf16[8,24,2592]{2,1,0:T(8,128)(2,1)}, bf16[8,24,2592]{2,1,0:T(8,128)(2,1)S(1)}, u32[]{:S(2)}, u32[]{:S(2)}) collective-permute-start(bf16[8,24,2592]{2,1,0:T(8,128)(2,1)} %get-tuple-element.46), channel_id=1, source_target_pairs={{0,1},{1,0},{2,3},{3,2},{4,5},{5,4},{6,7},{7,6},{8,9},{9,8},{10,11... | collective-permute-start | bytes 2985992 | tf_op jit(solution)/shard_map/ppermute | solution.py:371
  57.9 4.6 %shard_map.115 = (bf16[256,192]{1,0:T(8,128)(2,1)}, bf16[2,24,24,128]{3,2,1,0:T(8,128)(2,1)}) custom-call(s32[512]{0:T(512)} %counts_in.5, bf16[256,768]{1,0:T(8,128)(2,1)} %fine_in.3, bf16[3456,192]{1,0:T(8,128)(2,1)} %get-tuple-element.41.taps_in, bf16[8,32,16,128]{3,2,1,0:T(8,128)(2,1)} %copy-done.3, bf16[8,32,16,128]{3,2,1,0:T(8,128)(2,1)} %copy-done.4), custom_call_target="tpu_custom_call" | custom-call | flops 4000000000 | tf_op jit(solution)/shard_map/pallas_call | solution.py:414
  62.5 2.6 %all-gather = bf16[4,24,24,128]{3,2,1,0:T(8,128)(2,1)S(1)} all-gather(bf16[2,24,24,128]{3,2,1,0:T(8,128)(2,1)} %get-tuple-element.44), channel_id=2, replica_groups=mesh['zl'=2,'x'=4,'zh'=4,'y'=8,'c'=2] {'c'}, dimensions={0}, use_global_device_ids=true | all-gather | bytes 884736 | tf_op jit(solution)/shard_map/all_gather | solution.py:443
  65.8 11.3 %all-to-all-start.2 = ((bf16[32,24,128]{2,1,0:T(8,128)(2,1)}), bf16[32,24,128]{2,1,0:T(8,128)(2,1)S(1)}, u32[]{:S(2)}, u32[]{:S(2)}) async-start(bf16[32,24,128]{2,1,0:T(8,128)(2,1)} %shard_map.117), calls=%async_computation.2 | async-start | bytes 393216 | tf_op jit(solution)/shard_map/all_to_all | solution.py:342
  77.4 3.8 %collective-permute-start.6 = (bf16[2,24,2592]{2,1,0:T(8,128)(2,1)S(1)}, bf16[2,24,2592]{2,1,0:T(8,128)(2,1)S(1)}, u32[]{:S(2)}, u32[]{:S(2)}) collective-permute-start(bf16[2,24,2592]{2,1,0:T(8,128)(2,1)S(1)} %get-tuple-element.47), channel_id=1, source_target_pairs={{0,64},{64,128},{128,192},{192,0},{1,65},{65,129},{129,193},{193,1... | collective-permute-start | bytes 746504 | tf_op jit(solution)/shard_map/ppermute | solution.py:449
  81.2 4.3 %collective-permute-start.7 = (bf16[2,24,2592]{2,1,0:T(8,128)(2,1)S(1)}, bf16[2,24,2592]{2,1,0:T(8,128)(2,1)S(1)}, u32[]{:S(2)}, u32[]{:S(2)}) collective-permute-start(bf16[2,24,2592]{2,1,0:T(8,128)(2,1)S(1)} %get-tuple-element.48), channel_id=1, source_target_pairs={{0,128},{64,192},{128,0},{192,64},{1,129},{65,193},{129,1},{193,65... | collective-permute-start | bytes 746504 | tf_op jit(solution)/shard_map/ppermute | solution.py:449
  85.5 3.1 %collective-permute-start.8 = (bf16[2,24,2592]{2,1,0:T(8,128)(2,1)S(1)}, bf16[2,24,2592]{2,1,0:T(8,128)(2,1)S(1)}, u32[]{:S(2)}, u32[]{:S(2)}) collective-permute-start(bf16[2,24,2592]{2,1,0:T(8,128)(2,1)S(1)} %get-tuple-element.49), channel_id=1, source_target_pairs={{0,192},{64,0},{128,64},{192,128},{1,193},{65,1},{129,65},{193,129... | collective-permute-start | bytes 746504 | tf_op jit(solution)/shard_map/ppermute | solution.py:449
  89.0 5.7 %collective-permute-done.7.c = bf16[2,24,2592]{2,1,0:T(8,128)(2,1)S(1)} collective-permute-done((bf16[2,24,2592]{2,1,0:T(8,128)(2,1)S(1)}, bf16[2,24,2592]{2,1,0:T(8,128)(2,1)S(1)}, u32[]{:S(2)}, u32[]{:S(2)}) %collective-permute-start.7) | collective-permute-done | bytes 248864 | tf_op jit(solution)/shard_map/ppermute | solution.py:449
  94.7 1.3 collective-permute-done.8.d
  96.2 3.1 %collective-permute-start.9 = (bf16[24,2592]{1,0:T(8,128)(2,1)S(1)}, bf16[24,2592]{1,0:T(8,128)(2,1)S(1)}, u32[]{:S(2)}, u32[]{:S(2)}) collective-permute-start(bf16[24,2592]{1,0:T(8,128)(2,1)S(1)} %get-tuple-element.56), channel_id=1, source_target_pairs={{0,256},{256,0},{1,257},{257,1},{2,258},{258,2},{3,259},{259,3},{4... | collective-permute-start | bytes 373256 | tf_op jit(solution)/shard_map/ppermute | solution.py:454
  99.2 9.7 %all_to_all.25.parts = bf16[8,24,128]{2,1,0:T(8,128)(2,1)S(1)} all-to-all(bf16[8,24,128]{2,1,0:T(8,128)(2,1)S(1)} %shard_map.118), channel_id=1, replica_groups=mesh['zl'=2,'x'=4,'zh'=4,'y'=8,'c'=2] {'zl','x'}, dimensions={0} | all-to-all | bytes 98304 | tf_op jit(solution)/shard_map/all_to_all | solution.py:342
  109.8 11.6 %all-to-all-start.4 = ((bf16[32,2,24,128]{3,2,1,0:T(8,128)(2,1)}), bf16[32,2,24,128]{3,2,1,0:T(8,128)(2,1)S(1)}, u32[]{:S(2)}, u32[]{:S(2)}) async-start(bf16[32,2,24,128]{3,2,1,0:T(8,128)(2,1)} %shard_map.121), calls=%async_computation.4 | async-start | bytes 786432 | tf_op jit(solution)/shard_map/all_to_all | solution.py:342
  122.7 11.7 %all-to-all-done.4 = bf16[32,2,24,128]{3,2,1,0:T(8,128)(2,1)S(1)} async-done(((bf16[32,2,24,128]{3,2,1,0:T(8,128)(2,1)}), bf16[32,2,24,128]{3,2,1,0:T(8,128)(2,1)S(1)}, u32[]{:S(2)}, u32[]{:S(2)}) %all-to-all-start.4) | async-done | bytes 393248 | tf_op jit(solution)/shard_map/all_to_all | solution.py:342
  134.4 7.0 %all-gather.1 = bf16[64,2,24,128]{3,2,1,0:T(8,128)(2,1)S(1)} all-gather(bf16[32,2,24,128]{3,2,1,0:T(8,128)(2,1)S(1)} %all-to-all-done.4), channel_id=3, replica_groups=mesh['zl'=2,'x'=4,'zh'=4,'y'=8,'c'=2] {'c'}, dimensions={0}, use_global_device_ids=true | all-gather | bytes 1179648 | tf_op jit(solution)/shard_map/all_gather | solution.py:457
  (38 shorter events, 10.7 us)
Async XLA Ops:
  2.8 34.1 %copy-start.7 = (bf16[1,4,16,192]{3,2,1,0:T(8,128)(2,1)S(1)}, bf16[1,4,16,192]{3,2,1,0:T(8,128)(2,1)}, u32[]{:S(2)}) copy-start(bf16[1,4,16,192]{3,2,1,0:T(8,128)(2,1)} %get-tuple-element.39) | copy-start | bytes 73732
  2.8 28.1 %all-to-all-start = ((bf16[32,16,128]{2,1,0:T(8,128)(2,1)}), bf16[32,16,128]{2,1,0:T(8,128)(2,1)S(1)}, u32[]{:S(2)}, u32[]{:S(2)}) async-start(bf16[32,16,128]{2,1,0:T(8,128)(2,1)} %get-tuple-element.31), calls=%async_computation | async-start | bytes 262144 | tf_op jit(solution)/shard_map/all_to_all | solution.py:342
  19.3 8.6 %collective-permute-start = (bf16[4,4,16,192]{3,2,1,0:T(8,128)(2,1)}, bf16[4,4,16,192]{3,2,1,0:T(8,128)(2,1)S(1)}, u32[]{:S(2)}, u32[]{:S(2)}) collective-permute-start(bf16[4,4,16,192]{3,2,1,0:T(8,128)(2,1)} %get-tuple-element.32.grad), channel_id=1, source_target_pairs={{0,64},{64,128},{128,192},{192,256},{256,320},{320,384},{384,448},... | collective-permute-start | bytes 294920 | tf_op jit(solution)/shard_map/ppermute | solution.py:368
  22.5 6.2 %collective-permute-start.1 = (bf16[4,4,16,192]{3,2,1,0:T(8,128)(2,1)}, bf16[4,4,16,192]{3,2,1,0:T(8,128)(2,1)S(1)}, u32[]{:S(2)}, u32[]{:S(2)}) collective-permute-start(bf16[4,4,16,192]{3,2,1,0:T(8,128)(2,1)} %get-tuple-element.32.grad), channel_id=1, source_target_pairs={{64,0},{128,64},{192,128},{256,192},{320,256},{384,320},{448,384},... | collective-permute-start | bytes 294920 | tf_op jit(solution)/shard_map/ppermute | solution.py:368
  23.8 4.2 %collective-permute-start.2 = (bf16[1,4,16,192]{3,2,1,0:T(8,128)(2,1)}, bf16[1,4,16,192]{3,2,1,0:T(8,128)(2,1)S(1)}, u32[]{:S(2)}, u32[]{:S(2)}) collective-permute-start(bf16[1,4,16,192]{3,2,1,0:T(8,128)(2,1)} %get-tuple-element.33), channel_id=1, source_target_pairs={{0,1},{1,0},{2,3},{3,2},{4,5},{5,4},{6,7},{7,6},{8,9},{9,8},{10,11... | collective-permute-start | bytes 73736 | tf_op jit(solution)/shard_map/ppermute | solution.py:371
  28.0 16.0 %copy-start.8 = (bf16[1,4,16,192]{3,2,1,0:T(8,128)(2,1)}, bf16[1,4,16,192]{3,2,1,0:T(8,128)(2,1)S(1)}, u32[]{:S(2)}) copy-start(bf16[1,4,16,192]{3,2,1,0:T(8,128)(2,1)S(1)} %collective-permute-done.2.dev_near) | copy-start | bytes 73732
  28.0 16.0 %copy-start.5 = (bf16[4,4,16,192]{3,2,1,0:T(8,128)(2,1)}, bf16[4,4,16,192]{3,2,1,0:T(8,128)(2,1)S(1)}, u32[]{:S(2)}) copy-start(bf16[4,4,16,192]{3,2,1,0:T(8,128)(2,1)S(1)} %collective-permute-done.slab_low) | copy-start | bytes 294916
  28.7 15.3 %copy-start.6 = (bf16[4,4,16,192]{3,2,1,0:T(8,128)(2,1)}, bf16[4,4,16,192]{3,2,1,0:T(8,128)(2,1)S(1)}, u32[]{:S(2)}) copy-start(bf16[4,4,16,192]{3,2,1,0:T(8,128)(2,1)S(1)} %collective-permute-done.1.slab_high) | copy-start | bytes 294916
  32.0 19.6 %all-to-all-start.1 = ((bf16[8,32,16,128]{3,2,1,0:T(8,128)(2,1)}), bf16[8,32,16,128]{3,2,1,0:T(8,128)(2,1)S(1)}, u32[]{:S(2)}, u32[]{:S(2)}) async-start(bf16[8,32,16,128]{3,2,1,0:T(8,128)(2,1)} %shard_map.113), calls=%async_computation.1 | async-start | bytes 2097152 | tf_op jit(solution)/shard_map/all_to_all | solution.py:342
  36.9 7.1 %collective-permute-start.3 = (bf16[1,4,16,192]{3,2,1,0:T(8,128)(2,1)S(1)}, bf16[1,4,16,192]{3,2,1,0:T(8,128)(2,1)S(1)}, u32[]{:S(2)}, u32[]{:S(2)}) collective-permute-start(bf16[1,4,16,192]{3,2,1,0:T(8,128)(2,1)S(1)} %copy-done.7), channel_id=1, source_target_pairs={{1,2},{3,4},{5,6},{7,8},{9,10},{11,12},{13,14},{15,16},{17,18},{19... | collective-permute-start | bytes 73736 | tf_op jit(solution)/shard_map/ppermute | solution.py:381
  44.0 0.6 copy-start.9
  51.7 5.2 %copy-start.3 = (bf16[8,32,16,128]{3,2,1,0:T(8,128)(2,1)}, bf16[8,32,16,128]{3,2,1,0:T(8,128)(2,1)S(1)}, u32[]{:S(2)}) copy-start(bf16[8,32,16,128]{3,2,1,0:T(8,128)(2,1)S(1)} %all-to-all-done.1.mine) | copy-start | bytes 3145732
  51.7 5.2 %collective-permute-start.4 = (bf16[8,32,16,128]{3,2,1,0:T(8,128)(2,1)S(1)}, bf16[8,32,16,128]{3,2,1,0:T(8,128)(2,1)S(1)}, u32[]{:S(2)}, u32[]{:S(2)}) collective-permute-start(bf16[8,32,16,128]{3,2,1,0:T(8,128)(2,1)S(1)} %all-to-all-done.1.mine), channel_id=1, source_target_pairs={{0,1},{1,0},{2,3},{3,2},{4,5},{5,4},{6,7},{7,6},{8,9},{9,8},{10,11... | collective-permute-start | bytes 3145736 | tf_op jit(solution)/shard_map/ppermute | solution.py:371
  54.6 22.5 %collective-permute-start.5 = (bf16[8,24,2592]{2,1,0:T(8,128)(2,1)}, bf16[8,24,2592]{2,1,0:T(8,128)(2,1)S(1)}, u32[]{:S(2)}, u32[]{:S(2)}) collective-permute-start(bf16[8,24,2592]{2,1,0:T(8,128)(2,1)} %get-tuple-element.46), channel_id=1, source_target_pairs={{0,1},{1,0},{2,3},{3,2},{4,5},{5,4},{6,7},{7,6},{8,9},{9,8},{10,11... | collective-permute-start | bytes 2985992 | tf_op jit(solution)/shard_map/ppermute | solution.py:371
  56.9 1.0 copy-start.4
  62.5 14.6 %copy-start = (bf16[8,24,2592]{2,1,0:T(8,128)(2,1)S(1)}, bf16[8,24,2592]{2,1,0:T(8,128)(2,1)}, u32[]{:S(2)}) copy-start(bf16[8,24,2592]{2,1,0:T(8,128)(2,1)} %get-tuple-element.45.keep) | copy-start | bytes 2985988
  65.8 23.2 %all-to-all-start.2 = ((bf16[32,24,128]{2,1,0:T(8,128)(2,1)}), bf16[32,24,128]{2,1,0:T(8,128)(2,1)S(1)}, u32[]{:S(2)}, u32[]{:S(2)}) async-start(bf16[32,24,128]{2,1,0:T(8,128)(2,1)} %shard_map.117), calls=%async_computation.2 | async-start | bytes 393216 | tf_op jit(solution)/shard_map/all_to_all | solution.py:342
  77.4 44.1 %copy-start.1 = (bf16[768,192]{0,1:T(8,128)(2,1)S(1)}, bf16[768,192]{0,1:T(8,128)(2,1)}, u32[]{:S(2)}) copy-start(bf16[768,192]{0,1:T(8,128)(2,1)} %param.10) | copy-start | bytes 884740
  77.4 44.1 %copy-start.2 = (bf16[256,192]{1,0:T(8,128)(2,1)S(1)}, bf16[256,192]{1,0:T(8,128)(2,1)}, u32[]{:S(2)}) copy-start(bf16[256,192]{1,0:T(8,128)(2,1)} %get-tuple-element.43.gm_in) | copy-start | bytes 294916
  77.4 11.6 %collective-permute-start.6 = (bf16[2,24,2592]{2,1,0:T(8,128)(2,1)S(1)}, bf16[2,24,2592]{2,1,0:T(8,128)(2,1)S(1)}, u32[]{:S(2)}, u32[]{:S(2)}) collective-permute-start(bf16[2,24,2592]{2,1,0:T(8,128)(2,1)S(1)} %get-tuple-element.47), channel_id=1, source_target_pairs={{0,64},{64,128},{128,192},{192,0},{1,65},{65,129},{129,193},{193,1... | collective-permute-start | bytes 746504 | tf_op jit(solution)/shard_map/ppermute | solution.py:449
  81.2 13.5 %collective-permute-start.7 = (bf16[2,24,2592]{2,1,0:T(8,128)(2,1)S(1)}, bf16[2,24,2592]{2,1,0:T(8,128)(2,1)S(1)}, u32[]{:S(2)}, u32[]{:S(2)}) collective-permute-start(bf16[2,24,2592]{2,1,0:T(8,128)(2,1)S(1)} %get-tuple-element.48), channel_id=1, source_target_pairs={{0,128},{64,192},{128,0},{192,64},{1,129},{65,193},{129,1},{193,65... | collective-permute-start | bytes 746504 | tf_op jit(solution)/shard_map/ppermute | solution.py:449
  85.5 10.5 %collective-permute-start.8 = (bf16[2,24,2592]{2,1,0:T(8,128)(2,1)S(1)}, bf16[2,24,2592]{2,1,0:T(8,128)(2,1)S(1)}, u32[]{:S(2)}, u32[]{:S(2)}) collective-permute-start(bf16[2,24,2592]{2,1,0:T(8,128)(2,1)S(1)} %get-tuple-element.49), channel_id=1, source_target_pairs={{0,192},{64,0},{128,64},{192,128},{1,193},{65,1},{129,65},{193,129... | collective-permute-start | bytes 746504 | tf_op jit(solution)/shard_map/ppermute | solution.py:449
  96.2 12.7 %collective-permute-start.9 = (bf16[24,2592]{1,0:T(8,128)(2,1)S(1)}, bf16[24,2592]{1,0:T(8,128)(2,1)S(1)}, u32[]{:S(2)}, u32[]{:S(2)}) collective-permute-start(bf16[24,2592]{1,0:T(8,128)(2,1)S(1)} %get-tuple-element.56), channel_id=1, source_target_pairs={{0,256},{256,0},{1,257},{257,1},{2,258},{258,2},{3,259},{259,3},{4... | collective-permute-start | bytes 373256 | tf_op jit(solution)/shard_map/ppermute | solution.py:454
  109.8 24.6 %all-to-all-start.4 = ((bf16[32,2,24,128]{3,2,1,0:T(8,128)(2,1)}), bf16[32,2,24,128]{3,2,1,0:T(8,128)(2,1)S(1)}, u32[]{:S(2)}, u32[]{:S(2)}) async-start(bf16[32,2,24,128]{3,2,1,0:T(8,128)(2,1)} %shard_map.121), calls=%async_computation.4 | async-start | bytes 786432 | tf_op jit(solution)/shard_map/all_to_all | solution.py:342

commit v12 on v10

--- a/solution.py
+++ b/solution.py
@@ -360,10 +360,10 @@
     slab_low = shifted(grad, SLAB, SLABS, 1)
     slab_high = shifted(grad, SLAB, SLABS, -1)
     frames = swap(frames, ("zh", "y"))
-    frames, slab_low, slab_high, near, far = lax.optimization_barrier(
-        (frames, slab_low, slab_high, near, far)
-    )
     dev_near = flipped(near)
+    frames, slab_low, slab_high, dev_near, far = lax.optimization_barrier(
+        (frames, slab_low, slab_high, dev_near, far)
+    )
     ups = [(i, i + 1) for i in range(1, DEVS - 1, 2)]
     dev_far = lax.ppermute(far, DEV, ups + [(j, i) for i, j in ups])
     frames = call(repeat_kernel, shape(SLABS, 32, 16, 128), [VMEM])(frames)

time: 139 us -> 137 us (0.986)
  waiting for transfers between devices: 32.8 us -> 28.7 us
  starting transfers between devices: 56.1 us -> 58.2 us
    ppermute x1, starting transfers between devices: 2.83 us -> 5.17 us  [local(): dev_far = lax.ppermute(far, DEV, ups + [(j, i) for i, j in ups])]
    all_to_all x4, waiting for transfers between devices: 27.7 us -> 25.4 us  [swap(): return lax.all_to_all(x, axes, 0, 0, tiled=True)]
    ppermute x2, waiting for transfers between devices: 2.24 us -> 0.01 us  [shifted(): return lax.ppermute(x, axes, pairs)]
  transfers between devices with their start and end apart: 10 -> 10, of which waited for: 7 -> 6; matrix products, arithmetic and copies ran while one was open for 0% -> 0% of each run, Pallas kernels for 10% -> 10%
where the time goes in v12:
time: 137 us; the launch traced here: 136 us
  starting transfers between devices  58.2 us (42%)
  waiting for transfers between devices  28.7 us (21%)
  blocking collectives  27.6 us (20%)
  Pallas kernels  19 us (14%)
  local copies, waits for them, and re-layouts  1.63 us (1%)
    all_to_all x4, starting transfers between devices, swap(): return lax.all_to_all(x, axes, 0, 0, tiled=True)  39.4 us
    all_to_all x4, waiting for transfers between devices, swap(): return lax.all_to_all(x, axes, 0, 0, tiled=True)  25.4 us
    all_to_all x1, blocking collectives, swap(): return lax.all_to_all(x, axes, 0, 0, tiled=True)  18.2 us
    all_gather x2, blocking collectives, local(): term = lax.all_gather(term, 'c', axis=0, tiled=False)  9.44 us
    ppermute x3, starting transfers between devices, flipped(): return lax.ppermute(x, 'c', [(0, 1), (1, 0)])  8.27 us
    pallas_call x1, Pallas kernels, local(): call(conv_kernel, (shape(SLABS, COLS, HALF), shape(SLABS, COLS, HALF), sh...  7.02 us
    ppermute x2, starting transfers between devices, shifted(): return lax.ppermute(x, axes, pairs)  5.28 us
    ppermute x1, starting transfers between devices, local(): dev_far = lax.ppermute(far, DEV, ups + [(j, i) for i, j in ups])  5.17 us
  transfers between devices with their start and end apart: 10, of which 6 were waited for; matrix products, arithmetic and copies ran while one was open for 0% of the time, Pallas kernels for 10%

profile of v12, /device:TPU:1, one launch (start us, length us, event | category | flops | bytes accessed | tf_op | source)
XLA Modules:
  0.0 136.0 jit_solution(11267211497034761454)
XLA Ops:
  0.6 2.2 %shard_map.112 = (bf16[4,4,16,192]{3,2,1,0:T(8,128)(2,1)}, bf16[1,4,16,192]{3,2,1,0:T(8,128)(2,1)}, bf16[1,4,16,192]{3,2,1,0:T(8,128)(2,1)}, bf16[32,16,128]{2,1,0:T(8,128)(2,1)}) custom-call(s32[512]{0:T(512)} %counts_in.5, bf16[4,16,768]{2,1,0:T(8,128)(2,1)} %pre_in.1, bf16[4,16,768]{2,1,0:T(8,128)(2,1)} %cot_in.1, f32[1,192]{1,0:T(1,128)} %bitcast.11, ...), custom_call_target="tpu_custom_call" | custom-call | tf_op jit(solution)/shard_map/pallas_call | solution.py:336
  2.8 16.5 %all-to-all-start = ((bf16[32,16,128]{2,1,0:T(8,128)(2,1)}), bf16[32,16,128]{2,1,0:T(8,128)(2,1)S(1)}, u32[]{:S(2)}, u32[]{:S(2)}) async-start(bf16[32,16,128]{2,1,0:T(8,128)(2,1)} %get-tuple-element.21), calls=%async_computation | async-start | bytes 262144 | tf_op jit(solution)/shard_map/all_to_all | solution.py:329
  19.3 1.3 collective-permute-start.1
  20.6 4.0 %collective-permute-start = (bf16[4,4,16,192]{3,2,1,0:T(8,128)(2,1)}, bf16[4,4,16,192]{3,2,1,0:T(8,128)(2,1)S(1)}, u32[]{:S(2)}, u32[]{:S(2)}) collective-permute-start(bf16[4,4,16,192]{3,2,1,0:T(8,128)(2,1)} %get-tuple-element.22.grad), channel_id=1, source_target_pairs={{0,64},{64,128},{128,192},{192,256},{256,320},{320,384},{384,448},... | collective-permute-start | bytes 294920 | tf_op jit(solution)/shard_map/ppermute | solution.py:355
  24.6 3.4 %collective-permute-start.2 = (bf16[1,4,16,192]{3,2,1,0:T(8,128)(2,1)}, bf16[1,4,16,192]{3,2,1,0:T(8,128)(2,1)S(1)}, u32[]{:S(2)}, u32[]{:S(2)}) collective-permute-start(bf16[1,4,16,192]{3,2,1,0:T(8,128)(2,1)} %get-tuple-element.23), channel_id=1, source_target_pairs={{0,1},{1,0},{2,3},{3,2},{4,5},{5,4},{6,7},{7,6},{8,9},{9,8},{10,11... | collective-permute-start | bytes 73736 | tf_op jit(solution)/shard_map/ppermute | solution.py:358
  28.1 1.0 collective-permute-done.2.dev_near
  29.1 1.8 %all-to-all-done.block = bf16[32,16,128]{2,1,0:T(8,128)(2,1)S(1)} async-done(((bf16[32,16,128]{2,1,0:T(8,128)(2,1)}), bf16[32,16,128]{2,1,0:T(8,128)(2,1)S(1)}, u32[]{:S(2)}, u32[]{:S(2)}) %all-to-all-start) | async-done | bytes 131104 | tf_op jit(solution)/shard_map/all_to_all | solution.py:329
  30.9 1.1 shard_map.113
  32.0 4.9 %all-to-all-start.1 = ((bf16[8,32,16,128]{3,2,1,0:T(8,128)(2,1)}), bf16[8,32,16,128]{3,2,1,0:T(8,128)(2,1)S(1)}, u32[]{:S(2)}, u32[]{:S(2)}) async-start(bf16[8,32,16,128]{3,2,1,0:T(8,128)(2,1)} %shard_map.113), calls=%async_computation.1 | async-start | bytes 2097152 | tf_op jit(solution)/shard_map/all_to_all | solution.py:329
  37.0 5.2 %collective-permute-start.3 = (bf16[1,4,16,192]{3,2,1,0:T(8,128)(2,1)S(1)}, bf16[1,4,16,192]{3,2,1,0:T(8,128)(2,1)S(1)}, u32[]{:S(2)}, u32[]{:S(2)}) collective-permute-start(bf16[1,4,16,192]{3,2,1,0:T(8,128)(2,1)S(1)} %copy-done.7), channel_id=1, source_target_pairs={{1,2},{3,4},{5,6},{7,8},{9,10},{11,12},{13,14},{15,16},{17,18},{19... | collective-permute-start | bytes 73736 | tf_op jit(solution)/shard_map/ppermute | solution.py:368
  42.1 1.9 %collective-permute-done.3.dev_far = bf16[1,4,16,192]{3,2,1,0:T(8,128)(2,1)S(1)} collective-permute-done((bf16[1,4,16,192]{3,2,1,0:T(8,128)(2,1)S(1)}, bf16[1,4,16,192]{3,2,1,0:T(8,128)(2,1)S(1)}, u32[]{:S(2)}, u32[]{:S(2)}) %collective-permute-start.3) | collective-permute-done | bytes 24608 | tf_op jit(solution)/shard_map/ppermute | solution.py:368
  44.6 7.0 %shard_map.114 = (bf16[8,24,2592]{2,1,0:T(8,128)(2,1)}, bf16[8,24,2592]{2,1,0:T(8,128)(2,1)}, bf16[3456,192]{1,0:T(8,128)(2,1)}) custom-call(s32[512]{0:T(512)} %counts_in.5, s32[4,27]{1,0:T(4,128)} %near_in.1, bf16[256,768]{1,0:T(8,128)(2,1)} %fine_in.3, bf16[192,768]{1,0:T(8,128)(2,1)} %bitcast.9, bf16[4,4,16,192]{3,2,1,0:T(8,128)(2,1)} %get-tuple-element.22.grad, ...), custom_call_target="tpu_custom_call" | custom-call | flops 6000000000 | tf_op jit(solution)/shard_map/pallas_call | solution.py:375
  51.7 2.9 %collective-permute-start.4 = (bf16[8,32,16,128]{3,2,1,0:T(8,128)(2,1)S(1)}, bf16[8,32,16,128]{3,2,1,0:T(8,128)(2,1)S(1)}, u32[]{:S(2)}, u32[]{:S(2)}) collective-permute-start(bf16[8,32,16,128]{3,2,1,0:T(8,128)(2,1)S(1)} %all-to-all-done.1.mine), channel_id=1, source_target_pairs={{0,1},{1,0},{2,3},{3,2},{4,5},{5,4},{6,7},{7,6},{8,9},{9,8},{10,11... | collective-permute-start | bytes 3145736 | tf_op jit(solution)/shard_map/ppermute | solution.py:358
  54.6 1.9 %collective-permute-start.5 = (bf16[8,24,2592]{2,1,0:T(8,128)(2,1)}, bf16[8,24,2592]{2,1,0:T(8,128)(2,1)S(1)}, u32[]{:S(2)}, u32[]{:S(2)}) collective-permute-start(bf16[8,24,2592]{2,1,0:T(8,128)(2,1)} %get-tuple-element.36), channel_id=1, source_target_pairs={{0,1},{1,0},{2,3},{3,2},{4,5},{5,4},{6,7},{7,6},{8,9},{9,8},{10,11... | collective-permute-start | bytes 2985992 | tf_op jit(solution)/shard_map/ppermute | solution.py:358
  56.9 1.0 copy-done.4
  57.9 4.6 %shard_map.115 = (bf16[256,192]{1,0:T(8,128)(2,1)}, bf16[2,24,24,128]{3,2,1,0:T(8,128)(2,1)}) custom-call(s32[512]{0:T(512)} %counts_in.5, bf16[256,768]{1,0:T(8,128)(2,1)} %fine_in.3, bf16[3456,192]{1,0:T(8,128)(2,1)} %get-tuple-element.31.taps_in, bf16[8,32,16,128]{3,2,1,0:T(8,128)(2,1)} %copy-done.3, bf16[8,32,16,128]{3,2,1,0:T(8,128)(2,1)} %copy-done.4), custom_call_target="tpu_custom_call" | custom-call | flops 4000000000 | tf_op jit(solution)/shard_map/pallas_call | solution.py:401
  62.5 2.6 %all-gather = bf16[4,24,24,128]{3,2,1,0:T(8,128)(2,1)S(1)} all-gather(bf16[2,24,24,128]{3,2,1,0:T(8,128)(2,1)} %get-tuple-element.34), channel_id=2, replica_groups=mesh['zl'=2,'x'=4,'zh'=4,'y'=8,'c'=2] {'c'}, dimensions={0}, use_global_device_ids=true | all-gather | bytes 884736 | tf_op jit(solution)/shard_map/all_gather | solution.py:430
  65.8 11.4 %all-to-all-start.2 = ((bf16[32,24,128]{2,1,0:T(8,128)(2,1)}), bf16[32,24,128]{2,1,0:T(8,128)(2,1)S(1)}, u32[]{:S(2)}, u32[]{:S(2)}) async-start(bf16[32,24,128]{2,1,0:T(8,128)(2,1)} %shard_map.117), calls=%async_computation.2 | async-start | bytes 393216 | tf_op jit(solution)/shard_map/all_to_all | solution.py:329
  77.2 11.9 %all-to-all-done.2.parts = bf16[32,24,128]{2,1,0:T(8,128)(2,1)S(1)} async-done(((bf16[32,24,128]{2,1,0:T(8,128)(2,1)}), bf16[32,24,128]{2,1,0:T(8,128)(2,1)S(1)}, u32[]{:S(2)}, u32[]{:S(2)}) %all-to-all-start.2) | async-done | bytes 196640 | tf_op jit(solution)/shard_map/all_to_all | solution.py:329
  89.3 18.2 %all_to_all.25.parts = bf16[8,24,2816]{2,1,0:T(8,128)(2,1)S(1)} all-to-all(bf16[8,24,2816]{2,1,0:T(8,128)(2,1)S(1)} %shard_map.118), channel_id=1, replica_groups=mesh['zl'=2,'x'=4,'zh'=4,'y'=8,'c'=2] {'zl','x'}, dimensions={0} | all-to-all | bytes 2162688 | tf_op jit(solution)/shard_map/all_to_all | solution.py:329
  108.5 6.7 %all-to-all-start.4 = ((bf16[32,2,24,128]{3,2,1,0:T(8,128)(2,1)}), bf16[32,2,24,128]{3,2,1,0:T(8,128)(2,1)S(1)}, u32[]{:S(2)}, u32[]{:S(2)}) async-start(bf16[32,2,24,128]{3,2,1,0:T(8,128)(2,1)} %shard_map.119), calls=%async_computation.4 | async-start | bytes 786432 | tf_op jit(solution)/shard_map/all_to_all | solution.py:329
  115.2 1.3 shard_map.116
  116.4 11.8 %all-to-all-done.4 = bf16[32,2,24,128]{3,2,1,0:T(8,128)(2,1)S(1)} async-done(((bf16[32,2,24,128]{3,2,1,0:T(8,128)(2,1)}), bf16[32,2,24,128]{3,2,1,0:T(8,128)(2,1)S(1)}, u32[]{:S(2)}, u32[]{:S(2)}) %all-to-all-start.4) | async-done | bytes 393248 | tf_op jit(solution)/shard_map/all_to_all | solution.py:329
  128.2 6.9 %all-gather.1 = bf16[64,2,24,128]{3,2,1,0:T(8,128)(2,1)S(1)} all-gather(bf16[32,2,24,128]{3,2,1,0:T(8,128)(2,1)S(1)} %all-to-all-done.4), channel_id=3, replica_groups=mesh['zl'=2,'x'=4,'zh'=4,'y'=8,'c'=2] {'c'}, dimensions={0}, use_global_device_ids=true | all-gather | bytes 1179648 | tf_op jit(solution)/shard_map/all_gather | solution.py:439
  (28 shorter events, 3.8 us)
Async XLA Ops:
  2.8 28.1 %all-to-all-start = ((bf16[32,16,128]{2,1,0:T(8,128)(2,1)}), bf16[32,16,128]{2,1,0:T(8,128)(2,1)S(1)}, u32[]{:S(2)}, u32[]{:S(2)}) async-start(bf16[32,16,128]{2,1,0:T(8,128)(2,1)} %get-tuple-element.21), calls=%async_computation | async-start | bytes 262144 | tf_op jit(solution)/shard_map/all_to_all | solution.py:329
  19.3 9.8 %collective-permute-start.1 = (bf16[4,4,16,192]{3,2,1,0:T(8,128)(2,1)}, bf16[4,4,16,192]{3,2,1,0:T(8,128)(2,1)S(1)}, u32[]{:S(2)}, u32[]{:S(2)}) collective-permute-start(bf16[4,4,16,192]{3,2,1,0:T(8,128)(2,1)} %get-tuple-element.22.grad), channel_id=1, source_target_pairs={{64,0},{128,64},{192,128},{256,192},{320,256},{384,320},{448,384},... | collective-permute-start | bytes 294920 | tf_op jit(solution)/shard_map/ppermute | solution.py:355
  20.6 8.5 %collective-permute-start = (bf16[4,4,16,192]{3,2,1,0:T(8,128)(2,1)}, bf16[4,4,16,192]{3,2,1,0:T(8,128)(2,1)S(1)}, u32[]{:S(2)}, u32[]{:S(2)}) collective-permute-start(bf16[4,4,16,192]{3,2,1,0:T(8,128)(2,1)} %get-tuple-element.22.grad), channel_id=1, source_target_pairs={{0,64},{64,128},{128,192},{192,256},{256,320},{320,384},{384,448},... | collective-permute-start | bytes 294920 | tf_op jit(solution)/shard_map/ppermute | solution.py:355
  24.6 4.5 %collective-permute-start.2 = (bf16[1,4,16,192]{3,2,1,0:T(8,128)(2,1)}, bf16[1,4,16,192]{3,2,1,0:T(8,128)(2,1)S(1)}, u32[]{:S(2)}, u32[]{:S(2)}) collective-permute-start(bf16[1,4,16,192]{3,2,1,0:T(8,128)(2,1)} %get-tuple-element.23), channel_id=1, source_target_pairs={{0,1},{1,0},{2,3},{3,2},{4,5},{5,4},{6,7},{7,6},{8,9},{9,8},{10,11... | collective-permute-start | bytes 73736 | tf_op jit(solution)/shard_map/ppermute | solution.py:358
  29.1 2.9 %copy-start.8 = (bf16[1,4,16,192]{3,2,1,0:T(8,128)(2,1)}, bf16[1,4,16,192]{3,2,1,0:T(8,128)(2,1)S(1)}, u32[]{:S(2)}) copy-start(bf16[1,4,16,192]{3,2,1,0:T(8,128)(2,1)S(1)} %collective-permute-done.2.dev_near) | copy-start | bytes 73732
  29.1 2.9 %copy-start.5 = (bf16[4,4,16,192]{3,2,1,0:T(8,128)(2,1)}, bf16[4,4,16,192]{3,2,1,0:T(8,128)(2,1)S(1)}, u32[]{:S(2)}) copy-start(bf16[4,4,16,192]{3,2,1,0:T(8,128)(2,1)S(1)} %collective-permute-done.1.slab_high) | copy-start | bytes 294916
  29.1 2.9 %copy-start.6 = (bf16[4,4,16,192]{3,2,1,0:T(8,128)(2,1)}, bf16[4,4,16,192]{3,2,1,0:T(8,128)(2,1)S(1)}, u32[]{:S(2)}) copy-start(bf16[4,4,16,192]{3,2,1,0:T(8,128)(2,1)S(1)} %collective-permute-done.slab_low) | copy-start | bytes 294916
  32.0 4.9 %copy-start.7 = (bf16[1,4,16,192]{3,2,1,0:T(8,128)(2,1)S(1)}, bf16[1,4,16,192]{3,2,1,0:T(8,128)(2,1)}, u32[]{:S(2)}) copy-start(bf16[1,4,16,192]{3,2,1,0:T(8,128)(2,1)} %get-tuple-element.29) | copy-start | bytes 73732
  32.0 19.6 %all-to-all-start.1 = ((bf16[8,32,16,128]{3,2,1,0:T(8,128)(2,1)}), bf16[8,32,16,128]{3,2,1,0:T(8,128)(2,1)S(1)}, u32[]{:S(2)}, u32[]{:S(2)}) async-start(bf16[8,32,16,128]{3,2,1,0:T(8,128)(2,1)} %shard_map.113), calls=%async_computation.1 | async-start | bytes 2097152 | tf_op jit(solution)/shard_map/all_to_all | solution.py:329
  37.0 7.1 %collective-permute-start.3 = (bf16[1,4,16,192]{3,2,1,0:T(8,128)(2,1)S(1)}, bf16[1,4,16,192]{3,2,1,0:T(8,128)(2,1)S(1)}, u32[]{:S(2)}, u32[]{:S(2)}) collective-permute-start(bf16[1,4,16,192]{3,2,1,0:T(8,128)(2,1)S(1)} %copy-done.7), channel_id=1, source_target_pairs={{1,2},{3,4},{5,6},{7,8},{9,10},{11,12},{13,14},{15,16},{17,18},{19... | collective-permute-start | bytes 73736 | tf_op jit(solution)/shard_map/ppermute | solution.py:368
  44.0 0.6 copy-start.9
  51.7 5.2 %copy-start.3 = (bf16[8,32,16,128]{3,2,1,0:T(8,128)(2,1)}, bf16[8,32,16,128]{3,2,1,0:T(8,128)(2,1)S(1)}, u32[]{:S(2)}) copy-start(bf16[8,32,16,128]{3,2,1,0:T(8,128)(2,1)S(1)} %all-to-all-done.1.mine) | copy-start | bytes 3145732
  51.7 5.2 %collective-permute-start.4 = (bf16[8,32,16,128]{3,2,1,0:T(8,128)(2,1)S(1)}, bf16[8,32,16,128]{3,2,1,0:T(8,128)(2,1)S(1)}, u32[]{:S(2)}, u32[]{:S(2)}) collective-permute-start(bf16[8,32,16,128]{3,2,1,0:T(8,128)(2,1)S(1)} %all-to-all-done.1.mine), channel_id=1, source_target_pairs={{0,1},{1,0},{2,3},{3,2},{4,5},{5,4},{6,7},{7,6},{8,9},{9,8},{10,11... | collective-permute-start | bytes 3145736 | tf_op jit(solution)/shard_map/ppermute | solution.py:358
  54.6 22.6 %collective-permute-start.5 = (bf16[8,24,2592]{2,1,0:T(8,128)(2,1)}, bf16[8,24,2592]{2,1,0:T(8,128)(2,1)S(1)}, u32[]{:S(2)}, u32[]{:S(2)}) collective-permute-start(bf16[8,24,2592]{2,1,0:T(8,128)(2,1)} %get-tuple-element.36), channel_id=1, source_target_pairs={{0,1},{1,0},{2,3},{3,2},{4,5},{5,4},{6,7},{7,6},{8,9},{9,8},{10,11... | collective-permute-start | bytes 2985992 | tf_op jit(solution)/shard_map/ppermute | solution.py:358
  56.9 1.0 copy-start.4
  62.5 26.5 %copy-start = (bf16[8,24,2592]{2,1,0:T(8,128)(2,1)S(1)}, bf16[8,24,2592]{2,1,0:T(8,128)(2,1)}, u32[]{:S(2)}) copy-start(bf16[8,24,2592]{2,1,0:T(8,128)(2,1)} %get-tuple-element.35.keep) | copy-start | bytes 2985988
  65.8 23.2 %all-to-all-start.2 = ((bf16[32,24,128]{2,1,0:T(8,128)(2,1)}), bf16[32,24,128]{2,1,0:T(8,128)(2,1)S(1)}, u32[]{:S(2)}, u32[]{:S(2)}) async-start(bf16[32,24,128]{2,1,0:T(8,128)(2,1)} %shard_map.117), calls=%async_computation.2 | async-start | bytes 393216 | tf_op jit(solution)/shard_map/all_to_all | solution.py:329
  107.5 7.7 %copy-start.1 = (bf16[768,192]{0,1:T(8,128)(2,1)S(1)}, bf16[768,192]{0,1:T(8,128)(2,1)}, u32[]{:S(2)}) copy-start(bf16[768,192]{0,1:T(8,128)(2,1)} %param.10) | copy-start | bytes 884740
  107.5 7.7 %copy-start.2 = (bf16[256,192]{1,0:T(8,128)(2,1)S(1)}, bf16[256,192]{1,0:T(8,128)(2,1)}, u32[]{:S(2)}) copy-start(bf16[256,192]{1,0:T(8,128)(2,1)} %get-tuple-element.33.gm_in) | copy-start | bytes 294916
  108.5 19.8 %all-to-all-start.4 = ((bf16[32,2,24,128]{3,2,1,0:T(8,128)(2,1)}), bf16[32,2,24,128]{3,2,1,0:T(8,128)(2,1)S(1)}, u32[]{:S(2)}, u32[]{:S(2)}) async-start(bf16[32,2,24,128]{3,2,1,0:T(8,128)(2,1)} %shard_map.119), calls=%async_computation.4 | async-start | bytes 786432 | tf_op jit(solution)/shard_map/all_to_all | solution.py:329

commit v13 on v12

--- a/solution.py
+++ b/solution.py
@@ -361,11 +361,11 @@
     slab_high = shifted(grad, SLAB, SLABS, -1)
     frames = swap(frames, ("zh", "y"))
     dev_near = flipped(near)
-    frames, slab_low, slab_high, dev_near, far = lax.optimization_barrier(
-        (frames, slab_low, slab_high, dev_near, far)
-    )
     ups = [(i, i + 1) for i in range(1, DEVS - 1, 2)]
     dev_far = lax.ppermute(far, DEV, ups + [(j, i) for i, j in ups])
+    frames, slab_low, slab_high, dev_near, dev_far = lax.optimization_barrier(
+        (frames, slab_low, slab_high, dev_near, dev_far)
+    )
     frames = call(repeat_kernel, shape(SLABS, 32, 16, 128), [VMEM])(frames)
     frames = swap(frames, SLAB)
 

time: 137 us -> 139 us (1.015)
  waiting for transfers between devices: 28.7 us -> 33.2 us
  blocking collectives: 27.6 us -> 25.6 us
    all_to_all x4, waiting for transfers between devices: 25.4 us -> 30.9 us  [swap(): return lax.all_to_all(x, axes, 0, 0, tiled=True)]
    all_to_all x4, starting transfers between devices: 39.4 us -> 42.3 us  [swap(): return lax.all_to_all(x, axes, 0, 0, tiled=True)]
    all_to_all x1, blocking collectives: 18.2 us -> 16.1 us  [swap(): return lax.all_to_all(x, axes, 0, 0, tiled=True)]
    ppermute x1, starting transfers between devices: 5.17 us -> 3.31 us  [local(): dev_far = lax.ppermute(far, DEV, ups + [(j, i) for i, j in ups])]
  transfers between devices with their start and end apart: 10 -> 10, of which waited for: 6 -> 5; matrix products, arithmetic and copies ran while one was open for 0% -> 0% of each run, Pallas kernels for 10% -> 10%
where the time goes in v13:
time: 139 us; the launch traced here: 138 us
  starting transfers between devices  58.7 us (42%)
  waiting for transfers between devices  33.2 us (24%)
  blocking collectives  25.6 us (18%)
  Pallas kernels  19.1 us (14%)
    all_to_all x4, starting transfers between devices, swap(): return lax.all_to_all(x, axes, 0, 0, tiled=True)  42.3 us
    all_to_all x4, waiting for transfers between devices, swap(): return lax.all_to_all(x, axes, 0, 0, tiled=True)  30.9 us
    all_to_all x1, blocking collectives, swap(): return lax.all_to_all(x, axes, 0, 0, tiled=True)  16.1 us
    all_gather x2, blocking collectives, local(): term = lax.all_gather(term, 'c', axis=0, tiled=False)  9.44 us
    ppermute x3, starting transfers between devices, flipped(): return lax.ppermute(x, 'c', [(0, 1), (1, 0)])  7.74 us
    pallas_call x1, Pallas kernels, local(): call(conv_kernel, (shape(SLABS, COLS, HALF), shape(SLABS, COLS, HALF), sh...  7.02 us
    ppermute x2, starting transfers between devices, shifted(): return lax.ppermute(x, axes, pairs)  5.28 us
    pallas_call x1, Pallas kernels, local(): call(back_kernel, (shape(256, C), shape(2, 24, 24, 128)), [HBM] * 5, [cou...  4.63 us
  transfers between devices with their start and end apart: 10, of which 5 were waited for; matrix products, arithmetic and copies ran while one was open for 0% of the time, Pallas kernels for 10%

profile of v13, /device:TPU:1, one launch (start us, length us, event | category | flops | bytes accessed | tf_op | source)
XLA Modules:
  0.0 138.4 jit_solution(15706849710740451468)
XLA Ops:
  0.6 2.2 %shard_map.112 = (bf16[4,4,16,192]{3,2,1,0:T(8,128)(2,1)}, bf16[1,4,16,192]{3,2,1,0:T(8,128)(2,1)}, bf16[1,4,16,192]{3,2,1,0:T(8,128)(2,1)}, bf16[32,16,128]{2,1,0:T(8,128)(2,1)}) custom-call(s32[512]{0:T(512)} %counts_in.5, bf16[4,16,768]{2,1,0:T(8,128)(2,1)} %pre_in.1, bf16[4,16,768]{2,1,0:T(8,128)(2,1)} %cot_in.1, f32[1,192]{1,0:T(1,128)} %bitcast.11, ...), custom_call_target="tpu_custom_call" | custom-call | tf_op jit(solution)/shard_map/pallas_call | solution.py:336
  2.8 16.5 %all-to-all-start = ((bf16[32,16,128]{2,1,0:T(8,128)(2,1)}), bf16[32,16,128]{2,1,0:T(8,128)(2,1)S(1)}, u32[]{:S(2)}, u32[]{:S(2)}) async-start(bf16[32,16,128]{2,1,0:T(8,128)(2,1)} %get-tuple-element.21), calls=%async_computation | async-start | bytes 262144 | tf_op jit(solution)/shard_map/all_to_all | solution.py:329
  19.3 1.3 collective-permute-start.1
  20.6 4.0 %collective-permute-start = (bf16[4,4,16,192]{3,2,1,0:T(8,128)(2,1)}, bf16[4,4,16,192]{3,2,1,0:T(8,128)(2,1)S(1)}, u32[]{:S(2)}, u32[]{:S(2)}) collective-permute-start(bf16[4,4,16,192]{3,2,1,0:T(8,128)(2,1)} %get-tuple-element.22.grad), channel_id=1, source_target_pairs={{0,64},{64,128},{128,192},{192,256},{256,320},{320,384},{384,448},... | collective-permute-start | bytes 294920 | tf_op jit(solution)/shard_map/ppermute | solution.py:355
  24.6 3.4 %collective-permute-start.2 = (bf16[1,4,16,192]{3,2,1,0:T(8,128)(2,1)}, bf16[1,4,16,192]{3,2,1,0:T(8,128)(2,1)S(1)}, u32[]{:S(2)}, u32[]{:S(2)}) collective-permute-start(bf16[1,4,16,192]{3,2,1,0:T(8,128)(2,1)} %get-tuple-element.23), channel_id=1, source_target_pairs={{0,1},{1,0},{2,3},{3,2},{4,5},{5,4},{6,7},{7,6},{8,9},{9,8},{10,11... | collective-permute-start | bytes 73736 | tf_op jit(solution)/shard_map/ppermute | solution.py:358
  28.1 3.3 %collective-permute-start.3 = (bf16[1,4,16,192]{3,2,1,0:T(8,128)(2,1)}, bf16[1,4,16,192]{3,2,1,0:T(8,128)(2,1)S(1)}, u32[]{:S(2)}, u32[]{:S(2)}) collective-permute-start(bf16[1,4,16,192]{3,2,1,0:T(8,128)(2,1)} %get-tuple-element.24), channel_id=1, source_target_pairs={{1,2},{3,4},{5,6},{7,8},{9,10},{11,12},{13,14},{15,16},{17,18},{19... | collective-permute-start | bytes 73736 | tf_op jit(solution)/shard_map/ppermute | solution.py:365
  31.4 2.1 %collective-permute-done.3.dev_far = bf16[1,4,16,192]{3,2,1,0:T(8,128)(2,1)S(1)} collective-permute-done((bf16[1,4,16,192]{3,2,1,0:T(8,128)(2,1)}, bf16[1,4,16,192]{3,2,1,0:T(8,128)(2,1)S(1)}, u32[]{:S(2)}, u32[]{:S(2)}) %collective-permute-start.3) | collective-permute-done | bytes 24608 | tf_op jit(solution)/shard_map/ppermute | solution.py:365
  33.5 1.1 shard_map.113
  34.7 5.9 %all-to-all-start.1 = ((bf16[8,32,16,128]{3,2,1,0:T(8,128)(2,1)}), bf16[8,32,16,128]{3,2,1,0:T(8,128)(2,1)S(1)}, u32[]{:S(2)}, u32[]{:S(2)}) async-start(bf16[8,32,16,128]{3,2,1,0:T(8,128)(2,1)} %shard_map.113), calls=%async_computation.1 | async-start | bytes 2097152 | tf_op jit(solution)/shard_map/all_to_all | solution.py:329
  40.6 7.0 %shard_map.114 = (bf16[8,24,2592]{2,1,0:T(8,128)(2,1)}, bf16[8,24,2592]{2,1,0:T(8,128)(2,1)}, bf16[3456,192]{1,0:T(8,128)(2,1)}) custom-call(s32[512]{0:T(512)} %counts_in.5, s32[4,27]{1,0:T(4,128)} %near_in.1, bf16[256,768]{1,0:T(8,128)(2,1)} %fine_in.3, bf16[192,768]{1,0:T(8,128)(2,1)} %bitcast.9, bf16[4,4,16,192]{3,2,1,0:T(8,128)(2,1)} %get-tuple-element.22.grad, ...), custom_call_target="tpu_custom_call" | custom-call | flops 6000000000 | tf_op jit(solution)/shard_map/pallas_call | solution.py:375
  47.6 7.3 %all-to-all-done.1.mine = bf16[8,32,16,128]{3,2,1,0:T(8,128)(2,1)S(1)} async-done(((bf16[8,32,16,128]{3,2,1,0:T(8,128)(2,1)}), bf16[8,32,16,128]{3,2,1,0:T(8,128)(2,1)S(1)}, u32[]{:S(2)}, u32[]{:S(2)}) %all-to-all-start.1) | async-done | bytes 1048608 | tf_op jit(solution)/shard_map/all_to_all | solution.py:329
  54.9 2.2 %collective-permute-start.4 = (bf16[8,32,16,128]{3,2,1,0:T(8,128)(2,1)S(1)}, bf16[8,32,16,128]{3,2,1,0:T(8,128)(2,1)S(1)}, u32[]{:S(2)}, u32[]{:S(2)}) collective-permute-start(bf16[8,32,16,128]{3,2,1,0:T(8,128)(2,1)S(1)} %all-to-all-done.1.mine), channel_id=1, source_target_pairs={{0,1},{1,0},{2,3},{3,2},{4,5},{5,4},{6,7},{7,6},{8,9},{9,8},{10,11... | collective-permute-start | bytes 3145736 | tf_op jit(solution)/shard_map/ppermute | solution.py:358
  57.1 2.1 %collective-permute-start.5 = (bf16[8,24,2592]{2,1,0:T(8,128)(2,1)}, bf16[8,24,2592]{2,1,0:T(8,128)(2,1)S(1)}, u32[]{:S(2)}, u32[]{:S(2)}) collective-permute-start(bf16[8,24,2592]{2,1,0:T(8,128)(2,1)} %get-tuple-element.36), channel_id=1, source_target_pairs={{0,1},{1,0},{2,3},{3,2},{4,5},{5,4},{6,7},{7,6},{8,9},{9,8},{10,11... | collective-permute-start | bytes 2985992 | tf_op jit(solution)/shard_map/ppermute | solution.py:358
  59.4 1.0 copy-done.4
  60.4 4.6 %shard_map.115 = (bf16[256,192]{1,0:T(8,128)(2,1)}, bf16[2,24,24,128]{3,2,1,0:T(8,128)(2,1)}) custom-call(s32[512]{0:T(512)} %counts_in.5, bf16[256,768]{1,0:T(8,128)(2,1)} %fine_in.3, bf16[3456,192]{1,0:T(8,128)(2,1)} %get-tuple-element.31.taps_in, bf16[8,32,16,128]{3,2,1,0:T(8,128)(2,1)} %copy-done.3, bf16[8,32,16,128]{3,2,1,0:T(8,128)(2,1)} %copy-done.4), custom_call_target="tpu_custom_call" | custom-call | flops 4000000000 | tf_op jit(solution)/shard_map/pallas_call | solution.py:401
  65.1 2.6 %all-gather = bf16[4,24,24,128]{3,2,1,0:T(8,128)(2,1)S(1)} all-gather(bf16[2,24,24,128]{3,2,1,0:T(8,128)(2,1)} %get-tuple-element.34), channel_id=2, replica_groups=mesh['zl'=2,'x'=4,'zh'=4,'y'=8,'c'=2] {'c'}, dimensions={0}, use_global_device_ids=true | all-gather | bytes 884736 | tf_op jit(solution)/shard_map/all_gather | solution.py:430
  68.3 13.3 %all-to-all-start.2 = ((bf16[32,24,128]{2,1,0:T(8,128)(2,1)}), bf16[32,24,128]{2,1,0:T(8,128)(2,1)S(1)}, u32[]{:S(2)}, u32[]{:S(2)}) async-start(bf16[32,24,128]{2,1,0:T(8,128)(2,1)} %shard_map.117), calls=%async_computation.2 | async-start | bytes 393216 | tf_op jit(solution)/shard_map/all_to_all | solution.py:329
  81.7 11.8 %all-to-all-done.2.parts = bf16[32,24,128]{2,1,0:T(8,128)(2,1)S(1)} async-done(((bf16[32,24,128]{2,1,0:T(8,128)(2,1)}), bf16[32,24,128]{2,1,0:T(8,128)(2,1)S(1)}, u32[]{:S(2)}, u32[]{:S(2)}) %all-to-all-start.2) | async-done | bytes 196640 | tf_op jit(solution)/shard_map/all_to_all | solution.py:329
  93.8 16.1 %all_to_all.25.parts = bf16[8,24,2816]{2,1,0:T(8,128)(2,1)S(1)} all-to-all(bf16[8,24,2816]{2,1,0:T(8,128)(2,1)S(1)} %shard_map.118), channel_id=1, replica_groups=mesh['zl'=2,'x'=4,'zh'=4,'y'=8,'c'=2] {'zl','x'}, dimensions={0} | all-to-all | bytes 2162688 | tf_op jit(solution)/shard_map/all_to_all | solution.py:329
  109.9 1.0 shard_map.119
  110.9 6.7 %all-to-all-start.4 = ((bf16[32,2,24,128]{3,2,1,0:T(8,128)(2,1)}), bf16[32,2,24,128]{3,2,1,0:T(8,128)(2,1)S(1)}, u32[]{:S(2)}, u32[]{:S(2)}) async-start(bf16[32,2,24,128]{3,2,1,0:T(8,128)(2,1)} %shard_map.119), calls=%async_computation.4 | async-start | bytes 786432 | tf_op jit(solution)/shard_map/all_to_all | solution.py:329
  117.6 1.3 shard_map.116
  118.8 11.8 %all-to-all-done.4 = bf16[32,2,24,128]{3,2,1,0:T(8,128)(2,1)S(1)} async-done(((bf16[32,2,24,128]{3,2,1,0:T(8,128)(2,1)}), bf16[32,2,24,128]{3,2,1,0:T(8,128)(2,1)S(1)}, u32[]{:S(2)}, u32[]{:S(2)}) %all-to-all-start.4) | async-done | bytes 393248 | tf_op jit(solution)/shard_map/all_to_all | solution.py:329
  130.6 6.9 %all-gather.1 = bf16[64,2,24,128]{3,2,1,0:T(8,128)(2,1)S(1)} all-gather(bf16[32,2,24,128]{3,2,1,0:T(8,128)(2,1)S(1)} %all-to-all-done.4), channel_id=3, replica_groups=mesh['zl'=2,'x'=4,'zh'=4,'y'=8,'c'=2] {'c'}, dimensions={0}, use_global_device_ids=true | all-gather | bytes 1179648 | tf_op jit(solution)/shard_map/all_gather | solution.py:439
  (26 shorter events, 2.1 us)
Async XLA Ops:
  2.8 30.7 %all-to-all-start = ((bf16[32,16,128]{2,1,0:T(8,128)(2,1)}), bf16[32,16,128]{2,1,0:T(8,128)(2,1)S(1)}, u32[]{:S(2)}, u32[]{:S(2)}) async-start(bf16[32,16,128]{2,1,0:T(8,128)(2,1)} %get-tuple-element.21), calls=%async_computation | async-start | bytes 262144 | tf_op jit(solution)/shard_map/all_to_all | solution.py:329
  19.3 14.2 %collective-permute-start.1 = (bf16[4,4,16,192]{3,2,1,0:T(8,128)(2,1)}, bf16[4,4,16,192]{3,2,1,0:T(8,128)(2,1)S(1)}, u32[]{:S(2)}, u32[]{:S(2)}) collective-permute-start(bf16[4,4,16,192]{3,2,1,0:T(8,128)(2,1)} %get-tuple-element.22.grad), channel_id=1, source_target_pairs={{64,0},{128,64},{192,128},{256,192},{320,256},{384,320},{448,384},... | collective-permute-start | bytes 294920 | tf_op jit(solution)/shard_map/ppermute | solution.py:355
  20.6 12.9 %collective-permute-start = (bf16[4,4,16,192]{3,2,1,0:T(8,128)(2,1)}, bf16[4,4,16,192]{3,2,1,0:T(8,128)(2,1)S(1)}, u32[]{:S(2)}, u32[]{:S(2)}) collective-permute-start(bf16[4,4,16,192]{3,2,1,0:T(8,128)(2,1)} %get-tuple-element.22.grad), channel_id=1, source_target_pairs={{0,64},{64,128},{128,192},{192,256},{256,320},{320,384},{384,448},... | collective-permute-start | bytes 294920 | tf_op jit(solution)/shard_map/ppermute | solution.py:355
  24.6 6.8 %collective-permute-start.2 = (bf16[1,4,16,192]{3,2,1,0:T(8,128)(2,1)}, bf16[1,4,16,192]{3,2,1,0:T(8,128)(2,1)S(1)}, u32[]{:S(2)}, u32[]{:S(2)}) collective-permute-start(bf16[1,4,16,192]{3,2,1,0:T(8,128)(2,1)} %get-tuple-element.23), channel_id=1, source_target_pairs={{0,1},{1,0},{2,3},{3,2},{4,5},{5,4},{6,7},{7,6},{8,9},{9,8},{10,11... | collective-permute-start | bytes 73736 | tf_op jit(solution)/shard_map/ppermute | solution.py:358
  28.1 5.4 %collective-permute-start.3 = (bf16[1,4,16,192]{3,2,1,0:T(8,128)(2,1)}, bf16[1,4,16,192]{3,2,1,0:T(8,128)(2,1)S(1)}, u32[]{:S(2)}, u32[]{:S(2)}) collective-permute-start(bf16[1,4,16,192]{3,2,1,0:T(8,128)(2,1)} %get-tuple-element.24), channel_id=1, source_target_pairs={{1,2},{3,4},{5,6},{7,8},{9,10},{11,12},{13,14},{15,16},{17,18},{19... | collective-permute-start | bytes 73736 | tf_op jit(solution)/shard_map/ppermute | solution.py:365
  31.4 3.3 %copy-start.7 = (bf16[1,4,16,192]{3,2,1,0:T(8,128)(2,1)}, bf16[1,4,16,192]{3,2,1,0:T(8,128)(2,1)S(1)}, u32[]{:S(2)}) copy-start(bf16[1,4,16,192]{3,2,1,0:T(8,128)(2,1)S(1)} %collective-permute-done.2.dev_near) | copy-start | bytes 73732
  33.5 1.2 copy-start.8
  33.5 1.2 copy-start.5
  33.5 1.2 copy-start.6
  34.7 20.2 %all-to-all-start.1 = ((bf16[8,32,16,128]{3,2,1,0:T(8,128)(2,1)}), bf16[8,32,16,128]{3,2,1,0:T(8,128)(2,1)S(1)}, u32[]{:S(2)}, u32[]{:S(2)}) async-start(bf16[8,32,16,128]{3,2,1,0:T(8,128)(2,1)} %shard_map.113), calls=%async_computation.1 | async-start | bytes 2097152 | tf_op jit(solution)/shard_map/all_to_all | solution.py:329
  54.9 4.5 %copy-start.3 = (bf16[8,32,16,128]{3,2,1,0:T(8,128)(2,1)}, bf16[8,32,16,128]{3,2,1,0:T(8,128)(2,1)S(1)}, u32[]{:S(2)}) copy-start(bf16[8,32,16,128]{3,2,1,0:T(8,128)(2,1)S(1)} %all-to-all-done.1.mine) | copy-start | bytes 3145732
  54.9 4.5 %collective-permute-start.4 = (bf16[8,32,16,128]{3,2,1,0:T(8,128)(2,1)S(1)}, bf16[8,32,16,128]{3,2,1,0:T(8,128)(2,1)S(1)}, u32[]{:S(2)}, u32[]{:S(2)}) collective-permute-start(bf16[8,32,16,128]{3,2,1,0:T(8,128)(2,1)S(1)} %all-to-all-done.1.mine), channel_id=1, source_target_pairs={{0,1},{1,0},{2,3},{3,2},{4,5},{5,4},{6,7},{7,6},{8,9},{9,8},{10,11... | collective-permute-start | bytes 3145736 | tf_op jit(solution)/shard_map/ppermute | solution.py:358
  57.1 24.5 %collective-permute-start.5 = (bf16[8,24,2592]{2,1,0:T(8,128)(2,1)}, bf16[8,24,2592]{2,1,0:T(8,128)(2,1)S(1)}, u32[]{:S(2)}, u32[]{:S(2)}) collective-permute-start(bf16[8,24,2592]{2,1,0:T(8,128)(2,1)} %get-tuple-element.36), channel_id=1, source_target_pairs={{0,1},{1,0},{2,3},{3,2},{4,5},{5,4},{6,7},{7,6},{8,9},{9,8},{10,11... | collective-permute-start | bytes 2985992 | tf_op jit(solution)/shard_map/ppermute | solution.py:358
  59.4 1.0 copy-start.4
  65.0 28.5 %copy-start = (bf16[8,24,2592]{2,1,0:T(8,128)(2,1)S(1)}, bf16[8,24,2592]{2,1,0:T(8,128)(2,1)}, u32[]{:S(2)}) copy-start(bf16[8,24,2592]{2,1,0:T(8,128)(2,1)} %get-tuple-element.35.keep) | copy-start | bytes 2985988
  68.3 25.1 %all-to-all-start.2 = ((bf16[32,24,128]{2,1,0:T(8,128)(2,1)}), bf16[32,24,128]{2,1,0:T(8,128)(2,1)S(1)}, u32[]{:S(2)}, u32[]{:S(2)}) async-start(bf16[32,24,128]{2,1,0:T(8,128)(2,1)} %shard_map.117), calls=%async_computation.2 | async-start | bytes 393216 | tf_op jit(solution)/shard_map/all_to_all | solution.py:329
  109.9 7.7 %copy-start.1 = (bf16[768,192]{0,1:T(8,128)(2,1)S(1)}, bf16[768,192]{0,1:T(8,128)(2,1)}, u32[]{:S(2)}) copy-start(bf16[768,192]{0,1:T(8,128)(2,1)} %param.10) | copy-start | bytes 884740
  109.9 7.7 %copy-start.2 = (bf16[256,192]{1,0:T(8,128)(2,1)S(1)}, bf16[256,192]{1,0:T(8,128)(2,1)}, u32[]{:S(2)}) copy-start(bf16[256,192]{1,0:T(8,128)(2,1)} %get-tuple-element.33.gm_in) | copy-start | bytes 294916
  110.9 19.8 %all-to-all-start.4 = ((bf16[32,2,24,128]{3,2,1,0:T(8,128)(2,1)}), bf16[32,2,24,128]{3,2,1,0:T(8,128)(2,1)S(1)}, u32[]{:S(2)}, u32[]{:S(2)}) async-start(bf16[32,2,24,128]{3,2,1,0:T(8,128)(2,1)} %shard_map.119), calls=%async_computation.4 | async-start | bytes 786432 | tf_op jit(solution)/shard_map/all_to_all | solution.py:329

commit v14 on v12

--- a/solution.py
+++ b/solution.py
@@ -132,10 +132,23 @@
     far[0] = grad[jnp.where(core == 0, 0, count - 1)]
 
 
+def merged_kernel(counts_in, fine_in, weight_in, out, counts, fine, weight, sems):
+    copies = fetch(sems, (counts_in, counts), (fine_in, fine), (weight_in, weight))
+    place = my_place()
+    for copy in copies:
+        copy.wait()
+    count = counts[place]
+    merged = lax.dot_general(
+        fine[...], weight[...], (((1,), (1,)), ((), ())), preferred_element_type=F32
+    )
+    brick_of = lax.broadcasted_iota(jnp.int32, (256, C), 0) // 64
+    merged = jnp.where(brick_of < count, merged, 0.0).astype(BF16)
+    out[...] = jnp.transpose(dot(row_order(False), merged)).astype(BF16)
+
+
 def conv_kernel(
-    counts_in, near_in, fine_in, weight_in, grad, slab_low, slab_high, dev_near, dev_far,
-    keep_out, send_out, taps_out, counts, near, fine, weight, sems, bricks, block, total, taps,
-    keep, send,
+    near_in, merged_in, grad, slab_low, slab_high, dev_near, dev_far,
+    keep_out, send_out, taps_out, near, merged, sems, bricks, block, total, taps, keep, send,
 ):
     place = my_place()
     core = jnp.bitwise_and(place, 1)
@@ -143,7 +156,7 @@
         sems, (near_in, near), (grad, bricks.at[0:4]), (slab_low, bricks.at[4:8]),
         (slab_high, bricks.at[8:12]), (dev_near, bricks.at[pl.ds(13 - core, 1)]),
         (dev_far, bricks.at[pl.ds(12 + core, 1)]),
-        (counts_in, counts), (fine_in, fine), (weight_in, weight),
+        (merged_in, merged),
     )
     bricks[14:15] = jnp.zeros((1, 4, 16, C), BF16)
     window = window_matrix()
@@ -174,16 +187,9 @@
     leave[0].start()
     for copy in copies[6:]:
         copy.wait()
-    count = counts[place]
-    merged = lax.dot_general(
-        fine[...], weight[...], (((1,), (1,)), ((), ())), preferred_element_type=F32
-    )
-    brick_of = lax.broadcasted_iota(jnp.int32, (256, C), 0) // 64
-    merged = jnp.where(brick_of < count, merged, 0.0).astype(BF16)
-    merged = jnp.transpose(dot(row_order(False), merged)).astype(BF16)
     for tap in range(27):
         row = tap_rows(tap)
-        term = dot(merged, taps[row : row + 256])
+        term = dot(merged[...], taps[row : row + 256])
         at = tap * C
         end = at + C
         while at < end:
@@ -372,15 +378,21 @@
     fine_scratch = pltpu.VMEM((256, 768), BF16)
     weight_scratch = pltpu.VMEM((C, 768), BF16)
     merge_weight = merge_weight.T
+    merged = call(
+        merged_kernel,
+        shape(C, 256),
+        [HBM] * 3,
+        [counts_scratch, fine_scratch, weight_scratch, pltpu.SemaphoreType.DMA((3,))],
+        flops=10**9,
+        vmem=60,
+    )(counts, fine_input, merge_weight)
     keep, send, taps = call(
         conv_kernel,
         (shape(SLABS, COLS, HALF), shape(SLABS, COLS, HALF), shape(3456, C)),
-        [HBM] * 9,
+        [HBM] * 7,
         [
-            counts_scratch,
             pltpu.SMEM((B, 27), jnp.int32),
-            fine_scratch,
-            weight_scratch,
+            pltpu.VMEM((C, 256), BF16),
             pltpu.SemaphoreType.DMA((12,)),
             pltpu.VMEM((15, 4, 16, C), BF16),
             pltpu.VMEM((6, 144, C), BF16),
@@ -393,7 +405,7 @@
         out_spec=(HBM, HBM, HBM),
         vmem=60,
     )(
-        counts, neighbours, fine_input, merge_weight, grad, slab_low, slab_high, dev_near, dev_far
+        neighbours, merged, grad, slab_low, slab_high, dev_near, dev_far
     )
 
     frames, taps = lax.optimization_barrier((frames, taps))

time: 137 us -> 136 us (level)
  waiting for transfers between devices: 28.7 us -> 26.8 us
  Pallas kernels: 19 us -> 20.8 us
    pallas_call x0 -> x1, Pallas kernels: none -> 2.32 us  [local(): call(merged_kernel, shape(C, 256), [HBM] * 3, [counts_scratch, fine_scrat...]
    ppermute x1, waiting for transfers between devices: 1.88 us -> 0.01 us  [local(): dev_far = lax.ppermute(far, DEV, ups + [(j, i) for i, j in ups])]
  transfers between devices with their start and end apart: 10 -> 10, of which waited for: 6 -> 5; matrix products, arithmetic and copies ran while one was open for 0% -> 0% of each run, Pallas kernels for 10% -> 11%
where the time goes in v14:
time: 136 us; the launch traced here: 135 us
  starting transfers between devices  58.1 us (43%)
  blocking collectives  27.3 us (20%)
  waiting for transfers between devices  26.8 us (20%)
  Pallas kernels  20.8 us (15%)
  local copies, waits for them, and re-layouts  1.61 us (1%)
    all_to_all x4, starting transfers between devices, swap(): return lax.all_to_all(x, axes, 0, 0, tiled=True)  39.2 us
    all_to_all x4, waiting for transfers between devices, swap(): return lax.all_to_all(x, axes, 0, 0, tiled=True)  25.4 us
    all_to_all x1, blocking collectives, swap(): return lax.all_to_all(x, axes, 0, 0, tiled=True)  17.8 us
    all_gather x2, blocking collectives, local(): term = lax.all_gather(term, 'c', axis=0, tiled=False)  9.44 us
    ppermute x3, starting transfers between devices, flipped(): return lax.ppermute(x, 'c', [(0, 1), (1, 0)])  8.41 us
    pallas_call x1, Pallas kernels, local(): call(conv_kernel, (shape(SLABS, COLS, HALF), shape(SLABS, COLS, HALF), sh...  6.43 us
    ppermute x2, starting transfers between devices, shifted(): return lax.ppermute(x, axes, pairs)  5.28 us
    ppermute x1, starting transfers between devices, local(): dev_far = lax.ppermute(far, DEV, ups + [(j, i) for i, j in ups])  5.17 us
  transfers between devices with their start and end apart: 10, of which 5 were waited for; matrix products, arithmetic and copies ran while one was open for 0% of the time, Pallas kernels for 11%

profile of v14, /device:TPU:1, one launch (start us, length us, event | category | flops | bytes accessed | tf_op | source)
XLA Modules:
  0.0 135.3 jit_solution(11065536923088629464)
XLA Ops:
  0.6 2.2 %shard_map.112 = (bf16[4,4,16,192]{3,2,1,0:T(8,128)(2,1)}, bf16[1,4,16,192]{3,2,1,0:T(8,128)(2,1)}, bf16[1,4,16,192]{3,2,1,0:T(8,128)(2,1)}, bf16[32,16,128]{2,1,0:T(8,128)(2,1)}) custom-call(s32[512]{0:T(512)} %counts_in.5, bf16[4,16,768]{2,1,0:T(8,128)(2,1)} %pre_in.1, bf16[4,16,768]{2,1,0:T(8,128)(2,1)} %cot_in.1, f32[1,192]{1,0:T(1,128)} %bitcast.11, ...), custom_call_target="tpu_custom_call" | custom-call | tf_op jit(solution)/shard_map/pallas_call | solution.py:342
  2.8 16.5 %all-to-all-start = ((bf16[32,16,128]{2,1,0:T(8,128)(2,1)}), bf16[32,16,128]{2,1,0:T(8,128)(2,1)S(1)}, u32[]{:S(2)}, u32[]{:S(2)}) async-start(bf16[32,16,128]{2,1,0:T(8,128)(2,1)} %get-tuple-element.21), calls=%async_computation | async-start | bytes 262144 | tf_op jit(solution)/shard_map/all_to_all | solution.py:335
  19.3 1.3 collective-permute-start.1
  20.6 4.0 %collective-permute-start = (bf16[4,4,16,192]{3,2,1,0:T(8,128)(2,1)}, bf16[4,4,16,192]{3,2,1,0:T(8,128)(2,1)S(1)}, u32[]{:S(2)}, u32[]{:S(2)}) collective-permute-start(bf16[4,4,16,192]{3,2,1,0:T(8,128)(2,1)} %get-tuple-element.22.grad), channel_id=1, source_target_pairs={{0,64},{64,128},{128,192},{192,256},{256,320},{320,384},{384,448},... | collective-permute-start | bytes 294920 | tf_op jit(solution)/shard_map/ppermute | solution.py:361
  24.6 3.4 %collective-permute-start.2 = (bf16[1,4,16,192]{3,2,1,0:T(8,128)(2,1)}, bf16[1,4,16,192]{3,2,1,0:T(8,128)(2,1)S(1)}, u32[]{:S(2)}, u32[]{:S(2)}) collective-permute-start(bf16[1,4,16,192]{3,2,1,0:T(8,128)(2,1)} %get-tuple-element.23), channel_id=1, source_target_pairs={{0,1},{1,0},{2,3},{3,2},{4,5},{5,4},{6,7},{7,6},{8,9},{9,8},{10,11... | collective-permute-start | bytes 73736 | tf_op jit(solution)/shard_map/ppermute | solution.py:364
  28.1 1.0 collective-permute-done.2.dev_near
  29.1 1.8 %all-to-all-done.block = bf16[32,16,128]{2,1,0:T(8,128)(2,1)S(1)} async-done(((bf16[32,16,128]{2,1,0:T(8,128)(2,1)}), bf16[32,16,128]{2,1,0:T(8,128)(2,1)S(1)}, u32[]{:S(2)}, u32[]{:S(2)}) %all-to-all-start) | async-done | bytes 131104 | tf_op jit(solution)/shard_map/all_to_all | solution.py:335
  30.9 1.1 shard_map.113
  32.0 4.9 %all-to-all-start.1 = ((bf16[8,32,16,128]{3,2,1,0:T(8,128)(2,1)}), bf16[8,32,16,128]{3,2,1,0:T(8,128)(2,1)S(1)}, u32[]{:S(2)}, u32[]{:S(2)}) async-start(bf16[8,32,16,128]{3,2,1,0:T(8,128)(2,1)} %shard_map.113), calls=%async_computation.1 | async-start | bytes 2097152 | tf_op jit(solution)/shard_map/all_to_all | solution.py:335
  37.0 5.2 %collective-permute-start.3 = (bf16[1,4,16,192]{3,2,1,0:T(8,128)(2,1)S(1)}, bf16[1,4,16,192]{3,2,1,0:T(8,128)(2,1)S(1)}, u32[]{:S(2)}, u32[]{:S(2)}) collective-permute-start(bf16[1,4,16,192]{3,2,1,0:T(8,128)(2,1)S(1)} %copy-done.7), channel_id=1, source_target_pairs={{1,2},{3,4},{5,6},{7,8},{9,10},{11,12},{13,14},{15,16},{17,18},{19... | collective-permute-start | bytes 73736 | tf_op jit(solution)/shard_map/ppermute | solution.py:374
  42.1 2.3 %shard_map.114.merged_in = bf16[192,256]{1,0:T(8,128)(2,1)} custom-call(s32[512]{0:T(512)} %counts_in.5, bf16[256,768]{1,0:T(8,128)(2,1)} %fine_in.3, bf16[192,768]{1,0:T(8,128)(2,1)} %bitcast.9), custom_call_target="tpu_custom_call" | custom-call | flops 1000000000 | tf_op jit(solution)/shard_map/pallas_call | solution.py:381
  45.1 6.4 %shard_map.115 = (bf16[8,24,2592]{2,1,0:T(8,128)(2,1)}, bf16[8,24,2592]{2,1,0:T(8,128)(2,1)}, bf16[3456,192]{1,0:T(8,128)(2,1)}) custom-call(s32[4,27]{1,0:T(4,128)} %near_in.1, bf16[192,256]{1,0:T(8,128)(2,1)} %shard_map.114.merged_in, bf16[4,4,16,192]{3,2,1,0:T(8,128)(2,1)} %get-tuple-element.22.grad, bf16[4,4,16,192]{3,2,1,0:T(8,128)(2,1)} %copy-done.6, ...), custom_call_target="tpu_custom_call" | custom-call | flops 6000000000 | tf_op jit(solution)/shard_map/pallas_call | solution.py:389
  51.5 3.1 %collective-permute-start.4 = (bf16[8,32,16,128]{3,2,1,0:T(8,128)(2,1)S(1)}, bf16[8,32,16,128]{3,2,1,0:T(8,128)(2,1)S(1)}, u32[]{:S(2)}, u32[]{:S(2)}) collective-permute-start(bf16[8,32,16,128]{3,2,1,0:T(8,128)(2,1)S(1)} %all-to-all-done.1.mine), channel_id=1, source_target_pairs={{0,1},{1,0},{2,3},{3,2},{4,5},{5,4},{6,7},{7,6},{8,9},{9,8},{10,11... | collective-permute-start | bytes 3145736 | tf_op jit(solution)/shard_map/ppermute | solution.py:364
  54.6 1.9 %collective-permute-start.5 = (bf16[8,24,2592]{2,1,0:T(8,128)(2,1)}, bf16[8,24,2592]{2,1,0:T(8,128)(2,1)S(1)}, u32[]{:S(2)}, u32[]{:S(2)}) collective-permute-start(bf16[8,24,2592]{2,1,0:T(8,128)(2,1)} %get-tuple-element.36), channel_id=1, source_target_pairs={{0,1},{1,0},{2,3},{3,2},{4,5},{5,4},{6,7},{7,6},{8,9},{9,8},{10,11... | collective-permute-start | bytes 2985992 | tf_op jit(solution)/shard_map/ppermute | solution.py:364
  56.9 1.0 copy-done.4
  57.9 4.6 %shard_map.116 = (bf16[256,192]{1,0:T(8,128)(2,1)}, bf16[2,24,24,128]{3,2,1,0:T(8,128)(2,1)}) custom-call(s32[512]{0:T(512)} %counts_in.5, bf16[256,768]{1,0:T(8,128)(2,1)} %fine_in.3, bf16[3456,192]{1,0:T(8,128)(2,1)} %get-tuple-element.31.taps_in, bf16[8,32,16,128]{3,2,1,0:T(8,128)(2,1)} %copy-done.3, bf16[8,32,16,128]{3,2,1,0:T(8,128)(2,1)} %copy-done.4), custom_call_target="tpu_custom_call" | custom-call | flops 4000000000 | tf_op jit(solution)/shard_map/pallas_call | solution.py:413
  62.5 2.6 %all-gather = bf16[4,24,24,128]{3,2,1,0:T(8,128)(2,1)S(1)} all-gather(bf16[2,24,24,128]{3,2,1,0:T(8,128)(2,1)} %get-tuple-element.34), channel_id=2, replica_groups=mesh['zl'=2,'x'=4,'zh'=4,'y'=8,'c'=2] {'c'}, dimensions={0}, use_global_device_ids=true | all-gather | bytes 884736 | tf_op jit(solution)/shard_map/all_gather | solution.py:442
  65.8 11.1 %all-to-all-start.2 = ((bf16[32,24,128]{2,1,0:T(8,128)(2,1)}), bf16[32,24,128]{2,1,0:T(8,128)(2,1)S(1)}, u32[]{:S(2)}, u32[]{:S(2)}) async-start(bf16[32,24,128]{2,1,0:T(8,128)(2,1)} %shard_map.118), calls=%async_computation.2 | async-start | bytes 393216 | tf_op jit(solution)/shard_map/all_to_all | solution.py:335
  76.9 11.8 %all-to-all-done.2.parts = bf16[32,24,128]{2,1,0:T(8,128)(2,1)S(1)} async-done(((bf16[32,24,128]{2,1,0:T(8,128)(2,1)}), bf16[32,24,128]{2,1,0:T(8,128)(2,1)S(1)}, u32[]{:S(2)}, u32[]{:S(2)}) %all-to-all-start.2) | async-done | bytes 196640 | tf_op jit(solution)/shard_map/all_to_all | solution.py:335
  89.0 17.8 %all_to_all.25.parts = bf16[8,24,2816]{2,1,0:T(8,128)(2,1)S(1)} all-to-all(bf16[8,24,2816]{2,1,0:T(8,128)(2,1)S(1)} %shard_map.119), channel_id=1, replica_groups=mesh['zl'=2,'x'=4,'zh'=4,'y'=8,'c'=2] {'zl','x'}, dimensions={0} | all-to-all | bytes 2162688 | tf_op jit(solution)/shard_map/all_to_all | solution.py:335
  107.9 6.7 %all-to-all-start.4 = ((bf16[32,2,24,128]{3,2,1,0:T(8,128)(2,1)}), bf16[32,2,24,128]{3,2,1,0:T(8,128)(2,1)S(1)}, u32[]{:S(2)}, u32[]{:S(2)}) async-start(bf16[32,2,24,128]{3,2,1,0:T(8,128)(2,1)} %shard_map.120), calls=%async_computation.4 | async-start | bytes 786432 | tf_op jit(solution)/shard_map/all_to_all | solution.py:335
  114.5 1.3 shard_map.117
  115.8 11.8 %all-to-all-done.4 = bf16[32,2,24,128]{3,2,1,0:T(8,128)(2,1)S(1)} async-done(((bf16[32,2,24,128]{3,2,1,0:T(8,128)(2,1)}), bf16[32,2,24,128]{3,2,1,0:T(8,128)(2,1)S(1)}, u32[]{:S(2)}, u32[]{:S(2)}) %all-to-all-start.4) | async-done | bytes 393248 | tf_op jit(solution)/shard_map/all_to_all | solution.py:335
  127.6 6.9 %all-gather.1 = bf16[64,2,24,128]{3,2,1,0:T(8,128)(2,1)S(1)} all-gather(bf16[32,2,24,128]{3,2,1,0:T(8,128)(2,1)S(1)} %all-to-all-done.4), channel_id=3, replica_groups=mesh['zl'=2,'x'=4,'zh'=4,'y'=8,'c'=2] {'c'}, dimensions={0}, use_global_device_ids=true | all-gather | bytes 1179648 | tf_op jit(solution)/shard_map/all_gather | solution.py:451
  (29 shorter events, 3.8 us)
Async XLA Ops:
  2.8 28.1 %all-to-all-start = ((bf16[32,16,128]{2,1,0:T(8,128)(2,1)}), bf16[32,16,128]{2,1,0:T(8,128)(2,1)S(1)}, u32[]{:S(2)}, u32[]{:S(2)}) async-start(bf16[32,16,128]{2,1,0:T(8,128)(2,1)} %get-tuple-element.21), calls=%async_computation | async-start | bytes 262144 | tf_op jit(solution)/shard_map/all_to_all | solution.py:335
  19.3 9.8 %collective-permute-start.1 = (bf16[4,4,16,192]{3,2,1,0:T(8,128)(2,1)}, bf16[4,4,16,192]{3,2,1,0:T(8,128)(2,1)S(1)}, u32[]{:S(2)}, u32[]{:S(2)}) collective-permute-start(bf16[4,4,16,192]{3,2,1,0:T(8,128)(2,1)} %get-tuple-element.22.grad), channel_id=1, source_target_pairs={{64,0},{128,64},{192,128},{256,192},{320,256},{384,320},{448,384},... | collective-permute-start | bytes 294920 | tf_op jit(solution)/shard_map/ppermute | solution.py:361
  20.6 8.5 %collective-permute-start = (bf16[4,4,16,192]{3,2,1,0:T(8,128)(2,1)}, bf16[4,4,16,192]{3,2,1,0:T(8,128)(2,1)S(1)}, u32[]{:S(2)}, u32[]{:S(2)}) collective-permute-start(bf16[4,4,16,192]{3,2,1,0:T(8,128)(2,1)} %get-tuple-element.22.grad), channel_id=1, source_target_pairs={{0,64},{64,128},{128,192},{192,256},{256,320},{320,384},{384,448},... | collective-permute-start | bytes 294920 | tf_op jit(solution)/shard_map/ppermute | solution.py:361
  24.6 4.5 %collective-permute-start.2 = (bf16[1,4,16,192]{3,2,1,0:T(8,128)(2,1)}, bf16[1,4,16,192]{3,2,1,0:T(8,128)(2,1)S(1)}, u32[]{:S(2)}, u32[]{:S(2)}) collective-permute-start(bf16[1,4,16,192]{3,2,1,0:T(8,128)(2,1)} %get-tuple-element.23), channel_id=1, source_target_pairs={{0,1},{1,0},{2,3},{3,2},{4,5},{5,4},{6,7},{7,6},{8,9},{9,8},{10,11... | collective-permute-start | bytes 73736 | tf_op jit(solution)/shard_map/ppermute | solution.py:364
  29.1 2.9 %copy-start.8 = (bf16[1,4,16,192]{3,2,1,0:T(8,128)(2,1)}, bf16[1,4,16,192]{3,2,1,0:T(8,128)(2,1)S(1)}, u32[]{:S(2)}) copy-start(bf16[1,4,16,192]{3,2,1,0:T(8,128)(2,1)S(1)} %collective-permute-done.2.dev_near) | copy-start | bytes 73732
  29.1 2.9 %copy-start.5 = (bf16[4,4,16,192]{3,2,1,0:T(8,128)(2,1)}, bf16[4,4,16,192]{3,2,1,0:T(8,128)(2,1)S(1)}, u32[]{:S(2)}) copy-start(bf16[4,4,16,192]{3,2,1,0:T(8,128)(2,1)S(1)} %collective-permute-done.1.slab_high) | copy-start | bytes 294916
  29.1 2.9 %copy-start.6 = (bf16[4,4,16,192]{3,2,1,0:T(8,128)(2,1)}, bf16[4,4,16,192]{3,2,1,0:T(8,128)(2,1)S(1)}, u32[]{:S(2)}) copy-start(bf16[4,4,16,192]{3,2,1,0:T(8,128)(2,1)S(1)} %collective-permute-done.slab_low) | copy-start | bytes 294916
  32.0 4.9 %copy-start.7 = (bf16[1,4,16,192]{3,2,1,0:T(8,128)(2,1)S(1)}, bf16[1,4,16,192]{3,2,1,0:T(8,128)(2,1)}, u32[]{:S(2)}) copy-start(bf16[1,4,16,192]{3,2,1,0:T(8,128)(2,1)} %get-tuple-element.29) | copy-start | bytes 73732
  32.0 19.5 %all-to-all-start.1 = ((bf16[8,32,16,128]{3,2,1,0:T(8,128)(2,1)}), bf16[8,32,16,128]{3,2,1,0:T(8,128)(2,1)S(1)}, u32[]{:S(2)}, u32[]{:S(2)}) async-start(bf16[8,32,16,128]{3,2,1,0:T(8,128)(2,1)} %shard_map.113), calls=%async_computation.1 | async-start | bytes 2097152 | tf_op jit(solution)/shard_map/all_to_all | solution.py:335
  37.0 7.5 %collective-permute-start.3 = (bf16[1,4,16,192]{3,2,1,0:T(8,128)(2,1)S(1)}, bf16[1,4,16,192]{3,2,1,0:T(8,128)(2,1)S(1)}, u32[]{:S(2)}, u32[]{:S(2)}) collective-permute-start(bf16[1,4,16,192]{3,2,1,0:T(8,128)(2,1)S(1)} %copy-done.7), channel_id=1, source_target_pairs={{1,2},{3,4},{5,6},{7,8},{9,10},{11,12},{13,14},{15,16},{17,18},{19... | collective-permute-start | bytes 73736 | tf_op jit(solution)/shard_map/ppermute | solution.py:374
  44.5 0.6 copy-start.9
  51.5 5.4 %copy-start.3 = (bf16[8,32,16,128]{3,2,1,0:T(8,128)(2,1)}, bf16[8,32,16,128]{3,2,1,0:T(8,128)(2,1)S(1)}, u32[]{:S(2)}) copy-start(bf16[8,32,16,128]{3,2,1,0:T(8,128)(2,1)S(1)} %all-to-all-done.1.mine) | copy-start | bytes 3145732
  51.5 5.3 %collective-permute-start.4 = (bf16[8,32,16,128]{3,2,1,0:T(8,128)(2,1)S(1)}, bf16[8,32,16,128]{3,2,1,0:T(8,128)(2,1)S(1)}, u32[]{:S(2)}, u32[]{:S(2)}) collective-permute-start(bf16[8,32,16,128]{3,2,1,0:T(8,128)(2,1)S(1)} %all-to-all-done.1.mine), channel_id=1, source_target_pairs={{0,1},{1,0},{2,3},{3,2},{4,5},{5,4},{6,7},{7,6},{8,9},{9,8},{10,11... | collective-permute-start | bytes 3145736 | tf_op jit(solution)/shard_map/ppermute | solution.py:364
  54.6 22.3 %collective-permute-start.5 = (bf16[8,24,2592]{2,1,0:T(8,128)(2,1)}, bf16[8,24,2592]{2,1,0:T(8,128)(2,1)S(1)}, u32[]{:S(2)}, u32[]{:S(2)}) collective-permute-start(bf16[8,24,2592]{2,1,0:T(8,128)(2,1)} %get-tuple-element.36), channel_id=1, source_target_pairs={{0,1},{1,0},{2,3},{3,2},{4,5},{5,4},{6,7},{7,6},{8,9},{9,8},{10,11... | collective-permute-start | bytes 2985992 | tf_op jit(solution)/shard_map/ppermute | solution.py:364
  56.9 1.0 copy-start.4
  62.5 26.3 %copy-start = (bf16[8,24,2592]{2,1,0:T(8,128)(2,1)S(1)}, bf16[8,24,2592]{2,1,0:T(8,128)(2,1)}, u32[]{:S(2)}) copy-start(bf16[8,24,2592]{2,1,0:T(8,128)(2,1)} %get-tuple-element.35.keep) | copy-start | bytes 2985988
  65.8 22.9 %all-to-all-start.2 = ((bf16[32,24,128]{2,1,0:T(8,128)(2,1)}), bf16[32,24,128]{2,1,0:T(8,128)(2,1)S(1)}, u32[]{:S(2)}, u32[]{:S(2)}) async-start(bf16[32,24,128]{2,1,0:T(8,128)(2,1)} %shard_map.118), calls=%async_computation.2 | async-start | bytes 393216 | tf_op jit(solution)/shard_map/all_to_all | solution.py:335
  106.9 7.7 %copy-start.1 = (bf16[768,192]{0,1:T(8,128)(2,1)S(1)}, bf16[768,192]{0,1:T(8,128)(2,1)}, u32[]{:S(2)}) copy-start(bf16[768,192]{0,1:T(8,128)(2,1)} %param.10) | copy-start | bytes 884740
  106.9 7.7 %copy-start.2 = (bf16[256,192]{1,0:T(8,128)(2,1)S(1)}, bf16[256,192]{1,0:T(8,128)(2,1)}, u32[]{:S(2)}) copy-start(bf16[256,192]{1,0:T(8,128)(2,1)} %get-tuple-element.33.gm_in) | copy-start | bytes 294916
  107.9 19.8 %all-to-all-start.4 = ((bf16[32,2,24,128]{3,2,1,0:T(8,128)(2,1)}), bf16[32,2,24,128]{3,2,1,0:T(8,128)(2,1)S(1)}, u32[]{:S(2)}, u32[]{:S(2)}) async-start(bf16[32,2,24,128]{3,2,1,0:T(8,128)(2,1)} %shard_map.120), calls=%async_computation.4 | async-start | bytes 786432 | tf_op jit(solution)/shard_map/all_to_all | solution.py:335
